TPU v7x, 128 devices: a whole 4x4x4 slice. The times are simulated.
128 devices in a mesh: gx: 8 (over z, core), gy: 4 (over y), gz: 4 (over x).
Axes of the slice: x: 4, y: 4, z: 4, core: 2. Of those that a mesh axis runs over, the one named last changes fastest.
Arguments:
- features: bfloat16 [256, 64, 64, 128], P('gx', 'gy', 'gz'), may hold values from -6 to 6
- occupancy: int32 [32, 8, 8], P('gx', 'gy', 'gz'), may hold values from 0 to 1, as said below
- weight: bfloat16 [3, 3, 3, 128, 128], replicated, may hold values from -0.109375 to 0.109375
- cotangent: bfloat16 [256, 64, 64, 128], P('gx', 'gy', 'gz'), may hold values from -6 to 6
Outputs:
- outputs: bfloat16 [256, 64, 64, 128], P('gx', 'gy', 'gz')
- input_grad: bfloat16 [256, 64, 64, 128], P('gx', 'gy', 'gz')
- weight_grad: float32 [3, 3, 3, 128, 128], replicated
Inputs may be any that keep to these rules, and one draw needn't show every extreme that they name: `occupancy`: in every plane of devices that share a gx index, the regions of the 16 devices hold 16, 16, 12, 12, 10, 10, 8, 8, 8, 6, 6, 4, 4, 3, 3 and 2 occupied bricks, in an order drawn from the seed; so each plane holds exactly 128 occupied bricks and some device holds 16. Which bricks of a region are occupied is drawn from the seed.
All inputs are finite; a program needn't handle non-finite values.
Results may differ from a plain program's by a relative error of at most 0.001.
Values may be sent and summed in bfloat16 or wider, within the bound.
No kernel may reach another device: no remote copies, remote signals or barrier semaphores. Data moves between devices by JAX's collectives and lax.ppermute only.
A program may use at most 128 MiB of HBM per device.

v0:
```python
import math

import jax
import jax.numpy as jnp
from jax import lax
from jax.experimental import pallas as pl
from jax.experimental.pallas import tpu as pltpu
from jax.sharding import PartitionSpec as P

SHARE = 8
X, Y, Z, C = 32, 16, 16, 128
E = 8
ROWS = Y * Z
GROUP = 4
TAPS = 9 * C
WIDE = 3 * C
HALF = 14
F32 = jnp.float32
BF16 = jnp.bfloat16
VMEM = pl.BlockSpec(memory_space=pltpu.VMEM)
SMEM = pl.BlockSpec(memory_space=pltpu.SMEM)
ANY = pl.BlockSpec(memory_space=pl.ANY)
DEPTH_FIRST = (((0,), (0,)), ((), ()))


def shape(dims, dtype):
    return jax.ShapeDtypeStruct(dims, dtype)


def params(mebibytes=24):
    return pltpu.CompilerParams(vmem_limit_bytes=mebibytes * 1024 * 1024)


def cost(slabs, moved):
    return pl.CostEstimate(flops=2 * 27 * C * C * slabs * ROWS, bytes_accessed=moved, transcendentals=0)


def inside(axis, side):
    at = lax.axis_index(axis)
    return at > 0 if side == 0 else at < lax.axis_size(axis) - 1


def held(value, axis, side):
    return jnp.where(inside(axis, side), value, jnp.zeros_like(value))


def brick_flags(occ_ref, brick):
    low_z = lax.broadcasted_iota(jnp.int32, (E, Z, C), 1) < E
    halves = [jnp.where(low_z, occ_ref[brick, j, 0], occ_ref[brick, j, 1]) for j in range(2)]
    return jnp.concatenate(halves, axis=0) == 1


def prepare_kernel(occ_ref, f_ref, c_ref, s_ref, zlo_ref, zhi_ref, ylo_ref, yhi_ref):
    for end in (0, X + 1):
        s_ref[:, end] = jnp.zeros((2, Y, Z, C), BF16)
    for brick in range(X // E):
        keep = brick_flags(occ_ref, brick)
        span = slice(brick * E, (brick + 1) * E)
        for part, ref in enumerate((f_ref, c_ref)):
            value = jnp.where(keep[None], ref[span].astype(F32), 0.0).astype(BF16)
            s_ref[part, brick * E + 1 : (brick + 1) * E + 1] = value
            zlo_ref[part, span] = value[:, :, 0, :]
            zhi_ref[part, span] = value[:, :, Z - 1, :]
            ylo_ref[part, span] = value[:, 0]
            yhi_ref[part, span] = value[:, Y - 1]


def prepare(occupancy, features, cotangent):
    return pl.pallas_call(
        prepare_kernel,
        in_specs=[SMEM, VMEM, VMEM],
        out_specs=[VMEM] * 5,
        out_shape=[shape((2, X + 2, Y, Z, C), BF16)] + [shape((2, X, Z, C), BF16)] * 4,
        compiler_params=params(),
        cost_estimate=pl.CostEstimate(flops=1000000, bytes_accessed=9 << 20, transcendentals=0),
    )(occupancy, features, cotangent)


def moved_z(whole, step):
    rows = whole.shape[0] * whole.shape[1]
    flat = whole.reshape(rows, C)
    return pltpu.roll(flat, -step % rows, 0).reshape(whole.shape)


def put_slab(scratch, slot, center, ylo, yhi, zlo, zhi):
    whole = jnp.concatenate([ylo[None], center, yhi[None]], axis=0)
    scratch[1, slot] = whole
    whole = whole.astype(F32)
    at = lax.broadcasted_iota(jnp.int32, (Y + 2, Z, C), 1)
    low = zlo.astype(F32)[: Y + 2, None, :]
    high = zhi.astype(F32)[: Y + 2, None, :]
    scratch[0, slot] = jnp.where(at == 0, low, moved_z(whole, -1)).astype(BF16)
    scratch[2, slot] = jnp.where(at == Z - 1, high, moved_z(whole, 1)).astype(BF16)


def put_own(scratch, slot, center):
    scratch[1, slot, 1 : Y + 1] = center
    whole = center.astype(F32)
    at = lax.broadcasted_iota(jnp.int32, (Y, Z, C), 1)
    scratch[0, slot, 1 : Y + 1] = jnp.where(at == 0, 0.0, moved_z(whole, -1)).astype(BF16)
    scratch[2, slot, 1 : Y + 1] = jnp.where(at == Z - 1, 0.0, moved_z(whole, 1)).astype(BF16)


def patches(shifted, slots):
    pieces = []
    for ty in range(3):
        for tz in range(3):
            pieces.append(shifted[tz, :slots, ty : ty + Y].reshape(slots * ROWS, C))
    return jnp.concatenate(pieces, axis=1)


def put_far(scratch, slot, far_ref, part, side):
    slab = held(far_ref[part], "gx", side)
    rims = slab[Y + 2 :].reshape(-1, C)
    put_slab(scratch, slot, slab[:Y], slab[Y], slab[Y + 1], rims[:24], rims[24:])


def own_grad_kernel(first, groups, more, s_ref, *refs):
    total, even, odd = refs[-3:]
    for shifted in (even, odd):
        shifted[:, :, 0:1] = jnp.zeros((3, GROUP, 1, Z, C), BF16)
        shifted[:, :, Y + 1 :] = jnp.zeros((3, GROUP, 1, Z, C), BF16)

    def put(shifted, x):
        for slot in range(GROUP):
            put_own(shifted, slot, s_ref[0, x + 1 + slot])

    def product(shifted, x):
        columns = [s_ref[1, pl.ds(x + 2 - tx, GROUP)].reshape(GROUP * ROWS, C) for tx in range(3)]
        beside = jnp.concatenate(columns, axis=1)
        return lax.dot_general(patches(shifted, GROUP), beside, DEPTH_FIRST, preferred_element_type=F32)

    put(even, first)
    total[...] = refs[0][...] if more else jnp.zeros_like(total)

    def trip(i, carry):
        x = first + i * 2 * GROUP
        total[...] += product(even, x)
        put(odd, x + GROUP)
        total[...] += product(odd, x + GROUP)
        put(even, jnp.minimum(x + 2 * GROUP, X - GROUP))
        return carry

    lax.fori_loop(0, groups // 2, trip, 0)


def own_grad(stacked, first, groups, before, tie):
    more = before is not None
    return pl.pallas_call(
        lambda *refs: own_grad_kernel(first, groups, more, *refs),
        in_specs=[VMEM] * (1 + more) + [ANY],
        out_specs=VMEM,
        out_shape=shape((TAPS, WIDE), F32),
        scratch_shapes=[pltpu.VMEM((3, GROUP, Y + 2, Z, C), BF16)] * 2,
        compiler_params=params(),
        cost_estimate=cost(groups * GROUP, 8 << 20),
    )(stacked, *([before] if more else []), tie)


def rim_grad_kernel(
    own_ref, s_ref, gzlo, gzhi, gylo, gyhi, nzlo, nzhi, nylo, nyhi, elo, ehi, far_lo, far_hi,
    keep_ref, send_ref, scratch, total,
):
    put_far(scratch, 0, far_lo, 0, 0)
    put_far(scratch, 1, far_hi, 0, 1)
    none = jnp.zeros((ROWS, C), BF16)
    first = jnp.concatenate([s_ref[1, 1].reshape(ROWS, C), none], axis=0)
    last = jnp.concatenate([none, s_ref[1, X].reshape(ROWS, C)], axis=0)
    beside = jnp.concatenate([first, jnp.zeros_like(first), last], axis=1)
    total[...] = own_ref[...] + lax.dot_general(
        patches(scratch, 2), beside, DEPTH_FIRST, preferred_element_type=F32
    )
    blank = jnp.zeros((1, Z, C), BF16)
    at = lax.broadcasted_iota(jnp.int32, (X, Z, C), 1)

    def add(row, stride, trio, face_ref):
        padded = jnp.concatenate([blank, face_ref[1], blank], axis=0)
        around = jnp.concatenate([padded[2 - tx : 2 - tx + X].reshape(X * Z, C) for tx in range(3)], axis=1)
        left = jnp.concatenate([a.astype(BF16).reshape(X * Z, C) for a in trio], axis=1)
        made = lax.dot_general(left, around, DEPTH_FIRST, preferred_element_type=F32)
        for k in range(3):
            start = (row + k * stride) * C
            total[start : start + C] += made[k * C : (k + 1) * C]

    for side, row, near, edges, face in ((0, 0, nylo, elo, gylo), (1, 6, nyhi, ehi, gyhi)):
        whole = near[0].astype(F32)
        corners = held(edges[0].astype(F32), "gy", side)
        low = corners[0][:, None, :]
        high = corners[1][:, None, :]
        before = jnp.where(at == 0, low, moved_z(whole, -1))
        after = jnp.where(at == Z - 1, high, moved_z(whole, 1))
        add(row, 1, (before, whole, after), face)
    for side, row, near, face in ((0, 0, nzlo, gzlo), (1, 2, nzhi, gzhi)):
        whole = held(near[0].astype(F32), "gz", side)
        before = jnp.where(at == 0, 0.0, moved_z(whole, -1))
        after = jnp.where(at == Z - 1, 0.0, moved_z(whole, 1))
        add(row, 3, (before, whole, after), face)

    scale = 1.0 / math.sqrt(SHARE * 128 * E**3)
    core = lax.axis_index("gx") % 2
    for mine in range(2):

        @pl.when(core == mine)
        def _():
            for tap in range(27):
                tx, row = tap // 9, tap % 9
                ref = keep_ref if tap // HALF == mine else send_ref
                ref[tap % HALF] = total[row * C : (row + 1) * C, tx * C : (tx + 1) * C] * scale
            ref = keep_ref if mine == 1 else send_ref
            ref[HALF - 1] = jnp.zeros((C, C), F32)


def rim_grad(own, stacked, operands):
    return pl.pallas_call(
        rim_grad_kernel,
        in_specs=[VMEM] * (2 + len(operands)),
        out_specs=[VMEM, VMEM],
        out_shape=[shape((HALF, C, C), F32)] * 2,
        scratch_shapes=[pltpu.VMEM((3, 2, Y + 2, Z, C), BF16), pltpu.VMEM((TAPS, WIDE), F32)],
        compiler_params=params(),
        cost_estimate=cost(3, 6 << 20),
    )(own, stacked, *operands)


def conv_kernel(part, first, groups, following, occ_ref, *refs):
    starts, ends = first == 0, first + groups * GROUP == X
    refs = list(refs)
    field = [refs.pop(0) for _ in range(5)]
    w_ref = refs.pop(0)
    far_lo = refs.pop(0) if starts else None
    far_hi = refs.pop(0) if ends else None
    before = None if starts else refs.pop(0)
    whole = groups * GROUP == X
    ready = None if whole else refs.pop(0)
    o_ref, carry_ref, even, odd, edge, made_ref, left = refs[-7:]
    count = groups * GROUP

    def put(shifted, at, x):
        s_ref, ylo_ref, yhi_ref, zlo_ref, zhi_ref = field
        for slot in range(GROUP):
            put_slab(shifted, slot, s_ref[at, x + 1 + slot], *(ref[at, x + slot] for ref in field[1:]))

    def finish(x, total):
        flags = brick_flags(occ_ref, jnp.maximum(x, 0) // E)
        made_ref[x - first + 1] = jnp.where(flags, total.reshape(Y, Z, C), 0.0).astype(BF16)

    def copy(slot, start, size):
        target = o_ref.at[pl.ds(first - 1 + start, size)]
        return pltpu.make_async_copy(made_ref.at[pl.ds(start, size)], target, left.at[slot])

    def group(shifted, x, near, next_):
        made = jnp.dot(patches(shifted, GROUP), w_ref[...], preferred_element_type=F32)

        def term(slot, tx):
            return made[slot * ROWS : (slot + 1) * ROWS, tx * C : (tx + 1) * C]

        if not (isinstance(x, int) and x == 0):
            finish(x - 1, near + term(0, 2))
        finish(x, next_ + term(0, 1) + term(1, 2))
        for slot in range(1, GROUP - 1):
            finish(x + slot, term(slot - 1, 0) + term(slot, 1) + term(slot + 1, 2))
        return term(GROUP - 2, 0) + term(GROUP - 1, 1), term(GROUP - 1, 0)

    if starts:
        put_far(edge, 0, far_lo, part, 0)
        near = jnp.zeros((ROWS, C), F32)
        next_ = jnp.dot(patches(edge, 1), w_ref[:, :C], preferred_element_type=F32)
    else:
        near, next_ = before[0], before[1]
    if whole:
        put(even, part, 0)
        carry_ref[0] = near
        carry_ref[1] = next_

        def trip(i, carry):
            x = i * 2 * GROUP
            near, next_ = group(even, x, carry_ref[0], carry_ref[1])
            put(odd, part, x + GROUP)
            near, next_ = group(odd, x + GROUP, near, next_)
            after = i + 1 == groups // 2
            put(even, jnp.where(after, following[0], part), jnp.where(after, following[1], x + 2 * GROUP))
            carry_ref[0] = near
            carry_ref[1] = next_
            return carry

        lax.fori_loop(0, groups // 2, trip, 0)
        near = carry_ref[0]
        parts = [(1, count - 1)]
    else:
        near, next_ = group(ready, first, near, next_)
        parts = [(1, GROUP - 1) if starts else (0, GROUP), (GROUP, GROUP)]
        copy(0, *parts[0]).start()
        put(odd, part, first + GROUP)
        near, next_ = group(odd, first + GROUP, near, next_)
        if following is not None:
            put(even, *following)
        carry_ref[0] = near
        carry_ref[1] = next_
    copy(len(parts) - 1, *parts[-1]).start()
    if ends:
        put_far(edge, 0, far_hi, part, 1)
        last = jnp.dot(patches(edge, 1), w_ref[:, 2 * C :], preferred_element_type=F32)
        finish(X - 1, near + last)
        parts.append((count, 1))
        copy(len(parts) - 1, *parts[-1]).start()
    for slot, span in enumerate(parts):
        copy(slot, *span).wait()


def conv_piece(part, first, groups, following, occupancy, field, far, weight, before, ready, done, tie):
    operands = [occupancy, *field, weight]
    starts, ends = first == 0, first + groups * GROUP == X
    if starts:
        operands.append(far[0])
    if ends:
        operands.append(far[1])
    if not starts:
        operands.append(before)
    if groups * GROUP < X:
        operands.append(ready)
    aliases = {}
    specs = [SMEM] + [VMEM] * (len(operands) - 1)
    operands.append(tie)
    specs.append(ANY)
    if not starts:
        aliases = {len(operands): 0}
        operands.append(done)
        specs.append(ANY)
    shifted = (3, GROUP, Y + 2, Z, C)
    return pl.pallas_call(
        lambda *refs: conv_kernel(part, first, groups, following, *refs),
        in_specs=specs,
        out_specs=[ANY, VMEM, VMEM],
        out_shape=[shape((X, Y, Z, C), BF16), shape((2, ROWS, C), F32), shape(shifted, BF16)],
        scratch_shapes=[
            pltpu.VMEM(shifted, BF16),
            pltpu.VMEM((3, 1, Y + 2, Z, C), BF16),
            pltpu.VMEM((groups * GROUP + 1, Y, Z, C), BF16),
            pltpu.SemaphoreType.DMA((3,)),
        ],
        input_output_aliases=aliases,
        compiler_params=params(),
        cost_estimate=cost(groups * GROUP, 2 << 20),
    )(*operands)


def small_kernel(kernel, out_shape, operands, ties=(), specs=None):
    count = len(operands)

    def run(*refs):
        kernel(*refs[:count], *refs[count + len(ties) :])

    return pl.pallas_call(
        run,
        in_specs=(specs or [VMEM] * count) + [ANY] * len(ties),
        out_specs=jax.tree.map(lambda _: VMEM, out_shape),
        out_shape=out_shape,
        compiler_params=params(),
        cost_estimate=pl.CostEstimate(flops=1000, bytes_accessed=1 << 20, transcendentals=0),
    )(*operands, *ties)


def edge_kernel(zlo, zhi, lo, hi):
    for side, ref in enumerate((zlo, zhi)):
        lo[:, side] = held(ref[:, :, 0, :], "gz", side)
        hi[:, side] = held(ref[:, :, Y - 1, :], "gz", side)


def message_kernel(s_ref, ylo, yhi, zlo, zhi, elo, ehi, held_ylo, held_yhi, col_lo, col_hi, to_lo, to_hi):
    held_ylo[...] = held(ylo[...], "gy", 0)
    held_yhi[...] = held(yhi[...], "gy", 1)
    tail = jnp.zeros((2, X, 24 - Y - 2, C), F32)
    for side, (near, col) in enumerate(((zlo, col_lo), (zhi, col_hi))):
        own = held(near[...].astype(F32), "gz", side)
        low = held(elo[:, side].astype(F32), "gy", 0)[:, :, None, :]
        high = held(ehi[:, side].astype(F32), "gy", 1)[:, :, None, :]
        col[...] = jnp.concatenate([low, own, high, tail], axis=2).astype(BF16)
    for at, to in ((0, to_lo), (X - 1, to_hi)):
        to[:, :Y] = s_ref[:, at + 1]
        to[:, Y] = held_ylo[:, at]
        to[:, Y + 1] = held_yhi[:, at]
        rims = jnp.concatenate([col_lo[:, at], col_hi[:, at]], axis=1)
        to[:, Y + 2 :] = rims.reshape(2, 3, Z, C)


def arrange_kernel(w_ref, forward, flipped):
    for tap in range(27):
        tx, row = tap // 9, tap % 9
        forward[row * C : (row + 1) * C, tx * C : (tx + 1) * C] = w_ref[tap]
        flipped[row * C : (row + 1) * C, tx * C : (tx + 1) * C] = w_ref[26 - tap].astype(F32).T.astype(BF16)


def place(axis):
    at = lax.axis_index(axis)
    return at // 2 if axis == "gx" else at


def ring(axis, step):
    if axis == "gx":
        return [(2 * z + c, 2 * ((z + step) % 4) + c) for z in range(4) for c in range(2)]
    return [(i, (i + step) % 4) for i in range(4)]


def deal(axis, terms, ties=()):
    rows = terms[0].shape[0] // 4

    def kernel(*refs):
        me = place(axis)
        for step in range(4):
            at = pl.ds((me + step) % 4 * rows, rows)
            total = refs[0][at]
            for ref in refs[1 : len(terms)]:
                total = total + ref[at]
            refs[len(terms) + step][...] = total

    return small_kernel(kernel, [shape((rows, C), F32)] * 4, terms, ties)


def collect(axis, parts, ties=()):
    rows = parts[0].shape[0]

    def kernel(*refs):
        me = place(axis)
        for step in range(4):
            refs[4][pl.ds((me + 4 - step) % 4 * rows, rows)] = refs[step][...]

    return small_kernel(kernel, shape((4 * rows, C), F32), parts, ties)


def rotate(axis, values):
    return [lax.ppermute(value, axis, ring(axis, step)) for step, value in zip((1, 2, 3), values, strict=True)]


def sum_kernel(a, b, c, d, o):
    o[...] = (a[...] + c[...]) + (b[...] + d[...])


def final_kernel(own, other, o):
    core = lax.axis_index("gx") % 2
    for mine in range(2):

        @pl.when(core == mine)
        def _():
            halves = (own, other) if mine == 0 else (other, own)
            o[: HALF * C] = halves[0][...]
            o[HALF * C :] = halves[1][: 27 * C - HALF * C]


def shift(value, axis, step):
    count = lax.axis_size(axis)
    return lax.ppermute(value, axis, [(i, (i + step) % count) for i in range(count)])


def body(features, occupancy, weight, cotangent):
    stacked, zlo, zhi, ylo, yhi = prepare(occupancy, features, cotangent)
    near_zlo = shift(zhi, "gz", 1)
    near_zhi = shift(zlo, "gz", -1)
    near_ylo = shift(yhi, "gy", 1)
    near_yhi = shift(ylo, "gy", -1)
    own = own_grad(stacked, 0, 4, None, zlo)

    edge = shape((2, 2, X, C), BF16)
    edge_lo, edge_hi = small_kernel(edge_kernel, [edge, edge], [near_zlo, near_zhi], [own])
    edges = (shift(edge_hi, "gy", 1), shift(edge_lo, "gy", -1))
    forward, flipped = small_kernel(
        arrange_kernel, [shape((TAPS, WIDE), BF16)] * 2, [weight.reshape(27, C, C)], [edge_lo]
    )

    face = shape((2, X, Z, C), BF16)
    column = shape((2, X, 24, C), BF16)
    message = shape((2, Y + 5, Z, C), BF16)
    held_ylo, held_yhi, col_lo, col_hi, to_lo, to_hi = small_kernel(
        message_kernel,
        [face, face, column, column, message, message],
        [stacked, near_ylo, near_yhi, near_zlo, near_zhi, *edges],
        [forward],
    )
    far = (shift(to_hi, "gx", 1), shift(to_lo, "gx", -1))
    own = own_grad(stacked, X // 2, 4, own, to_lo)
    rims = [zlo, zhi, ylo, yhi, near_zlo, near_zhi, held_ylo, held_yhi, *edges, *far]
    keep, send = rim_grad(own, stacked, rims)

    field = [stacked, held_ylo, held_yhi, col_lo, col_hi]
    made = [None, None]
    weights = (forward, flipped)
    step = 2 * GROUP
    order = [(0, 0, X // GROUP)] + [(1, at, 2) for at in range(0, X, step)]
    state = {"carry": None, "ready": None}

    def convolve(tie):
        part, first, groups = order.pop(0)
        following = order[0][:2] if order else None
        made[part], state["carry"], state["ready"] = conv_piece(
            part, first, groups, following, occupancy, field, far, weights[part],
            state["carry"], state["ready"], made[part], tie,
        )
        return [state["carry"]]

    swap = [(i, i ^ 1) for i in range(8)]
    came = lax.ppermute(send, "gx", swap)
    flat = (HALF * C, C)
    own, *parts = deal("gx", [keep.reshape(flat), came.reshape(flat)])
    came = rotate("gx", parts)
    ties = convolve(parts[0])
    own, *parts = deal("gy", [own, *came], ties)
    came = rotate("gy", parts)
    ties = convolve(parts[0])
    part_shape = shape(own.shape, F32)
    mine = small_kernel(sum_kernel, part_shape, [own, *came], ties)
    came = rotate("gz", [mine] * 3)
    ties = convolve(mine)
    summed = small_kernel(sum_kernel, part_shape, [mine, *came], ties)
    came = rotate("gy", [summed] * 3)
    ties = convolve(summed)
    whole = collect("gy", [summed, *came], ties)
    came = rotate("gx", [whole] * 3)
    ties = convolve(whole)
    whole = collect("gx", [whole, *came], ties)
    other = lax.ppermute(whole, "gx", swap)
    full = small_kernel(final_kernel, shape((27 * C, C), F32), [whole, other])
    return (made[0], made[1], full.reshape(3, 3, 3, C, C))


def solution(mesh):
    placed = (P("gx", "gy", "gz", None), P("gx", "gy", "gz"), P(), P("gx", "gy", "gz", None))
    return jax.shard_map(
        body,
        mesh=mesh,
        in_specs=placed,
        out_specs=(P("gx", "gy", "gz", None), P("gx", "gy", "gz", None), P()),
        check_vma=False,
    )
```

profile of v0, /device:TPU:1, one launch (start us, length us, event | category | flops | bytes accessed | tf_op | source)
XLA Modules:
  0.0 101.2 jit_solution(1599557422819103754)
XLA Ops:
  1.4 1.6 %copy-done = bf16[32,16,16,128]{3,2,1,0:T(8,128)(2,1)S(1)} copy-done((bf16[32,16,16,128]{3,2,1,0:T(8,128)(2,1)S(1)}, bf16[32,16,16,128]{3,2,1,0:T(8,128)(2,1)}, u32[]{:S(2)}) %copy-start) | copy-done | bytes 2097176
  3.0 1.6 %copy-done.1 = bf16[32,16,16,128]{3,2,1,0:T(8,128)(2,1)S(1)} copy-done((bf16[32,16,16,128]{3,2,1,0:T(8,128)(2,1)S(1)}, bf16[32,16,16,128]{3,2,1,0:T(8,128)(2,1)}, u32[]{:S(2)}) %copy-start.1) | copy-done | bytes 2097176
  4.6 2.1 %shard_map.67 = (bf16[2,34,16,16,128]{4,3,2,1,0:T(8,128)(2,1)S(1)}, bf16[2,32,16,128]{3,2,1,0:T(8,128)(2,1)S(1)}, bf16[2,32,16,128]{3,2,1,0:T(8,128)(2,1)S(1)}, ...) custom-call(s32[4,2,2]{2,1,0:T(2,128)S(1)} %copy.11.occ_ref.refs_0_, ...), custom_call_target="tpu_custom_call" | custom-call | flops 1000000 | bytes 9437184 | tf_op jit(solution)/shard_map/pallas_call | solution.py:69
  6.7 2.2 %collective-permute-start = (bf16[2,32,16,128]{3,2,1,0:T(8,128)(2,1)S(1)}, bf16[2,32,16,128]{3,2,1,0:T(8,128)(2,1)S(1)}, u32[]{:S(2)}, u32[]{:S(2)}) collective-permute-start(bf16[2,32,16,128]{3,2,1,0:T(8,128)(2,1)S(1)} %get-tuple-element.43.gyhi), channel_id=1, source_target_pairs={{0,4},{4,8},{8,12},{12,0},{1,5},{5,9},{9,13},{13,1},{2,6},{6,10},{... | collective-permute-start | bytes 786440 | tf_op jit(solution)/shard_map/ppermute | solution.py:451
  8.9 1.5 %collective-permute-start.1 = (bf16[2,32,16,128]{3,2,1,0:T(8,128)(2,1)S(1)}, bf16[2,32,16,128]{3,2,1,0:T(8,128)(2,1)S(1)}, u32[]{:S(2)}, u32[]{:S(2)}) collective-permute-start(bf16[2,32,16,128]{3,2,1,0:T(8,128)(2,1)S(1)} %get-tuple-element.44.gylo), channel_id=1, source_target_pairs={{0,12},{4,0},{8,4},{12,8},{1,13},{5,1},{9,5},{13,9},{2,14},{6,2},{... | collective-permute-start | bytes 786440 | tf_op jit(solution)/shard_map/ppermute | solution.py:451
  10.4 1.2 %collective-permute-start.2 = (bf16[2,32,16,128]{3,2,1,0:T(8,128)(2,1)S(1)}, bf16[2,32,16,128]{3,2,1,0:T(8,128)(2,1)S(1)}, u32[]{:S(2)}, u32[]{:S(2)}) collective-permute-start(bf16[2,32,16,128]{3,2,1,0:T(8,128)(2,1)S(1)} %get-tuple-element.45.gzhi), channel_id=1, source_target_pairs={{0,1},{1,2},{2,3},{3,0},{4,5},{5,6},{6,7},{7,4},{8,9},{9,10},{10,1... | collective-permute-start | bytes 786440 | tf_op jit(solution)/shard_map/ppermute | solution.py:451
  11.6 1.5 %collective-permute-start.3 = (bf16[2,32,16,128]{3,2,1,0:T(8,128)(2,1)S(1)}, bf16[2,32,16,128]{3,2,1,0:T(8,128)(2,1)S(1)}, u32[]{:S(2)}, u32[]{:S(2)}) collective-permute-start(bf16[2,32,16,128]{3,2,1,0:T(8,128)(2,1)S(1)} %get-tuple-element.46.refs_1_.gzlo), channel_id=1, source_target_pairs={{0,3},{1,0},{2,1},{3,2},{4,7},{5,4},{6,5},{7,6},{8,11},{9,8},{10,9... | collective-permute-start | bytes 786440 | tf_op jit(solution)/shard_map/ppermute | solution.py:451
  13.1 5.8 %shard_map.68.refs_2_.refs_1_ = f32[1152,384]{1,0:T(8,128)S(1)} custom-call(bf16[2,34,16,16,128]{4,3,2,1,0:T(8,128)(2,1)S(1)} %get-tuple-element.42.refs_0_.s_ref.refs_1_, bf16[2,32,16,128]{3,2,1,0:T(8,128)(2,1)S(1)} %get-tuple-element.46.refs_1_.gzlo), custom_call_target="tpu_custom_call" | custom-call | flops 3623878656 | bytes 8388608 | tf_op jit(solution)/shard_map/pallas_call | solution.py:149
  19.1 2.7 %collective-permute-start.5 = (bf16[2,2,32,128]{3,2,1,0:T(8,128)(2,1)S(1)}, bf16[2,2,32,128]{3,2,1,0:T(8,128)(2,1)S(1)}, u32[]{:S(2)}, u32[]{:S(2)}) collective-permute-start(bf16[2,2,32,128]{3,2,1,0:T(8,128)(2,1)S(1)} %get-tuple-element.48.refs_1_), channel_id=1, source_target_pairs={{0,12},{4,0},{8,4},{12,8},{1,13},{5,1},{9,5},{13,9},{2,14},{6,2},{... | collective-permute-start | bytes 98312 | tf_op jit(solution)/shard_map/ppermute | solution.py:451
  22.2 0.9 collective-permute-done.4.refs_5_.elo
  23.6 4.3 %collective-permute-start.6 = (bf16[2,21,16,128]{3,2,1,0:T(8,128)(2,1)S(1)}, bf16[2,21,16,128]{3,2,1,0:T(8,128)(2,1)S(1)}, u32[]{:S(2)}, u32[]{:S(2)}) collective-permute-start(bf16[2,21,16,128]{3,2,1,0:T(8,128)(2,1)S(1)} %get-tuple-element.54), channel_id=1, source_target_pairs={{0,16},{16,32},{32,48},{48,64},{64,80},{80,96},{96,112},{112,0},{1... | collective-permute-start | bytes 516104 | tf_op jit(solution)/shard_map/ppermute | solution.py:451
  28.0 5.7 %shard_map.72.own_ref = f32[1152,384]{1,0:T(8,128)S(1)} custom-call(bf16[2,34,16,16,128]{4,3,2,1,0:T(8,128)(2,1)S(1)} %get-tuple-element.42.refs_0_.s_ref.refs_1_, f32[1152,384]{1,0:T(8,128)S(1)} %shard_map.68.refs_2_.refs_1_, bf16[2,21,16,128]{3,2,1,0:T(8,128)(2,1)S(1)} %get-tuple-element.55.refs_2_), custom_call_target="tpu_custom_call" | custom-call | flops 3623878656 | bytes 8388608 | tf_op jit(solution)/shard_map/pallas_call | solution.py:149
  33.7 1.9 %shard_map.73 = (f32[14,128,128]{2,1,0:T(8,128)S(1)}, f32[14,128,128]{2,1,0:T(8,128)S(1)}) custom-call(f32[1152,384]{1,0:T(8,128)S(1)} %shard_map.72.own_ref, bf16[2,34,16,16,128]{4,3,2,1,0:T(8,128)(2,1)S(1)} %get-tuple-element.42.refs_0_.s_ref.refs_1_, bf16[2,32,16,128]{3,2,1,0:T(8,128)(2,1)S(1)} %get-tuple-element.46.refs_1_.gzlo, ...), custom_call_target="tpu_custom_call" | custom-call | flops 679477248 | bytes 6291456 | tf_op jit(solution)/shard_map/pallas_call | solution.py:214
  35.6 1.6 %collective-permute-start.8 = (f32[14,128,128]{2,1,0:T(8,128)S(1)}, f32[14,128,128]{2,1,0:T(8,128)S(1)}, u32[]{:S(2)}, u32[]{:S(2)}) collective-permute-start(f32[14,128,128]{2,1,0:T(8,128)S(1)} %get-tuple-element.57), channel_id=1, source_target_pairs={{0,16},{16,0},{32,48},{48,32},{64,80},{80,64},{96,112},{112,96},{1... | collective-permute-start | bytes 2752520 | tf_op jit(solution)/shard_map/ppermute | solution.py:500
  37.2 2.1 %collective-permute-done.8 = f32[14,128,128]{2,1,0:T(8,128)S(1)} collective-permute-done((f32[14,128,128]{2,1,0:T(8,128)S(1)}, f32[14,128,128]{2,1,0:T(8,128)S(1)}, u32[]{:S(2)}, u32[]{:S(2)}) %collective-permute-start.8) | collective-permute-done | bytes 917536 | tf_op jit(solution)/shard_map/ppermute | solution.py:500
  39.4 2.5 %collective-permute-start.10 = (f32[448,128]{1,0:T(8,128)S(1)}, f32[448,128]{1,0:T(8,128)S(1)}, u32[]{:S(2)}, u32[]{:S(2)}) collective-permute-start(f32[448,128]{1,0:T(8,128)S(1)} %get-tuple-element.63), channel_id=1, source_target_pairs={{0,64},{16,80},{32,96},{48,112},{64,0},{80,16},{96,32},{112,48},{1... | collective-permute-start | bytes 688136 | tf_op jit(solution)/shard_map/ppermute | solution.py:431
  42.6 0.9 collective-permute-start.9
  43.4 13.7 %shard_map.75 = (bf16[32,16,16,128]{3,2,1,0:T(8,128)(2,1)}, f32[2,256,128]{2,1,0:T(8,128)S(1)}, bf16[3,4,18,16,128]{4,3,2,1,0:T(8,128)(2,1)S(1)}) custom-call(s32[4,2,2]{2,1,0:T(2,128)S(1)} %copy.11.occ_ref.refs_0_, bf16[2,34,16,16,128]{4,3,2,1,0:T(8,128)(2,1)S(1)} %get-tuple-element.42.refs_0_.s_ref.refs_1_, ...), custom_call_target="tpu_custom_call" | custom-call | flops 7247757312 | bytes 2097152 | tf_op jit(solution)/shard_map/pallas_call | solution.py:330
  57.2 1.9 %collective-permute-start.13 = (f32[112,128]{1,0:T(8,128)S(1)}, f32[112,128]{1,0:T(8,128)S(1)}, u32[]{:S(2)}, u32[]{:S(2)}) collective-permute-start(f32[112,128]{1,0:T(8,128)S(1)} %get-tuple-element.70), channel_id=1, source_target_pairs={{0,8},{4,12},{8,0},{12,4},{1,9},{5,13},{9,1},{13,5},{2,10},{6,14},... | collective-permute-start | bytes 172040 | tf_op jit(solution)/shard_map/ppermute | solution.py:431
  59.1 1.3 %collective-permute-start.14 = (f32[112,128]{1,0:T(8,128)S(1)}, f32[112,128]{1,0:T(8,128)S(1)}, u32[]{:S(2)}, u32[]{:S(2)}) collective-permute-start(f32[112,128]{1,0:T(8,128)S(1)} %get-tuple-element.71), channel_id=1, source_target_pairs={{0,12},{4,0},{8,4},{12,8},{1,13},{5,1},{9,5},{13,9},{2,14},{6,2},{... | collective-permute-start | bytes 172040 | tf_op jit(solution)/shard_map/ppermute | solution.py:431
  60.9 4.3 %shard_map.77 = (bf16[32,16,16,128]{3,2,1,0:T(8,128)(2,1)}, f32[2,256,128]{2,1,0:T(8,128)S(1)}, bf16[3,4,18,16,128]{4,3,2,1,0:T(8,128)(2,1)S(1)}) custom-call(s32[4,2,2]{2,1,0:T(2,128)S(1)} %copy.11.occ_ref.refs_0_, bf16[2,34,16,16,128]{4,3,2,1,0:T(8,128)(2,1)S(1)} %get-tuple-element.42.refs_0_.s_ref.refs_1_, ...), custom_call_target="tpu_custom_call" | custom-call | flops 1811939328 | bytes 2097152 | tf_op jit(solution)/shard_map/pallas_call | solution.py:330
  65.2 2.5 %collective-permute-start.17 = (f32[112,128]{1,0:T(8,128)S(1)}, f32[112,128]{1,0:T(8,128)S(1)}, u32[]{:S(2)}, u32[]{:S(2)}) collective-permute-start(f32[112,128]{1,0:T(8,128)S(1)} %shard_map.78.refs_9_.refs_0_), channel_id=1, source_target_pairs={{0,3},{1,0},{2,1},{3,2},{4,7},{5,4},{6,5},{7,6},{8,11},{9,8},{10,9... | collective-permute-start | bytes 172040 | tf_op jit(solution)/shard_map/ppermute | solution.py:431
  68.4 4.1 %shard_map.79 = (bf16[32,16,16,128]{3,2,1,0:T(8,128)(2,1)}, f32[2,256,128]{2,1,0:T(8,128)S(1)}, bf16[3,4,18,16,128]{4,3,2,1,0:T(8,128)(2,1)S(1)}) custom-call(s32[4,2,2]{2,1,0:T(2,128)S(1)} %copy.11.occ_ref.refs_0_, bf16[2,34,16,16,128]{4,3,2,1,0:T(8,128)(2,1)S(1)} %get-tuple-element.42.refs_0_.s_ref.refs_1_, ...), custom_call_target="tpu_custom_call", output_to_operand_aliasing={{0}: (10, {})} | custom-call | flops 1811939328 | bytes 2097152 | tf_op jit(solution)/shard_map/pallas_call | solution.py:330
  72.9 2.3 %collective-permute-start.20 = (f32[112,128]{1,0:T(8,128)S(1)}, f32[112,128]{1,0:T(8,128)S(1)}, u32[]{:S(2)}, u32[]{:S(2)}) collective-permute-start(f32[112,128]{1,0:T(8,128)S(1)} %shard_map.80.refs_9_.refs_0_), channel_id=1, source_target_pairs={{0,12},{4,0},{8,4},{12,8},{1,13},{5,1},{9,5},{13,9},{2,14},{6,2},{... | collective-permute-start | bytes 172040 | tf_op jit(solution)/shard_map/ppermute | solution.py:431
  75.2 1.1 %collective-permute-start.19 = (f32[112,128]{1,0:T(8,128)S(1)}, f32[112,128]{1,0:T(8,128)S(1)}, u32[]{:S(2)}, u32[]{:S(2)}) collective-permute-start(f32[112,128]{1,0:T(8,128)S(1)} %shard_map.80.refs_9_.refs_0_), channel_id=1, source_target_pairs={{0,8},{4,12},{8,0},{12,4},{1,9},{5,13},{9,1},{13,5},{2,10},{6,14},... | collective-permute-start | bytes 172040 | tf_op jit(solution)/shard_map/ppermute | solution.py:431
  76.2 4.1 %shard_map.81 = (bf16[32,16,16,128]{3,2,1,0:T(8,128)(2,1)}, f32[2,256,128]{2,1,0:T(8,128)S(1)}, bf16[3,4,18,16,128]{4,3,2,1,0:T(8,128)(2,1)S(1)}) custom-call(s32[4,2,2]{2,1,0:T(2,128)S(1)} %copy.11.occ_ref.refs_0_, bf16[2,34,16,16,128]{4,3,2,1,0:T(8,128)(2,1)S(1)} %get-tuple-element.42.refs_0_.s_ref.refs_1_, ...), custom_call_target="tpu_custom_call", output_to_operand_aliasing={{0}: (10, {})} | custom-call | flops 1811939328 | bytes 2097152 | tf_op jit(solution)/shard_map/pallas_call | solution.py:330
  80.5 1.9 %collective-permute-start.23 = (f32[448,128]{1,0:T(8,128)S(1)}, f32[448,128]{1,0:T(8,128)S(1)}, u32[]{:S(2)}, u32[]{:S(2)}) collective-permute-start(f32[448,128]{1,0:T(8,128)S(1)} %shard_map.82.refs_10_.refs_0_), channel_id=1, source_target_pairs={{0,96},{16,112},{32,0},{48,16},{64,32},{80,48},{96,64},{112,80},{1... | collective-permute-start | bytes 688136 | tf_op jit(solution)/shard_map/ppermute | solution.py:431
  83.1 5.1 %shard_map.83 = (bf16[32,16,16,128]{3,2,1,0:T(8,128)(2,1)}, f32[2,256,128]{2,1,0:T(8,128)S(1)}, bf16[3,4,18,16,128]{4,3,2,1,0:T(8,128)(2,1)}) custom-call(s32[4,2,2]{2,1,0:T(2,128)S(1)} %copy.11.occ_ref.refs_0_, bf16[2,34,16,16,128]{4,3,2,1,0:T(8,128)(2,1)S(1)} %get-tuple-element.42.refs_0_.s_ref.refs_1_, ...), custom_call_target="tpu_custom_call", output_to_operand_aliasing={{0}: (11, {})} | custom-call | flops 1811939328 | bytes 2097152 | tf_op jit(solution)/shard_map/pallas_call | solution.py:330
  88.9 2.4 %collective-permute-done.21.refs_1_ = f32[448,128]{1,0:T(8,128)S(1)} collective-permute-done((f32[448,128]{1,0:T(8,128)S(1)}, f32[448,128]{1,0:T(8,128)S(1)}, u32[]{:S(2)}, u32[]{:S(2)}) %collective-permute-start.21) | collective-permute-done | bytes 229408 | tf_op jit(solution)/shard_map/ppermute | solution.py:431
  91.3 6.5 %collective-permute-start.24 = (f32[1792,128]{1,0:T(8,128)S(1)}, f32[1792,128]{1,0:T(8,128)S(1)}, u32[]{:S(2)}, u32[]{:S(2)}) collective-permute-start(f32[1792,128]{1,0:T(8,128)S(1)} %shard_map.84.refs_0_), channel_id=1, source_target_pairs={{0,16},{16,0},{32,48},{48,32},{64,80},{80,64},{96,112},{112,96},{1... | collective-permute-start | bytes 2752520 | tf_op jit(solution)/shard_map/ppermute | solution.py:519
  97.8 2.1 %collective-permute-done.24.refs_1_ = f32[1792,128]{1,0:T(8,128)S(1)} collective-permute-done((f32[1792,128]{1,0:T(8,128)S(1)}, f32[1792,128]{1,0:T(8,128)S(1)}, u32[]{:S(2)}, u32[]{:S(2)}) %collective-permute-start.24) | collective-permute-done | bytes 917536 | tf_op jit(solution)/shard_map/ppermute | solution.py:519
  99.9 1.3 %shard_map.85 = f32[3456,128]{1,0:T(8,128)} custom-call(f32[1792,128]{1,0:T(8,128)S(1)} %shard_map.84.refs_0_, f32[1792,128]{1,0:T(8,128)S(1)} %collective-permute-done.24.refs_1_), custom_call_target="tpu_custom_call" | custom-call | flops 1000 | bytes 1048576 | tf_op jit(solution)/shard_map/pallas_call | solution.py:353
  (44 shorter events, 5.8 us)
Async XLA Ops:
  1.4 1.6 %copy-start = (bf16[32,16,16,128]{3,2,1,0:T(8,128)(2,1)S(1)}, bf16[32,16,16,128]{3,2,1,0:T(8,128)(2,1)}, u32[]{:S(2)}) copy-start(bf16[32,16,16,128]{3,2,1,0:T(8,128)(2,1)} %f_ref.1) | copy-start | bytes 6291460
  3.0 1.6 %copy-start.1 = (bf16[32,16,16,128]{3,2,1,0:T(8,128)(2,1)S(1)}, bf16[32,16,16,128]{3,2,1,0:T(8,128)(2,1)}, u32[]{:S(2)}) copy-start(bf16[32,16,16,128]{3,2,1,0:T(8,128)(2,1)} %c_ref.1) | copy-start | bytes 6291460
  6.7 15.5 %collective-permute-start = (bf16[2,32,16,128]{3,2,1,0:T(8,128)(2,1)S(1)}, bf16[2,32,16,128]{3,2,1,0:T(8,128)(2,1)S(1)}, u32[]{:S(2)}, u32[]{:S(2)}) collective-permute-start(bf16[2,32,16,128]{3,2,1,0:T(8,128)(2,1)S(1)} %get-tuple-element.43.gyhi), channel_id=1, source_target_pairs={{0,4},{4,8},{8,12},{12,0},{1,5},{5,9},{9,13},{13,1},{2,6},{6,10},{... | collective-permute-start | bytes 786440 | tf_op jit(solution)/shard_map/ppermute | solution.py:451
  8.9 13.3 %collective-permute-start.1 = (bf16[2,32,16,128]{3,2,1,0:T(8,128)(2,1)S(1)}, bf16[2,32,16,128]{3,2,1,0:T(8,128)(2,1)S(1)}, u32[]{:S(2)}, u32[]{:S(2)}) collective-permute-start(bf16[2,32,16,128]{3,2,1,0:T(8,128)(2,1)S(1)} %get-tuple-element.44.gylo), channel_id=1, source_target_pairs={{0,12},{4,0},{8,4},{12,8},{1,13},{5,1},{9,5},{13,9},{2,14},{6,2},{... | collective-permute-start | bytes 786440 | tf_op jit(solution)/shard_map/ppermute | solution.py:451
  10.4 8.5 %collective-permute-start.2 = (bf16[2,32,16,128]{3,2,1,0:T(8,128)(2,1)S(1)}, bf16[2,32,16,128]{3,2,1,0:T(8,128)(2,1)S(1)}, u32[]{:S(2)}, u32[]{:S(2)}) collective-permute-start(bf16[2,32,16,128]{3,2,1,0:T(8,128)(2,1)S(1)} %get-tuple-element.45.gzhi), channel_id=1, source_target_pairs={{0,1},{1,2},{2,3},{3,0},{4,5},{5,6},{6,7},{7,4},{8,9},{9,10},{10,1... | collective-permute-start | bytes 786440 | tf_op jit(solution)/shard_map/ppermute | solution.py:451
  11.6 7.3 %collective-permute-start.3 = (bf16[2,32,16,128]{3,2,1,0:T(8,128)(2,1)S(1)}, bf16[2,32,16,128]{3,2,1,0:T(8,128)(2,1)S(1)}, u32[]{:S(2)}, u32[]{:S(2)}) collective-permute-start(bf16[2,32,16,128]{3,2,1,0:T(8,128)(2,1)S(1)} %get-tuple-element.46.refs_1_.gzlo), channel_id=1, source_target_pairs={{0,3},{1,0},{2,1},{3,2},{4,7},{5,4},{6,5},{7,6},{8,11},{9,8},{10,9... | collective-permute-start | bytes 786440 | tf_op jit(solution)/shard_map/ppermute | solution.py:451
  18.8 2.9 %copy-start.2 = (bf16[3,3,3,128,128]{4,3,2,1,0:T(8,128)(2,1)S(1)}, bf16[3,3,3,128,128]{4,3,2,1,0:T(8,128)(2,1)}, u32[]{:S(2)}) copy-start(bf16[3,3,3,128,128]{4,3,2,1,0:T(8,128)(2,1)} %param.6) | copy-start | bytes 2654212
  19.0 4.0 %collective-permute-start.4 = (bf16[2,2,32,128]{3,2,1,0:T(8,128)(2,1)S(1)}, bf16[2,2,32,128]{3,2,1,0:T(8,128)(2,1)S(1)}, u32[]{:S(2)}, u32[]{:S(2)}) collective-permute-start(bf16[2,2,32,128]{3,2,1,0:T(8,128)(2,1)S(1)} %get-tuple-element.47), channel_id=1, source_target_pairs={{0,4},{4,8},{8,12},{12,0},{1,5},{5,9},{9,13},{13,1},{2,6},{6,10},{... | collective-permute-start | bytes 98312 | tf_op jit(solution)/shard_map/ppermute | solution.py:451
  19.1 4.0 %collective-permute-start.5 = (bf16[2,2,32,128]{3,2,1,0:T(8,128)(2,1)S(1)}, bf16[2,2,32,128]{3,2,1,0:T(8,128)(2,1)S(1)}, u32[]{:S(2)}, u32[]{:S(2)}) collective-permute-start(bf16[2,2,32,128]{3,2,1,0:T(8,128)(2,1)S(1)} %get-tuple-element.48.refs_1_), channel_id=1, source_target_pairs={{0,12},{4,0},{8,4},{12,8},{1,13},{5,1},{9,5},{13,9},{2,14},{6,2},{... | collective-permute-start | bytes 98312 | tf_op jit(solution)/shard_map/ppermute | solution.py:451
  23.6 10.1 %collective-permute-start.6 = (bf16[2,21,16,128]{3,2,1,0:T(8,128)(2,1)S(1)}, bf16[2,21,16,128]{3,2,1,0:T(8,128)(2,1)S(1)}, u32[]{:S(2)}, u32[]{:S(2)}) collective-permute-start(bf16[2,21,16,128]{3,2,1,0:T(8,128)(2,1)S(1)} %get-tuple-element.54), channel_id=1, source_target_pairs={{0,16},{16,32},{32,48},{48,64},{64,80},{80,96},{96,112},{112,0},{1... | collective-permute-start | bytes 516104 | tf_op jit(solution)/shard_map/ppermute | solution.py:451
  28.0 5.8 %collective-permute-start.7 = (bf16[2,21,16,128]{3,2,1,0:T(8,128)(2,1)S(1)}, bf16[2,21,16,128]{3,2,1,0:T(8,128)(2,1)S(1)}, u32[]{:S(2)}, u32[]{:S(2)}) collective-permute-start(bf16[2,21,16,128]{3,2,1,0:T(8,128)(2,1)S(1)} %get-tuple-element.55.refs_2_), channel_id=1, source_target_pairs={{0,112},{16,0},{32,16},{48,32},{64,48},{80,64},{96,80},{112,96},{1... | collective-permute-start | bytes 516104 | tf_op jit(solution)/shard_map/ppermute | solution.py:451
  35.6 3.7 %collective-permute-start.8 = (f32[14,128,128]{2,1,0:T(8,128)S(1)}, f32[14,128,128]{2,1,0:T(8,128)S(1)}, u32[]{:S(2)}, u32[]{:S(2)}) collective-permute-start(f32[14,128,128]{2,1,0:T(8,128)S(1)} %get-tuple-element.57), channel_id=1, source_target_pairs={{0,16},{16,0},{32,48},{48,32},{64,80},{80,64},{96,112},{112,96},{1... | collective-permute-start | bytes 2752520 | tf_op jit(solution)/shard_map/ppermute | solution.py:500
  39.4 17.7 %collective-permute-start.10 = (f32[448,128]{1,0:T(8,128)S(1)}, f32[448,128]{1,0:T(8,128)S(1)}, u32[]{:S(2)}, u32[]{:S(2)}) collective-permute-start(f32[448,128]{1,0:T(8,128)S(1)} %get-tuple-element.63), channel_id=1, source_target_pairs={{0,64},{16,80},{32,96},{48,112},{64,0},{80,16},{96,32},{112,48},{1... | collective-permute-start | bytes 688136 | tf_op jit(solution)/shard_map/ppermute | solution.py:431
  42.0 15.2 %collective-permute-start.11 = (f32[448,128]{1,0:T(8,128)S(1)}, f32[448,128]{1,0:T(8,128)S(1)}, u32[]{:S(2)}, u32[]{:S(2)}) collective-permute-start(f32[448,128]{1,0:T(8,128)S(1)} %get-tuple-element.64), channel_id=1, source_target_pairs={{0,96},{16,112},{32,0},{48,16},{64,32},{80,48},{96,64},{112,80},{1... | collective-permute-start | bytes 688136 | tf_op jit(solution)/shard_map/ppermute | solution.py:431
  42.6 14.6 %collective-permute-start.9 = (f32[448,128]{1,0:T(8,128)S(1)}, f32[448,128]{1,0:T(8,128)S(1)}, u32[]{:S(2)}, u32[]{:S(2)}) collective-permute-start(f32[448,128]{1,0:T(8,128)S(1)} %get-tuple-element.58.refs_9_), channel_id=1, source_target_pairs={{0,32},{16,48},{32,64},{48,80},{64,96},{80,112},{96,0},{112,16},{1... | collective-permute-start | bytes 688136 | tf_op jit(solution)/shard_map/ppermute | solution.py:431
  57.2 7.9 %collective-permute-start.13 = (f32[112,128]{1,0:T(8,128)S(1)}, f32[112,128]{1,0:T(8,128)S(1)}, u32[]{:S(2)}, u32[]{:S(2)}) collective-permute-start(f32[112,128]{1,0:T(8,128)S(1)} %get-tuple-element.70), channel_id=1, source_target_pairs={{0,8},{4,12},{8,0},{12,4},{1,9},{5,13},{9,1},{13,5},{2,10},{6,14},... | collective-permute-start | bytes 172040 | tf_op jit(solution)/shard_map/ppermute | solution.py:431
  59.1 6.1 %collective-permute-start.14 = (f32[112,128]{1,0:T(8,128)S(1)}, f32[112,128]{1,0:T(8,128)S(1)}, u32[]{:S(2)}, u32[]{:S(2)}) collective-permute-start(f32[112,128]{1,0:T(8,128)S(1)} %get-tuple-element.71), channel_id=1, source_target_pairs={{0,12},{4,0},{8,4},{12,8},{1,13},{5,1},{9,5},{13,9},{2,14},{6,2},{... | collective-permute-start | bytes 172040 | tf_op jit(solution)/shard_map/ppermute | solution.py:431
  60.4 4.8 %collective-permute-start.12 = (f32[112,128]{1,0:T(8,128)S(1)}, f32[112,128]{1,0:T(8,128)S(1)}, u32[]{:S(2)}, u32[]{:S(2)}) collective-permute-start(f32[112,128]{1,0:T(8,128)S(1)} %get-tuple-element.66.refs_9_), channel_id=1, source_target_pairs={{0,4},{4,8},{8,12},{12,0},{1,5},{5,9},{9,13},{13,1},{2,6},{6,10},{... | collective-permute-start | bytes 172040 | tf_op jit(solution)/shard_map/ppermute | solution.py:431
  65.2 7.4 %collective-permute-start.17 = (f32[112,128]{1,0:T(8,128)S(1)}, f32[112,128]{1,0:T(8,128)S(1)}, u32[]{:S(2)}, u32[]{:S(2)}) collective-permute-start(f32[112,128]{1,0:T(8,128)S(1)} %shard_map.78.refs_9_.refs_0_), channel_id=1, source_target_pairs={{0,3},{1,0},{2,1},{3,2},{4,7},{5,4},{6,5},{7,6},{8,11},{9,8},{10,9... | collective-permute-start | bytes 172040 | tf_op jit(solution)/shard_map/ppermute | solution.py:431
  67.7 4.8 %collective-permute-start.16 = (f32[112,128]{1,0:T(8,128)S(1)}, f32[112,128]{1,0:T(8,128)S(1)}, u32[]{:S(2)}, u32[]{:S(2)}) collective-permute-start(f32[112,128]{1,0:T(8,128)S(1)} %shard_map.78.refs_9_.refs_0_), channel_id=1, source_target_pairs={{0,2},{1,3},{2,0},{3,1},{4,6},{5,7},{6,4},{7,5},{8,10},{9,11},{10,... | collective-permute-start | bytes 172040 | tf_op jit(solution)/shard_map/ppermute | solution.py:431
  68.1 4.8 %collective-permute-start.15 = (f32[112,128]{1,0:T(8,128)S(1)}, f32[112,128]{1,0:T(8,128)S(1)}, u32[]{:S(2)}, u32[]{:S(2)}) collective-permute-start(f32[112,128]{1,0:T(8,128)S(1)} %shard_map.78.refs_9_.refs_0_), channel_id=1, source_target_pairs={{0,1},{1,2},{2,3},{3,0},{4,5},{5,6},{6,7},{7,4},{8,9},{9,10},{10,1... | collective-permute-start | bytes 172040 | tf_op jit(solution)/shard_map/ppermute | solution.py:431
  72.9 7.5 %collective-permute-start.20 = (f32[112,128]{1,0:T(8,128)S(1)}, f32[112,128]{1,0:T(8,128)S(1)}, u32[]{:S(2)}, u32[]{:S(2)}) collective-permute-start(f32[112,128]{1,0:T(8,128)S(1)} %shard_map.80.refs_9_.refs_0_), channel_id=1, source_target_pairs={{0,12},{4,0},{8,4},{12,8},{1,13},{5,1},{9,5},{13,9},{2,14},{6,2},{... | collective-permute-start | bytes 172040 | tf_op jit(solution)/shard_map/ppermute | solution.py:431
  75.2 5.2 %collective-permute-start.19 = (f32[112,128]{1,0:T(8,128)S(1)}, f32[112,128]{1,0:T(8,128)S(1)}, u32[]{:S(2)}, u32[]{:S(2)}) collective-permute-start(f32[112,128]{1,0:T(8,128)S(1)} %shard_map.80.refs_9_.refs_0_), channel_id=1, source_target_pairs={{0,8},{4,12},{8,0},{12,4},{1,9},{5,13},{9,1},{13,5},{2,10},{6,14},... | collective-permute-start | bytes 172040 | tf_op jit(solution)/shard_map/ppermute | solution.py:431
  76.2 4.2 %collective-permute-start.18 = (f32[112,128]{1,0:T(8,128)S(1)}, f32[112,128]{1,0:T(8,128)S(1)}, u32[]{:S(2)}, u32[]{:S(2)}) collective-permute-start(f32[112,128]{1,0:T(8,128)S(1)} %shard_map.80.refs_9_.refs_0_), channel_id=1, source_target_pairs={{0,4},{4,8},{8,12},{12,0},{1,5},{5,9},{9,13},{13,1},{2,6},{6,10},{... | collective-permute-start | bytes 172040 | tf_op jit(solution)/shard_map/ppermute | solution.py:431
  80.5 7.7 %collective-permute-start.23 = (f32[448,128]{1,0:T(8,128)S(1)}, f32[448,128]{1,0:T(8,128)S(1)}, u32[]{:S(2)}, u32[]{:S(2)}) collective-permute-start(f32[448,128]{1,0:T(8,128)S(1)} %shard_map.82.refs_10_.refs_0_), channel_id=1, source_target_pairs={{0,96},{16,112},{32,0},{48,16},{64,32},{80,48},{96,64},{112,80},{1... | collective-permute-start | bytes 688136 | tf_op jit(solution)/shard_map/ppermute | solution.py:431
  82.4 6.5 %collective-permute-start.22 = (f32[448,128]{1,0:T(8,128)S(1)}, f32[448,128]{1,0:T(8,128)S(1)}, u32[]{:S(2)}, u32[]{:S(2)}) collective-permute-start(f32[448,128]{1,0:T(8,128)S(1)} %shard_map.82.refs_10_.refs_0_), channel_id=1, source_target_pairs={{0,64},{16,80},{32,96},{48,112},{64,0},{80,16},{96,32},{112,48},{1... | collective-permute-start | bytes 688136 | tf_op jit(solution)/shard_map/ppermute | solution.py:431
  83.1 8.1 %collective-permute-start.21 = (f32[448,128]{1,0:T(8,128)S(1)}, f32[448,128]{1,0:T(8,128)S(1)}, u32[]{:S(2)}, u32[]{:S(2)}) collective-permute-start(f32[448,128]{1,0:T(8,128)S(1)} %shard_map.82.refs_10_.refs_0_), channel_id=1, source_target_pairs={{0,32},{16,48},{32,64},{48,80},{64,96},{80,112},{96,0},{112,16},{1... | collective-permute-start | bytes 688136 | tf_op jit(solution)/shard_map/ppermute | solution.py:431
  91.3 8.6 %collective-permute-start.24 = (f32[1792,128]{1,0:T(8,128)S(1)}, f32[1792,128]{1,0:T(8,128)S(1)}, u32[]{:S(2)}, u32[]{:S(2)}) collective-permute-start(f32[1792,128]{1,0:T(8,128)S(1)} %shard_map.84.refs_0_), channel_id=1, source_target_pairs={{0,16},{16,0},{32,48},{48,32},{64,80},{80,64},{96,112},{112,96},{1... | collective-permute-start | bytes 2752520 | tf_op jit(solution)/shard_map/ppermute | solution.py:519
where the time goes:
time: 101 us
  Pallas kernels  49.5 us (49%)
  starting transfers between devices  38.3 us (38%)
  waiting for transfers between devices  8.51 us (8%)
  local copies, waits for them, and re-layouts  3.96 us (4%)
    pallas_call x5, Pallas kernels, conv_piece(): pl.pallas_call(lambda *refs: conv_kernel(part, first, groups, following,...  31.4 us
    ppermute x15, starting transfers between devices, rotate(): lax.ppermute(value, axis, ring(axis, step))  16.8 us
    ppermute x8, starting transfers between devices, shift(): lax.ppermute(value, axis, [(i, (i + step) % count) for i in range(count)])  13.5 us
    pallas_call x2, Pallas kernels, own_grad(): pl.pallas_call(lambda *refs: own_grad_kernel(first, groups, more, *refs),...  11.5 us
    ppermute x1, starting transfers between devices, body(): other = lax.ppermute(whole, 'gx', swap)  6.53 us
    unnamed x7, local copies, waits for them, and re-layouts  3.96 us
    ppermute x15, waiting for transfers between devices, rotate(): lax.ppermute(value, axis, ring(axis, step))  3.42 us
    pallas_call x10, Pallas kernels, small_kernel(): pl.pallas_call(run, in_specs=(specs or [VMEM] * count) + [ANY] * len(ties...  2.72 us
  transfers between devices with their start and end apart: 25, of which 7 were waited for; matrix products, arithmetic and copies ran while one was open for 0% of the time, Pallas kernels for 43%

commit v1 on v0

--- a/solution.py
+++ b/solution.py
@@ -12,6 +12,7 @@
 E = 8
 ROWS = Y * Z
 GROUP = 4
+SPAN = 8
 TAPS = 9 * C
 WIDE = 3 * C
 HALF = 14
@@ -115,45 +116,38 @@
     put_slab(scratch, slot, slab[:Y], slab[Y], slab[Y + 1], rims[:24], rims[24:])
 
 
-def own_grad_kernel(first, groups, more, s_ref, *refs):
+def own_grad_kernel(first, more, s_ref, *refs):
     total, even, odd = refs[-3:]
     for shifted in (even, odd):
-        shifted[:, :, 0:1] = jnp.zeros((3, GROUP, 1, Z, C), BF16)
-        shifted[:, :, Y + 1 :] = jnp.zeros((3, GROUP, 1, Z, C), BF16)
+        shifted[:, :, 0:1] = jnp.zeros((3, SPAN, 1, Z, C), BF16)
+        shifted[:, :, Y + 1 :] = jnp.zeros((3, SPAN, 1, Z, C), BF16)
 
     def put(shifted, x):
-        for slot in range(GROUP):
+        for slot in range(SPAN):
             put_own(shifted, slot, s_ref[0, x + 1 + slot])
 
     def product(shifted, x):
-        columns = [s_ref[1, pl.ds(x + 2 - tx, GROUP)].reshape(GROUP * ROWS, C) for tx in range(3)]
+        columns = [s_ref[1, x + 2 - tx : x + 2 - tx + SPAN].reshape(SPAN * ROWS, C) for tx in range(3)]
         beside = jnp.concatenate(columns, axis=1)
-        return lax.dot_general(patches(shifted, GROUP), beside, DEPTH_FIRST, preferred_element_type=F32)
+        return lax.dot_general(patches(shifted, SPAN), beside, DEPTH_FIRST, preferred_element_type=F32)
 
     put(even, first)
-    total[...] = refs[0][...] if more else jnp.zeros_like(total)
-
-    def trip(i, carry):
-        x = first + i * 2 * GROUP
-        total[...] += product(even, x)
-        put(odd, x + GROUP)
-        total[...] += product(odd, x + GROUP)
-        put(even, jnp.minimum(x + 2 * GROUP, X - GROUP))
-        return carry
-
-    lax.fori_loop(0, groups // 2, trip, 0)
-
-
-def own_grad(stacked, first, groups, before, tie):
+    made = product(even, first)
+    put(odd, first + SPAN)
+    total[...] = refs[0][...] + made if more else made
+    total[...] += product(odd, first + SPAN)
+
+
+def own_grad(stacked, first, before, tie):
     more = before is not None
     return pl.pallas_call(
-        lambda *refs: own_grad_kernel(first, groups, more, *refs),
+        lambda *refs: own_grad_kernel(first, more, *refs),
         in_specs=[VMEM] * (1 + more) + [ANY],
         out_specs=VMEM,
         out_shape=shape((TAPS, WIDE), F32),
-        scratch_shapes=[pltpu.VMEM((3, GROUP, Y + 2, Z, C), BF16)] * 2,
+        scratch_shapes=[pltpu.VMEM((3, SPAN, Y + 2, Z, C), BF16)] * 2,
         compiler_params=params(),
-        cost_estimate=cost(groups * GROUP, 8 << 20),
+        cost_estimate=cost(2 * SPAN, 8 << 20),
     )(stacked, *([before] if more else []), tie)
 
 
@@ -230,8 +224,7 @@
     far_lo = refs.pop(0) if starts else None
     far_hi = refs.pop(0) if ends else None
     before = None if starts else refs.pop(0)
-    whole = groups * GROUP == X
-    ready = None if whole else refs.pop(0)
+    ready = None if starts and part == 0 else refs.pop(0)
     o_ref, carry_ref, even, odd, edge, made_ref, left = refs[-7:]
     count = groups * GROUP
 
@@ -244,21 +237,28 @@
         flags = brick_flags(occ_ref, jnp.maximum(x, 0) // E)
         made_ref[x - first + 1] = jnp.where(flags, total.reshape(Y, Z, C), 0.0).astype(BF16)
 
-    def copy(slot, start, size):
-        target = o_ref.at[pl.ds(first - 1 + start, size)]
-        return pltpu.make_async_copy(made_ref.at[pl.ds(start, size)], target, left.at[slot])
-
-    def group(shifted, x, near, next_):
+    def copy(x, size, sem):
+        source = made_ref.at[pl.ds(x - first, size)]
+        return pltpu.make_async_copy(source, o_ref.at[pl.ds(x - 1, size)], left.at[sem])
+
+    def group(shifted, x, sem, near, next_, opens):
         made = jnp.dot(patches(shifted, GROUP), w_ref[...], preferred_element_type=F32)
 
         def term(slot, tx):
             return made[slot * ROWS : (slot + 1) * ROWS, tx * C : (tx + 1) * C]
 
-        if not (isinstance(x, int) and x == 0):
+        if opens is not True:
             finish(x - 1, near + term(0, 2))
         finish(x, next_ + term(0, 1) + term(1, 2))
         for slot in range(1, GROUP - 1):
             finish(x + slot, term(slot - 1, 0) + term(slot, 1) + term(slot + 1, 2))
+        if opens is None:
+            pl.when(sem == 0)(lambda: copy(x + 1, GROUP - 1, sem).start())
+            pl.when(sem > 0)(lambda: copy(x, GROUP, sem).start())
+        elif opens:
+            copy(x + 1, GROUP - 1, sem).start()
+        else:
+            copy(x, GROUP, sem).start()
         return term(GROUP - 2, 0) + term(GROUP - 1, 1), term(GROUP - 1, 0)
 
     if starts:
@@ -267,44 +267,49 @@
         next_ = jnp.dot(patches(edge, 1), w_ref[:, :C], preferred_element_type=F32)
     else:
         near, next_ = before[0], before[1]
-    if whole:
-        put(even, part, 0)
+    if groups > 2:
+        if ready is None:
+            put(even, part, 0)
+        else:
+            even[...] = ready[...]
         carry_ref[0] = near
         carry_ref[1] = next_
 
         def trip(i, carry):
-            x = i * 2 * GROUP
-            near, next_ = group(even, x, carry_ref[0], carry_ref[1])
+            x = first + i * 2 * GROUP
+            near, next_ = group(even, x, 2 * i, carry_ref[0], carry_ref[1], None if starts else False)
             put(odd, part, x + GROUP)
-            near, next_ = group(odd, x + GROUP, near, next_)
+            near, next_ = group(odd, x + GROUP, 2 * i + 1, near, next_, False)
             after = i + 1 == groups // 2
-            put(even, jnp.where(after, following[0], part), jnp.where(after, following[1], x + 2 * GROUP))
+            at, then = following or (part, X - GROUP)
+            put(even, jnp.where(after, at, part), jnp.where(after, then, x + 2 * GROUP))
             carry_ref[0] = near
             carry_ref[1] = next_
             return carry
 
         lax.fori_loop(0, groups // 2, trip, 0)
         near = carry_ref[0]
-        parts = [(1, count - 1)]
     else:
-        near, next_ = group(ready, first, near, next_)
-        parts = [(1, GROUP - 1) if starts else (0, GROUP), (GROUP, GROUP)]
-        copy(0, *parts[0]).start()
-        put(odd, part, first + GROUP)
-        near, next_ = group(odd, first + GROUP, near, next_)
-        if following is not None:
-            put(even, *following)
+        near, next_ = group(ready, first, 0, near, next_, starts)
+        if groups == 2:
+            put(odd, part, first + GROUP)
+            near, next_ = group(odd, first + GROUP, 1, near, next_, False)
+        put(even, *following)
         carry_ref[0] = near
         carry_ref[1] = next_
-    copy(len(parts) - 1, *parts[-1]).start()
     if ends:
         put_far(edge, 0, far_hi, part, 1)
         last = jnp.dot(patches(edge, 1), w_ref[:, 2 * C :], preferred_element_type=F32)
         finish(X - 1, near + last)
-        parts.append((count, 1))
-        copy(len(parts) - 1, *parts[-1]).start()
-    for slot, span in enumerate(parts):
-        copy(slot, *span).wait()
+        copy(X, 1, groups).start()
+    for sem in range(groups):
+        x = first + sem * GROUP
+        if starts and sem == 0:
+            copy(x + 1, GROUP - 1, sem).wait()
+        else:
+            copy(x, GROUP, sem).wait()
+    if ends:
+        copy(X, 1, groups).wait()
 
 
 def conv_piece(part, first, groups, following, occupancy, field, far, weight, before, ready, done, tie):
@@ -316,7 +321,7 @@
         operands.append(far[1])
     if not starts:
         operands.append(before)
-    if groups * GROUP < X:
+    if ready is not None:
         operands.append(ready)
     aliases = {}
     specs = [SMEM] + [VMEM] * (len(operands) - 1)
@@ -327,17 +332,32 @@
         operands.append(done)
         specs.append(ANY)
     shifted = (3, GROUP, Y + 2, Z, C)
+    more = following is not None
+    buffers = [shape((2, ROWS, C), F32), shape(shifted, BF16)]
+    small = shape((8, C), F32)
+
+    scratch = [
+        pltpu.VMEM(shifted, BF16),
+        pltpu.VMEM((3, 1, Y + 2, Z, C), BF16),
+        pltpu.VMEM((groups * GROUP + 1, Y, Z, C), BF16),
+        pltpu.SemaphoreType.DMA((groups + 1,)),
+    ]
+    if not more:
+        scratch = [pltpu.VMEM(b.shape, b.dtype) for b in buffers] + scratch
+
+    def plain(*refs):
+        conv_kernel(part, first, groups, following, *refs)
+
+    def final(*refs):
+        refs[-7][...] = jnp.zeros((8, C), F32)
+        conv_kernel(part, first, groups, following, *refs[:-7], *refs[-6:])
+
     return pl.pallas_call(
-        lambda *refs: conv_kernel(part, first, groups, following, *refs),
+        plain if more else final,
         in_specs=specs,
-        out_specs=[ANY, VMEM, VMEM],
-        out_shape=[shape((X, Y, Z, C), BF16), shape((2, ROWS, C), F32), shape(shifted, BF16)],
-        scratch_shapes=[
-            pltpu.VMEM(shifted, BF16),
-            pltpu.VMEM((3, 1, Y + 2, Z, C), BF16),
-            pltpu.VMEM((groups * GROUP + 1, Y, Z, C), BF16),
-            pltpu.SemaphoreType.DMA((3,)),
-        ],
+        out_specs=[ANY] + [VMEM] * (2 if more else 1),
+        out_shape=[shape((X, Y, Z, C), BF16)] + (buffers if more else [small]),
+        scratch_shapes=scratch,
         input_output_aliases=aliases,
         compiler_params=params(),
         cost_estimate=cost(groups * GROUP, 2 << 20),
@@ -395,10 +415,10 @@
     return at // 2 if axis == "gx" else at
 
 
-def ring(axis, step):
+def pairs(axis, step):
     if axis == "gx":
-        return [(2 * z + c, 2 * ((z + step) % 4) + c) for z in range(4) for c in range(2)]
-    return [(i, (i + step) % 4) for i in range(4)]
+        return [(2 * z + c, 2 * (z ^ step) + c) for z in range(4) for c in range(2)]
+    return [(i, i ^ step) for i in range(4)]
 
 
 def deal(axis, terms, ties=()):
@@ -407,7 +427,7 @@
     def kernel(*refs):
         me = place(axis)
         for step in range(4):
-            at = pl.ds((me + step) % 4 * rows, rows)
+            at = pl.ds((me ^ step) * rows, rows)
             total = refs[0][at]
             for ref in refs[1 : len(terms)]:
                 total = total + ref[at]
@@ -422,28 +442,45 @@
     def kernel(*refs):
         me = place(axis)
         for step in range(4):
-            refs[4][pl.ds((me + 4 - step) % 4 * rows, rows)] = refs[step][...]
+            refs[4][pl.ds((me ^ step) * rows, rows)] = refs[step][...]
 
     return small_kernel(kernel, shape((4 * rows, C), F32), parts, ties)
 
 
-def rotate(axis, values):
-    return [lax.ppermute(value, axis, ring(axis, step)) for step, value in zip((1, 2, 3), values, strict=True)]
+def exchange(axis, values):
+    return [lax.ppermute(value, axis, pairs(axis, step)) for step, value in zip((1, 2, 3), values, strict=True)]
 
 
 def sum_kernel(a, b, c, d, o):
     o[...] = (a[...] + c[...]) + (b[...] + d[...])
 
 
-def final_kernel(own, other, o):
-    core = lax.axis_index("gx") % 2
-    for mine in range(2):
-
-        @pl.when(core == mine)
-        def _():
-            halves = (own, other) if mine == 0 else (other, own)
-            o[: HALF * C] = halves[0][...]
-            o[HALF * C :] = halves[1][: 27 * C - HALF * C]
+def write_half(source, target, left, half):
+    rows = (HALF if half == 0 else 27 - HALF) * C
+    copy = pltpu.make_async_copy(source.at[pl.ds(0, rows)], target.at[pl.ds(half * HALF * C, rows)], left)
+    copy.start()
+    copy.wait()
+
+
+def write(source, mine, target):
+    def kernel(*refs):
+        o_ref, left = refs[-2:]
+        core = lax.axis_index("gx") % 2
+        half = core if mine else 1 - core
+        for side in range(2):
+            pl.when(half == side)(lambda side=side: write_half(refs[0], o_ref, left, side))
+
+    operands = [source] + ([] if target is None else [target])
+    return pl.pallas_call(
+        kernel,
+        in_specs=[VMEM, ANY][: len(operands)],
+        out_specs=ANY,
+        out_shape=shape((27 * C, C), F32),
+        scratch_shapes=[pltpu.SemaphoreType.DMA],
+        input_output_aliases={} if target is None else {1: 0},
+        compiler_params=params(),
+        cost_estimate=pl.CostEstimate(flops=1000, bytes_accessed=1 << 20, transcendentals=0),
+    )(*operands)
 
 
 def shift(value, axis, step):
@@ -457,7 +494,7 @@
     near_zhi = shift(zlo, "gz", -1)
     near_ylo = shift(yhi, "gy", 1)
     near_yhi = shift(ylo, "gy", -1)
-    own = own_grad(stacked, 0, 4, None, zlo)
+    own = own_grad(stacked, 0, None, zlo)
 
     edge = shape((2, 2, X, C), BF16)
     edge_lo, edge_hi = small_kernel(edge_kernel, [edge, edge], [near_zlo, near_zhi], [own])
@@ -476,48 +513,49 @@
         [forward],
     )
     far = (shift(to_hi, "gx", 1), shift(to_lo, "gx", -1))
-    own = own_grad(stacked, X // 2, 4, own, to_lo)
+    own = own_grad(stacked, X // 2, own, to_lo)
     rims = [zlo, zhi, ylo, yhi, near_zlo, near_zhi, held_ylo, held_yhi, *edges, *far]
     keep, send = rim_grad(own, stacked, rims)
 
     field = [stacked, held_ylo, held_yhi, col_lo, col_hi]
     made = [None, None]
     weights = (forward, flipped)
-    step = 2 * GROUP
-    order = [(0, 0, X // GROUP)] + [(1, at, 2) for at in range(0, X, step)]
+    order = [(0, 0, 6), (0, 24, 2), (1, 0, 1), (1, 4, 1), (1, 8, 6)]
     state = {"carry": None, "ready": None}
 
     def convolve(tie):
         part, first, groups = order.pop(0)
         following = order[0][:2] if order else None
-        made[part], state["carry"], state["ready"] = conv_piece(
+        made[part], *rest = conv_piece(
             part, first, groups, following, occupancy, field, far, weights[part],
             state["carry"], state["ready"], made[part], tie,
         )
-        return [state["carry"]]
+        if order:
+            state["carry"], state["ready"] = rest
+        return rest[:1]
 
     swap = [(i, i ^ 1) for i in range(8)]
     came = lax.ppermute(send, "gx", swap)
     flat = (HALF * C, C)
     own, *parts = deal("gx", [keep.reshape(flat), came.reshape(flat)])
-    came = rotate("gx", parts)
+    came = exchange("gx", parts)
     ties = convolve(parts[0])
     own, *parts = deal("gy", [own, *came], ties)
-    came = rotate("gy", parts)
+    came = exchange("gy", parts)
     ties = convolve(parts[0])
     part_shape = shape(own.shape, F32)
     mine = small_kernel(sum_kernel, part_shape, [own, *came], ties)
-    came = rotate("gz", [mine] * 3)
+    came = exchange("gz", [mine] * 3)
     ties = convolve(mine)
     summed = small_kernel(sum_kernel, part_shape, [mine, *came], ties)
-    came = rotate("gy", [summed] * 3)
+    came = exchange("gy", [summed] * 3)
     ties = convolve(summed)
     whole = collect("gy", [summed, *came], ties)
-    came = rotate("gx", [whole] * 3)
+    came = exchange("gx", [whole] * 3)
     ties = convolve(whole)
     whole = collect("gx", [whole, *came], ties)
     other = lax.ppermute(whole, "gx", swap)
-    full = small_kernel(final_kernel, shape((27 * C, C), F32), [whole, other])
+    full = write(other, False, write(whole, True, None))
     return (made[0], made[1], full.reshape(3, 3, 3, C, C))
 
 

time: 101 us -> 97 us (0.960)
  waiting for transfers between devices: 8.51 us -> 6.17 us
  Pallas kernels: 49.5 us -> 48.3 us
    ppermute x15, waiting for transfers between devices: 3.42 us -> 2 us  [exchange(): lax.ppermute(value, axis, pairs(axis, step))]
    pallas_call x10 -> x9, Pallas kernels: 2.72 us -> 1.39 us  [small_kernel(): pl.pallas_call(run, in_specs=(specs or [VMEM] * count) + [ANY] * len(ties...]
    ppermute x1, starting transfers between devices: 6.53 us -> 5.31 us  [body(): other = lax.ppermute(whole, 'gx', swap)]
    pallas_call x7 -> x9, Pallas kernels: 42.8 us -> 42.9 us  [the longest x5 30.3 us: conv_piece(): pl.pallas_call(plain if more else final, in_specs=specs, out_specs=[ANY]...]
  transfers between devices with their start and end apart: 25 -> 25, of which waited for: 7 -> 6; matrix products, arithmetic and copies ran while one was open for 0% -> 0% of each run, Pallas kernels for 43% -> 44%
where the time goes in v1:
time: 97 us; the launch traced here: 96.8 us
  Pallas kernels  48.3 us (50%)
  starting transfers between devices  37.3 us (38%)
  waiting for transfers between devices  6.17 us (6%)
  local copies, waits for them, and re-layouts  3.96 us (4%)
  between operations  1.08 us (1%)
    pallas_call x5, Pallas kernels, conv_piece(): pl.pallas_call(plain if more else final, in_specs=specs, out_specs=[ANY]...  30.3 us
    ppermute x15, starting transfers between devices, exchange(): lax.ppermute(value, axis, pairs(axis, step))  16.9 us
    ppermute x8, starting transfers between devices, shift(): lax.ppermute(value, axis, [(i, (i + step) % count) for i in range(count)])  13.6 us
    pallas_call x2, Pallas kernels, own_grad(): pl.pallas_call(lambda *refs: own_grad_kernel(first, more, *refs), in_spec...  10.8 us
    ppermute x1, starting transfers between devices, body(): other = lax.ppermute(whole, 'gx', swap)  5.31 us
    unnamed x7, local copies, waits for them, and re-layouts  3.96 us
    ppermute x1, waiting for transfers between devices, body(): came = lax.ppermute(send, 'gx', swap)  2.1 us
    pallas_call x1, Pallas kernels, prepare(): pl.pallas_call(prepare_kernel, in_specs=[SMEM, VMEM, VMEM], out_specs=[VM...  2.08 us
  transfers between devices with their start and end apart: 25, of which 6 were waited for; matrix products, arithmetic and copies ran while one was open for 0% of the time, Pallas kernels for 44%

profile of v1, /device:TPU:1, one launch (start us, length us, event | category | flops | bytes accessed | tf_op | source)
XLA Modules:
  0.0 96.8 jit_solution(8265397290437276036)
XLA Ops:
  0.6 0.8 copy.13.occ_ref.refs_0_
  1.4 1.6 %copy-done = bf16[32,16,16,128]{3,2,1,0:T(8,128)(2,1)S(1)} copy-done((bf16[32,16,16,128]{3,2,1,0:T(8,128)(2,1)S(1)}, bf16[32,16,16,128]{3,2,1,0:T(8,128)(2,1)}, u32[]{:S(2)}) %copy-start) | copy-done | bytes 2097176
  3.0 1.6 %copy-done.1 = bf16[32,16,16,128]{3,2,1,0:T(8,128)(2,1)S(1)} copy-done((bf16[32,16,16,128]{3,2,1,0:T(8,128)(2,1)S(1)}, bf16[32,16,16,128]{3,2,1,0:T(8,128)(2,1)}, u32[]{:S(2)}) %copy-start.1) | copy-done | bytes 2097176
  4.6 2.1 %shard_map.67 = (bf16[2,34,16,16,128]{4,3,2,1,0:T(8,128)(2,1)S(1)}, bf16[2,32,16,128]{3,2,1,0:T(8,128)(2,1)S(1)}, bf16[2,32,16,128]{3,2,1,0:T(8,128)(2,1)S(1)}, ...) custom-call(s32[4,2,2]{2,1,0:T(2,128)S(1)} %copy.13.occ_ref.refs_0_, ...), custom_call_target="tpu_custom_call" | custom-call | flops 1000000 | bytes 9437184 | tf_op jit(solution)/shard_map/pallas_call | solution.py:70
  6.7 2.2 %collective-permute-start = (bf16[2,32,16,128]{3,2,1,0:T(8,128)(2,1)S(1)}, bf16[2,32,16,128]{3,2,1,0:T(8,128)(2,1)S(1)}, u32[]{:S(2)}, u32[]{:S(2)}) collective-permute-start(bf16[2,32,16,128]{3,2,1,0:T(8,128)(2,1)S(1)} %get-tuple-element.43.gyhi), channel_id=1, source_target_pairs={{0,4},{4,8},{8,12},{12,0},{1,5},{5,9},{9,13},{13,1},{2,6},{6,10},{... | collective-permute-start | bytes 786440 | tf_op jit(solution)/shard_map/ppermute | solution.py:488
  8.9 1.5 %collective-permute-start.1 = (bf16[2,32,16,128]{3,2,1,0:T(8,128)(2,1)S(1)}, bf16[2,32,16,128]{3,2,1,0:T(8,128)(2,1)S(1)}, u32[]{:S(2)}, u32[]{:S(2)}) collective-permute-start(bf16[2,32,16,128]{3,2,1,0:T(8,128)(2,1)S(1)} %get-tuple-element.44.gylo), channel_id=1, source_target_pairs={{0,12},{4,0},{8,4},{12,8},{1,13},{5,1},{9,5},{13,9},{2,14},{6,2},{... | collective-permute-start | bytes 786440 | tf_op jit(solution)/shard_map/ppermute | solution.py:488
  10.4 1.2 %collective-permute-start.2 = (bf16[2,32,16,128]{3,2,1,0:T(8,128)(2,1)S(1)}, bf16[2,32,16,128]{3,2,1,0:T(8,128)(2,1)S(1)}, u32[]{:S(2)}, u32[]{:S(2)}) collective-permute-start(bf16[2,32,16,128]{3,2,1,0:T(8,128)(2,1)S(1)} %get-tuple-element.45.gzhi), channel_id=1, source_target_pairs={{0,1},{1,2},{2,3},{3,0},{4,5},{5,6},{6,7},{7,4},{8,9},{9,10},{10,1... | collective-permute-start | bytes 786440 | tf_op jit(solution)/shard_map/ppermute | solution.py:488
  11.6 1.5 %collective-permute-start.3 = (bf16[2,32,16,128]{3,2,1,0:T(8,128)(2,1)S(1)}, bf16[2,32,16,128]{3,2,1,0:T(8,128)(2,1)S(1)}, u32[]{:S(2)}, u32[]{:S(2)}) collective-permute-start(bf16[2,32,16,128]{3,2,1,0:T(8,128)(2,1)S(1)} %get-tuple-element.46.refs_1_.gzlo), channel_id=1, source_target_pairs={{0,3},{1,0},{2,1},{3,2},{4,7},{5,4},{6,5},{7,6},{8,11},{9,8},{10,9... | collective-permute-start | bytes 786440 | tf_op jit(solution)/shard_map/ppermute | solution.py:488
  13.1 5.4 %shard_map.68.refs_2_.refs_1_ = f32[1152,384]{1,0:T(8,128)S(1)} custom-call(bf16[2,34,16,16,128]{4,3,2,1,0:T(8,128)(2,1)S(1)} %get-tuple-element.42.refs_0_.s_ref.refs_1_, bf16[2,32,16,128]{3,2,1,0:T(8,128)(2,1)S(1)} %get-tuple-element.46.refs_1_.gzlo), custom_call_target="tpu_custom_call" | custom-call | flops 3623878656 | bytes 8388608 | tf_op jit(solution)/shard_map/pallas_call | solution.py:143
  18.8 2.7 %collective-permute-start.5 = (bf16[2,2,32,128]{3,2,1,0:T(8,128)(2,1)S(1)}, bf16[2,2,32,128]{3,2,1,0:T(8,128)(2,1)S(1)}, u32[]{:S(2)}, u32[]{:S(2)}) collective-permute-start(bf16[2,2,32,128]{3,2,1,0:T(8,128)(2,1)S(1)} %get-tuple-element.48.refs_1_), channel_id=1, source_target_pairs={{0,12},{4,0},{8,4},{12,8},{1,13},{5,1},{9,5},{13,9},{2,14},{6,2},{... | collective-permute-start | bytes 98312 | tf_op jit(solution)/shard_map/ppermute | solution.py:488
  21.8 0.9 collective-permute-done.4.refs_5_.elo
  23.3 4.5 %collective-permute-start.7 = (bf16[2,21,16,128]{3,2,1,0:T(8,128)(2,1)S(1)}, bf16[2,21,16,128]{3,2,1,0:T(8,128)(2,1)S(1)}, u32[]{:S(2)}, u32[]{:S(2)}) collective-permute-start(bf16[2,21,16,128]{3,2,1,0:T(8,128)(2,1)S(1)} %get-tuple-element.55), channel_id=1, source_target_pairs={{0,16},{16,32},{32,48},{48,64},{64,80},{80,96},{96,112},{112,0},{1... | collective-permute-start | bytes 516104 | tf_op jit(solution)/shard_map/ppermute | solution.py:488
  27.8 5.4 %shard_map.72.own_ref = f32[1152,384]{1,0:T(8,128)S(1)} custom-call(bf16[2,34,16,16,128]{4,3,2,1,0:T(8,128)(2,1)S(1)} %get-tuple-element.42.refs_0_.s_ref.refs_1_, f32[1152,384]{1,0:T(8,128)S(1)} %shard_map.68.refs_2_.refs_1_, bf16[2,21,16,128]{3,2,1,0:T(8,128)(2,1)S(1)} %get-tuple-element.54.refs_2_), custom_call_target="tpu_custom_call" | custom-call | flops 3623878656 | bytes 8388608 | tf_op jit(solution)/shard_map/pallas_call | solution.py:143
  33.2 1.9 %shard_map.73 = (f32[14,128,128]{2,1,0:T(8,128)S(1)}, f32[14,128,128]{2,1,0:T(8,128)S(1)}) custom-call(f32[1152,384]{1,0:T(8,128)S(1)} %shard_map.72.own_ref, bf16[2,34,16,16,128]{4,3,2,1,0:T(8,128)(2,1)S(1)} %get-tuple-element.42.refs_0_.s_ref.refs_1_, bf16[2,32,16,128]{3,2,1,0:T(8,128)(2,1)S(1)} %get-tuple-element.46.refs_1_.gzlo, ...), custom_call_target="tpu_custom_call" | custom-call | flops 679477248 | bytes 6291456 | tf_op jit(solution)/shard_map/pallas_call | solution.py:208
  35.1 1.5 %collective-permute-start.8 = (f32[14,128,128]{2,1,0:T(8,128)S(1)}, f32[14,128,128]{2,1,0:T(8,128)S(1)}, u32[]{:S(2)}, u32[]{:S(2)}) collective-permute-start(f32[14,128,128]{2,1,0:T(8,128)S(1)} %get-tuple-element.57), channel_id=1, source_target_pairs={{0,16},{16,0},{32,48},{48,32},{64,80},{80,64},{96,112},{112,96},{1... | collective-permute-start | bytes 2752520 | tf_op jit(solution)/shard_map/ppermute | solution.py:538
  36.6 2.1 %collective-permute-done.8 = f32[14,128,128]{2,1,0:T(8,128)S(1)} collective-permute-done((f32[14,128,128]{2,1,0:T(8,128)S(1)}, f32[14,128,128]{2,1,0:T(8,128)S(1)}, u32[]{:S(2)}, u32[]{:S(2)}) %collective-permute-start.8) | collective-permute-done | bytes 917536 | tf_op jit(solution)/shard_map/ppermute | solution.py:538
  38.8 2.5 %collective-permute-start.10 = (f32[448,128]{1,0:T(8,128)S(1)}, f32[448,128]{1,0:T(8,128)S(1)}, u32[]{:S(2)}, u32[]{:S(2)}) collective-permute-start(f32[448,128]{1,0:T(8,128)S(1)} %get-tuple-element.62), channel_id=1, source_target_pairs={{0,64},{16,80},{32,96},{48,112},{64,0},{80,16},{96,32},{112,48},{1... | collective-permute-start | bytes 688136 | tf_op jit(solution)/shard_map/ppermute | solution.py:451
  42.0 10.2 %shard_map.75 = (bf16[32,16,16,128]{3,2,1,0:T(8,128)(2,1)}, f32[2,256,128]{2,1,0:T(8,128)S(1)}, bf16[3,4,18,16,128]{4,3,2,1,0:T(8,128)(2,1)S(1)}) custom-call(s32[4,2,2]{2,1,0:T(2,128)S(1)} %copy.13.occ_ref.refs_0_, bf16[2,34,16,16,128]{4,3,2,1,0:T(8,128)(2,1)S(1)} %get-tuple-element.42.refs_0_.s_ref.refs_1_, ...), custom_call_target="tpu_custom_call" | custom-call | flops 5435817984 | bytes 2097152 | tf_op jit(solution)/shard_map/pallas_call | solution.py:355
  52.9 1.7 %collective-permute-start.13 = (f32[112,128]{1,0:T(8,128)S(1)}, f32[112,128]{1,0:T(8,128)S(1)}, u32[]{:S(2)}, u32[]{:S(2)}) collective-permute-start(f32[112,128]{1,0:T(8,128)S(1)} %get-tuple-element.70), channel_id=1, source_target_pairs={{0,8},{4,12},{8,0},{12,4},{1,9},{5,13},{9,1},{13,5},{2,10},{6,14},... | collective-permute-start | bytes 172040 | tf_op jit(solution)/shard_map/ppermute | solution.py:451
  54.6 1.4 %collective-permute-start.14 = (f32[112,128]{1,0:T(8,128)S(1)}, f32[112,128]{1,0:T(8,128)S(1)}, u32[]{:S(2)}, u32[]{:S(2)}) collective-permute-start(f32[112,128]{1,0:T(8,128)S(1)} %get-tuple-element.71), channel_id=1, source_target_pairs={{0,12},{4,8},{8,4},{12,0},{1,13},{5,9},{9,5},{13,1},{2,14},{6,10},... | collective-permute-start | bytes 172040 | tf_op jit(solution)/shard_map/ppermute | solution.py:451
  56.5 4.3 %shard_map.77 = (bf16[32,16,16,128]{3,2,1,0:T(8,128)(2,1)}, f32[2,256,128]{2,1,0:T(8,128)S(1)}, bf16[3,4,18,16,128]{4,3,2,1,0:T(8,128)(2,1)S(1)}) custom-call(s32[4,2,2]{2,1,0:T(2,128)S(1)} %copy.13.occ_ref.refs_0_, bf16[2,34,16,16,128]{4,3,2,1,0:T(8,128)(2,1)S(1)} %get-tuple-element.42.refs_0_.s_ref.refs_1_, ...), custom_call_target="tpu_custom_call", output_to_operand_aliasing={{0}: (11, {})} | custom-call | flops 1811939328 | bytes 2097152 | tf_op jit(solution)/shard_map/pallas_call | solution.py:355
  60.9 2.7 %collective-permute-start.17 = (f32[112,128]{1,0:T(8,128)S(1)}, f32[112,128]{1,0:T(8,128)S(1)}, u32[]{:S(2)}, u32[]{:S(2)}) collective-permute-start(f32[112,128]{1,0:T(8,128)S(1)} %shard_map.78.refs_9_.refs_0_), channel_id=1, source_target_pairs={{0,3},{1,2},{2,1},{3,0},{4,7},{5,6},{6,5},{7,4},{8,11},{9,10},{10,... | collective-permute-start | bytes 172040 | tf_op jit(solution)/shard_map/ppermute | solution.py:451
  64.3 3.0 %shard_map.79 = (bf16[32,16,16,128]{3,2,1,0:T(8,128)(2,1)}, f32[2,256,128]{2,1,0:T(8,128)S(1)}, bf16[3,4,18,16,128]{4,3,2,1,0:T(8,128)(2,1)S(1)}) custom-call(s32[4,2,2]{2,1,0:T(2,128)S(1)} %copy.13.occ_ref.refs_0_, bf16[2,34,16,16,128]{4,3,2,1,0:T(8,128)(2,1)S(1)} %get-tuple-element.42.refs_0_.s_ref.refs_1_, ...), custom_call_target="tpu_custom_call" | custom-call | flops 905969664 | bytes 2097152 | tf_op jit(solution)/shard_map/pallas_call | solution.py:355
  67.3 0.9 collective-permute-done.16.refs_2_
  68.2 2.1 %collective-permute-start.20 = (f32[112,128]{1,0:T(8,128)S(1)}, f32[112,128]{1,0:T(8,128)S(1)}, u32[]{:S(2)}, u32[]{:S(2)}) collective-permute-start(f32[112,128]{1,0:T(8,128)S(1)} %shard_map.80.refs_9_.refs_0_), channel_id=1, source_target_pairs={{0,12},{4,8},{8,4},{12,0},{1,13},{5,9},{9,5},{13,1},{2,14},{6,10},... | collective-permute-start | bytes 172040 | tf_op jit(solution)/shard_map/ppermute | solution.py:451
  71.5 2.8 %shard_map.81 = (bf16[32,16,16,128]{3,2,1,0:T(8,128)(2,1)}, f32[2,256,128]{2,1,0:T(8,128)S(1)}, bf16[3,4,18,16,128]{4,3,2,1,0:T(8,128)(2,1)S(1)}) custom-call(s32[4,2,2]{2,1,0:T(2,128)S(1)} %copy.13.occ_ref.refs_0_, bf16[2,34,16,16,128]{4,3,2,1,0:T(8,128)(2,1)S(1)} %get-tuple-element.42.refs_0_.s_ref.refs_1_, ...), custom_call_target="tpu_custom_call", output_to_operand_aliasing={{0}: (10, {})} | custom-call | flops 905969664 | bytes 2097152 | tf_op jit(solution)/shard_map/pallas_call | solution.py:355
  74.9 2.6 %collective-permute-start.23 = (f32[448,128]{1,0:T(8,128)S(1)}, f32[448,128]{1,0:T(8,128)S(1)}, u32[]{:S(2)}, u32[]{:S(2)}) collective-permute-start(f32[448,128]{1,0:T(8,128)S(1)} %shard_map.82.refs_10_.refs_0_), channel_id=1, source_target_pairs={{0,96},{16,112},{32,64},{48,80},{64,32},{80,48},{96,0},{112,16},{1... | collective-permute-start | bytes 688136 | tf_op jit(solution)/shard_map/ppermute | solution.py:451
  78.2 9.9 %shard_map.83 = (bf16[32,16,16,128]{3,2,1,0:T(8,128)(2,1)}, f32[8,128]{1,0:T(8,128)S(1)}) custom-call(s32[4,2,2]{2,1,0:T(2,128)S(1)} %copy.13.occ_ref.refs_0_, bf16[2,34,16,16,128]{4,3,2,1,0:T(8,128)(2,1)S(1)} %get-tuple-element.42.refs_0_.s_ref.refs_1_, ...), custom_call_target="tpu_custom_call", output_to_operand_aliasing={{0}: (11, {})} | custom-call | flops 5435817984 | bytes 2097152 | tf_op jit(solution)/shard_map/pallas_call | solution.py:355
  88.3 5.3 %collective-permute-start.24 = (f32[1792,128]{1,0:T(8,128)S(1)}, f32[1792,128]{1,0:T(8,128)S(1)}, u32[]{:S(2)}, u32[]{:S(2)}) collective-permute-start(f32[1792,128]{1,0:T(8,128)S(1)} %shard_map.84.refs_0_), channel_id=1, source_target_pairs={{0,16},{16,0},{32,48},{48,32},{64,80},{80,64},{96,112},{112,96},{1... | collective-permute-start | bytes 2752520 | tf_op jit(solution)/shard_map/ppermute | solution.py:557
  93.6 0.9 shard_map.85.refs_1_
  94.5 1.2 %collective-permute-done.24.refs_0_ = f32[1792,128]{1,0:T(8,128)S(1)} collective-permute-done((f32[1792,128]{1,0:T(8,128)S(1)}, f32[1792,128]{1,0:T(8,128)S(1)}, u32[]{:S(2)}, u32[]{:S(2)}) %collective-permute-start.24) | collective-permute-done | bytes 917536 | tf_op jit(solution)/shard_map/ppermute | solution.py:557
  95.7 0.9 shard_map.86
  (45 shorter events, 6.4 us)
Async XLA Ops:
  1.4 1.6 %copy-start = (bf16[32,16,16,128]{3,2,1,0:T(8,128)(2,1)S(1)}, bf16[32,16,16,128]{3,2,1,0:T(8,128)(2,1)}, u32[]{:S(2)}) copy-start(bf16[32,16,16,128]{3,2,1,0:T(8,128)(2,1)} %f_ref.1) | copy-start | bytes 6291460
  3.0 1.6 %copy-start.1 = (bf16[32,16,16,128]{3,2,1,0:T(8,128)(2,1)S(1)}, bf16[32,16,16,128]{3,2,1,0:T(8,128)(2,1)}, u32[]{:S(2)}) copy-start(bf16[32,16,16,128]{3,2,1,0:T(8,128)(2,1)} %c_ref.1) | copy-start | bytes 6291460
  6.7 15.2 %collective-permute-start = (bf16[2,32,16,128]{3,2,1,0:T(8,128)(2,1)S(1)}, bf16[2,32,16,128]{3,2,1,0:T(8,128)(2,1)S(1)}, u32[]{:S(2)}, u32[]{:S(2)}) collective-permute-start(bf16[2,32,16,128]{3,2,1,0:T(8,128)(2,1)S(1)} %get-tuple-element.43.gyhi), channel_id=1, source_target_pairs={{0,4},{4,8},{8,12},{12,0},{1,5},{5,9},{9,13},{13,1},{2,6},{6,10},{... | collective-permute-start | bytes 786440 | tf_op jit(solution)/shard_map/ppermute | solution.py:488
  8.9 13.0 %collective-permute-start.1 = (bf16[2,32,16,128]{3,2,1,0:T(8,128)(2,1)S(1)}, bf16[2,32,16,128]{3,2,1,0:T(8,128)(2,1)S(1)}, u32[]{:S(2)}, u32[]{:S(2)}) collective-permute-start(bf16[2,32,16,128]{3,2,1,0:T(8,128)(2,1)S(1)} %get-tuple-element.44.gylo), channel_id=1, source_target_pairs={{0,12},{4,0},{8,4},{12,8},{1,13},{5,1},{9,5},{13,9},{2,14},{6,2},{... | collective-permute-start | bytes 786440 | tf_op jit(solution)/shard_map/ppermute | solution.py:488
  10.4 8.1 %collective-permute-start.2 = (bf16[2,32,16,128]{3,2,1,0:T(8,128)(2,1)S(1)}, bf16[2,32,16,128]{3,2,1,0:T(8,128)(2,1)S(1)}, u32[]{:S(2)}, u32[]{:S(2)}) collective-permute-start(bf16[2,32,16,128]{3,2,1,0:T(8,128)(2,1)S(1)} %get-tuple-element.45.gzhi), channel_id=1, source_target_pairs={{0,1},{1,2},{2,3},{3,0},{4,5},{5,6},{6,7},{7,4},{8,9},{9,10},{10,1... | collective-permute-start | bytes 786440 | tf_op jit(solution)/shard_map/ppermute | solution.py:488
  11.6 6.9 %collective-permute-start.3 = (bf16[2,32,16,128]{3,2,1,0:T(8,128)(2,1)S(1)}, bf16[2,32,16,128]{3,2,1,0:T(8,128)(2,1)S(1)}, u32[]{:S(2)}, u32[]{:S(2)}) collective-permute-start(bf16[2,32,16,128]{3,2,1,0:T(8,128)(2,1)S(1)} %get-tuple-element.46.refs_1_.gzlo), channel_id=1, source_target_pairs={{0,3},{1,0},{2,1},{3,2},{4,7},{5,4},{6,5},{7,6},{8,11},{9,8},{10,9... | collective-permute-start | bytes 786440 | tf_op jit(solution)/shard_map/ppermute | solution.py:488
  18.5 2.9 %copy-start.2 = (bf16[3,3,3,128,128]{4,3,2,1,0:T(8,128)(2,1)S(1)}, bf16[3,3,3,128,128]{4,3,2,1,0:T(8,128)(2,1)}, u32[]{:S(2)}) copy-start(bf16[3,3,3,128,128]{4,3,2,1,0:T(8,128)(2,1)} %param.6) | copy-start | bytes 2654212
  18.7 4.0 %collective-permute-start.4 = (bf16[2,2,32,128]{3,2,1,0:T(8,128)(2,1)S(1)}, bf16[2,2,32,128]{3,2,1,0:T(8,128)(2,1)S(1)}, u32[]{:S(2)}, u32[]{:S(2)}) collective-permute-start(bf16[2,2,32,128]{3,2,1,0:T(8,128)(2,1)S(1)} %get-tuple-element.47), channel_id=1, source_target_pairs={{0,4},{4,8},{8,12},{12,0},{1,5},{5,9},{9,13},{13,1},{2,6},{6,10},{... | collective-permute-start | bytes 98312 | tf_op jit(solution)/shard_map/ppermute | solution.py:488
  18.8 4.0 %collective-permute-start.5 = (bf16[2,2,32,128]{3,2,1,0:T(8,128)(2,1)S(1)}, bf16[2,2,32,128]{3,2,1,0:T(8,128)(2,1)S(1)}, u32[]{:S(2)}, u32[]{:S(2)}) collective-permute-start(bf16[2,2,32,128]{3,2,1,0:T(8,128)(2,1)S(1)} %get-tuple-element.48.refs_1_), channel_id=1, source_target_pairs={{0,12},{4,0},{8,4},{12,8},{1,13},{5,1},{9,5},{13,9},{2,14},{6,2},{... | collective-permute-start | bytes 98312 | tf_op jit(solution)/shard_map/ppermute | solution.py:488
  23.3 9.9 %collective-permute-start.7 = (bf16[2,21,16,128]{3,2,1,0:T(8,128)(2,1)S(1)}, bf16[2,21,16,128]{3,2,1,0:T(8,128)(2,1)S(1)}, u32[]{:S(2)}, u32[]{:S(2)}) collective-permute-start(bf16[2,21,16,128]{3,2,1,0:T(8,128)(2,1)S(1)} %get-tuple-element.55), channel_id=1, source_target_pairs={{0,16},{16,32},{32,48},{48,64},{64,80},{80,96},{96,112},{112,0},{1... | collective-permute-start | bytes 516104 | tf_op jit(solution)/shard_map/ppermute | solution.py:488
  27.8 5.4 %collective-permute-start.6 = (bf16[2,21,16,128]{3,2,1,0:T(8,128)(2,1)S(1)}, bf16[2,21,16,128]{3,2,1,0:T(8,128)(2,1)S(1)}, u32[]{:S(2)}, u32[]{:S(2)}) collective-permute-start(bf16[2,21,16,128]{3,2,1,0:T(8,128)(2,1)S(1)} %get-tuple-element.54.refs_2_), channel_id=1, source_target_pairs={{0,112},{16,0},{32,16},{48,32},{64,48},{80,64},{96,80},{112,96},{1... | collective-permute-start | bytes 516104 | tf_op jit(solution)/shard_map/ppermute | solution.py:488
  35.1 3.6 %collective-permute-start.8 = (f32[14,128,128]{2,1,0:T(8,128)S(1)}, f32[14,128,128]{2,1,0:T(8,128)S(1)}, u32[]{:S(2)}, u32[]{:S(2)}) collective-permute-start(f32[14,128,128]{2,1,0:T(8,128)S(1)} %get-tuple-element.57), channel_id=1, source_target_pairs={{0,16},{16,0},{32,48},{48,32},{64,80},{80,64},{96,112},{112,96},{1... | collective-permute-start | bytes 2752520 | tf_op jit(solution)/shard_map/ppermute | solution.py:538
  38.8 13.5 %collective-permute-start.10 = (f32[448,128]{1,0:T(8,128)S(1)}, f32[448,128]{1,0:T(8,128)S(1)}, u32[]{:S(2)}, u32[]{:S(2)}) collective-permute-start(f32[448,128]{1,0:T(8,128)S(1)} %get-tuple-element.62), channel_id=1, source_target_pairs={{0,64},{16,80},{32,96},{48,112},{64,0},{80,16},{96,32},{112,48},{1... | collective-permute-start | bytes 688136 | tf_op jit(solution)/shard_map/ppermute | solution.py:451
  41.2 11.6 %collective-permute-start.11 = (f32[448,128]{1,0:T(8,128)S(1)}, f32[448,128]{1,0:T(8,128)S(1)}, u32[]{:S(2)}, u32[]{:S(2)}) collective-permute-start(f32[448,128]{1,0:T(8,128)S(1)} %get-tuple-element.63), channel_id=1, source_target_pairs={{0,96},{16,112},{32,64},{48,80},{64,32},{80,48},{96,0},{112,16},{1... | collective-permute-start | bytes 688136 | tf_op jit(solution)/shard_map/ppermute | solution.py:451
  41.8 11.0 %collective-permute-start.9 = (f32[448,128]{1,0:T(8,128)S(1)}, f32[448,128]{1,0:T(8,128)S(1)}, u32[]{:S(2)}, u32[]{:S(2)}) collective-permute-start(f32[448,128]{1,0:T(8,128)S(1)} %get-tuple-element.58.refs_8_), channel_id=1, source_target_pairs={{0,32},{16,48},{32,0},{48,16},{64,96},{80,112},{96,64},{112,80},{1... | collective-permute-start | bytes 688136 | tf_op jit(solution)/shard_map/ppermute | solution.py:451
  52.9 8.0 %collective-permute-start.13 = (f32[112,128]{1,0:T(8,128)S(1)}, f32[112,128]{1,0:T(8,128)S(1)}, u32[]{:S(2)}, u32[]{:S(2)}) collective-permute-start(f32[112,128]{1,0:T(8,128)S(1)} %get-tuple-element.70), channel_id=1, source_target_pairs={{0,8},{4,12},{8,0},{12,4},{1,9},{5,13},{9,1},{13,5},{2,10},{6,14},... | collective-permute-start | bytes 172040 | tf_op jit(solution)/shard_map/ppermute | solution.py:451
  54.6 6.3 %collective-permute-start.14 = (f32[112,128]{1,0:T(8,128)S(1)}, f32[112,128]{1,0:T(8,128)S(1)}, u32[]{:S(2)}, u32[]{:S(2)}) collective-permute-start(f32[112,128]{1,0:T(8,128)S(1)} %get-tuple-element.71), channel_id=1, source_target_pairs={{0,12},{4,8},{8,4},{12,0},{1,13},{5,9},{9,5},{13,1},{2,14},{6,10},... | collective-permute-start | bytes 172040 | tf_op jit(solution)/shard_map/ppermute | solution.py:451
  56.0 4.9 %collective-permute-start.12 = (f32[112,128]{1,0:T(8,128)S(1)}, f32[112,128]{1,0:T(8,128)S(1)}, u32[]{:S(2)}, u32[]{:S(2)}) collective-permute-start(f32[112,128]{1,0:T(8,128)S(1)} %get-tuple-element.64.refs_10_), channel_id=1, source_target_pairs={{0,4},{4,0},{8,12},{12,8},{1,5},{5,1},{9,13},{13,9},{2,6},{6,2},{1... | collective-permute-start | bytes 172040 | tf_op jit(solution)/shard_map/ppermute | solution.py:451
  60.9 6.4 %collective-permute-start.17 = (f32[112,128]{1,0:T(8,128)S(1)}, f32[112,128]{1,0:T(8,128)S(1)}, u32[]{:S(2)}, u32[]{:S(2)}) collective-permute-start(f32[112,128]{1,0:T(8,128)S(1)} %shard_map.78.refs_9_.refs_0_), channel_id=1, source_target_pairs={{0,3},{1,2},{2,1},{3,0},{4,7},{5,6},{6,5},{7,4},{8,11},{9,10},{10,... | collective-permute-start | bytes 172040 | tf_op jit(solution)/shard_map/ppermute | solution.py:451
  63.6 4.5 %collective-permute-start.16 = (f32[112,128]{1,0:T(8,128)S(1)}, f32[112,128]{1,0:T(8,128)S(1)}, u32[]{:S(2)}, u32[]{:S(2)}) collective-permute-start(f32[112,128]{1,0:T(8,128)S(1)} %shard_map.78.refs_9_.refs_0_), channel_id=1, source_target_pairs={{0,2},{1,3},{2,0},{3,1},{4,6},{5,7},{6,4},{7,5},{8,10},{9,11},{10,... | collective-permute-start | bytes 172040 | tf_op jit(solution)/shard_map/ppermute | solution.py:451
  63.9 4.2 %collective-permute-start.15 = (f32[112,128]{1,0:T(8,128)S(1)}, f32[112,128]{1,0:T(8,128)S(1)}, u32[]{:S(2)}, u32[]{:S(2)}) collective-permute-start(f32[112,128]{1,0:T(8,128)S(1)} %shard_map.78.refs_9_.refs_0_), channel_id=1, source_target_pairs={{0,1},{1,0},{2,3},{3,2},{4,5},{5,4},{6,7},{7,6},{8,9},{9,8},{10,11... | collective-permute-start | bytes 172040 | tf_op jit(solution)/shard_map/ppermute | solution.py:451
  68.2 6.2 %collective-permute-start.20 = (f32[112,128]{1,0:T(8,128)S(1)}, f32[112,128]{1,0:T(8,128)S(1)}, u32[]{:S(2)}, u32[]{:S(2)}) collective-permute-start(f32[112,128]{1,0:T(8,128)S(1)} %shard_map.80.refs_9_.refs_0_), channel_id=1, source_target_pairs={{0,12},{4,8},{8,4},{12,0},{1,13},{5,9},{9,5},{13,1},{2,14},{6,10},... | collective-permute-start | bytes 172040 | tf_op jit(solution)/shard_map/ppermute | solution.py:451
  70.3 4.5 %collective-permute-start.19 = (f32[112,128]{1,0:T(8,128)S(1)}, f32[112,128]{1,0:T(8,128)S(1)}, u32[]{:S(2)}, u32[]{:S(2)}) collective-permute-start(f32[112,128]{1,0:T(8,128)S(1)} %shard_map.80.refs_9_.refs_0_), channel_id=1, source_target_pairs={{0,8},{4,12},{8,0},{12,4},{1,9},{5,13},{9,1},{13,5},{2,10},{6,14},... | collective-permute-start | bytes 172040 | tf_op jit(solution)/shard_map/ppermute | solution.py:451
  71.0 3.8 %collective-permute-start.18 = (f32[112,128]{1,0:T(8,128)S(1)}, f32[112,128]{1,0:T(8,128)S(1)}, u32[]{:S(2)}, u32[]{:S(2)}) collective-permute-start(f32[112,128]{1,0:T(8,128)S(1)} %shard_map.80.refs_9_.refs_0_), channel_id=1, source_target_pairs={{0,4},{4,0},{8,12},{12,8},{1,5},{5,1},{9,13},{13,9},{2,6},{6,2},{1... | collective-permute-start | bytes 172040 | tf_op jit(solution)/shard_map/ppermute | solution.py:451
  74.9 13.3 %collective-permute-start.23 = (f32[448,128]{1,0:T(8,128)S(1)}, f32[448,128]{1,0:T(8,128)S(1)}, u32[]{:S(2)}, u32[]{:S(2)}) collective-permute-start(f32[448,128]{1,0:T(8,128)S(1)} %shard_map.82.refs_10_.refs_0_), channel_id=1, source_target_pairs={{0,96},{16,112},{32,64},{48,80},{64,32},{80,48},{96,0},{112,16},{1... | collective-permute-start | bytes 688136 | tf_op jit(solution)/shard_map/ppermute | solution.py:451
  77.5 10.6 %collective-permute-start.22 = (f32[448,128]{1,0:T(8,128)S(1)}, f32[448,128]{1,0:T(8,128)S(1)}, u32[]{:S(2)}, u32[]{:S(2)}) collective-permute-start(f32[448,128]{1,0:T(8,128)S(1)} %shard_map.82.refs_10_.refs_0_), channel_id=1, source_target_pairs={{0,64},{16,80},{32,96},{48,112},{64,0},{80,16},{96,32},{112,48},{1... | collective-permute-start | bytes 688136 | tf_op jit(solution)/shard_map/ppermute | solution.py:451
  77.8 10.4 %collective-permute-start.21 = (f32[448,128]{1,0:T(8,128)S(1)}, f32[448,128]{1,0:T(8,128)S(1)}, u32[]{:S(2)}, u32[]{:S(2)}) collective-permute-start(f32[448,128]{1,0:T(8,128)S(1)} %shard_map.82.refs_10_.refs_0_), channel_id=1, source_target_pairs={{0,32},{16,48},{32,0},{48,16},{64,96},{80,112},{96,64},{112,80},{1... | collective-permute-start | bytes 688136 | tf_op jit(solution)/shard_map/ppermute | solution.py:451
  88.3 7.4 %collective-permute-start.24 = (f32[1792,128]{1,0:T(8,128)S(1)}, f32[1792,128]{1,0:T(8,128)S(1)}, u32[]{:S(2)}, u32[]{:S(2)}) collective-permute-start(f32[1792,128]{1,0:T(8,128)S(1)} %shard_map.84.refs_0_), channel_id=1, source_target_pairs={{0,16},{16,0},{32,48},{48,32},{64,80},{80,64},{96,112},{112,96},{1... | collective-permute-start | bytes 2752520 | tf_op jit(solution)/shard_map/ppermute | solution.py:557

commit v2 on v1

--- a/solution.py
+++ b/solution.py
@@ -47,34 +47,59 @@
 
 def brick_flags(occ_ref, brick):
     low_z = lax.broadcasted_iota(jnp.int32, (E, Z, C), 1) < E
-    halves = [jnp.where(low_z, occ_ref[brick, j, 0], occ_ref[brick, j, 1]) for j in range(2)]
+    halves = [jnp.where(low_z, occ_ref[j, 0, brick], occ_ref[j, 1, brick]) for j in range(2)]
     return jnp.concatenate(halves, axis=0) == 1
 
 
-def prepare_kernel(occ_ref, f_ref, c_ref, s_ref, zlo_ref, zhi_ref, ylo_ref, yhi_ref):
+def mask_slabs(part, source, mask_ref, s_ref, faces):
+    zlo_ref, zhi_ref, ylo_ref, yhi_ref = faces
     for end in (0, X + 1):
-        s_ref[:, end] = jnp.zeros((2, Y, Z, C), BF16)
+        s_ref[end] = jnp.zeros((Y, Z, C), BF16)
     for brick in range(X // E):
-        keep = brick_flags(occ_ref, brick)
         span = slice(brick * E, (brick + 1) * E)
-        for part, ref in enumerate((f_ref, c_ref)):
-            value = jnp.where(keep[None], ref[span].astype(F32), 0.0).astype(BF16)
-            s_ref[part, brick * E + 1 : (brick + 1) * E + 1] = value
-            zlo_ref[part, span] = value[:, :, 0, :]
-            zhi_ref[part, span] = value[:, :, Z - 1, :]
-            ylo_ref[part, span] = value[:, 0]
-            yhi_ref[part, span] = value[:, Y - 1]
+        keep = mask_ref[brick].astype(F32) > 0.0
+        value = jnp.where(keep[None], source[span].astype(F32), 0.0).astype(BF16)
+        s_ref[brick * E + 1 : (brick + 1) * E + 1] = value
+        zlo_ref[part, span] = value[:, :, 0, :]
+        zhi_ref[part, span] = value[:, :, Z - 1, :]
+        ylo_ref[part, span] = value[:, 0]
+        yhi_ref[part, span] = value[:, Y - 1]
+
+
+def prepare_x_kernel(occ_ref, f_ref, s_ref, mask_ref, *faces):
+    for brick in range(X // E):
+        mask_ref[brick] = jnp.where(brick_flags(occ_ref, brick), 1.0, 0.0).astype(BF16)
+    mask_slabs(0, f_ref, mask_ref, s_ref, faces)
+
+
+def prepare_g_kernel(c_ref, mask_ref, *refs):
+    given, s_ref, faces = refs[:4], refs[4], refs[5:]
+    for face, ref in zip(faces, given, strict=True):
+        face[0] = ref[0]
+    mask_slabs(1, c_ref, mask_ref, s_ref, faces)
 
 
 def prepare(occupancy, features, cotangent):
-    return pl.pallas_call(
-        prepare_kernel,
-        in_specs=[SMEM, VMEM, VMEM],
+    slabs = shape((X + 2, Y, Z, C), BF16)
+    mask = shape((X // E, Y, Z, C), BF16)
+    own_cost = pl.CostEstimate(flops=1000000, bytes_accessed=5 << 20, transcendentals=0)
+    fields, mask, *given = pl.pallas_call(
+        prepare_x_kernel,
+        in_specs=[SMEM, VMEM],
+        out_specs=[VMEM] * 6,
+        out_shape=[slabs, mask] + [shape((1, X, Z, C), BF16)] * 4,
+        compiler_params=params(),
+        cost_estimate=own_cost,
+    )(jnp.transpose(occupancy, (1, 2, 0)), features)
+    cotangents, *faces = pl.pallas_call(
+        prepare_g_kernel,
+        in_specs=[VMEM] * 6,
         out_specs=[VMEM] * 5,
-        out_shape=[shape((2, X + 2, Y, Z, C), BF16)] + [shape((2, X, Z, C), BF16)] * 4,
+        out_shape=[slabs] + [shape((2, X, Z, C), BF16)] * 4,
         compiler_params=params(),
-        cost_estimate=pl.CostEstimate(flops=1000000, bytes_accessed=9 << 20, transcendentals=0),
-    )(occupancy, features, cotangent)
+        cost_estimate=own_cost,
+    )(cotangent, mask, *given)
+    return (fields, cotangents), mask, faces
 
 
 def moved_z(whole, step):
@@ -116,7 +141,7 @@
     put_slab(scratch, slot, slab[:Y], slab[Y], slab[Y + 1], rims[:24], rims[24:])
 
 
-def own_grad_kernel(first, more, s_ref, *refs):
+def own_grad_kernel(first, more, x_ref, g_ref, *refs):
     total, even, odd = refs[-3:]
     for shifted in (even, odd):
         shifted[:, :, 0:1] = jnp.zeros((3, SPAN, 1, Z, C), BF16)
@@ -124,10 +149,10 @@
 
     def put(shifted, x):
         for slot in range(SPAN):
-            put_own(shifted, slot, s_ref[0, x + 1 + slot])
+            put_own(shifted, slot, x_ref[x + 1 + slot])
 
     def product(shifted, x):
-        columns = [s_ref[1, x + 2 - tx : x + 2 - tx + SPAN].reshape(SPAN * ROWS, C) for tx in range(3)]
+        columns = [g_ref[x + 2 - tx : x + 2 - tx + SPAN].reshape(SPAN * ROWS, C) for tx in range(3)]
         beside = jnp.concatenate(columns, axis=1)
         return lax.dot_general(patches(shifted, SPAN), beside, DEPTH_FIRST, preferred_element_type=F32)
 
@@ -138,44 +163,52 @@
     total[...] += product(odd, first + SPAN)
 
 
-def own_grad(stacked, first, before, tie):
+def own_grad(slabs, first, before, tie):
     more = before is not None
     return pl.pallas_call(
         lambda *refs: own_grad_kernel(first, more, *refs),
-        in_specs=[VMEM] * (1 + more) + [ANY],
+        in_specs=[VMEM] * (2 + more) + [ANY],
         out_specs=VMEM,
         out_shape=shape((TAPS, WIDE), F32),
         scratch_shapes=[pltpu.VMEM((3, SPAN, Y + 2, Z, C), BF16)] * 2,
         compiler_params=params(),
         cost_estimate=cost(2 * SPAN, 8 << 20),
-    )(stacked, *([before] if more else []), tie)
+    )(*slabs, *([before] if more else []), tie)
+
+
+def add_rim(total, row, stride, trio, face_ref):
+    blank = jnp.zeros((1, Z, C), BF16)
+    padded = jnp.concatenate([blank, face_ref[1], blank], axis=0)
+    around = jnp.concatenate([padded[2 - tx : 2 - tx + X].reshape(X * Z, C) for tx in range(3)], axis=1)
+    left = jnp.concatenate([a.astype(BF16).reshape(X * Z, C) for a in trio], axis=1)
+    made = lax.dot_general(left, around, DEPTH_FIRST, preferred_element_type=F32)
+    for k in range(3):
+        start = (row + k * stride) * C
+        total[start : start + C] += made[k * C : (k + 1) * C]
+
+
+def z_rim_kernel(own_ref, gzlo, gzhi, nzlo, nzhi, total):
+    total[...] = own_ref[...]
+    at = lax.broadcasted_iota(jnp.int32, (X, Z, C), 1)
+    for side, row, near, face in ((0, 0, nzlo, gzlo), (1, 2, nzhi, gzhi)):
+        whole = held(near[0].astype(F32), "gz", side)
+        before = jnp.where(at == 0, 0.0, moved_z(whole, -1))
+        after = jnp.where(at == Z - 1, 0.0, moved_z(whole, 1))
+        add_rim(total, row, 3, (before, whole, after), face)
 
 
 def rim_grad_kernel(
-    own_ref, s_ref, gzlo, gzhi, gylo, gyhi, nzlo, nzhi, nylo, nyhi, elo, ehi, far_lo, far_hi,
-    keep_ref, send_ref, scratch, total,
+    own_ref, g_ref, gylo, gyhi, nylo, nyhi, elo, ehi, far_lo, far_hi, keep_ref, send_ref, scratch, total
 ):
-    put_far(scratch, 0, far_lo, 0, 0)
-    put_far(scratch, 1, far_hi, 0, 1)
-    none = jnp.zeros((ROWS, C), BF16)
-    first = jnp.concatenate([s_ref[1, 1].reshape(ROWS, C), none], axis=0)
-    last = jnp.concatenate([none, s_ref[1, X].reshape(ROWS, C)], axis=0)
-    beside = jnp.concatenate([first, jnp.zeros_like(first), last], axis=1)
-    total[...] = own_ref[...] + lax.dot_general(
-        patches(scratch, 2), beside, DEPTH_FIRST, preferred_element_type=F32
-    )
-    blank = jnp.zeros((1, Z, C), BF16)
+    total[...] = own_ref[...]
+    for side, far, plane, tx in ((0, far_lo, 1, 0), (1, far_hi, X, 2)):
+        put_far(scratch.at[:, side : side + 1], 0, far, 0, side)
+        left = patches(scratch.at[:, side : side + 1], 1)
+        beside = g_ref[plane].reshape(ROWS, C)
+        total[:, tx * C : (tx + 1) * C] += lax.dot_general(
+            left, beside, DEPTH_FIRST, preferred_element_type=F32
+        )
     at = lax.broadcasted_iota(jnp.int32, (X, Z, C), 1)
-
-    def add(row, stride, trio, face_ref):
-        padded = jnp.concatenate([blank, face_ref[1], blank], axis=0)
-        around = jnp.concatenate([padded[2 - tx : 2 - tx + X].reshape(X * Z, C) for tx in range(3)], axis=1)
-        left = jnp.concatenate([a.astype(BF16).reshape(X * Z, C) for a in trio], axis=1)
-        made = lax.dot_general(left, around, DEPTH_FIRST, preferred_element_type=F32)
-        for k in range(3):
-            start = (row + k * stride) * C
-            total[start : start + C] += made[k * C : (k + 1) * C]
-
     for side, row, near, edges, face in ((0, 0, nylo, elo, gylo), (1, 6, nyhi, ehi, gyhi)):
         whole = near[0].astype(F32)
         corners = held(edges[0].astype(F32), "gy", side)
@@ -183,12 +216,7 @@
         high = corners[1][:, None, :]
         before = jnp.where(at == 0, low, moved_z(whole, -1))
         after = jnp.where(at == Z - 1, high, moved_z(whole, 1))
-        add(row, 1, (before, whole, after), face)
-    for side, row, near, face in ((0, 0, nzlo, gzlo), (1, 2, nzhi, gzhi)):
-        whole = held(near[0].astype(F32), "gz", side)
-        before = jnp.where(at == 0, 0.0, moved_z(whole, -1))
-        after = jnp.where(at == Z - 1, 0.0, moved_z(whole, 1))
-        add(row, 3, (before, whole, after), face)
+        add_rim(total, row, 1, (before, whole, after), face)
 
     scale = 1.0 / math.sqrt(SHARE * 128 * E**3)
     core = lax.axis_index("gx") % 2
@@ -204,7 +232,7 @@
             ref[HALF - 1] = jnp.zeros((C, C), F32)
 
 
-def rim_grad(own, stacked, operands):
+def rim_grad(own, cotangents, operands):
     return pl.pallas_call(
         rim_grad_kernel,
         in_specs=[VMEM] * (2 + len(operands)),
@@ -213,13 +241,14 @@
         scratch_shapes=[pltpu.VMEM((3, 2, Y + 2, Z, C), BF16), pltpu.VMEM((TAPS, WIDE), F32)],
         compiler_params=params(),
         cost_estimate=cost(3, 6 << 20),
-    )(own, stacked, *operands)
-
-
-def conv_kernel(part, first, groups, following, occ_ref, *refs):
+    )(own, cotangents, *operands)
+
+
+def conv_kernel(part, first, groups, following, mask_ref, *refs):
     starts, ends = first == 0, first + groups * GROUP == X
     refs = list(refs)
-    field = [refs.pop(0) for _ in range(5)]
+    slabs = [refs.pop(0) for _ in range(2)]
+    rims = [refs.pop(0) for _ in range(4)]
     w_ref = refs.pop(0)
     far_lo = refs.pop(0) if starts else None
     far_hi = refs.pop(0) if ends else None
@@ -229,13 +258,12 @@
     count = groups * GROUP
 
     def put(shifted, at, x):
-        s_ref, ylo_ref, yhi_ref, zlo_ref, zhi_ref = field
         for slot in range(GROUP):
-            put_slab(shifted, slot, s_ref[at, x + 1 + slot], *(ref[at, x + slot] for ref in field[1:]))
+            put_slab(shifted, slot, slabs[at][x + 1 + slot], *(ref[at, x + slot] for ref in rims))
 
     def finish(x, total):
-        flags = brick_flags(occ_ref, jnp.maximum(x, 0) // E)
-        made_ref[x - first + 1] = jnp.where(flags, total.reshape(Y, Z, C), 0.0).astype(BF16)
+        keep = mask_ref[jnp.maximum(x, 0) // E].astype(F32) > 0.0
+        made_ref[x - first + 1] = jnp.where(keep, total.reshape(Y, Z, C), 0.0).astype(BF16)
 
     def copy(x, size, sem):
         source = made_ref.at[pl.ds(x - first, size)]
@@ -281,8 +309,8 @@
             put(odd, part, x + GROUP)
             near, next_ = group(odd, x + GROUP, 2 * i + 1, near, next_, False)
             after = i + 1 == groups // 2
-            at, then = following or (part, X - GROUP)
-            put(even, jnp.where(after, at, part), jnp.where(after, then, x + 2 * GROUP))
+            then = following[1] if following is not None else X - GROUP
+            put(even, part, jnp.where(after, then, x + 2 * GROUP))
             carry_ref[0] = near
             carry_ref[1] = next_
             return carry
@@ -290,10 +318,10 @@
         lax.fori_loop(0, groups // 2, trip, 0)
         near = carry_ref[0]
     else:
+        if ready is None:
+            ready = odd
+            put(odd, part, first)
         near, next_ = group(ready, first, 0, near, next_, starts)
-        if groups == 2:
-            put(odd, part, first + GROUP)
-            near, next_ = group(odd, first + GROUP, 1, near, next_, False)
         put(even, *following)
         carry_ref[0] = near
         carry_ref[1] = next_
@@ -312,8 +340,8 @@
         copy(X, 1, groups).wait()
 
 
-def conv_piece(part, first, groups, following, occupancy, field, far, weight, before, ready, done, tie):
-    operands = [occupancy, *field, weight]
+def conv_piece(part, first, groups, following, mask, field, far, weight, before, ready, done, tie):
+    operands = [mask, *field, weight]
     starts, ends = first == 0, first + groups * GROUP == X
     if starts:
         operands.append(far[0])
@@ -324,7 +352,7 @@
     if ready is not None:
         operands.append(ready)
     aliases = {}
-    specs = [SMEM] + [VMEM] * (len(operands) - 1)
+    specs = [VMEM] * len(operands)
     operands.append(tie)
     specs.append(ANY)
     if not starts:
@@ -386,7 +414,7 @@
         hi[:, side] = held(ref[:, :, Y - 1, :], "gz", side)
 
 
-def message_kernel(s_ref, ylo, yhi, zlo, zhi, elo, ehi, held_ylo, held_yhi, col_lo, col_hi, to_lo, to_hi):
+def message_kernel(x_ref, g_ref, ylo, yhi, zlo, zhi, elo, ehi, held_ylo, held_yhi, col_lo, col_hi, to_lo, to_hi):
     held_ylo[...] = held(ylo[...], "gy", 0)
     held_yhi[...] = held(yhi[...], "gy", 1)
     tail = jnp.zeros((2, X, 24 - Y - 2, C), F32)
@@ -396,7 +424,8 @@
         high = held(ehi[:, side].astype(F32), "gy", 1)[:, :, None, :]
         col[...] = jnp.concatenate([low, own, high, tail], axis=2).astype(BF16)
     for at, to in ((0, to_lo), (X - 1, to_hi)):
-        to[:, :Y] = s_ref[:, at + 1]
+        to[0, :Y] = x_ref[at + 1]
+        to[1, :Y] = g_ref[at + 1]
         to[:, Y] = held_ylo[:, at]
         to[:, Y + 1] = held_yhi[:, at]
         rims = jnp.concatenate([col_lo[:, at], col_hi[:, at]], axis=1)
@@ -455,46 +484,64 @@
     o[...] = (a[...] + c[...]) + (b[...] + d[...])
 
 
-def write_half(source, target, left, half):
-    rows = (HALF if half == 0 else 27 - HALF) * C
-    copy = pltpu.make_async_copy(source.at[pl.ds(0, rows)], target.at[pl.ds(half * HALF * C, rows)], left)
-    copy.start()
-    copy.wait()
-
-
-def write(source, mine, target):
+def write(sources, mine, target, tie):
+    arrays = [a for a, _ in sources]
+    rows = HALF * C // 4
+    short = 27 * C - 2 * HALF * C + rows
+    count = sum(len(steps) for _, steps in sources)
+
     def kernel(*refs):
         o_ref, left = refs[-2:]
         core = lax.axis_index("gx") % 2
         half = core if mine else 1 - core
-        for side in range(2):
-            pl.when(half == side)(lambda side=side: write_half(refs[0], o_ref, left, side))
-
-    operands = [source] + ([] if target is None else [target])
+        me = place("gx")
+        for act in ("start", "wait"):
+            sem = 0
+            for ref, (_, steps) in zip(refs, sources, strict=False):
+                for at, step in enumerate(steps):
+                    chunk = half * 4 + (me ^ step)
+
+                    def move(size, ref=ref, at=at, chunk=chunk, sem=sem):
+                        target = o_ref.at[pl.ds(chunk * rows, size)]
+                        copy = pltpu.make_async_copy(ref.at[pl.ds(at * rows, size)], target, left.at[sem])
+                        getattr(copy, act)()
+
+                    pl.when(chunk < 7)(lambda move=move: move(rows))
+                    pl.when(chunk == 7)(lambda move=move: move(short))
+                    sem += 1
+
+    operands = arrays + [tie] + ([] if target is None else [target])
     return pl.pallas_call(
         kernel,
-        in_specs=[VMEM, ANY][: len(operands)],
+        in_specs=[VMEM] * len(arrays) + [ANY] * (len(operands) - len(arrays)),
         out_specs=ANY,
         out_shape=shape((27 * C, C), F32),
-        scratch_shapes=[pltpu.SemaphoreType.DMA],
-        input_output_aliases={} if target is None else {1: 0},
+        scratch_shapes=[pltpu.SemaphoreType.DMA((count,))],
+        input_output_aliases={} if target is None else {len(operands) - 1: 0},
         compiler_params=params(),
         cost_estimate=pl.CostEstimate(flops=1000, bytes_accessed=1 << 20, transcendentals=0),
     )(*operands)
 
 
+def join_kernel(a, b, c, o):
+    rows = a.shape[0]
+    for k, ref in enumerate((a, b, c)):
+        o[k * rows : (k + 1) * rows] = ref[...]
+
+
 def shift(value, axis, step):
     count = lax.axis_size(axis)
     return lax.ppermute(value, axis, [(i, (i + step) % count) for i in range(count)])
 
 
 def body(features, occupancy, weight, cotangent):
-    stacked, zlo, zhi, ylo, yhi = prepare(occupancy, features, cotangent)
+    slabs, mask, faces = prepare(occupancy, features, cotangent)
+    zlo, zhi, ylo, yhi = faces
     near_zlo = shift(zhi, "gz", 1)
     near_zhi = shift(zlo, "gz", -1)
     near_ylo = shift(yhi, "gy", 1)
     near_yhi = shift(ylo, "gy", -1)
-    own = own_grad(stacked, 0, None, zlo)
+    own = own_grad(slabs, 0, None, zlo)
 
     edge = shape((2, 2, X, C), BF16)
     edge_lo, edge_hi = small_kernel(edge_kernel, [edge, edge], [near_zlo, near_zhi], [own])
@@ -502,6 +549,9 @@
     forward, flipped = small_kernel(
         arrange_kernel, [shape((TAPS, WIDE), BF16)] * 2, [weight.reshape(27, C, C)], [edge_lo]
     )
+    own = small_kernel(
+        z_rim_kernel, shape((TAPS, WIDE), F32), [own, zlo, zhi, near_zlo, near_zhi], [edge_lo]
+    )
 
     face = shape((2, X, Z, C), BF16)
     column = shape((2, X, 24, C), BF16)
@@ -509,25 +559,24 @@
     held_ylo, held_yhi, col_lo, col_hi, to_lo, to_hi = small_kernel(
         message_kernel,
         [face, face, column, column, message, message],
-        [stacked, near_ylo, near_yhi, near_zlo, near_zhi, *edges],
-        [forward],
+        [*slabs, near_ylo, near_yhi, near_zlo, near_zhi, *edges],
+        [forward, own],
     )
     far = (shift(to_hi, "gx", 1), shift(to_lo, "gx", -1))
-    own = own_grad(stacked, X // 2, own, to_lo)
-    rims = [zlo, zhi, ylo, yhi, near_zlo, near_zhi, held_ylo, held_yhi, *edges, *far]
-    keep, send = rim_grad(own, stacked, rims)
-
-    field = [stacked, held_ylo, held_yhi, col_lo, col_hi]
+    own = own_grad(slabs, X // 2, own, to_lo)
+    keep, send = rim_grad(own, slabs[1], [ylo, yhi, held_ylo, held_yhi, *edges, *far])
+
+    field = [*slabs, held_ylo, held_yhi, col_lo, col_hi]
     made = [None, None]
     weights = (forward, flipped)
-    order = [(0, 0, 6), (0, 24, 2), (1, 0, 1), (1, 4, 1), (1, 8, 6)]
+    order = [(0, 0, 1), (0, 4, 6), (0, 28, 1), (1, 0, 1), (1, 4, 1), (1, 8, 6)]
     state = {"carry": None, "ready": None}
 
     def convolve(tie):
         part, first, groups = order.pop(0)
         following = order[0][:2] if order else None
         made[part], *rest = conv_piece(
-            part, first, groups, following, occupancy, field, far, weights[part],
+            part, first, groups, following, mask, field, far, weights[part],
             state["carry"], state["ready"], made[part], tie,
         )
         if order:
@@ -536,8 +585,9 @@
 
     swap = [(i, i ^ 1) for i in range(8)]
     came = lax.ppermute(send, "gx", swap)
+    ties = convolve(send)
     flat = (HALF * C, C)
-    own, *parts = deal("gx", [keep.reshape(flat), came.reshape(flat)])
+    own, *parts = deal("gx", [keep.reshape(flat), came.reshape(flat)], ties)
     came = exchange("gx", parts)
     ties = convolve(parts[0])
     own, *parts = deal("gy", [own, *came], ties)
@@ -550,12 +600,15 @@
     summed = small_kernel(sum_kernel, part_shape, [mine, *came], ties)
     came = exchange("gy", [summed] * 3)
     ties = convolve(summed)
-    whole = collect("gy", [summed, *came], ties)
-    came = exchange("gx", [whole] * 3)
-    ties = convolve(whole)
-    whole = collect("gx", [whole, *came], ties)
-    other = lax.ppermute(whole, "gx", swap)
-    full = write(other, False, write(whole, True, None))
+    chunk = collect("gy", [summed, *came], ties)
+    came = exchange("gx", [chunk] * 3)
+    beside = lax.ppermute(chunk, "gx", swap)
+    (tie,) = convolve(chunk)
+    joined = small_kernel(join_kernel, shape((3 * chunk.shape[0], C), F32), came, [tie])
+    others = lax.ppermute(joined, "gx", swap)
+    full = write([(chunk, (0,)), (joined, (1, 2, 3))], True, None, joined)
+    full = write([(beside, (0,))], False, full, joined)
+    full = write([(others, (1, 2, 3))], False, full, joined)
     return (made[0], made[1], full.reshape(3, 3, 3, C, C))
 
 

time: 97 us -> 94.3 us (0.972)
  local copies, waits for them, and re-layouts: 3.96 us -> 2.28 us
    ppermute x15, waiting for transfers between devices: 2 us -> 4.48 us  [exchange(): lax.ppermute(value, axis, pairs(axis, step))]
    pallas_call x5 -> x6, Pallas kernels: 30.3 us -> 28.2 us  [conv_piece(): pl.pallas_call(plain if more else final, in_specs=specs, out_specs=[ANY]...]
    ppermute x1, waiting for transfers between devices: 2.1 us -> 0.01 us  [body(): came = lax.ppermute(send, 'gx', swap)]
    unnamed x7 -> x8, local copies, waits for them, and re-layouts: 3.96 us -> 2.28 us
    pallas_call x3 -> x5, Pallas kernels: 3.92 us -> 5.36 us  [the longest x3 2.51 us: write(): pl.pallas_call(kernel, in_specs=[VMEM] * len(arrays) + [ANY] * (len(opera...]
    pallas_call x9 -> x10, Pallas kernels: 1.39 us -> 2 us  [small_kernel(): pl.pallas_call(run, in_specs=(specs or [VMEM] * count) + [ANY] * len(ties...]
    ppermute x1 -> x2, starting transfers between devices: 5.31 us -> 5.04 us  [the longest x1 4.95 us: body(): others = lax.ppermute(joined, 'gx', swap)]
  transfers between devices with their start and end apart: 25 -> 26, of which waited for: 6 -> 7; matrix products, arithmetic and copies ran while one was open for 0% -> 0% of each run, Pallas kernels for 44% -> 44%
where the time goes in v2:
time: 94.3 us; the launch traced here: 94.1 us
  Pallas kernels  47.5 us (50%)
  starting transfers between devices  37.4 us (40%)
  waiting for transfers between devices  5.81 us (6%)
  local copies, waits for them, and re-layouts  2.28 us (2%)
  between operations  1.14 us (1%)
    pallas_call x6, Pallas kernels, conv_piece(): pl.pallas_call(plain if more else final, in_specs=specs, out_specs=[ANY]...  28.2 us
    ppermute x15, starting transfers between devices, exchange(): lax.ppermute(value, axis, pairs(axis, step))  17.3 us
    ppermute x8, starting transfers between devices, shift(): lax.ppermute(value, axis, [(i, (i + step) % count) for i in range(count)])  13.6 us
    pallas_call x2, Pallas kernels, own_grad(): pl.pallas_call(lambda *refs: own_grad_kernel(first, more, *refs), in_spec...  10.8 us
    ppermute x1, starting transfers between devices, body(): others = lax.ppermute(joined, 'gx', swap)  4.95 us
    ppermute x15, waiting for transfers between devices, exchange(): lax.ppermute(value, axis, pairs(axis, step))  4.48 us
    pallas_call x3, Pallas kernels, write(): pl.pallas_call(kernel, in_specs=[VMEM] * len(arrays) + [ANY] * (len(opera...  2.51 us
    unnamed x8, local copies, waits for them, and re-layouts  2.28 us
  transfers between devices with their start and end apart: 26, of which 7 were waited for; matrix products, arithmetic and copies ran while one was open for 0% of the time, Pallas kernels for 44%

profile of v2, /device:TPU:1, one launch (start us, length us, event | category | flops | bytes accessed | tf_op | source)
XLA Modules:
  0.0 94.1 jit_solution(3652203013854554523)
XLA Ops:
  0.6 1.6 %copy-done = bf16[32,16,16,128]{3,2,1,0:T(8,128)(2,1)S(1)} copy-done((bf16[32,16,16,128]{3,2,1,0:T(8,128)(2,1)S(1)}, bf16[32,16,16,128]{3,2,1,0:T(8,128)(2,1)}, u32[]{:S(2)}) %copy-start) | copy-done | bytes 2097176
  2.9 1.8 %shard_map.67 = (bf16[34,16,16,128]{3,2,1,0:T(8,128)(2,1)S(1)}, bf16[4,16,16,128]{3,2,1,0:T(8,128)(2,1)S(1)}, bf16[1,32,16,128]{3,2,1,0:T(8,128)(2,1)S(1)}, bf16...) custom-call(s32[2,2,4]{2,1,0:T(2,128)S(1)} %bitcast.8, ...), custom_call_target="tpu_custom_call" | custom-call | flops 1000000 | bytes 5242880 | tf_op jit(solution)/shard_map/pallas_call | solution.py:86
  4.7 1.1 %shard_map.68 = (bf16[34,16,16,128]{3,2,1,0:T(8,128)(2,1)S(1)}, bf16[2,32,16,128]{3,2,1,0:T(8,128)(2,1)S(1)}, bf16[2,32,16,128]{3,2,1,0:T(8,128)(2,1)S(1)}, bf16...) custom-call(bf16[32,16,16,128]{3,2,1,0:T(8,128)(2,1)S(1)} %copy-done.1, ...), custom_call_target="tpu_custom_call" | custom-call | flops 1000000 | bytes 5242880 | tf_op jit(solution)/shard_map/pallas_call | solution.py:94
  5.8 2.2 %collective-permute-start = (bf16[2,32,16,128]{3,2,1,0:T(8,128)(2,1)S(1)}, bf16[2,32,16,128]{3,2,1,0:T(8,128)(2,1)S(1)}, u32[]{:S(2)}, u32[]{:S(2)}) collective-permute-start(bf16[2,32,16,128]{3,2,1,0:T(8,128)(2,1)S(1)} %get-tuple-element.58.gyhi), channel_id=1, source_target_pairs={{0,4},{4,8},{8,12},{12,0},{1,5},{5,9},{9,13},{13,1},{2,6},{6,10},{... | collective-permute-start | bytes 786440 | tf_op jit(solution)/shard_map/ppermute | solution.py:534
  8.0 1.5 %collective-permute-start.1 = (bf16[2,32,16,128]{3,2,1,0:T(8,128)(2,1)S(1)}, bf16[2,32,16,128]{3,2,1,0:T(8,128)(2,1)S(1)}, u32[]{:S(2)}, u32[]{:S(2)}) collective-permute-start(bf16[2,32,16,128]{3,2,1,0:T(8,128)(2,1)S(1)} %get-tuple-element.59.gylo), channel_id=1, source_target_pairs={{0,12},{4,0},{8,4},{12,8},{1,13},{5,1},{9,5},{13,9},{2,14},{6,2},{... | collective-permute-start | bytes 786440 | tf_op jit(solution)/shard_map/ppermute | solution.py:534
  9.5 1.2 %collective-permute-start.2 = (bf16[2,32,16,128]{3,2,1,0:T(8,128)(2,1)S(1)}, bf16[2,32,16,128]{3,2,1,0:T(8,128)(2,1)S(1)}, u32[]{:S(2)}, u32[]{:S(2)}) collective-permute-start(bf16[2,32,16,128]{3,2,1,0:T(8,128)(2,1)S(1)} %get-tuple-element.60.refs_2_), channel_id=1, source_target_pairs={{0,1},{1,2},{2,3},{3,0},{4,5},{5,6},{6,7},{7,4},{8,9},{9,10},{10,1... | collective-permute-start | bytes 786440 | tf_op jit(solution)/shard_map/ppermute | solution.py:534
  10.7 1.5 %collective-permute-start.3 = (bf16[2,32,16,128]{3,2,1,0:T(8,128)(2,1)S(1)}, bf16[2,32,16,128]{3,2,1,0:T(8,128)(2,1)S(1)}, u32[]{:S(2)}, u32[]{:S(2)}) collective-permute-start(bf16[2,32,16,128]{3,2,1,0:T(8,128)(2,1)S(1)} %get-tuple-element.61.refs_2_.refs_1_), channel_id=1, source_target_pairs={{0,3},{1,0},{2,1},{3,2},{4,7},{5,4},{6,5},{7,6},{8,11},{9,8},{10,9... | collective-permute-start | bytes 786440 | tf_op jit(solution)/shard_map/ppermute | solution.py:534
  12.2 5.4 %shard_map.69.refs_2_.refs_0_ = f32[1152,384]{1,0:T(8,128)S(1)} custom-call(bf16[34,16,16,128]{3,2,1,0:T(8,128)(2,1)S(1)} %get-tuple-element.52.refs_0_.refs_1_, bf16[34,16,16,128]{3,2,1,0:T(8,128)(2,1)S(1)} %get-tuple-element.57.refs_1_.g_ref.refs_2_, bf16[2,32,16,128]{3,2,1,0:T(8,128)(2,1)S(1)} %get-tuple-element.61.refs_2_.refs_1_), custom_call_target="tpu_custom_call" | custom-call | flops 3623878656 | bytes 8388608 | tf_op jit(solution)/shard_map/pallas_call | solution.py:168
  17.8 2.7 %collective-permute-start.5 = (bf16[2,2,32,128]{3,2,1,0:T(8,128)(2,1)S(1)}, bf16[2,2,32,128]{3,2,1,0:T(8,128)(2,1)S(1)}, u32[]{:S(2)}, u32[]{:S(2)}) collective-permute-start(bf16[2,2,32,128]{3,2,1,0:T(8,128)(2,1)S(1)} %get-tuple-element.63.refs_1_.refs_5_), channel_id=1, source_target_pairs={{0,12},{4,0},{8,4},{12,8},{1,13},{5,1},{9,5},{13,9},{2,14},{6,2},{... | collective-permute-start | bytes 98312 | tf_op jit(solution)/shard_map/ppermute | solution.py:534
  22.4 4.5 %collective-permute-start.7 = (bf16[2,21,16,128]{3,2,1,0:T(8,128)(2,1)S(1)}, bf16[2,21,16,128]{3,2,1,0:T(8,128)(2,1)S(1)}, u32[]{:S(2)}, u32[]{:S(2)}) collective-permute-start(bf16[2,21,16,128]{3,2,1,0:T(8,128)(2,1)S(1)} %get-tuple-element.70), channel_id=1, source_target_pairs={{0,16},{16,32},{32,48},{48,64},{64,80},{80,96},{96,112},{112,0},{1... | collective-permute-start | bytes 516104 | tf_op jit(solution)/shard_map/ppermute | solution.py:534
  26.9 5.4 %shard_map.74.own_ref = f32[1152,384]{1,0:T(8,128)S(1)} custom-call(bf16[34,16,16,128]{3,2,1,0:T(8,128)(2,1)S(1)} %get-tuple-element.52.refs_0_.refs_1_, bf16[34,16,16,128]{3,2,1,0:T(8,128)(2,1)S(1)} %get-tuple-element.57.refs_1_.g_ref.refs_2_, f32[1152,384]{1,0:T(8,128)S(1)} %shard_map.72.refs_9_.refs_2_, bf16[2,21,16,128]{3,2,1,0:T(8,128)(2,1)S(1)} %get-tuple-element.69.refs_3_), custom_call_target="tpu_custom_call" | custom-call | flops 3623878656 | bytes 8388608 | tf_op jit(solution)/shard_map/pallas_call | solution.py:168
  32.3 1.1 %shard_map.75 = (f32[14,128,128]{2,1,0:T(8,128)S(1)}, f32[14,128,128]{2,1,0:T(8,128)S(1)}) custom-call(f32[1152,384]{1,0:T(8,128)S(1)} %shard_map.74.own_ref, bf16[34,16,16,128]{3,2,1,0:T(8,128)(2,1)S(1)} %get-tuple-element.57.refs_1_.g_ref.refs_2_, bf16[2,32,16,128]{3,2,1,0:T(8,128)(2,1)S(1)} %get-tuple-element.59.gylo, ...), custom_call_target="tpu_custom_call" | custom-call | flops 679477248 | bytes 6291456 | tf_op jit(solution)/shard_map/pallas_call | solution.py:236
  33.5 1.5 %collective-permute-start.8 = (f32[14,128,128]{2,1,0:T(8,128)S(1)}, f32[14,128,128]{2,1,0:T(8,128)S(1)}, u32[]{:S(2)}, u32[]{:S(2)}) collective-permute-start(f32[14,128,128]{2,1,0:T(8,128)S(1)} %get-tuple-element.71.refs_9_), channel_id=1, source_target_pairs={{0,16},{16,0},{32,48},{48,32},{64,80},{80,64},{96,112},{112,96},{1... | collective-permute-start | bytes 2752520 | tf_op jit(solution)/shard_map/ppermute | solution.py:587
  34.9 2.6 %shard_map.76 = (bf16[32,16,16,128]{3,2,1,0:T(8,128)(2,1)}, f32[2,256,128]{2,1,0:T(8,128)S(1)}, bf16[3,4,18,16,128]{4,3,2,1,0:T(8,128)(2,1)S(1)}) custom-call(bf16[4,16,16,128]{3,2,1,0:T(8,128)(2,1)S(1)} %get-tuple-element.51.mask_ref.refs_0_, bf16[34,16,16,128]{3,2,1,0:T(8,128)(2,1)S(1)} %get-tuple-element.52.refs_0_.refs_1_, ...), custom_call_target="tpu_custom_call" | custom-call | flops 905969664 | bytes 2097152 | tf_op jit(solution)/shard_map/pallas_call | solution.py:383
  37.7 2.5 %collective-permute-start.10 = (f32[448,128]{1,0:T(8,128)S(1)}, f32[448,128]{1,0:T(8,128)S(1)}, u32[]{:S(2)}, u32[]{:S(2)}) collective-permute-start(f32[448,128]{1,0:T(8,128)S(1)} %get-tuple-element.80), channel_id=1, source_target_pairs={{0,64},{16,80},{32,96},{48,112},{64,0},{80,16},{96,32},{112,48},{1... | collective-permute-start | bytes 688136 | tf_op jit(solution)/shard_map/ppermute | solution.py:480
  40.9 9.1 %shard_map.78 = (bf16[32,16,16,128]{3,2,1,0:T(8,128)(2,1)}, f32[2,256,128]{2,1,0:T(8,128)S(1)}, bf16[3,4,18,16,128]{4,3,2,1,0:T(8,128)(2,1)S(1)}) custom-call(bf16[4,16,16,128]{3,2,1,0:T(8,128)(2,1)S(1)} %get-tuple-element.51.mask_ref.refs_0_, bf16[34,16,16,128]{3,2,1,0:T(8,128)(2,1)S(1)} %get-tuple-element.52.refs_0_.refs_1_, ...), custom_call_target="tpu_custom_call", output_to_operand_aliasing={{0}: (11, {})} | custom-call | flops 5435817984 | bytes 2097152 | tf_op jit(solution)/shard_map/pallas_call | solution.py:383
  50.0 1.7 %collective-permute-done.11.refs_3_ = f32[448,128]{1,0:T(8,128)S(1)} collective-permute-done((f32[448,128]{1,0:T(8,128)S(1)}, f32[448,128]{1,0:T(8,128)S(1)}, u32[]{:S(2)}, u32[]{:S(2)}) %collective-permute-start.11) | collective-permute-done | bytes 229408 | tf_op jit(solution)/shard_map/ppermute | solution.py:480
  51.8 1.7 %collective-permute-start.13 = (f32[112,128]{1,0:T(8,128)S(1)}, f32[112,128]{1,0:T(8,128)S(1)}, u32[]{:S(2)}, u32[]{:S(2)}) collective-permute-start(f32[112,128]{1,0:T(8,128)S(1)} %get-tuple-element.88), channel_id=1, source_target_pairs={{0,8},{4,12},{8,0},{12,4},{1,9},{5,13},{9,1},{13,5},{2,10},{6,14},... | collective-permute-start | bytes 172040 | tf_op jit(solution)/shard_map/ppermute | solution.py:480
  53.5 1.4 %collective-permute-start.14 = (f32[112,128]{1,0:T(8,128)S(1)}, f32[112,128]{1,0:T(8,128)S(1)}, u32[]{:S(2)}, u32[]{:S(2)}) collective-permute-start(f32[112,128]{1,0:T(8,128)S(1)} %get-tuple-element.89), channel_id=1, source_target_pairs={{0,12},{4,8},{8,4},{12,0},{1,13},{5,9},{9,5},{13,1},{2,14},{6,10},... | collective-permute-start | bytes 172040 | tf_op jit(solution)/shard_map/ppermute | solution.py:480
  55.4 2.5 %shard_map.80 = (bf16[32,16,16,128]{3,2,1,0:T(8,128)(2,1)}, f32[2,256,128]{2,1,0:T(8,128)S(1)}, bf16[3,4,18,16,128]{4,3,2,1,0:T(8,128)(2,1)S(1)}) custom-call(bf16[4,16,16,128]{3,2,1,0:T(8,128)(2,1)S(1)} %get-tuple-element.51.mask_ref.refs_0_, bf16[34,16,16,128]{3,2,1,0:T(8,128)(2,1)S(1)} %get-tuple-element.52.refs_0_.refs_1_, ...), custom_call_target="tpu_custom_call", output_to_operand_aliasing={{0}: (12, {})} | custom-call | flops 905969664 | bytes 2097152 | tf_op jit(solution)/shard_map/pallas_call | solution.py:383
  58.4 2.8 %collective-permute-start.17 = (f32[112,128]{1,0:T(8,128)S(1)}, f32[112,128]{1,0:T(8,128)S(1)}, u32[]{:S(2)}, u32[]{:S(2)}) collective-permute-start(f32[112,128]{1,0:T(8,128)S(1)} %shard_map.81.refs_10_.refs_0_), channel_id=1, source_target_pairs={{0,3},{1,2},{2,1},{3,0},{4,7},{5,6},{6,5},{7,4},{8,11},{9,10},{10,... | collective-permute-start | bytes 172040 | tf_op jit(solution)/shard_map/ppermute | solution.py:480
  61.8 2.4 %shard_map.82 = (bf16[32,16,16,128]{3,2,1,0:T(8,128)(2,1)}, f32[2,256,128]{2,1,0:T(8,128)S(1)}, bf16[3,4,18,16,128]{4,3,2,1,0:T(8,128)(2,1)S(1)}) custom-call(bf16[4,16,16,128]{3,2,1,0:T(8,128)(2,1)S(1)} %get-tuple-element.51.mask_ref.refs_0_, bf16[34,16,16,128]{3,2,1,0:T(8,128)(2,1)S(1)} %get-tuple-element.52.refs_0_.refs_1_, ...), custom_call_target="tpu_custom_call" | custom-call | flops 905969664 | bytes 2097152 | tf_op jit(solution)/shard_map/pallas_call | solution.py:383
  64.2 1.5 %collective-permute-done.16.refs_2_ = f32[112,128]{1,0:T(8,128)S(1)} collective-permute-done((f32[112,128]{1,0:T(8,128)S(1)}, f32[112,128]{1,0:T(8,128)S(1)}, u32[]{:S(2)}, u32[]{:S(2)}) %collective-permute-start.16) | collective-permute-done | bytes 57376 | tf_op jit(solution)/shard_map/ppermute | solution.py:480
  65.7 1.8 %collective-permute-start.20 = (f32[112,128]{1,0:T(8,128)S(1)}, f32[112,128]{1,0:T(8,128)S(1)}, u32[]{:S(2)}, u32[]{:S(2)}) collective-permute-start(f32[112,128]{1,0:T(8,128)S(1)} %shard_map.83.refs_10_.refs_0_), channel_id=1, source_target_pairs={{0,12},{4,8},{8,4},{12,0},{1,13},{5,9},{9,5},{13,1},{2,14},{6,10},... | collective-permute-start | bytes 172040 | tf_op jit(solution)/shard_map/ppermute | solution.py:480
  68.1 0.9 %collective-permute-start.18 = (f32[112,128]{1,0:T(8,128)S(1)}, f32[112,128]{1,0:T(8,128)S(1)}, u32[]{:S(2)}, u32[]{:S(2)}) collective-permute-start(f32[112,128]{1,0:T(8,128)S(1)} %shard_map.83.refs_10_.refs_0_), channel_id=1, source_target_pairs={{0,4},{4,0},{8,12},{12,8},{1,5},{5,1},{9,13},{13,9},{2,6},{6,2},{1... | collective-permute-start | bytes 172040 | tf_op jit(solution)/shard_map/ppermute | solution.py:480
  69.1 2.2 %shard_map.84 = (bf16[32,16,16,128]{3,2,1,0:T(8,128)(2,1)}, f32[2,256,128]{2,1,0:T(8,128)S(1)}, bf16[3,4,18,16,128]{4,3,2,1,0:T(8,128)(2,1)S(1)}) custom-call(bf16[4,16,16,128]{3,2,1,0:T(8,128)(2,1)S(1)} %get-tuple-element.51.mask_ref.refs_0_, bf16[34,16,16,128]{3,2,1,0:T(8,128)(2,1)S(1)} %get-tuple-element.52.refs_0_.refs_1_, ...), custom_call_target="tpu_custom_call", output_to_operand_aliasing={{0}: (11, {})} | custom-call | flops 905969664 | bytes 2097152 | tf_op jit(solution)/shard_map/pallas_call | solution.py:383
  72.1 3.0 %collective-permute-start.23 = (f32[448,128]{1,0:T(8,128)S(1)}, f32[448,128]{1,0:T(8,128)S(1)}, u32[]{:S(2)}, u32[]{:S(2)}) collective-permute-start(f32[448,128]{1,0:T(8,128)S(1)} %shard_map.85.refs_11_.refs_0_), channel_id=1, source_target_pairs={{0,96},{16,112},{32,64},{48,80},{64,32},{80,48},{96,0},{112,16},{1... | collective-permute-start | bytes 688136 | tf_op jit(solution)/shard_map/ppermute | solution.py:480
  75.8 9.4 %shard_map.86 = (bf16[32,16,16,128]{3,2,1,0:T(8,128)(2,1)}, f32[8,128]{1,0:T(8,128)S(1)}) custom-call(bf16[4,16,16,128]{3,2,1,0:T(8,128)(2,1)S(1)} %get-tuple-element.51.mask_ref.refs_0_, bf16[34,16,16,128]{3,2,1,0:T(8,128)(2,1)S(1)} %get-tuple-element.52.refs_0_.refs_1_, ...), custom_call_target="tpu_custom_call", output_to_operand_aliasing={{0}: (12, {})} | custom-call | flops 5435817984 | bytes 2097152 | tf_op jit(solution)/shard_map/pallas_call | solution.py:383
  85.3 5.0 %collective-permute-start.24 = (f32[1344,128]{1,0:T(8,128)S(1)}, f32[1344,128]{1,0:T(8,128)S(1)}, u32[]{:S(2)}, u32[]{:S(2)}) collective-permute-start(f32[1344,128]{1,0:T(8,128)S(1)} %shard_map.87.refs_1_.refs_2_), channel_id=1, source_target_pairs={{0,16},{16,0},{32,48},{48,32},{64,80},{80,64},{96,112},{112,96},{1... | collective-permute-start | bytes 2064392 | tf_op jit(solution)/shard_map/ppermute | solution.py:608
  90.3 0.9 shard_map.88.refs_2_
  91.3 1.1 %collective-permute-done.25.refs_0_ = f32[448,128]{1,0:T(8,128)S(1)} collective-permute-done((f32[448,128]{1,0:T(8,128)S(1)}, f32[448,128]{1,0:T(8,128)S(1)}, u32[]{:S(2)}, u32[]{:S(2)}) %collective-permute-start.25) | collective-permute-done | bytes 229408 | tf_op jit(solution)/shard_map/ppermute | solution.py:605
  93.0 0.9 shard_map.90
  (52 shorter events, 8.2 us)
Async XLA Ops:
  0.6 1.6 %copy-start = (bf16[32,16,16,128]{3,2,1,0:T(8,128)(2,1)S(1)}, bf16[32,16,16,128]{3,2,1,0:T(8,128)(2,1)}, u32[]{:S(2)}) copy-start(bf16[32,16,16,128]{3,2,1,0:T(8,128)(2,1)} %f_ref.1) | copy-start | bytes 6291460
  2.2 0.7 copy-start.3
  2.9 1.8 %copy-start.1 = (bf16[32,16,16,128]{3,2,1,0:T(8,128)(2,1)S(1)}, bf16[32,16,16,128]{3,2,1,0:T(8,128)(2,1)}, u32[]{:S(2)}) copy-start(bf16[32,16,16,128]{3,2,1,0:T(8,128)(2,1)} %c_ref.1) | copy-start | bytes 6291460
  5.8 15.8 %collective-permute-start = (bf16[2,32,16,128]{3,2,1,0:T(8,128)(2,1)S(1)}, bf16[2,32,16,128]{3,2,1,0:T(8,128)(2,1)S(1)}, u32[]{:S(2)}, u32[]{:S(2)}) collective-permute-start(bf16[2,32,16,128]{3,2,1,0:T(8,128)(2,1)S(1)} %get-tuple-element.58.gyhi), channel_id=1, source_target_pairs={{0,4},{4,8},{8,12},{12,0},{1,5},{5,9},{9,13},{13,1},{2,6},{6,10},{... | collective-permute-start | bytes 786440 | tf_op jit(solution)/shard_map/ppermute | solution.py:534
  8.0 13.6 %collective-permute-start.1 = (bf16[2,32,16,128]{3,2,1,0:T(8,128)(2,1)S(1)}, bf16[2,32,16,128]{3,2,1,0:T(8,128)(2,1)S(1)}, u32[]{:S(2)}, u32[]{:S(2)}) collective-permute-start(bf16[2,32,16,128]{3,2,1,0:T(8,128)(2,1)S(1)} %get-tuple-element.59.gylo), channel_id=1, source_target_pairs={{0,12},{4,0},{8,4},{12,8},{1,13},{5,1},{9,5},{13,9},{2,14},{6,2},{... | collective-permute-start | bytes 786440 | tf_op jit(solution)/shard_map/ppermute | solution.py:534
  9.5 8.1 %collective-permute-start.2 = (bf16[2,32,16,128]{3,2,1,0:T(8,128)(2,1)S(1)}, bf16[2,32,16,128]{3,2,1,0:T(8,128)(2,1)S(1)}, u32[]{:S(2)}, u32[]{:S(2)}) collective-permute-start(bf16[2,32,16,128]{3,2,1,0:T(8,128)(2,1)S(1)} %get-tuple-element.60.refs_2_), channel_id=1, source_target_pairs={{0,1},{1,2},{2,3},{3,0},{4,5},{5,6},{6,7},{7,4},{8,9},{9,10},{10,1... | collective-permute-start | bytes 786440 | tf_op jit(solution)/shard_map/ppermute | solution.py:534
  10.7 6.9 %collective-permute-start.3 = (bf16[2,32,16,128]{3,2,1,0:T(8,128)(2,1)S(1)}, bf16[2,32,16,128]{3,2,1,0:T(8,128)(2,1)S(1)}, u32[]{:S(2)}, u32[]{:S(2)}) collective-permute-start(bf16[2,32,16,128]{3,2,1,0:T(8,128)(2,1)S(1)} %get-tuple-element.61.refs_2_.refs_1_), channel_id=1, source_target_pairs={{0,3},{1,0},{2,1},{3,2},{4,7},{5,4},{6,5},{7,6},{8,11},{9,8},{10,9... | collective-permute-start | bytes 786440 | tf_op jit(solution)/shard_map/ppermute | solution.py:534
  17.6 2.9 %copy-start.2 = (bf16[3,3,3,128,128]{4,3,2,1,0:T(8,128)(2,1)S(1)}, bf16[3,3,3,128,128]{4,3,2,1,0:T(8,128)(2,1)}, u32[]{:S(2)}) copy-start(bf16[3,3,3,128,128]{4,3,2,1,0:T(8,128)(2,1)} %param.6) | copy-start | bytes 2654212
  17.8 4.0 %collective-permute-start.4 = (bf16[2,2,32,128]{3,2,1,0:T(8,128)(2,1)S(1)}, bf16[2,2,32,128]{3,2,1,0:T(8,128)(2,1)S(1)}, u32[]{:S(2)}, u32[]{:S(2)}) collective-permute-start(bf16[2,2,32,128]{3,2,1,0:T(8,128)(2,1)S(1)} %get-tuple-element.62), channel_id=1, source_target_pairs={{0,4},{4,8},{8,12},{12,0},{1,5},{5,9},{9,13},{13,1},{2,6},{6,10},{... | collective-permute-start | bytes 98312 | tf_op jit(solution)/shard_map/ppermute | solution.py:534
  17.8 4.0 %collective-permute-start.5 = (bf16[2,2,32,128]{3,2,1,0:T(8,128)(2,1)S(1)}, bf16[2,2,32,128]{3,2,1,0:T(8,128)(2,1)S(1)}, u32[]{:S(2)}, u32[]{:S(2)}) collective-permute-start(bf16[2,2,32,128]{3,2,1,0:T(8,128)(2,1)S(1)} %get-tuple-element.63.refs_1_.refs_5_), channel_id=1, source_target_pairs={{0,12},{4,0},{8,4},{12,8},{1,13},{5,1},{9,5},{13,9},{2,14},{6,2},{... | collective-permute-start | bytes 98312 | tf_op jit(solution)/shard_map/ppermute | solution.py:534
  22.4 9.9 %collective-permute-start.7 = (bf16[2,21,16,128]{3,2,1,0:T(8,128)(2,1)S(1)}, bf16[2,21,16,128]{3,2,1,0:T(8,128)(2,1)S(1)}, u32[]{:S(2)}, u32[]{:S(2)}) collective-permute-start(bf16[2,21,16,128]{3,2,1,0:T(8,128)(2,1)S(1)} %get-tuple-element.70), channel_id=1, source_target_pairs={{0,16},{16,32},{32,48},{48,64},{64,80},{80,96},{96,112},{112,0},{1... | collective-permute-start | bytes 516104 | tf_op jit(solution)/shard_map/ppermute | solution.py:534
  26.9 5.4 %collective-permute-start.6 = (bf16[2,21,16,128]{3,2,1,0:T(8,128)(2,1)S(1)}, bf16[2,21,16,128]{3,2,1,0:T(8,128)(2,1)S(1)}, u32[]{:S(2)}, u32[]{:S(2)}) collective-permute-start(bf16[2,21,16,128]{3,2,1,0:T(8,128)(2,1)S(1)} %get-tuple-element.69.refs_3_), channel_id=1, source_target_pairs={{0,112},{16,0},{32,16},{48,32},{64,48},{80,64},{96,80},{112,96},{1... | collective-permute-start | bytes 516104 | tf_op jit(solution)/shard_map/ppermute | solution.py:534
  33.5 4.1 %collective-permute-start.8 = (f32[14,128,128]{2,1,0:T(8,128)S(1)}, f32[14,128,128]{2,1,0:T(8,128)S(1)}, u32[]{:S(2)}, u32[]{:S(2)}) collective-permute-start(f32[14,128,128]{2,1,0:T(8,128)S(1)} %get-tuple-element.71.refs_9_), channel_id=1, source_target_pairs={{0,16},{16,0},{32,48},{48,32},{64,80},{80,64},{96,112},{112,96},{1... | collective-permute-start | bytes 2752520 | tf_op jit(solution)/shard_map/ppermute | solution.py:587
  37.7 12.3 %collective-permute-start.10 = (f32[448,128]{1,0:T(8,128)S(1)}, f32[448,128]{1,0:T(8,128)S(1)}, u32[]{:S(2)}, u32[]{:S(2)}) collective-permute-start(f32[448,128]{1,0:T(8,128)S(1)} %get-tuple-element.80), channel_id=1, source_target_pairs={{0,64},{16,80},{32,96},{48,112},{64,0},{80,16},{96,32},{112,48},{1... | collective-permute-start | bytes 688136 | tf_op jit(solution)/shard_map/ppermute | solution.py:480
  40.1 11.6 %collective-permute-start.11 = (f32[448,128]{1,0:T(8,128)S(1)}, f32[448,128]{1,0:T(8,128)S(1)}, u32[]{:S(2)}, u32[]{:S(2)}) collective-permute-start(f32[448,128]{1,0:T(8,128)S(1)} %get-tuple-element.81), channel_id=1, source_target_pairs={{0,96},{16,112},{32,64},{48,80},{64,32},{80,48},{96,0},{112,16},{1... | collective-permute-start | bytes 688136 | tf_op jit(solution)/shard_map/ppermute | solution.py:480
  40.6 11.2 %collective-permute-start.9 = (f32[448,128]{1,0:T(8,128)S(1)}, f32[448,128]{1,0:T(8,128)S(1)}, u32[]{:S(2)}, u32[]{:S(2)}) collective-permute-start(f32[448,128]{1,0:T(8,128)S(1)} %get-tuple-element.75.refs_10_), channel_id=1, source_target_pairs={{0,32},{16,48},{32,0},{48,16},{64,96},{80,112},{96,64},{112,80},{1... | collective-permute-start | bytes 688136 | tf_op jit(solution)/shard_map/ppermute | solution.py:480
  51.8 6.1 %collective-permute-start.13 = (f32[112,128]{1,0:T(8,128)S(1)}, f32[112,128]{1,0:T(8,128)S(1)}, u32[]{:S(2)}, u32[]{:S(2)}) collective-permute-start(f32[112,128]{1,0:T(8,128)S(1)} %get-tuple-element.88), channel_id=1, source_target_pairs={{0,8},{4,12},{8,0},{12,4},{1,9},{5,13},{9,1},{13,5},{2,10},{6,14},... | collective-permute-start | bytes 172040 | tf_op jit(solution)/shard_map/ppermute | solution.py:480
  53.5 4.6 %collective-permute-start.14 = (f32[112,128]{1,0:T(8,128)S(1)}, f32[112,128]{1,0:T(8,128)S(1)}, u32[]{:S(2)}, u32[]{:S(2)}) collective-permute-start(f32[112,128]{1,0:T(8,128)S(1)} %get-tuple-element.89), channel_id=1, source_target_pairs={{0,12},{4,8},{8,4},{12,0},{1,13},{5,9},{9,5},{13,1},{2,14},{6,10},... | collective-permute-start | bytes 172040 | tf_op jit(solution)/shard_map/ppermute | solution.py:480
  54.9 3.5 %collective-permute-start.12 = (f32[112,128]{1,0:T(8,128)S(1)}, f32[112,128]{1,0:T(8,128)S(1)}, u32[]{:S(2)}, u32[]{:S(2)}) collective-permute-start(f32[112,128]{1,0:T(8,128)S(1)} %get-tuple-element.82.refs_11_), channel_id=1, source_target_pairs={{0,4},{4,0},{8,12},{12,8},{1,5},{5,1},{9,13},{13,9},{2,6},{6,2},{1... | collective-permute-start | bytes 172040 | tf_op jit(solution)/shard_map/ppermute | solution.py:480
  58.4 5.8 %collective-permute-start.17 = (f32[112,128]{1,0:T(8,128)S(1)}, f32[112,128]{1,0:T(8,128)S(1)}, u32[]{:S(2)}, u32[]{:S(2)}) collective-permute-start(f32[112,128]{1,0:T(8,128)S(1)} %shard_map.81.refs_10_.refs_0_), channel_id=1, source_target_pairs={{0,3},{1,2},{2,1},{3,0},{4,7},{5,6},{6,5},{7,4},{8,11},{9,10},{10,... | collective-permute-start | bytes 172040 | tf_op jit(solution)/shard_map/ppermute | solution.py:480
  61.2 4.5 %collective-permute-start.16 = (f32[112,128]{1,0:T(8,128)S(1)}, f32[112,128]{1,0:T(8,128)S(1)}, u32[]{:S(2)}, u32[]{:S(2)}) collective-permute-start(f32[112,128]{1,0:T(8,128)S(1)} %shard_map.81.refs_10_.refs_0_), channel_id=1, source_target_pairs={{0,2},{1,3},{2,0},{3,1},{4,6},{5,7},{6,4},{7,5},{8,10},{9,11},{10,... | collective-permute-start | bytes 172040 | tf_op jit(solution)/shard_map/ppermute | solution.py:480
  61.5 4.2 %collective-permute-start.15 = (f32[112,128]{1,0:T(8,128)S(1)}, f32[112,128]{1,0:T(8,128)S(1)}, u32[]{:S(2)}, u32[]{:S(2)}) collective-permute-start(f32[112,128]{1,0:T(8,128)S(1)} %shard_map.81.refs_10_.refs_0_), channel_id=1, source_target_pairs={{0,1},{1,0},{2,3},{3,2},{4,5},{5,4},{6,7},{7,6},{8,9},{9,8},{10,11... | collective-permute-start | bytes 172040 | tf_op jit(solution)/shard_map/ppermute | solution.py:480
  65.7 5.6 %collective-permute-start.20 = (f32[112,128]{1,0:T(8,128)S(1)}, f32[112,128]{1,0:T(8,128)S(1)}, u32[]{:S(2)}, u32[]{:S(2)}) collective-permute-start(f32[112,128]{1,0:T(8,128)S(1)} %shard_map.83.refs_10_.refs_0_), channel_id=1, source_target_pairs={{0,12},{4,8},{8,4},{12,0},{1,13},{5,9},{9,5},{13,1},{2,14},{6,10},... | collective-permute-start | bytes 172040 | tf_op jit(solution)/shard_map/ppermute | solution.py:480
  67.6 4.5 %collective-permute-start.19 = (f32[112,128]{1,0:T(8,128)S(1)}, f32[112,128]{1,0:T(8,128)S(1)}, u32[]{:S(2)}, u32[]{:S(2)}) collective-permute-start(f32[112,128]{1,0:T(8,128)S(1)} %shard_map.83.refs_10_.refs_0_), channel_id=1, source_target_pairs={{0,8},{4,12},{8,0},{12,4},{1,9},{5,13},{9,1},{13,5},{2,10},{6,14},... | collective-permute-start | bytes 172040 | tf_op jit(solution)/shard_map/ppermute | solution.py:480
  68.1 4.0 %collective-permute-start.18 = (f32[112,128]{1,0:T(8,128)S(1)}, f32[112,128]{1,0:T(8,128)S(1)}, u32[]{:S(2)}, u32[]{:S(2)}) collective-permute-start(f32[112,128]{1,0:T(8,128)S(1)} %shard_map.83.refs_10_.refs_0_), channel_id=1, source_target_pairs={{0,4},{4,0},{8,12},{12,8},{1,5},{5,1},{9,13},{13,9},{2,6},{6,2},{1... | collective-permute-start | bytes 172040 | tf_op jit(solution)/shard_map/ppermute | solution.py:480
  72.1 13.1 %collective-permute-start.23 = (f32[448,128]{1,0:T(8,128)S(1)}, f32[448,128]{1,0:T(8,128)S(1)}, u32[]{:S(2)}, u32[]{:S(2)}) collective-permute-start(f32[448,128]{1,0:T(8,128)S(1)} %shard_map.85.refs_11_.refs_0_), channel_id=1, source_target_pairs={{0,96},{16,112},{32,64},{48,80},{64,32},{80,48},{96,0},{112,16},{1... | collective-permute-start | bytes 688136 | tf_op jit(solution)/shard_map/ppermute | solution.py:480
  75.1 10.1 %collective-permute-start.22 = (f32[448,128]{1,0:T(8,128)S(1)}, f32[448,128]{1,0:T(8,128)S(1)}, u32[]{:S(2)}, u32[]{:S(2)}) collective-permute-start(f32[448,128]{1,0:T(8,128)S(1)} %shard_map.85.refs_11_.refs_0_), channel_id=1, source_target_pairs={{0,64},{16,80},{32,96},{48,112},{64,0},{80,16},{96,32},{112,48},{1... | collective-permute-start | bytes 688136 | tf_op jit(solution)/shard_map/ppermute | solution.py:480
  75.1 10.1 %collective-permute-start.21 = (f32[448,128]{1,0:T(8,128)S(1)}, f32[448,128]{1,0:T(8,128)S(1)}, u32[]{:S(2)}, u32[]{:S(2)}) collective-permute-start(f32[448,128]{1,0:T(8,128)S(1)} %shard_map.85.refs_11_.refs_0_), channel_id=1, source_target_pairs={{0,32},{16,48},{32,0},{48,16},{64,96},{80,112},{96,64},{112,80},{1... | collective-permute-start | bytes 688136 | tf_op jit(solution)/shard_map/ppermute | solution.py:480
  85.3 7.8 %collective-permute-start.24 = (f32[1344,128]{1,0:T(8,128)S(1)}, f32[1344,128]{1,0:T(8,128)S(1)}, u32[]{:S(2)}, u32[]{:S(2)}) collective-permute-start(f32[1344,128]{1,0:T(8,128)S(1)} %shard_map.87.refs_1_.refs_2_), channel_id=1, source_target_pairs={{0,16},{16,0},{32,48},{48,32},{64,80},{80,64},{96,112},{112,96},{1... | collective-permute-start | bytes 2064392 | tf_op jit(solution)/shard_map/ppermute | solution.py:608
  90.2 2.1 %collective-permute-start.25 = (f32[448,128]{1,0:T(8,128)S(1)}, f32[448,128]{1,0:T(8,128)S(1)}, u32[]{:S(2)}, u32[]{:S(2)}) collective-permute-start(f32[448,128]{1,0:T(8,128)S(1)} %shard_map.85.refs_11_.refs_0_), channel_id=1, source_target_pairs={{0,16},{16,0},{32,48},{48,32},{64,80},{80,64},{96,112},{112,96},{1... | collective-permute-start | bytes 688136 | tf_op jit(solution)/shard_map/ppermute | solution.py:605

commit v3 on v2

--- a/solution.py
+++ b/solution.py
@@ -55,20 +55,27 @@
     zlo_ref, zhi_ref, ylo_ref, yhi_ref = faces
     for end in (0, X + 1):
         s_ref[end] = jnp.zeros((Y, Z, C), BF16)
-    for brick in range(X // E):
-        span = slice(brick * E, (brick + 1) * E)
+
+    def one(brick, carry):
+        span = pl.ds(brick * E, E)
         keep = mask_ref[brick].astype(F32) > 0.0
         value = jnp.where(keep[None], source[span].astype(F32), 0.0).astype(BF16)
-        s_ref[brick * E + 1 : (brick + 1) * E + 1] = value
+        s_ref[pl.ds(brick * E + 1, E)] = value
         zlo_ref[part, span] = value[:, :, 0, :]
         zhi_ref[part, span] = value[:, :, Z - 1, :]
         ylo_ref[part, span] = value[:, 0]
         yhi_ref[part, span] = value[:, Y - 1]
-
-
-def prepare_x_kernel(occ_ref, f_ref, s_ref, mask_ref, *faces):
+        return carry
+
+    lax.fori_loop(0, X // E, one, 0)
+
+
+def mask_kernel(occ_ref, mask_ref):
     for brick in range(X // E):
         mask_ref[brick] = jnp.where(brick_flags(occ_ref, brick), 1.0, 0.0).astype(BF16)
+
+
+def prepare_x_kernel(f_ref, mask_ref, s_ref, *faces):
     mask_slabs(0, f_ref, mask_ref, s_ref, faces)
 
 
@@ -81,16 +88,18 @@
 
 def prepare(occupancy, features, cotangent):
     slabs = shape((X + 2, Y, Z, C), BF16)
-    mask = shape((X // E, Y, Z, C), BF16)
     own_cost = pl.CostEstimate(flops=1000000, bytes_accessed=5 << 20, transcendentals=0)
-    fields, mask, *given = pl.pallas_call(
+    mask = small_kernel(
+        mask_kernel, shape((X // E, Y, Z, C), BF16), [jnp.transpose(occupancy, (1, 2, 0))], specs=[SMEM]
+    )
+    fields, *given = pl.pallas_call(
         prepare_x_kernel,
-        in_specs=[SMEM, VMEM],
-        out_specs=[VMEM] * 6,
-        out_shape=[slabs, mask] + [shape((1, X, Z, C), BF16)] * 4,
+        in_specs=[VMEM] * 2,
+        out_specs=[VMEM] * 5,
+        out_shape=[slabs] + [shape((1, X, Z, C), BF16)] * 4,
         compiler_params=params(),
         cost_estimate=own_cost,
-    )(jnp.transpose(occupancy, (1, 2, 0)), features)
+    )(features, mask)
     cotangents, *faces = pl.pallas_call(
         prepare_g_kernel,
         in_specs=[VMEM] * 6,
@@ -253,9 +262,16 @@
     far_lo = refs.pop(0) if starts else None
     far_hi = refs.pop(0) if ends else None
     before = None if starts else refs.pop(0)
+    late_in = None if starts else refs.pop(0)
     ready = None if starts and part == 0 else refs.pop(0)
+    late = None if ends else refs.pop(-5)
     o_ref, carry_ref, even, odd, edge, made_ref, left = refs[-7:]
     count = groups * GROUP
+    own_copies = groups if ends else groups - 1
+    late_copy = None
+    if not starts:
+        late_copy = pltpu.make_async_copy(late_in, o_ref.at[pl.ds(first - GROUP - 1, GROUP)], left.at[groups + 1])
+        late_copy.start()
 
     def put(shifted, at, x):
         for slot in range(GROUP):
@@ -280,13 +296,12 @@
         finish(x, next_ + term(0, 1) + term(1, 2))
         for slot in range(1, GROUP - 1):
             finish(x + slot, term(slot - 1, 0) + term(slot, 1) + term(slot + 1, 2))
-        if opens is None:
-            pl.when(sem == 0)(lambda: copy(x + 1, GROUP - 1, sem).start())
-            pl.when(sem > 0)(lambda: copy(x, GROUP, sem).start())
-        elif opens:
+        if opens:
             copy(x + 1, GROUP - 1, sem).start()
+        elif ends:
+            copy(x, GROUP, sem).start()
         else:
-            copy(x, GROUP, sem).start()
+            pl.when(sem < own_copies)(lambda: copy(x, GROUP, sem).start())
         return term(GROUP - 2, 0) + term(GROUP - 1, 1), term(GROUP - 1, 0)
 
     if starts:
@@ -296,16 +311,13 @@
     else:
         near, next_ = before[0], before[1]
     if groups > 2:
-        if ready is None:
-            put(even, part, 0)
-        else:
-            even[...] = ready[...]
+        even[...] = ready[...]
         carry_ref[0] = near
         carry_ref[1] = next_
 
         def trip(i, carry):
             x = first + i * 2 * GROUP
-            near, next_ = group(even, x, 2 * i, carry_ref[0], carry_ref[1], None if starts else False)
+            near, next_ = group(even, x, 2 * i, carry_ref[0], carry_ref[1], False)
             put(odd, part, x + GROUP)
             near, next_ = group(odd, x + GROUP, 2 * i + 1, near, next_, False)
             after = i + 1 == groups // 2
@@ -319,9 +331,11 @@
         near = carry_ref[0]
     else:
         if ready is None:
-            ready = odd
-            put(odd, part, first)
+            ready = even
+            put(even, part, first)
         near, next_ = group(ready, first, 0, near, next_, starts)
+        put(odd, part, first + GROUP)
+        near, next_ = group(odd, first + GROUP, 1, near, next_, False)
         put(even, *following)
         carry_ref[0] = near
         carry_ref[1] = next_
@@ -330,7 +344,9 @@
         last = jnp.dot(patches(edge, 1), w_ref[:, 2 * C :], preferred_element_type=F32)
         finish(X - 1, near + last)
         copy(X, 1, groups).start()
-    for sem in range(groups):
+    if late is not None:
+        late[...] = made_ref[count - GROUP : count]
+    for sem in range(own_copies):
         x = first + sem * GROUP
         if starts and sem == 0:
             copy(x + 1, GROUP - 1, sem).wait()
@@ -338,9 +354,11 @@
             copy(x, GROUP, sem).wait()
     if ends:
         copy(X, 1, groups).wait()
-
-
-def conv_piece(part, first, groups, following, mask, field, far, weight, before, ready, done, tie):
+    if late_copy is not None:
+        late_copy.wait()
+
+
+def conv_piece(part, first, groups, following, mask, field, far, weight, state, done, tie):
     operands = [mask, *field, weight]
     starts, ends = first == 0, first + groups * GROUP == X
     if starts:
@@ -348,9 +366,9 @@
     if ends:
         operands.append(far[1])
     if not starts:
-        operands.append(before)
-    if ready is not None:
-        operands.append(ready)
+        operands += [state["carry"], state["late"]]
+    if "ready" in state:
+        operands.append(state["ready"])
     aliases = {}
     specs = [VMEM] * len(operands)
     operands.append(tie)
@@ -362,16 +380,16 @@
     shifted = (3, GROUP, Y + 2, Z, C)
     more = following is not None
     buffers = [shape((2, ROWS, C), F32), shape(shifted, BF16)]
-    small = shape((8, C), F32)
-
+    kept = buffers + ([] if ends else [shape((GROUP, Y, Z, C), BF16)])
     scratch = [
         pltpu.VMEM(shifted, BF16),
         pltpu.VMEM((3, 1, Y + 2, Z, C), BF16),
         pltpu.VMEM((groups * GROUP + 1, Y, Z, C), BF16),
-        pltpu.SemaphoreType.DMA((groups + 1,)),
+        pltpu.SemaphoreType.DMA((groups + 2,)),
     ]
     if not more:
         scratch = [pltpu.VMEM(b.shape, b.dtype) for b in buffers] + scratch
+        kept = [shape((8, C), F32)]
 
     def plain(*refs):
         conv_kernel(part, first, groups, following, *refs)
@@ -380,16 +398,17 @@
         refs[-7][...] = jnp.zeros((8, C), F32)
         conv_kernel(part, first, groups, following, *refs[:-7], *refs[-6:])
 
-    return pl.pallas_call(
+    made, *kept = pl.pallas_call(
         plain if more else final,
         in_specs=specs,
-        out_specs=[ANY] + [VMEM] * (2 if more else 1),
-        out_shape=[shape((X, Y, Z, C), BF16)] + (buffers if more else [small]),
+        out_specs=[ANY] + [VMEM] * len(kept),
+        out_shape=[shape((X, Y, Z, C), BF16)] + kept,
         scratch_shapes=scratch,
         input_output_aliases=aliases,
         compiler_params=params(),
         cost_estimate=cost(groups * GROUP, 2 << 20),
     )(*operands)
+    return made, dict(zip(("carry", "ready", "late"), kept, strict=False))
 
 
 def small_kernel(kernel, out_shape, operands, ties=(), specs=None):
@@ -439,22 +458,35 @@
         flipped[row * C : (row + 1) * C, tx * C : (tx + 1) * C] = w_ref[26 - tap].astype(F32).T.astype(BF16)
 
 
-def place(axis):
-    at = lax.axis_index(axis)
-    return at // 2 if axis == "gx" else at
-
-
-def pairs(axis, step):
-    if axis == "gx":
-        return [(2 * z + c, 2 * (z ^ step) + c) for z in range(4) for c in range(2)]
-    return [(i, i ^ step) for i in range(4)]
-
-
-def deal(axis, terms, ties=()):
+def places():
+    at = lax.axis_index("gx")
+    core, z, y = at % 2, at // 2, lax.axis_index("gy")
+    return core, z * (1 - core) + y * core, y * (1 - core) + z * core
+
+
+def pairs(turn, step):
+    found = []
+    for z in range(4):
+        for core in range(2):
+            for y in range(4):
+                along_z = (turn == 1) == (core == 0)
+                partner = (z ^ step, y) if along_z else (z, y ^ step)
+                found.append(((2 * z + core) * 4 + y, (2 * partner[0] + core) * 4 + partner[1]))
+    return found
+
+
+def exchange(turn, values):
+    steps = zip((1, 2, 3), values, strict=True)
+    if turn == 3:
+        return [lax.ppermute(value, "gz", [(i, i ^ step) for i in range(4)]) for step, value in steps]
+    return [lax.ppermute(value, ("gx", "gy"), pairs(turn, step)) for step, value in steps]
+
+
+def deal(turn, terms, ties=()):
     rows = terms[0].shape[0] // 4
 
     def kernel(*refs):
-        me = place(axis)
+        me = places()[turn]
         for step in range(4):
             at = pl.ds((me ^ step) * rows, rows)
             total = refs[0][at]
@@ -465,19 +497,15 @@
     return small_kernel(kernel, [shape((rows, C), F32)] * 4, terms, ties)
 
 
-def collect(axis, parts, ties=()):
+def collect(turn, parts, ties=()):
     rows = parts[0].shape[0]
 
     def kernel(*refs):
-        me = place(axis)
+        me = places()[turn]
         for step in range(4):
             refs[4][pl.ds((me ^ step) * rows, rows)] = refs[step][...]
 
     return small_kernel(kernel, shape((4 * rows, C), F32), parts, ties)
-
-
-def exchange(axis, values):
-    return [lax.ppermute(value, axis, pairs(axis, step)) for step, value in zip((1, 2, 3), values, strict=True)]
 
 
 def sum_kernel(a, b, c, d, o):
@@ -492,9 +520,9 @@
 
     def kernel(*refs):
         o_ref, left = refs[-2:]
-        core = lax.axis_index("gx") % 2
-        half = core if mine else 1 - core
-        me = place("gx")
+        at = lax.axis_index("gx")
+        half = at % 2 if mine else 1 - at % 2
+        me = at // 2 * (1 - half) + lax.axis_index("gy") * half
         for act in ("start", "wait"):
             sem = 0
             for ref, (_, steps) in zip(refs, sources, strict=False):
@@ -569,42 +597,40 @@
     field = [*slabs, held_ylo, held_yhi, col_lo, col_hi]
     made = [None, None]
     weights = (forward, flipped)
-    order = [(0, 0, 1), (0, 4, 6), (0, 28, 1), (1, 0, 1), (1, 4, 1), (1, 8, 6)]
-    state = {"carry": None, "ready": None}
+    order = [(0, 0, 2), (0, 8, 4), (0, 24, 2), (1, 0, 2), (1, 8, 2), (1, 16, 4)]
+    state = {}
 
     def convolve(tie):
         part, first, groups = order.pop(0)
         following = order[0][:2] if order else None
-        made[part], *rest = conv_piece(
-            part, first, groups, following, mask, field, far, weights[part],
-            state["carry"], state["ready"], made[part], tie,
+        made[part], kept = conv_piece(
+            part, first, groups, following, mask, field, far, weights[part], state, made[part], tie
         )
-        if order:
-            state["carry"], state["ready"] = rest
-        return rest[:1]
+        state.update(kept)
+        return [kept["carry"]]
 
     swap = [(i, i ^ 1) for i in range(8)]
     came = lax.ppermute(send, "gx", swap)
     ties = convolve(send)
     flat = (HALF * C, C)
-    own, *parts = deal("gx", [keep.reshape(flat), came.reshape(flat)], ties)
-    came = exchange("gx", parts)
+    own, *parts = deal(1, [keep.reshape(flat), came.reshape(flat)], ties)
+    came = exchange(1, parts)
     ties = convolve(parts[0])
-    own, *parts = deal("gy", [own, *came], ties)
-    came = exchange("gy", parts)
+    own, *parts = deal(2, [own, *came], ties)
+    came = exchange(2, parts)
     ties = convolve(parts[0])
     part_shape = shape(own.shape, F32)
     mine = small_kernel(sum_kernel, part_shape, [own, *came], ties)
-    came = exchange("gz", [mine] * 3)
+    came = exchange(3, [mine] * 3)
     ties = convolve(mine)
     summed = small_kernel(sum_kernel, part_shape, [mine, *came], ties)
-    came = exchange("gy", [summed] * 3)
+    came = exchange(2, [summed] * 3)
     ties = convolve(summed)
-    chunk = collect("gy", [summed, *came], ties)
-    came = exchange("gx", [chunk] * 3)
+    chunk = collect(2, [summed, *came], ties)
+    came = exchange(1, [chunk] * 3)
     beside = lax.ppermute(chunk, "gx", swap)
-    (tie,) = convolve(chunk)
-    joined = small_kernel(join_kernel, shape((3 * chunk.shape[0], C), F32), came, [tie])
+    ties = convolve(chunk)
+    joined = small_kernel(join_kernel, shape((3 * chunk.shape[0], C), F32), came, [beside, *ties])
     others = lax.ppermute(joined, "gx", swap)
     full = write([(chunk, (0,)), (joined, (1, 2, 3))], True, None, joined)
     full = write([(beside, (0,))], False, full, joined)

time: 94.3 us -> 88.7 us (0.941)
  waiting for transfers between devices: 5.81 us -> 1.36 us
  Pallas kernels: 47.5 us -> 45.1 us
    ppermute x1, starting transfers between devices: 0.09 us -> 5.04 us  [body(): beside = lax.ppermute(chunk, 'gx', swap)]
    ppermute x1, starting transfers between devices: 4.95 us -> 1 us  [body(): others = lax.ppermute(joined, 'gx', swap)]
    ppermute x15, waiting for transfers between devices: 4.48 us -> 1 us  [the longest x12 0.7 us: exchange(): lax.ppermute(value, ('gx', 'gy'), pairs(turn, step))]
    pallas_call x6, Pallas kernels: 28.2 us -> 26.2 us  [conv_piece(): pl.pallas_call(plain if more else final, in_specs=specs, out_specs=[ANY]...]
    ppermute x1, waiting for transfers between devices: 1.07 us -> 0.01 us  [body(): beside = lax.ppermute(chunk, 'gx', swap)]
    pallas_call x10 -> x11, Pallas kernels: 2 us -> 2.6 us  [small_kernel(): pl.pallas_call(run, in_specs=(specs or [VMEM] * count) + [ANY] * len(ties...]
  transfers between devices with their start and end apart: 26 -> 26, of which waited for: 7 -> 5; matrix products, arithmetic and copies ran while one was open for 0% -> 0% of each run, Pallas kernels for 44% -> 45%
where the time goes in v3:
time: 88.7 us; the launch traced here: 88.5 us
  Pallas kernels  45.1 us (51%)
  starting transfers between devices  37.9 us (43%)
  local copies, waits for them, and re-layouts  2.95 us (3%)
  waiting for transfers between devices  1.36 us (2%)
  between operations  1.18 us (1%)
    pallas_call x6, Pallas kernels, conv_piece(): pl.pallas_call(plain if more else final, in_specs=specs, out_specs=[ANY]...  26.2 us
    ppermute x8, starting transfers between devices, shift(): lax.ppermute(value, axis, [(i, (i + step) % count) for i in range(count)])  13.6 us
    ppermute x12, starting transfers between devices, exchange(): lax.ppermute(value, ('gx', 'gy'), pairs(turn, step))  13.3 us
    pallas_call x2, Pallas kernels, own_grad(): pl.pallas_call(lambda *refs: own_grad_kernel(first, more, *refs), in_spec...  10.8 us
    ppermute x1, starting transfers between devices, body(): beside = lax.ppermute(chunk, 'gx', swap)  5.04 us
    ppermute x3, starting transfers between devices, exchange(): lax.ppermute(value, 'gz', [(i, i ^ step) for i in range(4)])  3.42 us
    unnamed x8, local copies, waits for them, and re-layouts  2.95 us
    pallas_call x11, Pallas kernels, small_kernel(): pl.pallas_call(run, in_specs=(specs or [VMEM] * count) + [ANY] * len(ties...  2.6 us
  transfers between devices with their start and end apart: 26, of which 5 were waited for; matrix products, arithmetic and copies ran while one was open for 0% of the time, Pallas kernels for 45%

profile of v3, /device:TPU:1, one launch (start us, length us, event | category | flops | bytes accessed | tf_op | source)
XLA Modules:
  0.0 88.5 jit_solution(16225631966896392311)
XLA Ops:
  1.9 1.6 %copy-done = bf16[32,16,16,128]{3,2,1,0:T(8,128)(2,1)S(1)} copy-done((bf16[32,16,16,128]{3,2,1,0:T(8,128)(2,1)S(1)}, bf16[32,16,16,128]{3,2,1,0:T(8,128)(2,1)}, u32[]{:S(2)}) %copy-start) | copy-done | bytes 2097176
  3.5 0.9 %shard_map.68 = (bf16[34,16,16,128]{3,2,1,0:T(8,128)(2,1)S(1)}, bf16[1,32,16,128]{3,2,1,0:T(8,128)(2,1)S(1)}, bf16[1,32,16,128]{3,2,1,0:T(8,128)(2,1)S(1)}, bf16...) custom-call(bf16[32,16,16,128]{3,2,1,0:T(8,128)(2,1)S(1)} %copy-done, ...), custom_call_target="tpu_custom_call" | custom-call | flops 1000000 | bytes 5242880 | tf_op jit(solution)/shard_map/pallas_call | solution.py:95
  5.1 0.9 %shard_map.69 = (bf16[34,16,16,128]{3,2,1,0:T(8,128)(2,1)S(1)}, bf16[2,32,16,128]{3,2,1,0:T(8,128)(2,1)S(1)}, bf16[2,32,16,128]{3,2,1,0:T(8,128)(2,1)S(1)}, bf16...) custom-call(bf16[32,16,16,128]{3,2,1,0:T(8,128)(2,1)S(1)} %copy-done.1, ...), custom_call_target="tpu_custom_call" | custom-call | flops 1000000 | bytes 5242880 | tf_op jit(solution)/shard_map/pallas_call | solution.py:103
  6.0 2.2 %collective-permute-start = (bf16[2,32,16,128]{3,2,1,0:T(8,128)(2,1)S(1)}, bf16[2,32,16,128]{3,2,1,0:T(8,128)(2,1)S(1)}, u32[]{:S(2)}, u32[]{:S(2)}) collective-permute-start(bf16[2,32,16,128]{3,2,1,0:T(8,128)(2,1)S(1)} %get-tuple-element.60.gyhi), channel_id=1, source_target_pairs={{0,4},{4,8},{8,12},{12,0},{1,5},{5,9},{9,13},{13,1},{2,6},{6,10},{... | collective-permute-start | bytes 786440 | tf_op jit(solution)/shard_map/ppermute | solution.py:562
  8.2 1.5 %collective-permute-start.1 = (bf16[2,32,16,128]{3,2,1,0:T(8,128)(2,1)S(1)}, bf16[2,32,16,128]{3,2,1,0:T(8,128)(2,1)S(1)}, u32[]{:S(2)}, u32[]{:S(2)}) collective-permute-start(bf16[2,32,16,128]{3,2,1,0:T(8,128)(2,1)S(1)} %get-tuple-element.61.gylo), channel_id=1, source_target_pairs={{0,12},{4,0},{8,4},{12,8},{1,13},{5,1},{9,5},{13,9},{2,14},{6,2},{... | collective-permute-start | bytes 786440 | tf_op jit(solution)/shard_map/ppermute | solution.py:562
  9.7 1.2 %collective-permute-start.2 = (bf16[2,32,16,128]{3,2,1,0:T(8,128)(2,1)S(1)}, bf16[2,32,16,128]{3,2,1,0:T(8,128)(2,1)S(1)}, u32[]{:S(2)}, u32[]{:S(2)}) collective-permute-start(bf16[2,32,16,128]{3,2,1,0:T(8,128)(2,1)S(1)} %get-tuple-element.62.refs_2_), channel_id=1, source_target_pairs={{0,1},{1,2},{2,3},{3,0},{4,5},{5,6},{6,7},{7,4},{8,9},{9,10},{10,1... | collective-permute-start | bytes 786440 | tf_op jit(solution)/shard_map/ppermute | solution.py:562
  11.0 1.5 %collective-permute-start.3 = (bf16[2,32,16,128]{3,2,1,0:T(8,128)(2,1)S(1)}, bf16[2,32,16,128]{3,2,1,0:T(8,128)(2,1)S(1)}, u32[]{:S(2)}, u32[]{:S(2)}) collective-permute-start(bf16[2,32,16,128]{3,2,1,0:T(8,128)(2,1)S(1)} %get-tuple-element.63.refs_2_.refs_1_), channel_id=1, source_target_pairs={{0,3},{1,0},{2,1},{3,2},{4,7},{5,4},{6,5},{7,6},{8,11},{9,8},{10,9... | collective-permute-start | bytes 786440 | tf_op jit(solution)/shard_map/ppermute | solution.py:562
  12.4 5.4 %shard_map.70.refs_2_.refs_0_ = f32[1152,384]{1,0:T(8,128)S(1)} custom-call(bf16[34,16,16,128]{3,2,1,0:T(8,128)(2,1)S(1)} %get-tuple-element.54.refs_0_.refs_1_, bf16[34,16,16,128]{3,2,1,0:T(8,128)(2,1)S(1)} %get-tuple-element.59.refs_1_.g_ref.refs_2_, bf16[2,32,16,128]{3,2,1,0:T(8,128)(2,1)S(1)} %get-tuple-element.63.refs_2_.refs_1_), custom_call_target="tpu_custom_call" | custom-call | flops 3623878656 | bytes 8388608 | tf_op jit(solution)/shard_map/pallas_call | solution.py:177
  18.1 2.7 %collective-permute-start.5 = (bf16[2,2,32,128]{3,2,1,0:T(8,128)(2,1)S(1)}, bf16[2,2,32,128]{3,2,1,0:T(8,128)(2,1)S(1)}, u32[]{:S(2)}, u32[]{:S(2)}) collective-permute-start(bf16[2,2,32,128]{3,2,1,0:T(8,128)(2,1)S(1)} %get-tuple-element.65.refs_1_.refs_5_), channel_id=1, source_target_pairs={{0,12},{4,0},{8,4},{12,8},{1,13},{5,1},{9,5},{13,9},{2,14},{6,2},{... | collective-permute-start | bytes 98312 | tf_op jit(solution)/shard_map/ppermute | solution.py:562
  22.6 4.5 %collective-permute-start.7 = (bf16[2,21,16,128]{3,2,1,0:T(8,128)(2,1)S(1)}, bf16[2,21,16,128]{3,2,1,0:T(8,128)(2,1)S(1)}, u32[]{:S(2)}, u32[]{:S(2)}) collective-permute-start(bf16[2,21,16,128]{3,2,1,0:T(8,128)(2,1)S(1)} %get-tuple-element.72), channel_id=1, source_target_pairs={{0,16},{16,32},{32,48},{48,64},{64,80},{80,96},{96,112},{112,0},{1... | collective-permute-start | bytes 516104 | tf_op jit(solution)/shard_map/ppermute | solution.py:562
  27.1 5.4 %shard_map.75.own_ref = f32[1152,384]{1,0:T(8,128)S(1)} custom-call(bf16[34,16,16,128]{3,2,1,0:T(8,128)(2,1)S(1)} %get-tuple-element.54.refs_0_.refs_1_, bf16[34,16,16,128]{3,2,1,0:T(8,128)(2,1)S(1)} %get-tuple-element.59.refs_1_.g_ref.refs_2_, f32[1152,384]{1,0:T(8,128)S(1)} %shard_map.73.refs_9_.refs_2_, bf16[2,21,16,128]{3,2,1,0:T(8,128)(2,1)S(1)} %get-tuple-element.71.refs_3_), custom_call_target="tpu_custom_call" | custom-call | flops 3623878656 | bytes 8388608 | tf_op jit(solution)/shard_map/pallas_call | solution.py:177
  32.6 1.1 %shard_map.76 = (f32[14,128,128]{2,1,0:T(8,128)S(1)}, f32[14,128,128]{2,1,0:T(8,128)S(1)}) custom-call(f32[1152,384]{1,0:T(8,128)S(1)} %shard_map.75.own_ref, bf16[34,16,16,128]{3,2,1,0:T(8,128)(2,1)S(1)} %get-tuple-element.59.refs_1_.g_ref.refs_2_, bf16[2,32,16,128]{3,2,1,0:T(8,128)(2,1)S(1)} %get-tuple-element.61.gylo, ...), custom_call_target="tpu_custom_call" | custom-call | flops 679477248 | bytes 6291456 | tf_op jit(solution)/shard_map/pallas_call | solution.py:245
  33.7 1.5 %collective-permute-start.8 = (f32[14,128,128]{2,1,0:T(8,128)S(1)}, f32[14,128,128]{2,1,0:T(8,128)S(1)}, u32[]{:S(2)}, u32[]{:S(2)}) collective-permute-start(f32[14,128,128]{2,1,0:T(8,128)S(1)} %get-tuple-element.73.refs_9_), channel_id=1, source_target_pairs={{0,16},{16,0},{32,48},{48,32},{64,80},{80,64},{96,112},{112,96},{1... | collective-permute-start | bytes 2752520 | tf_op jit(solution)/shard_map/ppermute | solution.py:613
  35.2 3.3 %shard_map.77 = (bf16[32,16,16,128]{3,2,1,0:T(8,128)(2,1)}, f32[2,256,128]{2,1,0:T(8,128)S(1)}, bf16[3,4,18,16,128]{4,3,2,1,0:T(8,128)(2,1)S(1)}, bf16[4,16,16,128]{3,2,1,0:T(8,128)(2,1)S(1)}) custom-call(bf16[4,16,16,128]{3,2,1,0:T(8,128)(2,1)S(1)} %shard_map.67.mask_ref.refs_0_, bf16[34,16,16,128]{3,2,1,0:T(8,128)(2,1)S(1)} %get-tuple-element.54.refs_0_.refs_1_, ...), custom_call_target="tpu_custom_call" | custom-call | flops 1811939328 | bytes 2097152 | tf_op jit(solution)/shard_map/pallas_call | solution.py:401
  38.7 1.7 %collective-permute-start.10 = (f32[448,128]{1,0:T(8,128)S(1)}, f32[448,128]{1,0:T(8,128)S(1)}, u32[]{:S(2)}, u32[]{:S(2)}) collective-permute-start(f32[448,128]{1,0:T(8,128)S(1)} %get-tuple-element.84), channel_id=1, source_target_pairs={{0,64},{4,68},{8,72},{12,76},{16,24},{20,28},{24,16},{28,20},{32,9... | collective-permute-start | bytes 688136 | tf_op jit(solution)/shard_map/ppermute | solution.py:482
  40.4 1.4 %collective-permute-start.11 = (f32[448,128]{1,0:T(8,128)S(1)}, f32[448,128]{1,0:T(8,128)S(1)}, u32[]{:S(2)}, u32[]{:S(2)}) collective-permute-start(f32[448,128]{1,0:T(8,128)S(1)} %get-tuple-element.85), channel_id=1, source_target_pairs={{0,96},{4,100},{8,104},{12,108},{16,28},{20,24},{24,20},{28,16},{3... | collective-permute-start | bytes 688136 | tf_op jit(solution)/shard_map/ppermute | solution.py:482
  42.3 5.7 %shard_map.79 = (bf16[32,16,16,128]{3,2,1,0:T(8,128)(2,1)}, f32[2,256,128]{2,1,0:T(8,128)S(1)}, bf16[3,4,18,16,128]{4,3,2,1,0:T(8,128)(2,1)S(1)}, bf16[4,16,16,128]{3,2,1,0:T(8,128)(2,1)S(1)}) custom-call(bf16[4,16,16,128]{3,2,1,0:T(8,128)(2,1)S(1)} %shard_map.67.mask_ref.refs_0_, ...), custom_call_target="tpu_custom_call", output_to_operand_aliasing={{0}: (12, {})} | custom-call | flops 3623878656 | bytes 2097152 | tf_op jit(solution)/shard_map/pallas_call | solution.py:401
  48.5 2.2 %collective-permute-start.13 = (f32[112,128]{1,0:T(8,128)S(1)}, f32[112,128]{1,0:T(8,128)S(1)}, u32[]{:S(2)}, u32[]{:S(2)}) collective-permute-start(f32[112,128]{1,0:T(8,128)S(1)} %get-tuple-element.92), channel_id=1, source_target_pairs={{0,8},{4,12},{8,0},{12,4},{16,80},{20,84},{24,88},{28,92},{32,40},... | collective-permute-start | bytes 172040 | tf_op jit(solution)/shard_map/ppermute | solution.py:482
  50.7 0.7 collective-permute-start.14
  51.6 3.9 %shard_map.81 = (bf16[32,16,16,128]{3,2,1,0:T(8,128)(2,1)}, f32[2,256,128]{2,1,0:T(8,128)S(1)}, bf16[3,4,18,16,128]{4,3,2,1,0:T(8,128)(2,1)S(1)}) custom-call(bf16[4,16,16,128]{3,2,1,0:T(8,128)(2,1)S(1)} %shard_map.67.mask_ref.refs_0_, bf16[34,16,16,128]{3,2,1,0:T(8,128)(2,1)S(1)} %get-tuple-element.54.refs_0_.refs_1_, ...), custom_call_target="tpu_custom_call", output_to_operand_aliasing={{0}: (13, {})} | custom-call | flops 1811939328 | bytes 2097152 | tf_op jit(solution)/shard_map/pallas_call | solution.py:401
  55.6 2.8 %collective-permute-start.17 = (f32[112,128]{1,0:T(8,128)S(1)}, f32[112,128]{1,0:T(8,128)S(1)}, u32[]{:S(2)}, u32[]{:S(2)}) collective-permute-start(f32[112,128]{1,0:T(8,128)S(1)} %shard_map.82.refs_10_.refs_0_), channel_id=1, source_target_pairs={{0,3},{1,2},{2,1},{3,0},{4,7},{5,6},{6,5},{7,4},{8,11},{9,10},{10,... | collective-permute-start | bytes 172040 | tf_op jit(solution)/shard_map/ppermute | solution.py:481
  59.0 3.6 %shard_map.83 = (bf16[32,16,16,128]{3,2,1,0:T(8,128)(2,1)}, f32[2,256,128]{2,1,0:T(8,128)S(1)}, bf16[3,4,18,16,128]{4,3,2,1,0:T(8,128)(2,1)S(1)}, bf16[4,16,16,128]{3,2,1,0:T(8,128)(2,1)S(1)}) custom-call(bf16[4,16,16,128]{3,2,1,0:T(8,128)(2,1)S(1)} %shard_map.67.mask_ref.refs_0_, bf16[34,16,16,128]{3,2,1,0:T(8,128)(2,1)S(1)} %get-tuple-element.54.refs_0_.refs_1_, ...), custom_call_target="tpu_custom_call" | custom-call | flops 1811939328 | bytes 2097152 | tf_op jit(solution)/shard_map/pallas_call | solution.py:401
  62.9 2.1 %collective-permute-start.20 = (f32[112,128]{1,0:T(8,128)S(1)}, f32[112,128]{1,0:T(8,128)S(1)}, u32[]{:S(2)}, u32[]{:S(2)}) collective-permute-start(f32[112,128]{1,0:T(8,128)S(1)} %shard_map.84.refs_11_.refs_0_), channel_id=1, source_target_pairs={{0,12},{4,8},{8,4},{12,0},{16,112},{20,116},{24,120},{28,124},{32,... | collective-permute-start | bytes 172040 | tf_op jit(solution)/shard_map/ppermute | solution.py:482
  65.0 1.0 %collective-permute-start.19 = (f32[112,128]{1,0:T(8,128)S(1)}, f32[112,128]{1,0:T(8,128)S(1)}, u32[]{:S(2)}, u32[]{:S(2)}) collective-permute-start(f32[112,128]{1,0:T(8,128)S(1)} %shard_map.84.refs_11_.refs_0_), channel_id=1, source_target_pairs={{0,8},{4,12},{8,0},{12,4},{16,80},{20,84},{24,88},{28,92},{32,40},... | collective-permute-start | bytes 172040 | tf_op jit(solution)/shard_map/ppermute | solution.py:482
  66.2 3.2 %shard_map.85 = (bf16[32,16,16,128]{3,2,1,0:T(8,128)(2,1)}, f32[2,256,128]{2,1,0:T(8,128)S(1)}, bf16[3,4,18,16,128]{4,3,2,1,0:T(8,128)(2,1)S(1)}, bf16[4,16,16,128]{3,2,1,0:T(8,128)(2,1)S(1)}) custom-call(bf16[4,16,16,128]{3,2,1,0:T(8,128)(2,1)S(1)} %shard_map.67.mask_ref.refs_0_, ...), custom_call_target="tpu_custom_call", output_to_operand_aliasing={{0}: (12, {})} | custom-call | flops 1811939328 | bytes 2097152 | tf_op jit(solution)/shard_map/pallas_call | solution.py:401
  69.6 5.0 %collective-permute-start.24 = (f32[448,128]{1,0:T(8,128)S(1)}, f32[448,128]{1,0:T(8,128)S(1)}, u32[]{:S(2)}, u32[]{:S(2)}) collective-permute-start(f32[448,128]{1,0:T(8,128)S(1)} %shard_map.86.refs_12_.refs_0_), channel_id=1, source_target_pairs={{0,16},{16,0},{32,48},{48,32},{64,80},{80,64},{96,112},{112,96},{1... | collective-permute-start | bytes 688136 | tf_op jit(solution)/shard_map/ppermute | solution.py:631
  74.6 1.3 %collective-permute-start.23 = (f32[448,128]{1,0:T(8,128)S(1)}, f32[448,128]{1,0:T(8,128)S(1)}, u32[]{:S(2)}, u32[]{:S(2)}) collective-permute-start(f32[448,128]{1,0:T(8,128)S(1)} %shard_map.86.refs_12_.refs_0_), channel_id=1, source_target_pairs={{0,96},{4,100},{8,104},{12,108},{16,28},{20,24},{24,20},{28,16},{3... | collective-permute-start | bytes 688136 | tf_op jit(solution)/shard_map/ppermute | solution.py:482
  76.4 1.5 %collective-permute-start.21 = (f32[448,128]{1,0:T(8,128)S(1)}, f32[448,128]{1,0:T(8,128)S(1)}, u32[]{:S(2)}, u32[]{:S(2)}) collective-permute-start(f32[448,128]{1,0:T(8,128)S(1)} %shard_map.86.refs_12_.refs_0_), channel_id=1, source_target_pairs={{0,32},{4,36},{8,40},{12,44},{16,20},{20,16},{24,28},{28,24},{32,0... | collective-permute-start | bytes 688136 | tf_op jit(solution)/shard_map/ppermute | solution.py:482
  77.9 6.6 %shard_map.87 = (bf16[32,16,16,128]{3,2,1,0:T(8,128)(2,1)}, f32[8,128]{1,0:T(8,128)S(1)}) custom-call(bf16[4,16,16,128]{3,2,1,0:T(8,128)(2,1)S(1)} %shard_map.67.mask_ref.refs_0_, bf16[34,16,16,128]{3,2,1,0:T(8,128)(2,1)S(1)} %get-tuple-element.54.refs_0_.refs_1_, ...), custom_call_target="tpu_custom_call", output_to_operand_aliasing={{0}: (13, {})} | custom-call | flops 3623878656 | bytes 2097152 | tf_op jit(solution)/shard_map/pallas_call | solution.py:401
  84.6 1.0 %collective-permute-start.25 = (f32[1344,128]{1,0:T(8,128)S(1)}, f32[1344,128]{1,0:T(8,128)S(1)}, u32[]{:S(2)}, u32[]{:S(2)}) collective-permute-start(f32[1344,128]{1,0:T(8,128)S(1)} %shard_map.88.refs_1_.refs_2_), channel_id=1, source_target_pairs={{0,16},{16,0},{32,48},{48,32},{64,80},{80,64},{96,112},{112,96},{1... | collective-permute-start | bytes 2064392 | tf_op jit(solution)/shard_map/ppermute | solution.py:634
  85.6 0.9 %shard_map.89.refs_2_ = f32[3456,128]{1,0:T(8,128)} custom-call(f32[448,128]{1,0:T(8,128)S(1)} %shard_map.86.refs_12_.refs_0_, f32[1344,128]{1,0:T(8,128)S(1)} %shard_map.88.refs_1_.refs_2_, f32[1344,128]{1,0:T(8,128)S(1)} %shard_map.88.refs_1_.refs_2_), custom_call_target="tpu_custom_call" | custom-call | flops 1000 | bytes 1048576 | tf_op jit(solution)/shard_map/pallas_call | solution.py:542
  87.4 0.9 shard_map.91
  (53 shorter events, 8.1 us)
Async XLA Ops:
  0.6 0.7 copy-start.3
  1.9 1.6 %copy-start = (bf16[32,16,16,128]{3,2,1,0:T(8,128)(2,1)S(1)}, bf16[32,16,16,128]{3,2,1,0:T(8,128)(2,1)}, u32[]{:S(2)}) copy-start(bf16[32,16,16,128]{3,2,1,0:T(8,128)(2,1)} %f_ref.1) | copy-start | bytes 6291460
  3.5 1.6 %copy-start.1 = (bf16[32,16,16,128]{3,2,1,0:T(8,128)(2,1)S(1)}, bf16[32,16,16,128]{3,2,1,0:T(8,128)(2,1)}, u32[]{:S(2)}) copy-start(bf16[32,16,16,128]{3,2,1,0:T(8,128)(2,1)} %c_ref.1) | copy-start | bytes 6291460
  6.0 15.8 %collective-permute-start = (bf16[2,32,16,128]{3,2,1,0:T(8,128)(2,1)S(1)}, bf16[2,32,16,128]{3,2,1,0:T(8,128)(2,1)S(1)}, u32[]{:S(2)}, u32[]{:S(2)}) collective-permute-start(bf16[2,32,16,128]{3,2,1,0:T(8,128)(2,1)S(1)} %get-tuple-element.60.gyhi), channel_id=1, source_target_pairs={{0,4},{4,8},{8,12},{12,0},{1,5},{5,9},{9,13},{13,1},{2,6},{6,10},{... | collective-permute-start | bytes 786440 | tf_op jit(solution)/shard_map/ppermute | solution.py:562
  8.2 13.6 %collective-permute-start.1 = (bf16[2,32,16,128]{3,2,1,0:T(8,128)(2,1)S(1)}, bf16[2,32,16,128]{3,2,1,0:T(8,128)(2,1)S(1)}, u32[]{:S(2)}, u32[]{:S(2)}) collective-permute-start(bf16[2,32,16,128]{3,2,1,0:T(8,128)(2,1)S(1)} %get-tuple-element.61.gylo), channel_id=1, source_target_pairs={{0,12},{4,0},{8,4},{12,8},{1,13},{5,1},{9,5},{13,9},{2,14},{6,2},{... | collective-permute-start | bytes 786440 | tf_op jit(solution)/shard_map/ppermute | solution.py:562
  9.7 8.1 %collective-permute-start.2 = (bf16[2,32,16,128]{3,2,1,0:T(8,128)(2,1)S(1)}, bf16[2,32,16,128]{3,2,1,0:T(8,128)(2,1)S(1)}, u32[]{:S(2)}, u32[]{:S(2)}) collective-permute-start(bf16[2,32,16,128]{3,2,1,0:T(8,128)(2,1)S(1)} %get-tuple-element.62.refs_2_), channel_id=1, source_target_pairs={{0,1},{1,2},{2,3},{3,0},{4,5},{5,6},{6,7},{7,4},{8,9},{9,10},{10,1... | collective-permute-start | bytes 786440 | tf_op jit(solution)/shard_map/ppermute | solution.py:562
  11.0 6.9 %collective-permute-start.3 = (bf16[2,32,16,128]{3,2,1,0:T(8,128)(2,1)S(1)}, bf16[2,32,16,128]{3,2,1,0:T(8,128)(2,1)S(1)}, u32[]{:S(2)}, u32[]{:S(2)}) collective-permute-start(bf16[2,32,16,128]{3,2,1,0:T(8,128)(2,1)S(1)} %get-tuple-element.63.refs_2_.refs_1_), channel_id=1, source_target_pairs={{0,3},{1,0},{2,1},{3,2},{4,7},{5,4},{6,5},{7,6},{8,11},{9,8},{10,9... | collective-permute-start | bytes 786440 | tf_op jit(solution)/shard_map/ppermute | solution.py:562
  17.8 2.9 %copy-start.2 = (bf16[3,3,3,128,128]{4,3,2,1,0:T(8,128)(2,1)S(1)}, bf16[3,3,3,128,128]{4,3,2,1,0:T(8,128)(2,1)}, u32[]{:S(2)}) copy-start(bf16[3,3,3,128,128]{4,3,2,1,0:T(8,128)(2,1)} %param.6) | copy-start | bytes 2654212
  18.0 4.0 %collective-permute-start.4 = (bf16[2,2,32,128]{3,2,1,0:T(8,128)(2,1)S(1)}, bf16[2,2,32,128]{3,2,1,0:T(8,128)(2,1)S(1)}, u32[]{:S(2)}, u32[]{:S(2)}) collective-permute-start(bf16[2,2,32,128]{3,2,1,0:T(8,128)(2,1)S(1)} %get-tuple-element.64), channel_id=1, source_target_pairs={{0,4},{4,8},{8,12},{12,0},{1,5},{5,9},{9,13},{13,1},{2,6},{6,10},{... | collective-permute-start | bytes 98312 | tf_op jit(solution)/shard_map/ppermute | solution.py:562
  18.1 4.0 %collective-permute-start.5 = (bf16[2,2,32,128]{3,2,1,0:T(8,128)(2,1)S(1)}, bf16[2,2,32,128]{3,2,1,0:T(8,128)(2,1)S(1)}, u32[]{:S(2)}, u32[]{:S(2)}) collective-permute-start(bf16[2,2,32,128]{3,2,1,0:T(8,128)(2,1)S(1)} %get-tuple-element.65.refs_1_.refs_5_), channel_id=1, source_target_pairs={{0,12},{4,0},{8,4},{12,8},{1,13},{5,1},{9,5},{13,9},{2,14},{6,2},{... | collective-permute-start | bytes 98312 | tf_op jit(solution)/shard_map/ppermute | solution.py:562
  22.6 9.9 %collective-permute-start.7 = (bf16[2,21,16,128]{3,2,1,0:T(8,128)(2,1)S(1)}, bf16[2,21,16,128]{3,2,1,0:T(8,128)(2,1)S(1)}, u32[]{:S(2)}, u32[]{:S(2)}) collective-permute-start(bf16[2,21,16,128]{3,2,1,0:T(8,128)(2,1)S(1)} %get-tuple-element.72), channel_id=1, source_target_pairs={{0,16},{16,32},{32,48},{48,64},{64,80},{80,96},{96,112},{112,0},{1... | collective-permute-start | bytes 516104 | tf_op jit(solution)/shard_map/ppermute | solution.py:562
  27.1 5.4 %collective-permute-start.6 = (bf16[2,21,16,128]{3,2,1,0:T(8,128)(2,1)S(1)}, bf16[2,21,16,128]{3,2,1,0:T(8,128)(2,1)S(1)}, u32[]{:S(2)}, u32[]{:S(2)}) collective-permute-start(bf16[2,21,16,128]{3,2,1,0:T(8,128)(2,1)S(1)} %get-tuple-element.71.refs_3_), channel_id=1, source_target_pairs={{0,112},{16,0},{32,16},{48,32},{64,48},{80,64},{96,80},{112,96},{1... | collective-permute-start | bytes 516104 | tf_op jit(solution)/shard_map/ppermute | solution.py:562
  33.7 4.8 %collective-permute-start.8 = (f32[14,128,128]{2,1,0:T(8,128)S(1)}, f32[14,128,128]{2,1,0:T(8,128)S(1)}, u32[]{:S(2)}, u32[]{:S(2)}) collective-permute-start(f32[14,128,128]{2,1,0:T(8,128)S(1)} %get-tuple-element.73.refs_9_), channel_id=1, source_target_pairs={{0,16},{16,0},{32,48},{48,32},{64,80},{80,64},{96,112},{112,96},{1... | collective-permute-start | bytes 2752520 | tf_op jit(solution)/shard_map/ppermute | solution.py:613
  38.7 9.3 %collective-permute-start.10 = (f32[448,128]{1,0:T(8,128)S(1)}, f32[448,128]{1,0:T(8,128)S(1)}, u32[]{:S(2)}, u32[]{:S(2)}) collective-permute-start(f32[448,128]{1,0:T(8,128)S(1)} %get-tuple-element.84), channel_id=1, source_target_pairs={{0,64},{4,68},{8,72},{12,76},{16,24},{20,28},{24,16},{28,20},{32,9... | collective-permute-start | bytes 688136 | tf_op jit(solution)/shard_map/ppermute | solution.py:482
  40.4 7.6 %collective-permute-start.11 = (f32[448,128]{1,0:T(8,128)S(1)}, f32[448,128]{1,0:T(8,128)S(1)}, u32[]{:S(2)}, u32[]{:S(2)}) collective-permute-start(f32[448,128]{1,0:T(8,128)S(1)} %get-tuple-element.85), channel_id=1, source_target_pairs={{0,96},{4,100},{8,104},{12,108},{16,28},{20,24},{24,20},{28,16},{3... | collective-permute-start | bytes 688136 | tf_op jit(solution)/shard_map/ppermute | solution.py:482
  41.8 6.7 %collective-permute-start.9 = (f32[448,128]{1,0:T(8,128)S(1)}, f32[448,128]{1,0:T(8,128)S(1)}, u32[]{:S(2)}, u32[]{:S(2)}) collective-permute-start(f32[448,128]{1,0:T(8,128)S(1)} %get-tuple-element.78.refs_11_), channel_id=1, source_target_pairs={{0,32},{4,36},{8,40},{12,44},{16,20},{20,16},{24,28},{28,24},{32,0... | collective-permute-start | bytes 688136 | tf_op jit(solution)/shard_map/ppermute | solution.py:482
  48.5 7.0 %collective-permute-start.13 = (f32[112,128]{1,0:T(8,128)S(1)}, f32[112,128]{1,0:T(8,128)S(1)}, u32[]{:S(2)}, u32[]{:S(2)}) collective-permute-start(f32[112,128]{1,0:T(8,128)S(1)} %get-tuple-element.92), channel_id=1, source_target_pairs={{0,8},{4,12},{8,0},{12,4},{16,80},{20,84},{24,88},{28,92},{32,40},... | collective-permute-start | bytes 172040 | tf_op jit(solution)/shard_map/ppermute | solution.py:482
  50.7 4.8 %collective-permute-start.14 = (f32[112,128]{1,0:T(8,128)S(1)}, f32[112,128]{1,0:T(8,128)S(1)}, u32[]{:S(2)}, u32[]{:S(2)}) collective-permute-start(f32[112,128]{1,0:T(8,128)S(1)} %get-tuple-element.93), channel_id=1, source_target_pairs={{0,12},{4,8},{8,4},{12,0},{16,112},{20,116},{24,120},{28,124},{32,... | collective-permute-start | bytes 172040 | tf_op jit(solution)/shard_map/ppermute | solution.py:482
  51.4 4.1 %collective-permute-start.12 = (f32[112,128]{1,0:T(8,128)S(1)}, f32[112,128]{1,0:T(8,128)S(1)}, u32[]{:S(2)}, u32[]{:S(2)}) collective-permute-start(f32[112,128]{1,0:T(8,128)S(1)} %get-tuple-element.86.refs_12_), channel_id=1, source_target_pairs={{0,4},{4,0},{8,12},{12,8},{16,48},{20,52},{24,56},{28,60},{32,36},... | collective-permute-start | bytes 172040 | tf_op jit(solution)/shard_map/ppermute | solution.py:482
  55.6 7.0 %collective-permute-start.17 = (f32[112,128]{1,0:T(8,128)S(1)}, f32[112,128]{1,0:T(8,128)S(1)}, u32[]{:S(2)}, u32[]{:S(2)}) collective-permute-start(f32[112,128]{1,0:T(8,128)S(1)} %shard_map.82.refs_10_.refs_0_), channel_id=1, source_target_pairs={{0,3},{1,2},{2,1},{3,0},{4,7},{5,6},{6,5},{7,4},{8,11},{9,10},{10,... | collective-permute-start | bytes 172040 | tf_op jit(solution)/shard_map/ppermute | solution.py:481
  58.3 4.5 %collective-permute-start.16 = (f32[112,128]{1,0:T(8,128)S(1)}, f32[112,128]{1,0:T(8,128)S(1)}, u32[]{:S(2)}, u32[]{:S(2)}) collective-permute-start(f32[112,128]{1,0:T(8,128)S(1)} %shard_map.82.refs_10_.refs_0_), channel_id=1, source_target_pairs={{0,2},{1,3},{2,0},{3,1},{4,6},{5,7},{6,4},{7,5},{8,10},{9,11},{10,... | collective-permute-start | bytes 172040 | tf_op jit(solution)/shard_map/ppermute | solution.py:481
  58.7 4.2 %collective-permute-start.15 = (f32[112,128]{1,0:T(8,128)S(1)}, f32[112,128]{1,0:T(8,128)S(1)}, u32[]{:S(2)}, u32[]{:S(2)}) collective-permute-start(f32[112,128]{1,0:T(8,128)S(1)} %shard_map.82.refs_10_.refs_0_), channel_id=1, source_target_pairs={{0,1},{1,0},{2,3},{3,2},{4,5},{5,4},{6,7},{7,6},{8,9},{9,8},{10,11... | collective-permute-start | bytes 172040 | tf_op jit(solution)/shard_map/ppermute | solution.py:481
  62.9 6.5 %collective-permute-start.20 = (f32[112,128]{1,0:T(8,128)S(1)}, f32[112,128]{1,0:T(8,128)S(1)}, u32[]{:S(2)}, u32[]{:S(2)}) collective-permute-start(f32[112,128]{1,0:T(8,128)S(1)} %shard_map.84.refs_11_.refs_0_), channel_id=1, source_target_pairs={{0,12},{4,8},{8,4},{12,0},{16,112},{20,116},{24,120},{28,124},{32,... | collective-permute-start | bytes 172040 | tf_op jit(solution)/shard_map/ppermute | solution.py:482
  65.0 4.5 %collective-permute-start.19 = (f32[112,128]{1,0:T(8,128)S(1)}, f32[112,128]{1,0:T(8,128)S(1)}, u32[]{:S(2)}, u32[]{:S(2)}) collective-permute-start(f32[112,128]{1,0:T(8,128)S(1)} %shard_map.84.refs_11_.refs_0_), channel_id=1, source_target_pairs={{0,8},{4,12},{8,0},{12,4},{16,80},{20,84},{24,88},{28,92},{32,40},... | collective-permute-start | bytes 172040 | tf_op jit(solution)/shard_map/ppermute | solution.py:482
  66.0 3.5 %collective-permute-start.18 = (f32[112,128]{1,0:T(8,128)S(1)}, f32[112,128]{1,0:T(8,128)S(1)}, u32[]{:S(2)}, u32[]{:S(2)}) collective-permute-start(f32[112,128]{1,0:T(8,128)S(1)} %shard_map.84.refs_11_.refs_0_), channel_id=1, source_target_pairs={{0,4},{4,0},{8,12},{12,8},{16,48},{20,52},{24,56},{28,60},{32,36},... | collective-permute-start | bytes 172040 | tf_op jit(solution)/shard_map/ppermute | solution.py:482
  69.6 14.9 %collective-permute-start.24 = (f32[448,128]{1,0:T(8,128)S(1)}, f32[448,128]{1,0:T(8,128)S(1)}, u32[]{:S(2)}, u32[]{:S(2)}) collective-permute-start(f32[448,128]{1,0:T(8,128)S(1)} %shard_map.86.refs_12_.refs_0_), channel_id=1, source_target_pairs={{0,16},{16,0},{32,48},{48,32},{64,80},{80,64},{96,112},{112,96},{1... | collective-permute-start | bytes 688136 | tf_op jit(solution)/shard_map/ppermute | solution.py:631
  74.6 9.9 %collective-permute-start.23 = (f32[448,128]{1,0:T(8,128)S(1)}, f32[448,128]{1,0:T(8,128)S(1)}, u32[]{:S(2)}, u32[]{:S(2)}) collective-permute-start(f32[448,128]{1,0:T(8,128)S(1)} %shard_map.86.refs_12_.refs_0_), channel_id=1, source_target_pairs={{0,96},{4,100},{8,104},{12,108},{16,28},{20,24},{24,20},{28,16},{3... | collective-permute-start | bytes 688136 | tf_op jit(solution)/shard_map/ppermute | solution.py:482
  76.0 8.6 %collective-permute-start.22 = (f32[448,128]{1,0:T(8,128)S(1)}, f32[448,128]{1,0:T(8,128)S(1)}, u32[]{:S(2)}, u32[]{:S(2)}) collective-permute-start(f32[448,128]{1,0:T(8,128)S(1)} %shard_map.86.refs_12_.refs_0_), channel_id=1, source_target_pairs={{0,64},{4,68},{8,72},{12,76},{16,24},{20,28},{24,16},{28,20},{32,9... | collective-permute-start | bytes 688136 | tf_op jit(solution)/shard_map/ppermute | solution.py:482
  76.4 8.2 %collective-permute-start.21 = (f32[448,128]{1,0:T(8,128)S(1)}, f32[448,128]{1,0:T(8,128)S(1)}, u32[]{:S(2)}, u32[]{:S(2)}) collective-permute-start(f32[448,128]{1,0:T(8,128)S(1)} %shard_map.86.refs_12_.refs_0_), channel_id=1, source_target_pairs={{0,32},{4,36},{8,40},{12,44},{16,20},{20,16},{24,28},{28,24},{32,0... | collective-permute-start | bytes 688136 | tf_op jit(solution)/shard_map/ppermute | solution.py:482
  84.6 2.8 %collective-permute-start.25 = (f32[1344,128]{1,0:T(8,128)S(1)}, f32[1344,128]{1,0:T(8,128)S(1)}, u32[]{:S(2)}, u32[]{:S(2)}) collective-permute-start(f32[1344,128]{1,0:T(8,128)S(1)} %shard_map.88.refs_1_.refs_2_), channel_id=1, source_target_pairs={{0,16},{16,0},{32,48},{48,32},{64,80},{80,64},{96,112},{112,96},{1... | collective-permute-start | bytes 2064392 | tf_op jit(solution)/shard_map/ppermute | solution.py:634

commit v4 on v3

--- a/solution.py
+++ b/solution.py
@@ -90,7 +90,8 @@
     slabs = shape((X + 2, Y, Z, C), BF16)
     own_cost = pl.CostEstimate(flops=1000000, bytes_accessed=5 << 20, transcendentals=0)
     mask = small_kernel(
-        mask_kernel, shape((X // E, Y, Z, C), BF16), [jnp.transpose(occupancy, (1, 2, 0))], specs=[SMEM]
+        mask_kernel, shape((X // E, Y, Z, C), BF16), [jnp.transpose(occupancy, (1, 2, 0))], specs=[SMEM],
+        moved=16 << 20,
     )
     fields, *given = pl.pallas_call(
         prepare_x_kernel,
@@ -296,7 +297,10 @@
         finish(x, next_ + term(0, 1) + term(1, 2))
         for slot in range(1, GROUP - 1):
             finish(x + slot, term(slot - 1, 0) + term(slot, 1) + term(slot + 1, 2))
-        if opens:
+        if opens is None:
+            pl.when(sem == 0)(lambda: copy(x + 1, GROUP - 1, sem).start())
+            pl.when(sem > 0)(lambda: copy(x, GROUP, sem).start())
+        elif opens:
             copy(x + 1, GROUP - 1, sem).start()
         elif ends:
             copy(x, GROUP, sem).start()
@@ -311,13 +315,16 @@
     else:
         near, next_ = before[0], before[1]
     if groups > 2:
-        even[...] = ready[...]
+        if ready is None:
+            put(even, part, 0)
+        else:
+            even[...] = ready[...]
         carry_ref[0] = near
         carry_ref[1] = next_
 
         def trip(i, carry):
             x = first + i * 2 * GROUP
-            near, next_ = group(even, x, 2 * i, carry_ref[0], carry_ref[1], False)
+            near, next_ = group(even, x, 2 * i, carry_ref[0], carry_ref[1], None if starts else False)
             put(odd, part, x + GROUP)
             near, next_ = group(odd, x + GROUP, 2 * i + 1, near, next_, False)
             after = i + 1 == groups // 2
@@ -411,7 +418,7 @@
     return made, dict(zip(("carry", "ready", "late"), kept, strict=False))
 
 
-def small_kernel(kernel, out_shape, operands, ties=(), specs=None):
+def small_kernel(kernel, out_shape, operands, ties=(), specs=None, moved=1 << 20):
     count = len(operands)
 
     def run(*refs):
@@ -423,7 +430,7 @@
         out_specs=jax.tree.map(lambda _: VMEM, out_shape),
         out_shape=out_shape,
         compiler_params=params(),
-        cost_estimate=pl.CostEstimate(flops=1000, bytes_accessed=1 << 20, transcendentals=0),
+        cost_estimate=pl.CostEstimate(flops=1000, bytes_accessed=moved, transcendentals=0),
     )(*operands, *ties)
 
 
@@ -458,10 +465,11 @@
         flipped[row * C : (row + 1) * C, tx * C : (tx + 1) * C] = w_ref[26 - tap].astype(F32).T.astype(BF16)
 
 
-def places():
-    at = lax.axis_index("gx")
-    core, z, y = at % 2, at // 2, lax.axis_index("gy")
-    return core, z * (1 - core) + y * core, y * (1 - core) + z * core
+ORDER = ("zyx", "yxz")
+
+
+def first_place(core):
+    return lax.axis_index("gx") // 2 * (1 - core) + lax.axis_index("gy") * core
 
 
 def pairs(turn, step):
@@ -469,24 +477,24 @@
     for z in range(4):
         for core in range(2):
             for y in range(4):
-                along_z = (turn == 1) == (core == 0)
-                partner = (z ^ step, y) if along_z else (z, y ^ step)
-                found.append(((2 * z + core) * 4 + y, (2 * partner[0] + core) * 4 + partner[1]))
+                for x in range(4):
+                    at = {"z": z, "y": y, "x": x}
+                    to = dict(at)
+                    to[ORDER[core][turn]] ^= step
+                    found.append(tuple(((2 * p["z"] + core) * 4 + p["y"]) * 4 + p["x"] for p in (at, to)))
     return found
 
 
 def exchange(turn, values):
     steps = zip((1, 2, 3), values, strict=True)
-    if turn == 3:
-        return [lax.ppermute(value, "gz", [(i, i ^ step) for i in range(4)]) for step, value in steps]
-    return [lax.ppermute(value, ("gx", "gy"), pairs(turn, step)) for step, value in steps]
-
-
-def deal(turn, terms, ties=()):
+    return [lax.ppermute(value, ("gx", "gy", "gz"), pairs(turn, step)) for step, value in steps]
+
+
+def deal(terms, ties):
     rows = terms[0].shape[0] // 4
 
     def kernel(*refs):
-        me = places()[turn]
+        me = first_place(lax.axis_index("gx") % 2)
         for step in range(4):
             at = pl.ds((me ^ step) * rows, rows)
             total = refs[0][at]
@@ -497,17 +505,6 @@
     return small_kernel(kernel, [shape((rows, C), F32)] * 4, terms, ties)
 
 
-def collect(turn, parts, ties=()):
-    rows = parts[0].shape[0]
-
-    def kernel(*refs):
-        me = places()[turn]
-        for step in range(4):
-            refs[4][pl.ds((me ^ step) * rows, rows)] = refs[step][...]
-
-    return small_kernel(kernel, shape((4 * rows, C), F32), parts, ties)
-
-
 def sum_kernel(a, b, c, d, o):
     o[...] = (a[...] + c[...]) + (b[...] + d[...])
 
@@ -522,7 +519,7 @@
         o_ref, left = refs[-2:]
         at = lax.axis_index("gx")
         half = at % 2 if mine else 1 - at % 2
-        me = at // 2 * (1 - half) + lax.axis_index("gy") * half
+        me = first_place(half)
         for act in ("start", "wait"):
             sem = 0
             for ref, (_, steps) in zip(refs, sources, strict=False):
@@ -597,7 +594,7 @@
     field = [*slabs, held_ylo, held_yhi, col_lo, col_hi]
     made = [None, None]
     weights = (forward, flipped)
-    order = [(0, 0, 2), (0, 8, 4), (0, 24, 2), (1, 0, 2), (1, 8, 2), (1, 16, 4)]
+    order = [(0, 0, 2), (0, 8, 4), (0, 24, 2), (1, 0, 4), (1, 16, 4)]
     state = {}
 
     def convolve(tie):
@@ -613,21 +610,15 @@
     came = lax.ppermute(send, "gx", swap)
     ties = convolve(send)
     flat = (HALF * C, C)
-    own, *parts = deal(1, [keep.reshape(flat), came.reshape(flat)], ties)
-    came = exchange(1, parts)
-    ties = convolve(parts[0])
-    own, *parts = deal(2, [own, *came], ties)
-    came = exchange(2, parts)
-    ties = convolve(parts[0])
-    part_shape = shape(own.shape, F32)
-    mine = small_kernel(sum_kernel, part_shape, [own, *came], ties)
-    came = exchange(3, [mine] * 3)
-    ties = convolve(mine)
-    summed = small_kernel(sum_kernel, part_shape, [mine, *came], ties)
-    came = exchange(2, [summed] * 3)
-    ties = convolve(summed)
-    chunk = collect(2, [summed, *came], ties)
-    came = exchange(1, [chunk] * 3)
+    own, *parts = deal([keep.reshape(flat), came.reshape(flat)], ties)
+    came = exchange(0, parts)
+    chunk, ties = own, convolve(parts[0])
+    for turn in (1, 2):
+        chunk = small_kernel(sum_kernel, shape(chunk.shape, F32), [chunk, *came], ties)
+        came = exchange(turn, [chunk] * 3)
+        ties = convolve(chunk)
+    chunk = small_kernel(sum_kernel, shape(chunk.shape, F32), [chunk, *came], ties)
+    came = exchange(0, [chunk] * 3)
     beside = lax.ppermute(chunk, "gx", swap)
     ties = convolve(chunk)
     joined = small_kernel(join_kernel, shape((3 * chunk.shape[0], C), F32), came, [beside, *ties])

time: 88.7 us -> 84.7 us (0.955)
  starting transfers between devices: 37.9 us -> 32.7 us
  waiting for transfers between devices: 1.36 us -> 3.39 us
    ppermute x15 -> x12, starting transfers between devices: 16.7 us -> 13.7 us  [exchange(): lax.ppermute(value, ('gx', 'gy', 'gz'), pairs(turn, step))]
    ppermute x1, starting transfers between devices: 5.04 us -> 2.91 us  [body(): beside = lax.ppermute(chunk, 'gx', swap)]
    ppermute x15 -> x12, waiting for transfers between devices: 1 us -> 3.03 us  [exchange(): lax.ppermute(value, ('gx', 'gy', 'gz'), pairs(turn, step))]
    pallas_call x6 -> x5, Pallas kernels: 26.2 us -> 25.5 us  [conv_piece(): pl.pallas_call(plain if more else final, in_specs=specs, out_specs=[ANY]...]
    pallas_call x11 -> x10, Pallas kernels: 2.6 us -> 2.65 us  [small_kernel(): pl.pallas_call(run, in_specs=(specs or [VMEM] * count) + [ANY] * len(ties...]
  transfers between devices with their start and end apart: 26 -> 23, of which waited for: 5 -> 7; matrix products, arithmetic and copies ran while one was open for 0% -> 0% of each run, Pallas kernels for 45% -> 46%
where the time goes in v4:
time: 84.7 us; the launch traced here: 84.5 us
  Pallas kernels  44.4 us (52%)
  starting transfers between devices  32.7 us (39%)
  waiting for transfers between devices  3.39 us (4%)
  local copies, waits for them, and re-layouts  2.95 us (3%)
  between operations  1.13 us (1%)
    pallas_call x5, Pallas kernels, conv_piece(): pl.pallas_call(plain if more else final, in_specs=specs, out_specs=[ANY]...  25.5 us
    ppermute x12, starting transfers between devices, exchange(): lax.ppermute(value, ('gx', 'gy', 'gz'), pairs(turn, step))  13.7 us
    ppermute x8, starting transfers between devices, shift(): lax.ppermute(value, axis, [(i, (i + step) % count) for i in range(count)])  13.6 us
    pallas_call x2, Pallas kernels, own_grad(): pl.pallas_call(lambda *refs: own_grad_kernel(first, more, *refs), in_spec...  10.8 us
    ppermute x12, waiting for transfers between devices, exchange(): lax.ppermute(value, ('gx', 'gy', 'gz'), pairs(turn, step))  3.03 us
    unnamed x8, local copies, waits for them, and re-layouts  2.95 us
    ppermute x1, starting transfers between devices, body(): beside = lax.ppermute(chunk, 'gx', swap)  2.91 us
    pallas_call x10, Pallas kernels, small_kernel(): pl.pallas_call(run, in_specs=(specs or [VMEM] * count) + [ANY] * len(ties...  2.65 us
  transfers between devices with their start and end apart: 23, of which 7 were waited for; matrix products, arithmetic and copies ran while one was open for 0% of the time, Pallas kernels for 46%

profile of v4, /device:TPU:1, one launch (start us, length us, event | category | flops | bytes accessed | tf_op | source)
XLA Modules:
  0.0 84.5 jit_solution(2904927751678797108)
XLA Ops:
  1.9 1.6 %copy-done = bf16[32,16,16,128]{3,2,1,0:T(8,128)(2,1)S(1)} copy-done((bf16[32,16,16,128]{3,2,1,0:T(8,128)(2,1)S(1)}, bf16[32,16,16,128]{3,2,1,0:T(8,128)(2,1)}, u32[]{:S(2)}) %copy-start) | copy-done | bytes 2097176
  3.5 0.9 %shard_map.68 = (bf16[34,16,16,128]{3,2,1,0:T(8,128)(2,1)S(1)}, bf16[1,32,16,128]{3,2,1,0:T(8,128)(2,1)S(1)}, bf16[1,32,16,128]{3,2,1,0:T(8,128)(2,1)S(1)}, bf16...) custom-call(bf16[32,16,16,128]{3,2,1,0:T(8,128)(2,1)S(1)} %copy-done, ...), custom_call_target="tpu_custom_call" | custom-call | flops 1000000 | bytes 5242880 | tf_op jit(solution)/shard_map/pallas_call | solution.py:96
  4.4 0.7 copy-done.1
  5.1 0.9 %shard_map.69 = (bf16[34,16,16,128]{3,2,1,0:T(8,128)(2,1)S(1)}, bf16[2,32,16,128]{3,2,1,0:T(8,128)(2,1)S(1)}, bf16[2,32,16,128]{3,2,1,0:T(8,128)(2,1)S(1)}, bf16...) custom-call(bf16[32,16,16,128]{3,2,1,0:T(8,128)(2,1)S(1)} %copy-done.1, ...), custom_call_target="tpu_custom_call" | custom-call | flops 1000000 | bytes 5242880 | tf_op jit(solution)/shard_map/pallas_call | solution.py:104
  6.0 2.2 %collective-permute-start = (bf16[2,32,16,128]{3,2,1,0:T(8,128)(2,1)S(1)}, bf16[2,32,16,128]{3,2,1,0:T(8,128)(2,1)S(1)}, u32[]{:S(2)}, u32[]{:S(2)}) collective-permute-start(bf16[2,32,16,128]{3,2,1,0:T(8,128)(2,1)S(1)} %get-tuple-element.52.gyhi), channel_id=1, source_target_pairs={{0,4},{4,8},{8,12},{12,0},{1,5},{5,9},{9,13},{13,1},{2,6},{6,10},{... | collective-permute-start | bytes 786440 | tf_op jit(solution)/shard_map/ppermute | solution.py:559
  8.2 1.5 %collective-permute-start.1 = (bf16[2,32,16,128]{3,2,1,0:T(8,128)(2,1)S(1)}, bf16[2,32,16,128]{3,2,1,0:T(8,128)(2,1)S(1)}, u32[]{:S(2)}, u32[]{:S(2)}) collective-permute-start(bf16[2,32,16,128]{3,2,1,0:T(8,128)(2,1)S(1)} %get-tuple-element.53.gylo), channel_id=1, source_target_pairs={{0,12},{4,0},{8,4},{12,8},{1,13},{5,1},{9,5},{13,9},{2,14},{6,2},{... | collective-permute-start | bytes 786440 | tf_op jit(solution)/shard_map/ppermute | solution.py:559
  9.7 1.2 %collective-permute-start.2 = (bf16[2,32,16,128]{3,2,1,0:T(8,128)(2,1)S(1)}, bf16[2,32,16,128]{3,2,1,0:T(8,128)(2,1)S(1)}, u32[]{:S(2)}, u32[]{:S(2)}) collective-permute-start(bf16[2,32,16,128]{3,2,1,0:T(8,128)(2,1)S(1)} %get-tuple-element.54.refs_2_), channel_id=1, source_target_pairs={{0,1},{1,2},{2,3},{3,0},{4,5},{5,6},{6,7},{7,4},{8,9},{9,10},{10,1... | collective-permute-start | bytes 786440 | tf_op jit(solution)/shard_map/ppermute | solution.py:559
  11.0 1.5 %collective-permute-start.3 = (bf16[2,32,16,128]{3,2,1,0:T(8,128)(2,1)S(1)}, bf16[2,32,16,128]{3,2,1,0:T(8,128)(2,1)S(1)}, u32[]{:S(2)}, u32[]{:S(2)}) collective-permute-start(bf16[2,32,16,128]{3,2,1,0:T(8,128)(2,1)S(1)} %get-tuple-element.55.refs_2_.refs_1_), channel_id=1, source_target_pairs={{0,3},{1,0},{2,1},{3,2},{4,7},{5,4},{6,5},{7,6},{8,11},{9,8},{10,9... | collective-permute-start | bytes 786440 | tf_op jit(solution)/shard_map/ppermute | solution.py:559
  12.4 5.4 %shard_map.70.refs_2_.refs_0_ = f32[1152,384]{1,0:T(8,128)S(1)} custom-call(bf16[34,16,16,128]{3,2,1,0:T(8,128)(2,1)S(1)} %get-tuple-element.46.refs_0_.refs_1_, bf16[34,16,16,128]{3,2,1,0:T(8,128)(2,1)S(1)} %get-tuple-element.51.refs_1_.g_ref.refs_2_, bf16[2,32,16,128]{3,2,1,0:T(8,128)(2,1)S(1)} %get-tuple-element.55.refs_2_.refs_1_), custom_call_target="tpu_custom_call" | custom-call | flops 3623878656 | bytes 8388608 | tf_op jit(solution)/shard_map/pallas_call | solution.py:178
  18.1 2.7 %collective-permute-start.5 = (bf16[2,2,32,128]{3,2,1,0:T(8,128)(2,1)S(1)}, bf16[2,2,32,128]{3,2,1,0:T(8,128)(2,1)S(1)}, u32[]{:S(2)}, u32[]{:S(2)}) collective-permute-start(bf16[2,2,32,128]{3,2,1,0:T(8,128)(2,1)S(1)} %get-tuple-element.57.refs_1_.refs_5_), channel_id=1, source_target_pairs={{0,12},{4,0},{8,4},{12,8},{1,13},{5,1},{9,5},{13,9},{2,14},{6,2},{... | collective-permute-start | bytes 98312 | tf_op jit(solution)/shard_map/ppermute | solution.py:559
  22.6 4.5 %collective-permute-start.7 = (bf16[2,21,16,128]{3,2,1,0:T(8,128)(2,1)S(1)}, bf16[2,21,16,128]{3,2,1,0:T(8,128)(2,1)S(1)}, u32[]{:S(2)}, u32[]{:S(2)}) collective-permute-start(bf16[2,21,16,128]{3,2,1,0:T(8,128)(2,1)S(1)} %get-tuple-element.64), channel_id=1, source_target_pairs={{0,16},{16,32},{32,48},{48,64},{64,80},{80,96},{96,112},{112,0},{1... | collective-permute-start | bytes 516104 | tf_op jit(solution)/shard_map/ppermute | solution.py:559
  27.1 5.4 %shard_map.75.own_ref = f32[1152,384]{1,0:T(8,128)S(1)} custom-call(bf16[34,16,16,128]{3,2,1,0:T(8,128)(2,1)S(1)} %get-tuple-element.46.refs_0_.refs_1_, bf16[34,16,16,128]{3,2,1,0:T(8,128)(2,1)S(1)} %get-tuple-element.51.refs_1_.g_ref.refs_2_, f32[1152,384]{1,0:T(8,128)S(1)} %shard_map.73.refs_9_.refs_2_, bf16[2,21,16,128]{3,2,1,0:T(8,128)(2,1)S(1)} %get-tuple-element.63.refs_3_), custom_call_target="tpu_custom_call" | custom-call | flops 3623878656 | bytes 8388608 | tf_op jit(solution)/shard_map/pallas_call | solution.py:178
  32.6 1.1 %shard_map.76 = (f32[14,128,128]{2,1,0:T(8,128)S(1)}, f32[14,128,128]{2,1,0:T(8,128)S(1)}) custom-call(f32[1152,384]{1,0:T(8,128)S(1)} %shard_map.75.own_ref, bf16[34,16,16,128]{3,2,1,0:T(8,128)(2,1)S(1)} %get-tuple-element.51.refs_1_.g_ref.refs_2_, bf16[2,32,16,128]{3,2,1,0:T(8,128)(2,1)S(1)} %get-tuple-element.53.gylo, ...), custom_call_target="tpu_custom_call" | custom-call | flops 679477248 | bytes 6291456 | tf_op jit(solution)/shard_map/pallas_call | solution.py:246
  33.7 1.5 %collective-permute-start.8 = (f32[14,128,128]{2,1,0:T(8,128)S(1)}, f32[14,128,128]{2,1,0:T(8,128)S(1)}, u32[]{:S(2)}, u32[]{:S(2)}) collective-permute-start(f32[14,128,128]{2,1,0:T(8,128)S(1)} %get-tuple-element.65.refs_9_), channel_id=1, source_target_pairs={{0,16},{16,0},{32,48},{48,32},{64,80},{80,64},{96,112},{112,96},{1... | collective-permute-start | bytes 2752520 | tf_op jit(solution)/shard_map/ppermute | solution.py:610
  35.2 3.3 %shard_map.77 = (bf16[32,16,16,128]{3,2,1,0:T(8,128)(2,1)}, f32[2,256,128]{2,1,0:T(8,128)S(1)}, bf16[3,4,18,16,128]{4,3,2,1,0:T(8,128)(2,1)S(1)}, bf16[4,16,16,128]{3,2,1,0:T(8,128)(2,1)S(1)}) custom-call(bf16[4,16,16,128]{3,2,1,0:T(8,128)(2,1)S(1)} %shard_map.67.mask_ref.refs_0_, bf16[34,16,16,128]{3,2,1,0:T(8,128)(2,1)S(1)} %get-tuple-element.46.refs_0_.refs_1_, ...), custom_call_target="tpu_custom_call" | custom-call | flops 1811939328 | bytes 2097152 | tf_op jit(solution)/shard_map/pallas_call | solution.py:408
  38.7 1.7 %collective-permute-start.10 = (f32[448,128]{1,0:T(8,128)S(1)}, f32[448,128]{1,0:T(8,128)S(1)}, u32[]{:S(2)}, u32[]{:S(2)}) collective-permute-start(f32[448,128]{1,0:T(8,128)S(1)} %get-tuple-element.76), channel_id=1, source_target_pairs={{0,64},{1,65},{2,66},{3,67},{4,68},{5,69},{6,70},{7,71},{8,72},{9,... | collective-permute-start | bytes 688136 | tf_op jit(solution)/shard_map/ppermute | solution.py:490
  40.4 1.4 %collective-permute-start.11 = (f32[448,128]{1,0:T(8,128)S(1)}, f32[448,128]{1,0:T(8,128)S(1)}, u32[]{:S(2)}, u32[]{:S(2)}) collective-permute-start(f32[448,128]{1,0:T(8,128)S(1)} %get-tuple-element.77), channel_id=1, source_target_pairs={{0,96},{1,97},{2,98},{3,99},{4,100},{5,101},{6,102},{7,103},{8,104... | collective-permute-start | bytes 688136 | tf_op jit(solution)/shard_map/ppermute | solution.py:490
  42.3 5.7 %shard_map.79 = (bf16[32,16,16,128]{3,2,1,0:T(8,128)(2,1)}, f32[2,256,128]{2,1,0:T(8,128)S(1)}, bf16[3,4,18,16,128]{4,3,2,1,0:T(8,128)(2,1)S(1)}, bf16[4,16,16,128]{3,2,1,0:T(8,128)(2,1)S(1)}) custom-call(bf16[4,16,16,128]{3,2,1,0:T(8,128)(2,1)S(1)} %shard_map.67.mask_ref.refs_0_, ...), custom_call_target="tpu_custom_call", output_to_operand_aliasing={{0}: (12, {})} | custom-call | flops 3623878656 | bytes 2097152 | tf_op jit(solution)/shard_map/pallas_call | solution.py:408
  48.6 2.7 %collective-permute-start.14 = (f32[448,128]{1,0:T(8,128)S(1)}, f32[448,128]{1,0:T(8,128)S(1)}, u32[]{:S(2)}, u32[]{:S(2)}) collective-permute-start(f32[448,128]{1,0:T(8,128)S(1)} %shard_map.80.refs_12_.refs_0_), channel_id=1, source_target_pairs={{0,12},{1,13},{2,14},{3,15},{4,8},{5,9},{6,10},{7,11},{8,4},{9,5},... | collective-permute-start | bytes 688136 | tf_op jit(solution)/shard_map/ppermute | solution.py:490
  52.0 3.9 %shard_map.81 = (bf16[32,16,16,128]{3,2,1,0:T(8,128)(2,1)}, f32[2,256,128]{2,1,0:T(8,128)S(1)}, bf16[3,4,18,16,128]{4,3,2,1,0:T(8,128)(2,1)S(1)}) custom-call(bf16[4,16,16,128]{3,2,1,0:T(8,128)(2,1)S(1)} %shard_map.67.mask_ref.refs_0_, bf16[34,16,16,128]{3,2,1,0:T(8,128)(2,1)S(1)} %get-tuple-element.46.refs_0_.refs_1_, ...), custom_call_target="tpu_custom_call", output_to_operand_aliasing={{0}: (13, {})} | custom-call | flops 1811939328 | bytes 2097152 | tf_op jit(solution)/shard_map/pallas_call | solution.py:408
  55.9 0.8 collective-permute-done.14.refs_3_
  56.7 1.2 %collective-permute-done.13.refs_2_ = f32[448,128]{1,0:T(8,128)S(1)} collective-permute-done((f32[448,128]{1,0:T(8,128)S(1)}, f32[448,128]{1,0:T(8,128)S(1)}, u32[]{:S(2)}, u32[]{:S(2)}) %collective-permute-start.13) | collective-permute-done | bytes 229408 | tf_op jit(solution)/shard_map/ppermute | solution.py:490
  58.2 2.5 %collective-permute-start.17 = (f32[448,128]{1,0:T(8,128)S(1)}, f32[448,128]{1,0:T(8,128)S(1)}, u32[]{:S(2)}, u32[]{:S(2)}) collective-permute-start(f32[448,128]{1,0:T(8,128)S(1)} %shard_map.82.refs_10_.refs_0_), channel_id=1, source_target_pairs={{0,3},{1,2},{2,1},{3,0},{4,7},{5,6},{6,5},{7,4},{8,11},{9,10},{10,... | collective-permute-start | bytes 688136 | tf_op jit(solution)/shard_map/ppermute | solution.py:490
  60.7 0.8 collective-permute-start.15
  61.6 6.0 %shard_map.83 = (bf16[32,16,16,128]{3,2,1,0:T(8,128)(2,1)}, f32[2,256,128]{2,1,0:T(8,128)S(1)}, bf16[3,4,18,16,128]{4,3,2,1,0:T(8,128)(2,1)S(1)}, bf16[4,16,16,128]{3,2,1,0:T(8,128)(2,1)S(1)}) custom-call(bf16[4,16,16,128]{3,2,1,0:T(8,128)(2,1)S(1)} %shard_map.67.mask_ref.refs_0_, bf16[34,16,16,128]{3,2,1,0:T(8,128)(2,1)S(1)} %get-tuple-element.46.refs_0_.refs_1_, ...), custom_call_target="tpu_custom_call" | custom-call | flops 3623878656 | bytes 2097152 | tf_op jit(solution)/shard_map/pallas_call | solution.py:408
  67.8 2.9 %collective-permute-start.21 = (f32[448,128]{1,0:T(8,128)S(1)}, f32[448,128]{1,0:T(8,128)S(1)}, u32[]{:S(2)}, u32[]{:S(2)}) collective-permute-start(f32[448,128]{1,0:T(8,128)S(1)} %shard_map.84.refs_12_.refs_0_), channel_id=1, source_target_pairs={{0,16},{16,0},{32,48},{48,32},{64,80},{80,64},{96,112},{112,96},{1... | collective-permute-start | bytes 688136 | tf_op jit(solution)/shard_map/ppermute | solution.py:622
  70.7 2.7 %collective-permute-start.20 = (f32[448,128]{1,0:T(8,128)S(1)}, f32[448,128]{1,0:T(8,128)S(1)}, u32[]{:S(2)}, u32[]{:S(2)}) collective-permute-start(f32[448,128]{1,0:T(8,128)S(1)} %shard_map.84.refs_12_.refs_0_), channel_id=1, source_target_pairs={{0,96},{1,97},{2,98},{3,99},{4,100},{5,101},{6,102},{7,103},{8,104... | collective-permute-start | bytes 688136 | tf_op jit(solution)/shard_map/ppermute | solution.py:490
  74.0 6.6 %shard_map.85 = (bf16[32,16,16,128]{3,2,1,0:T(8,128)(2,1)}, f32[8,128]{1,0:T(8,128)S(1)}) custom-call(bf16[4,16,16,128]{3,2,1,0:T(8,128)(2,1)S(1)} %shard_map.67.mask_ref.refs_0_, bf16[34,16,16,128]{3,2,1,0:T(8,128)(2,1)S(1)} %get-tuple-element.46.refs_0_.refs_1_, ...), custom_call_target="tpu_custom_call", output_to_operand_aliasing={{0}: (13, {})} | custom-call | flops 3623878656 | bytes 2097152 | tf_op jit(solution)/shard_map/pallas_call | solution.py:408
  80.8 0.9 %collective-permute-start.22 = (f32[1344,128]{1,0:T(8,128)S(1)}, f32[1344,128]{1,0:T(8,128)S(1)}, u32[]{:S(2)}, u32[]{:S(2)}) collective-permute-start(f32[1344,128]{1,0:T(8,128)S(1)} %shard_map.86.refs_1_.refs_2_), channel_id=1, source_target_pairs={{0,16},{16,0},{32,48},{48,32},{64,80},{80,64},{96,112},{112,96},{1... | collective-permute-start | bytes 2064392 | tf_op jit(solution)/shard_map/ppermute | solution.py:625
  81.7 0.9 %shard_map.87.refs_2_ = f32[3456,128]{1,0:T(8,128)} custom-call(f32[448,128]{1,0:T(8,128)S(1)} %shard_map.84.refs_12_.refs_0_, f32[1344,128]{1,0:T(8,128)S(1)} %shard_map.86.refs_1_.refs_2_, f32[1344,128]{1,0:T(8,128)S(1)} %shard_map.86.refs_1_.refs_2_), custom_call_target="tpu_custom_call" | custom-call | flops 1000 | bytes 1048576 | tf_op jit(solution)/shard_map/pallas_call | solution.py:539
  82.6 0.7 shard_map.88.refs_2_
  83.5 0.9 %shard_map.89 = f32[3456,128]{1,0:T(8,128)} custom-call(f32[1344,128]{1,0:T(8,128)S(1)} %collective-permute-done.22.refs_0_, f32[1344,128]{1,0:T(8,128)S(1)} %shard_map.86.refs_1_.refs_2_, f32[3456,128]{1,0:T(8,128)} %shard_map.88.refs_2_), custom_call_target="tpu_custom_call", output_to_operand_aliasing={{}: (2, {})} | custom-call | flops 1000 | bytes 1048576 | tf_op jit(solution)/shard_map/pallas_call | solution.py:539
  (45 shorter events, 6.5 us)
Async XLA Ops:
  0.6 0.7 copy-start.3
  1.9 1.6 %copy-start = (bf16[32,16,16,128]{3,2,1,0:T(8,128)(2,1)S(1)}, bf16[32,16,16,128]{3,2,1,0:T(8,128)(2,1)}, u32[]{:S(2)}) copy-start(bf16[32,16,16,128]{3,2,1,0:T(8,128)(2,1)} %f_ref.1) | copy-start | bytes 6291460
  3.5 1.6 %copy-start.1 = (bf16[32,16,16,128]{3,2,1,0:T(8,128)(2,1)S(1)}, bf16[32,16,16,128]{3,2,1,0:T(8,128)(2,1)}, u32[]{:S(2)}) copy-start(bf16[32,16,16,128]{3,2,1,0:T(8,128)(2,1)} %c_ref.1) | copy-start | bytes 6291460
  6.0 15.8 %collective-permute-start = (bf16[2,32,16,128]{3,2,1,0:T(8,128)(2,1)S(1)}, bf16[2,32,16,128]{3,2,1,0:T(8,128)(2,1)S(1)}, u32[]{:S(2)}, u32[]{:S(2)}) collective-permute-start(bf16[2,32,16,128]{3,2,1,0:T(8,128)(2,1)S(1)} %get-tuple-element.52.gyhi), channel_id=1, source_target_pairs={{0,4},{4,8},{8,12},{12,0},{1,5},{5,9},{9,13},{13,1},{2,6},{6,10},{... | collective-permute-start | bytes 786440 | tf_op jit(solution)/shard_map/ppermute | solution.py:559
  8.2 13.6 %collective-permute-start.1 = (bf16[2,32,16,128]{3,2,1,0:T(8,128)(2,1)S(1)}, bf16[2,32,16,128]{3,2,1,0:T(8,128)(2,1)S(1)}, u32[]{:S(2)}, u32[]{:S(2)}) collective-permute-start(bf16[2,32,16,128]{3,2,1,0:T(8,128)(2,1)S(1)} %get-tuple-element.53.gylo), channel_id=1, source_target_pairs={{0,12},{4,0},{8,4},{12,8},{1,13},{5,1},{9,5},{13,9},{2,14},{6,2},{... | collective-permute-start | bytes 786440 | tf_op jit(solution)/shard_map/ppermute | solution.py:559
  9.7 8.1 %collective-permute-start.2 = (bf16[2,32,16,128]{3,2,1,0:T(8,128)(2,1)S(1)}, bf16[2,32,16,128]{3,2,1,0:T(8,128)(2,1)S(1)}, u32[]{:S(2)}, u32[]{:S(2)}) collective-permute-start(bf16[2,32,16,128]{3,2,1,0:T(8,128)(2,1)S(1)} %get-tuple-element.54.refs_2_), channel_id=1, source_target_pairs={{0,1},{1,2},{2,3},{3,0},{4,5},{5,6},{6,7},{7,4},{8,9},{9,10},{10,1... | collective-permute-start | bytes 786440 | tf_op jit(solution)/shard_map/ppermute | solution.py:559
  11.0 6.9 %collective-permute-start.3 = (bf16[2,32,16,128]{3,2,1,0:T(8,128)(2,1)S(1)}, bf16[2,32,16,128]{3,2,1,0:T(8,128)(2,1)S(1)}, u32[]{:S(2)}, u32[]{:S(2)}) collective-permute-start(bf16[2,32,16,128]{3,2,1,0:T(8,128)(2,1)S(1)} %get-tuple-element.55.refs_2_.refs_1_), channel_id=1, source_target_pairs={{0,3},{1,0},{2,1},{3,2},{4,7},{5,4},{6,5},{7,6},{8,11},{9,8},{10,9... | collective-permute-start | bytes 786440 | tf_op jit(solution)/shard_map/ppermute | solution.py:559
  17.8 2.9 %copy-start.2 = (bf16[3,3,3,128,128]{4,3,2,1,0:T(8,128)(2,1)S(1)}, bf16[3,3,3,128,128]{4,3,2,1,0:T(8,128)(2,1)}, u32[]{:S(2)}) copy-start(bf16[3,3,3,128,128]{4,3,2,1,0:T(8,128)(2,1)} %param.6) | copy-start | bytes 2654212
  18.0 4.0 %collective-permute-start.4 = (bf16[2,2,32,128]{3,2,1,0:T(8,128)(2,1)S(1)}, bf16[2,2,32,128]{3,2,1,0:T(8,128)(2,1)S(1)}, u32[]{:S(2)}, u32[]{:S(2)}) collective-permute-start(bf16[2,2,32,128]{3,2,1,0:T(8,128)(2,1)S(1)} %get-tuple-element.56), channel_id=1, source_target_pairs={{0,4},{4,8},{8,12},{12,0},{1,5},{5,9},{9,13},{13,1},{2,6},{6,10},{... | collective-permute-start | bytes 98312 | tf_op jit(solution)/shard_map/ppermute | solution.py:559
  18.1 4.0 %collective-permute-start.5 = (bf16[2,2,32,128]{3,2,1,0:T(8,128)(2,1)S(1)}, bf16[2,2,32,128]{3,2,1,0:T(8,128)(2,1)S(1)}, u32[]{:S(2)}, u32[]{:S(2)}) collective-permute-start(bf16[2,2,32,128]{3,2,1,0:T(8,128)(2,1)S(1)} %get-tuple-element.57.refs_1_.refs_5_), channel_id=1, source_target_pairs={{0,12},{4,0},{8,4},{12,8},{1,13},{5,1},{9,5},{13,9},{2,14},{6,2},{... | collective-permute-start | bytes 98312 | tf_op jit(solution)/shard_map/ppermute | solution.py:559
  22.6 9.9 %collective-permute-start.7 = (bf16[2,21,16,128]{3,2,1,0:T(8,128)(2,1)S(1)}, bf16[2,21,16,128]{3,2,1,0:T(8,128)(2,1)S(1)}, u32[]{:S(2)}, u32[]{:S(2)}) collective-permute-start(bf16[2,21,16,128]{3,2,1,0:T(8,128)(2,1)S(1)} %get-tuple-element.64), channel_id=1, source_target_pairs={{0,16},{16,32},{32,48},{48,64},{64,80},{80,96},{96,112},{112,0},{1... | collective-permute-start | bytes 516104 | tf_op jit(solution)/shard_map/ppermute | solution.py:559
  27.1 5.4 %collective-permute-start.6 = (bf16[2,21,16,128]{3,2,1,0:T(8,128)(2,1)S(1)}, bf16[2,21,16,128]{3,2,1,0:T(8,128)(2,1)S(1)}, u32[]{:S(2)}, u32[]{:S(2)}) collective-permute-start(bf16[2,21,16,128]{3,2,1,0:T(8,128)(2,1)S(1)} %get-tuple-element.63.refs_3_), channel_id=1, source_target_pairs={{0,112},{16,0},{32,16},{48,32},{64,48},{80,64},{96,80},{112,96},{1... | collective-permute-start | bytes 516104 | tf_op jit(solution)/shard_map/ppermute | solution.py:559
  33.7 4.8 %collective-permute-start.8 = (f32[14,128,128]{2,1,0:T(8,128)S(1)}, f32[14,128,128]{2,1,0:T(8,128)S(1)}, u32[]{:S(2)}, u32[]{:S(2)}) collective-permute-start(f32[14,128,128]{2,1,0:T(8,128)S(1)} %get-tuple-element.65.refs_9_), channel_id=1, source_target_pairs={{0,16},{16,0},{32,48},{48,32},{64,80},{80,64},{96,112},{112,96},{1... | collective-permute-start | bytes 2752520 | tf_op jit(solution)/shard_map/ppermute | solution.py:610
  38.7 9.3 %collective-permute-start.10 = (f32[448,128]{1,0:T(8,128)S(1)}, f32[448,128]{1,0:T(8,128)S(1)}, u32[]{:S(2)}, u32[]{:S(2)}) collective-permute-start(f32[448,128]{1,0:T(8,128)S(1)} %get-tuple-element.76), channel_id=1, source_target_pairs={{0,64},{1,65},{2,66},{3,67},{4,68},{5,69},{6,70},{7,71},{8,72},{9,... | collective-permute-start | bytes 688136 | tf_op jit(solution)/shard_map/ppermute | solution.py:490
  40.4 7.6 %collective-permute-start.11 = (f32[448,128]{1,0:T(8,128)S(1)}, f32[448,128]{1,0:T(8,128)S(1)}, u32[]{:S(2)}, u32[]{:S(2)}) collective-permute-start(f32[448,128]{1,0:T(8,128)S(1)} %get-tuple-element.77), channel_id=1, source_target_pairs={{0,96},{1,97},{2,98},{3,99},{4,100},{5,101},{6,102},{7,103},{8,104... | collective-permute-start | bytes 688136 | tf_op jit(solution)/shard_map/ppermute | solution.py:490
  41.8 6.7 %collective-permute-start.9 = (f32[448,128]{1,0:T(8,128)S(1)}, f32[448,128]{1,0:T(8,128)S(1)}, u32[]{:S(2)}, u32[]{:S(2)}) collective-permute-start(f32[448,128]{1,0:T(8,128)S(1)} %get-tuple-element.70.refs_11_), channel_id=1, source_target_pairs={{0,32},{1,33},{2,34},{3,35},{4,36},{5,37},{6,38},{7,39},{8,40},{9,... | collective-permute-start | bytes 688136 | tf_op jit(solution)/shard_map/ppermute | solution.py:490
  48.6 8.2 %collective-permute-start.14 = (f32[448,128]{1,0:T(8,128)S(1)}, f32[448,128]{1,0:T(8,128)S(1)}, u32[]{:S(2)}, u32[]{:S(2)}) collective-permute-start(f32[448,128]{1,0:T(8,128)S(1)} %shard_map.80.refs_12_.refs_0_), channel_id=1, source_target_pairs={{0,12},{1,13},{2,14},{3,15},{4,8},{5,9},{6,10},{7,11},{8,4},{9,5},... | collective-permute-start | bytes 688136 | tf_op jit(solution)/shard_map/ppermute | solution.py:490
  51.3 6.7 %collective-permute-start.13 = (f32[448,128]{1,0:T(8,128)S(1)}, f32[448,128]{1,0:T(8,128)S(1)}, u32[]{:S(2)}, u32[]{:S(2)}) collective-permute-start(f32[448,128]{1,0:T(8,128)S(1)} %shard_map.80.refs_12_.refs_0_), channel_id=1, source_target_pairs={{0,8},{1,9},{2,10},{3,11},{4,12},{5,13},{6,14},{7,15},{8,0},{9,1},... | collective-permute-start | bytes 688136 | tf_op jit(solution)/shard_map/ppermute | solution.py:490
  51.6 6.5 %collective-permute-start.12 = (f32[448,128]{1,0:T(8,128)S(1)}, f32[448,128]{1,0:T(8,128)S(1)}, u32[]{:S(2)}, u32[]{:S(2)}) collective-permute-start(f32[448,128]{1,0:T(8,128)S(1)} %shard_map.80.refs_12_.refs_0_), channel_id=1, source_target_pairs={{0,4},{1,5},{2,6},{3,7},{4,0},{5,1},{6,2},{7,3},{8,12},{9,13},{10,... | collective-permute-start | bytes 688136 | tf_op jit(solution)/shard_map/ppermute | solution.py:490
  58.2 9.3 %collective-permute-start.17 = (f32[448,128]{1,0:T(8,128)S(1)}, f32[448,128]{1,0:T(8,128)S(1)}, u32[]{:S(2)}, u32[]{:S(2)}) collective-permute-start(f32[448,128]{1,0:T(8,128)S(1)} %shard_map.82.refs_10_.refs_0_), channel_id=1, source_target_pairs={{0,3},{1,2},{2,1},{3,0},{4,7},{5,6},{6,5},{7,4},{8,11},{9,10},{10,... | collective-permute-start | bytes 688136 | tf_op jit(solution)/shard_map/ppermute | solution.py:490
  60.7 6.8 %collective-permute-start.16 = (f32[448,128]{1,0:T(8,128)S(1)}, f32[448,128]{1,0:T(8,128)S(1)}, u32[]{:S(2)}, u32[]{:S(2)}) collective-permute-start(f32[448,128]{1,0:T(8,128)S(1)} %shard_map.82.refs_10_.refs_0_), channel_id=1, source_target_pairs={{0,2},{1,3},{2,0},{3,1},{4,6},{5,7},{6,4},{7,5},{8,10},{9,11},{10,... | collective-permute-start | bytes 688136 | tf_op jit(solution)/shard_map/ppermute | solution.py:490
  60.7 7.0 %collective-permute-start.15 = (f32[448,128]{1,0:T(8,128)S(1)}, f32[448,128]{1,0:T(8,128)S(1)}, u32[]{:S(2)}, u32[]{:S(2)}) collective-permute-start(f32[448,128]{1,0:T(8,128)S(1)} %shard_map.82.refs_10_.refs_0_), channel_id=1, source_target_pairs={{0,1},{1,0},{2,3},{3,2},{4,5},{5,4},{6,7},{7,6},{8,9},{9,8},{10,11... | collective-permute-start | bytes 688136 | tf_op jit(solution)/shard_map/ppermute | solution.py:490
  67.8 12.8 %collective-permute-start.21 = (f32[448,128]{1,0:T(8,128)S(1)}, f32[448,128]{1,0:T(8,128)S(1)}, u32[]{:S(2)}, u32[]{:S(2)}) collective-permute-start(f32[448,128]{1,0:T(8,128)S(1)} %shard_map.84.refs_12_.refs_0_), channel_id=1, source_target_pairs={{0,16},{16,0},{32,48},{48,32},{64,80},{80,64},{96,112},{112,96},{1... | collective-permute-start | bytes 688136 | tf_op jit(solution)/shard_map/ppermute | solution.py:622
  70.7 9.9 %collective-permute-start.20 = (f32[448,128]{1,0:T(8,128)S(1)}, f32[448,128]{1,0:T(8,128)S(1)}, u32[]{:S(2)}, u32[]{:S(2)}) collective-permute-start(f32[448,128]{1,0:T(8,128)S(1)} %shard_map.84.refs_12_.refs_0_), channel_id=1, source_target_pairs={{0,96},{1,97},{2,98},{3,99},{4,100},{5,101},{6,102},{7,103},{8,104... | collective-permute-start | bytes 688136 | tf_op jit(solution)/shard_map/ppermute | solution.py:490
  73.5 7.2 %collective-permute-start.19 = (f32[448,128]{1,0:T(8,128)S(1)}, f32[448,128]{1,0:T(8,128)S(1)}, u32[]{:S(2)}, u32[]{:S(2)}) collective-permute-start(f32[448,128]{1,0:T(8,128)S(1)} %shard_map.84.refs_12_.refs_0_), channel_id=1, source_target_pairs={{0,64},{1,65},{2,66},{3,67},{4,68},{5,69},{6,70},{7,71},{8,72},{9,... | collective-permute-start | bytes 688136 | tf_op jit(solution)/shard_map/ppermute | solution.py:490
  73.5 7.2 %collective-permute-start.18 = (f32[448,128]{1,0:T(8,128)S(1)}, f32[448,128]{1,0:T(8,128)S(1)}, u32[]{:S(2)}, u32[]{:S(2)}) collective-permute-start(f32[448,128]{1,0:T(8,128)S(1)} %shard_map.84.refs_12_.refs_0_), channel_id=1, source_target_pairs={{0,32},{1,33},{2,34},{3,35},{4,36},{5,37},{6,38},{7,39},{8,40},{9,... | collective-permute-start | bytes 688136 | tf_op jit(solution)/shard_map/ppermute | solution.py:490
  80.8 2.7 %collective-permute-start.22 = (f32[1344,128]{1,0:T(8,128)S(1)}, f32[1344,128]{1,0:T(8,128)S(1)}, u32[]{:S(2)}, u32[]{:S(2)}) collective-permute-start(f32[1344,128]{1,0:T(8,128)S(1)} %shard_map.86.refs_1_.refs_2_), channel_id=1, source_target_pairs={{0,16},{16,0},{32,48},{48,32},{64,80},{80,64},{96,112},{112,96},{1... | collective-permute-start | bytes 2064392 | tf_op jit(solution)/shard_map/ppermute | solution.py:625

commit v5 on v4

--- a/solution.py
+++ b/solution.py
@@ -164,7 +164,7 @@
     def product(shifted, x):
         columns = [g_ref[x + 2 - tx : x + 2 - tx + SPAN].reshape(SPAN * ROWS, C) for tx in range(3)]
         beside = jnp.concatenate(columns, axis=1)
-        return lax.dot_general(patches(shifted, SPAN), beside, DEPTH_FIRST, preferred_element_type=F32)
+        return lax.dot_general(beside, patches(shifted, SPAN), DEPTH_FIRST, preferred_element_type=F32)
 
     put(even, first)
     made = product(even, first)
@@ -179,7 +179,7 @@
         lambda *refs: own_grad_kernel(first, more, *refs),
         in_specs=[VMEM] * (2 + more) + [ANY],
         out_specs=VMEM,
-        out_shape=shape((TAPS, WIDE), F32),
+        out_shape=shape((WIDE, TAPS), F32),
         scratch_shapes=[pltpu.VMEM((3, SPAN, Y + 2, Z, C), BF16)] * 2,
         compiler_params=params(),
         cost_estimate=cost(2 * SPAN, 8 << 20),
@@ -191,10 +191,10 @@
     padded = jnp.concatenate([blank, face_ref[1], blank], axis=0)
     around = jnp.concatenate([padded[2 - tx : 2 - tx + X].reshape(X * Z, C) for tx in range(3)], axis=1)
     left = jnp.concatenate([a.astype(BF16).reshape(X * Z, C) for a in trio], axis=1)
-    made = lax.dot_general(left, around, DEPTH_FIRST, preferred_element_type=F32)
+    made = lax.dot_general(around, left, DEPTH_FIRST, preferred_element_type=F32)
     for k in range(3):
         start = (row + k * stride) * C
-        total[start : start + C] += made[k * C : (k + 1) * C]
+        total[:, start : start + C] += made[:, k * C : (k + 1) * C]
 
 
 def z_rim_kernel(own_ref, gzlo, gzhi, nzlo, nzhi, total):
@@ -215,8 +215,8 @@
         put_far(scratch.at[:, side : side + 1], 0, far, 0, side)
         left = patches(scratch.at[:, side : side + 1], 1)
         beside = g_ref[plane].reshape(ROWS, C)
-        total[:, tx * C : (tx + 1) * C] += lax.dot_general(
-            left, beside, DEPTH_FIRST, preferred_element_type=F32
+        total[tx * C : (tx + 1) * C] += lax.dot_general(
+            beside, left, DEPTH_FIRST, preferred_element_type=F32
         )
     at = lax.broadcasted_iota(jnp.int32, (X, Z, C), 1)
     for side, row, near, edges, face in ((0, 0, nylo, elo, gylo), (1, 6, nyhi, ehi, gyhi)):
@@ -237,7 +237,7 @@
             for tap in range(27):
                 tx, row = tap // 9, tap % 9
                 ref = keep_ref if tap // HALF == mine else send_ref
-                ref[tap % HALF] = total[row * C : (row + 1) * C, tx * C : (tx + 1) * C] * scale
+                ref[tap % HALF] = total[tx * C : (tx + 1) * C, row * C : (row + 1) * C].T * scale
             ref = keep_ref if mine == 1 else send_ref
             ref[HALF - 1] = jnp.zeros((C, C), F32)
 
@@ -248,7 +248,7 @@
         in_specs=[VMEM] * (2 + len(operands)),
         out_specs=[VMEM, VMEM],
         out_shape=[shape((HALF, C, C), F32)] * 2,
-        scratch_shapes=[pltpu.VMEM((3, 2, Y + 2, Z, C), BF16), pltpu.VMEM((TAPS, WIDE), F32)],
+        scratch_shapes=[pltpu.VMEM((3, 2, Y + 2, Z, C), BF16), pltpu.VMEM((WIDE, TAPS), F32)],
         compiler_params=params(),
         cost_estimate=cost(3, 6 << 20),
     )(own, cotangents, *operands)
@@ -266,12 +266,15 @@
     late_in = None if starts else refs.pop(0)
     ready = None if starts and part == 0 else refs.pop(0)
     late = None if ends else refs.pop(-5)
-    o_ref, carry_ref, even, odd, edge, made_ref, left = refs[-7:]
+    o_ref, carry_ref, even, others, edge, made_ref, left = refs[-7:]
+    odd = others.at[0]
     count = groups * GROUP
     own_copies = groups if ends else groups - 1
     late_copy = None
     if not starts:
-        late_copy = pltpu.make_async_copy(late_in, o_ref.at[pl.ds(first - GROUP - 1, GROUP)], left.at[groups + 1])
+        skip = 1 if first == GROUP else 0
+        target = o_ref.at[pl.ds(first - GROUP - 1 + skip, GROUP - skip)]
+        late_copy = pltpu.make_async_copy(late_in.at[pl.ds(skip, GROUP - skip)], target, left.at[groups + 1])
         late_copy.start()
 
     def put(shifted, at, x):
@@ -292,7 +295,9 @@
         def term(slot, tx):
             return made[slot * ROWS : (slot + 1) * ROWS, tx * C : (tx + 1) * C]
 
-        if opens is not True:
+        if opens is True:
+            made_ref[0] = jnp.zeros((Y, Z, C), BF16)
+        else:
             finish(x - 1, near + term(0, 2))
         finish(x, next_ + term(0, 1) + term(1, 2))
         for slot in range(1, GROUP - 1):
@@ -301,7 +306,8 @@
             pl.when(sem == 0)(lambda: copy(x + 1, GROUP - 1, sem).start())
             pl.when(sem > 0)(lambda: copy(x, GROUP, sem).start())
         elif opens:
-            copy(x + 1, GROUP - 1, sem).start()
+            if own_copies > 0:
+                copy(x + 1, GROUP - 1, sem).start()
         elif ends:
             copy(x, GROUP, sem).start()
         else:
@@ -314,7 +320,7 @@
         next_ = jnp.dot(patches(edge, 1), w_ref[:, :C], preferred_element_type=F32)
     else:
         near, next_ = before[0], before[1]
-    if groups > 2:
+    if groups > 3:
         if ready is None:
             put(even, part, 0)
         else:
@@ -338,11 +344,13 @@
         near = carry_ref[0]
     else:
         if ready is None:
-            ready = even
-            put(even, part, first)
-        near, next_ = group(ready, first, 0, near, next_, starts)
-        put(odd, part, first + GROUP)
-        near, next_ = group(odd, first + GROUP, 1, near, next_, False)
+            put(odd, part, first)
+        shifted = [odd] if ready is None else [ready, odd, others.at[1]]
+        for at in range(groups):
+            x = first + at * GROUP
+            near, next_ = group(shifted[at], x, at, near, next_, starts and at == 0)
+            if at + 1 < groups:
+                put(shifted[at + 1], part, x + GROUP)
         put(even, *following)
         carry_ref[0] = near
         carry_ref[1] = next_
@@ -389,7 +397,7 @@
     buffers = [shape((2, ROWS, C), F32), shape(shifted, BF16)]
     kept = buffers + ([] if ends else [shape((GROUP, Y, Z, C), BF16)])
     scratch = [
-        pltpu.VMEM(shifted, BF16),
+        pltpu.VMEM((2, *shifted), BF16),
         pltpu.VMEM((3, 1, Y + 2, Z, C), BF16),
         pltpu.VMEM((groups * GROUP + 1, Y, Z, C), BF16),
         pltpu.SemaphoreType.DMA((groups + 2,)),
@@ -575,7 +583,7 @@
         arrange_kernel, [shape((TAPS, WIDE), BF16)] * 2, [weight.reshape(27, C, C)], [edge_lo]
     )
     own = small_kernel(
-        z_rim_kernel, shape((TAPS, WIDE), F32), [own, zlo, zhi, near_zlo, near_zhi], [edge_lo]
+        z_rim_kernel, shape((WIDE, TAPS), F32), [own, zlo, zhi, near_zlo, near_zhi], [edge_lo]
     )
 
     face = shape((2, X, Z, C), BF16)
@@ -594,7 +602,7 @@
     field = [*slabs, held_ylo, held_yhi, col_lo, col_hi]
     made = [None, None]
     weights = (forward, flipped)
-    order = [(0, 0, 2), (0, 8, 4), (0, 24, 2), (1, 0, 4), (1, 16, 4)]
+    order = [(0, 0, 1), (0, 4, 4), (0, 20, 3), (1, 0, 4), (1, 16, 4)]
     state = {}
 
     def convolve(tie):

time: 84.7 us -> 83.2 us (0.982)
  Pallas kernels: 44.4 us -> 42.6 us
    pallas_call x2, Pallas kernels: 10.8 us -> 8.77 us  [own_grad(): pl.pallas_call(lambda *refs: own_grad_kernel(first, more, *refs), in_spec...]
    ppermute x12, waiting for transfers between devices: 3.03 us -> 1.44 us  [exchange(): lax.ppermute(value, ('gx', 'gy', 'gz'), pairs(turn, step))]
    ppermute x8, waiting for transfers between devices: 0.25 us -> 1.6 us  [shift(): lax.ppermute(value, axis, [(i, (i + step) % count) for i in range(count)])]
  transfers between devices with their start and end apart: 23 -> 23, of which waited for: 7 -> 8; matrix products, arithmetic and copies ran while one was open for 0% -> 0% of each run, Pallas kernels for 46% -> 45%
where the time goes in v5:
time: 83.2 us; the launch traced here: 83 us
  Pallas kernels  42.6 us (51%)
  starting transfers between devices  33.2 us (40%)
  waiting for transfers between devices  3.26 us (4%)
  local copies, waits for them, and re-layouts  2.95 us (4%)
  between operations  1.1 us (1%)
    pallas_call x5, Pallas kernels, conv_piece(): pl.pallas_call(plain if more else final, in_specs=specs, out_specs=[ANY]...  25.5 us
    ppermute x12, starting transfers between devices, exchange(): lax.ppermute(value, ('gx', 'gy', 'gz'), pairs(turn, step))  13.9 us
    ppermute x8, starting transfers between devices, shift(): lax.ppermute(value, axis, [(i, (i + step) % count) for i in range(count)])  13.8 us
    pallas_call x2, Pallas kernels, own_grad(): pl.pallas_call(lambda *refs: own_grad_kernel(first, more, *refs), in_spec...  8.77 us
    ppermute x1, starting transfers between devices, body(): beside = lax.ppermute(chunk, 'gx', swap)  3.46 us
    unnamed x8, local copies, waits for them, and re-layouts  2.95 us
    pallas_call x10, Pallas kernels, small_kernel(): pl.pallas_call(run, in_specs=(specs or [VMEM] * count) + [ANY] * len(ties...  2.61 us
    pallas_call x3, Pallas kernels, write(): pl.pallas_call(kernel, in_specs=[VMEM] * len(arrays) + [ANY] * (len(opera...  2.51 us
  transfers between devices with their start and end apart: 23, of which 8 were waited for; matrix products, arithmetic and copies ran while one was open for 0% of the time, Pallas kernels for 45%

profile of v5, /device:TPU:1, one launch (start us, length us, event | category | flops | bytes accessed | tf_op | source)
XLA Modules:
  0.0 83.0 jit_solution(1035706237659759959)
XLA Ops:
  0.6 0.7 copy-done.3
  1.9 1.6 %copy-done = bf16[32,16,16,128]{3,2,1,0:T(8,128)(2,1)S(1)} copy-done((bf16[32,16,16,128]{3,2,1,0:T(8,128)(2,1)S(1)}, bf16[32,16,16,128]{3,2,1,0:T(8,128)(2,1)}, u32[]{:S(2)}) %copy-start) | copy-done | bytes 2097176
  3.5 0.9 %shard_map.68 = (bf16[34,16,16,128]{3,2,1,0:T(8,128)(2,1)S(1)}, bf16[1,32,16,128]{3,2,1,0:T(8,128)(2,1)S(1)}, bf16[1,32,16,128]{3,2,1,0:T(8,128)(2,1)S(1)}, bf16...) custom-call(bf16[32,16,16,128]{3,2,1,0:T(8,128)(2,1)S(1)} %copy-done, ...), custom_call_target="tpu_custom_call" | custom-call | flops 1000000 | bytes 5242880 | tf_op jit(solution)/shard_map/pallas_call | solution.py:96
  4.4 0.7 copy-done.1
  5.1 0.9 %shard_map.69 = (bf16[34,16,16,128]{3,2,1,0:T(8,128)(2,1)S(1)}, bf16[2,32,16,128]{3,2,1,0:T(8,128)(2,1)S(1)}, bf16[2,32,16,128]{3,2,1,0:T(8,128)(2,1)S(1)}, bf16...) custom-call(bf16[32,16,16,128]{3,2,1,0:T(8,128)(2,1)S(1)} %copy-done.1, ...), custom_call_target="tpu_custom_call" | custom-call | flops 1000000 | bytes 5242880 | tf_op jit(solution)/shard_map/pallas_call | solution.py:104
  6.0 2.2 %collective-permute-start = (bf16[2,32,16,128]{3,2,1,0:T(8,128)(2,1)S(1)}, bf16[2,32,16,128]{3,2,1,0:T(8,128)(2,1)S(1)}, u32[]{:S(2)}, u32[]{:S(2)}) collective-permute-start(bf16[2,32,16,128]{3,2,1,0:T(8,128)(2,1)S(1)} %get-tuple-element.52.gyhi), channel_id=1, source_target_pairs={{0,4},{4,8},{8,12},{12,0},{1,5},{5,9},{9,13},{13,1},{2,6},{6,10},{... | collective-permute-start | bytes 786440 | tf_op jit(solution)/shard_map/ppermute | solution.py:567
  8.2 1.5 %collective-permute-start.1 = (bf16[2,32,16,128]{3,2,1,0:T(8,128)(2,1)S(1)}, bf16[2,32,16,128]{3,2,1,0:T(8,128)(2,1)S(1)}, u32[]{:S(2)}, u32[]{:S(2)}) collective-permute-start(bf16[2,32,16,128]{3,2,1,0:T(8,128)(2,1)S(1)} %get-tuple-element.53.gylo), channel_id=1, source_target_pairs={{0,12},{4,0},{8,4},{12,8},{1,13},{5,1},{9,5},{13,9},{2,14},{6,2},{... | collective-permute-start | bytes 786440 | tf_op jit(solution)/shard_map/ppermute | solution.py:567
  9.7 1.2 %collective-permute-start.2 = (bf16[2,32,16,128]{3,2,1,0:T(8,128)(2,1)S(1)}, bf16[2,32,16,128]{3,2,1,0:T(8,128)(2,1)S(1)}, u32[]{:S(2)}, u32[]{:S(2)}) collective-permute-start(bf16[2,32,16,128]{3,2,1,0:T(8,128)(2,1)S(1)} %get-tuple-element.54.refs_2_), channel_id=1, source_target_pairs={{0,1},{1,2},{2,3},{3,0},{4,5},{5,6},{6,7},{7,4},{8,9},{9,10},{10,1... | collective-permute-start | bytes 786440 | tf_op jit(solution)/shard_map/ppermute | solution.py:567
  11.0 1.5 %collective-permute-start.3 = (bf16[2,32,16,128]{3,2,1,0:T(8,128)(2,1)S(1)}, bf16[2,32,16,128]{3,2,1,0:T(8,128)(2,1)S(1)}, u32[]{:S(2)}, u32[]{:S(2)}) collective-permute-start(bf16[2,32,16,128]{3,2,1,0:T(8,128)(2,1)S(1)} %get-tuple-element.55.refs_2_.refs_1_), channel_id=1, source_target_pairs={{0,3},{1,0},{2,1},{3,2},{4,7},{5,4},{6,5},{7,6},{8,11},{9,8},{10,9... | collective-permute-start | bytes 786440 | tf_op jit(solution)/shard_map/ppermute | solution.py:567
  12.4 4.4 %shard_map.70.refs_2_.refs_0_ = f32[384,1152]{1,0:T(8,128)S(1)} custom-call(bf16[34,16,16,128]{3,2,1,0:T(8,128)(2,1)S(1)} %get-tuple-element.46.refs_0_.refs_1_, bf16[34,16,16,128]{3,2,1,0:T(8,128)(2,1)S(1)} %get-tuple-element.51.refs_1_.g_ref.refs_2_, bf16[2,32,16,128]{3,2,1,0:T(8,128)(2,1)S(1)} %get-tuple-element.55.refs_2_.refs_1_), custom_call_target="tpu_custom_call" | custom-call | flops 3623878656 | bytes 8388608 | tf_op jit(solution)/shard_map/pallas_call | solution.py:178
  16.8 0.9 %collective-permute-done.2.refs_0_.refs_3_.refs_4_ = bf16[2,32,16,128]{3,2,1,0:T(8,128)(2,1)S(1)} collective-permute-done((bf16[2,32,16,128]{3,2,1,0:T(8,128)(2,1)S(1)}, bf16[2,32,16,128]{3,2,1,0:T(8,128)(2,1)S(1)}, u32[]{:S(2)}, u32[]{:S(2)}) %collective-permute-start.2) | collective-permute-done | bytes 262176 | tf_op jit(solution)/shard_map/ppermute | solution.py:567
  18.0 2.7 %collective-permute-start.5 = (bf16[2,2,32,128]{3,2,1,0:T(8,128)(2,1)S(1)}, bf16[2,2,32,128]{3,2,1,0:T(8,128)(2,1)S(1)}, u32[]{:S(2)}, u32[]{:S(2)}) collective-permute-start(bf16[2,2,32,128]{3,2,1,0:T(8,128)(2,1)S(1)} %get-tuple-element.57.refs_1_.refs_5_), channel_id=1, source_target_pairs={{0,12},{4,0},{8,4},{12,8},{1,13},{5,1},{9,5},{13,9},{2,14},{6,2},{... | collective-permute-start | bytes 98312 | tf_op jit(solution)/shard_map/ppermute | solution.py:567
  22.5 4.6 %collective-permute-start.7 = (bf16[2,21,16,128]{3,2,1,0:T(8,128)(2,1)S(1)}, bf16[2,21,16,128]{3,2,1,0:T(8,128)(2,1)S(1)}, u32[]{:S(2)}, u32[]{:S(2)}) collective-permute-start(bf16[2,21,16,128]{3,2,1,0:T(8,128)(2,1)S(1)} %get-tuple-element.64), channel_id=1, source_target_pairs={{0,16},{16,32},{32,48},{48,64},{64,80},{80,96},{96,112},{112,0},{1... | collective-permute-start | bytes 516104 | tf_op jit(solution)/shard_map/ppermute | solution.py:567
  27.1 4.4 %shard_map.75.own_ref = f32[384,1152]{1,0:T(8,128)S(1)} custom-call(bf16[34,16,16,128]{3,2,1,0:T(8,128)(2,1)S(1)} %get-tuple-element.46.refs_0_.refs_1_, bf16[34,16,16,128]{3,2,1,0:T(8,128)(2,1)S(1)} %get-tuple-element.51.refs_1_.g_ref.refs_2_, f32[384,1152]{1,0:T(8,128)S(1)} %shard_map.73.refs_9_.refs_2_, bf16[2,21,16,128]{3,2,1,0:T(8,128)(2,1)S(1)} %get-tuple-element.63.refs_3_), custom_call_target="tpu_custom_call" | custom-call | flops 3623878656 | bytes 8388608 | tf_op jit(solution)/shard_map/pallas_call | solution.py:178
  32.0 1.4 %shard_map.76 = (f32[14,128,128]{2,1,0:T(8,128)S(1)}, f32[14,128,128]{2,1,0:T(8,128)S(1)}) custom-call(f32[384,1152]{1,0:T(8,128)S(1)} %shard_map.75.own_ref, bf16[34,16,16,128]{3,2,1,0:T(8,128)(2,1)S(1)} %get-tuple-element.51.refs_1_.g_ref.refs_2_, bf16[2,32,16,128]{3,2,1,0:T(8,128)(2,1)S(1)} %get-tuple-element.53.gylo, ...), custom_call_target="tpu_custom_call" | custom-call | flops 679477248 | bytes 6291456 | tf_op jit(solution)/shard_map/pallas_call | solution.py:246
  33.3 1.1 %collective-permute-start.8 = (f32[14,128,128]{2,1,0:T(8,128)S(1)}, f32[14,128,128]{2,1,0:T(8,128)S(1)}, u32[]{:S(2)}, u32[]{:S(2)}) collective-permute-start(f32[14,128,128]{2,1,0:T(8,128)S(1)} %get-tuple-element.65.refs_9_), channel_id=1, source_target_pairs={{0,16},{16,0},{32,48},{48,32},{64,80},{80,64},{96,112},{112,96},{1... | collective-permute-start | bytes 2752520 | tf_op jit(solution)/shard_map/ppermute | solution.py:618
  34.4 2.0 %shard_map.77 = (bf16[32,16,16,128]{3,2,1,0:T(8,128)(2,1)}, f32[2,256,128]{2,1,0:T(8,128)S(1)}, bf16[3,4,18,16,128]{4,3,2,1,0:T(8,128)(2,1)S(1)}, bf16[4,16,16,128]{3,2,1,0:T(8,128)(2,1)S(1)}) custom-call(bf16[4,16,16,128]{3,2,1,0:T(8,128)(2,1)S(1)} %shard_map.67.mask_ref.refs_0_, bf16[34,16,16,128]{3,2,1,0:T(8,128)(2,1)S(1)} %get-tuple-element.46.refs_0_.refs_1_, ...), custom_call_target="tpu_custom_call" | custom-call | flops 905969664 | bytes 2097152 | tf_op jit(solution)/shard_map/pallas_call | solution.py:416
  36.6 1.7 %collective-permute-start.10 = (f32[448,128]{1,0:T(8,128)S(1)}, f32[448,128]{1,0:T(8,128)S(1)}, u32[]{:S(2)}, u32[]{:S(2)}) collective-permute-start(f32[448,128]{1,0:T(8,128)S(1)} %get-tuple-element.76), channel_id=1, source_target_pairs={{0,64},{1,65},{2,66},{3,67},{4,68},{5,69},{6,70},{7,71},{8,72},{9,... | collective-permute-start | bytes 688136 | tf_op jit(solution)/shard_map/ppermute | solution.py:498
  38.3 1.4 %collective-permute-start.11 = (f32[448,128]{1,0:T(8,128)S(1)}, f32[448,128]{1,0:T(8,128)S(1)}, u32[]{:S(2)}, u32[]{:S(2)}) collective-permute-start(f32[448,128]{1,0:T(8,128)S(1)} %get-tuple-element.77), channel_id=1, source_target_pairs={{0,96},{1,97},{2,98},{3,99},{4,100},{5,101},{6,102},{7,103},{8,104... | collective-permute-start | bytes 688136 | tf_op jit(solution)/shard_map/ppermute | solution.py:498
  40.2 5.7 %shard_map.79 = (bf16[32,16,16,128]{3,2,1,0:T(8,128)(2,1)}, f32[2,256,128]{2,1,0:T(8,128)S(1)}, bf16[3,4,18,16,128]{4,3,2,1,0:T(8,128)(2,1)S(1)}, bf16[4,16,16,128]{3,2,1,0:T(8,128)(2,1)S(1)}) custom-call(bf16[4,16,16,128]{3,2,1,0:T(8,128)(2,1)S(1)} %shard_map.67.mask_ref.refs_0_, ...), custom_call_target="tpu_custom_call", output_to_operand_aliasing={{0}: (12, {})} | custom-call | flops 3623878656 | bytes 2097152 | tf_op jit(solution)/shard_map/pallas_call | solution.py:416
  46.5 3.0 %collective-permute-start.14 = (f32[448,128]{1,0:T(8,128)S(1)}, f32[448,128]{1,0:T(8,128)S(1)}, u32[]{:S(2)}, u32[]{:S(2)}) collective-permute-start(f32[448,128]{1,0:T(8,128)S(1)} %shard_map.80.refs_12_.refs_0_), channel_id=1, source_target_pairs={{0,12},{1,13},{2,14},{3,15},{4,8},{5,9},{6,10},{7,11},{8,4},{9,5},... | collective-permute-start | bytes 688136 | tf_op jit(solution)/shard_map/ppermute | solution.py:498
  50.1 5.3 %shard_map.81 = (bf16[32,16,16,128]{3,2,1,0:T(8,128)(2,1)}, f32[2,256,128]{2,1,0:T(8,128)S(1)}, bf16[3,4,18,16,128]{4,3,2,1,0:T(8,128)(2,1)S(1)}) custom-call(bf16[4,16,16,128]{3,2,1,0:T(8,128)(2,1)S(1)} %shard_map.67.mask_ref.refs_0_, bf16[34,16,16,128]{3,2,1,0:T(8,128)(2,1)S(1)} %get-tuple-element.46.refs_0_.refs_1_, ...), custom_call_target="tpu_custom_call", output_to_operand_aliasing={{0}: (13, {})} | custom-call | flops 2717908992 | bytes 2097152 | tf_op jit(solution)/shard_map/pallas_call | solution.py:416
  55.4 0.7 collective-permute-done.13.refs_2_
  56.4 2.6 %collective-permute-start.17 = (f32[448,128]{1,0:T(8,128)S(1)}, f32[448,128]{1,0:T(8,128)S(1)}, u32[]{:S(2)}, u32[]{:S(2)}) collective-permute-start(f32[448,128]{1,0:T(8,128)S(1)} %shard_map.82.refs_10_.refs_0_), channel_id=1, source_target_pairs={{0,3},{1,2},{2,1},{3,0},{4,7},{5,6},{6,5},{7,4},{8,11},{9,10},{10,... | collective-permute-start | bytes 688136 | tf_op jit(solution)/shard_map/ppermute | solution.py:498
  59.7 6.0 %shard_map.83 = (bf16[32,16,16,128]{3,2,1,0:T(8,128)(2,1)}, f32[2,256,128]{2,1,0:T(8,128)S(1)}, bf16[3,4,18,16,128]{4,3,2,1,0:T(8,128)(2,1)S(1)}, bf16[4,16,16,128]{3,2,1,0:T(8,128)(2,1)S(1)}) custom-call(bf16[4,16,16,128]{3,2,1,0:T(8,128)(2,1)S(1)} %shard_map.67.mask_ref.refs_0_, bf16[34,16,16,128]{3,2,1,0:T(8,128)(2,1)S(1)} %get-tuple-element.46.refs_0_.refs_1_, ...), custom_call_target="tpu_custom_call" | custom-call | flops 3623878656 | bytes 2097152 | tf_op jit(solution)/shard_map/pallas_call | solution.py:416
  65.8 3.5 %collective-permute-start.21 = (f32[448,128]{1,0:T(8,128)S(1)}, f32[448,128]{1,0:T(8,128)S(1)}, u32[]{:S(2)}, u32[]{:S(2)}) collective-permute-start(f32[448,128]{1,0:T(8,128)S(1)} %shard_map.84.refs_12_.refs_0_), channel_id=1, source_target_pairs={{0,16},{16,0},{32,48},{48,32},{64,80},{80,64},{96,112},{112,96},{1... | collective-permute-start | bytes 688136 | tf_op jit(solution)/shard_map/ppermute | solution.py:630
  69.2 2.7 %collective-permute-start.20 = (f32[448,128]{1,0:T(8,128)S(1)}, f32[448,128]{1,0:T(8,128)S(1)}, u32[]{:S(2)}, u32[]{:S(2)}) collective-permute-start(f32[448,128]{1,0:T(8,128)S(1)} %shard_map.84.refs_12_.refs_0_), channel_id=1, source_target_pairs={{0,96},{1,97},{2,98},{3,99},{4,100},{5,101},{6,102},{7,103},{8,104... | collective-permute-start | bytes 688136 | tf_op jit(solution)/shard_map/ppermute | solution.py:498
  72.6 6.6 %shard_map.85 = (bf16[32,16,16,128]{3,2,1,0:T(8,128)(2,1)}, f32[8,128]{1,0:T(8,128)S(1)}) custom-call(bf16[4,16,16,128]{3,2,1,0:T(8,128)(2,1)S(1)} %shard_map.67.mask_ref.refs_0_, bf16[34,16,16,128]{3,2,1,0:T(8,128)(2,1)S(1)} %get-tuple-element.46.refs_0_.refs_1_, ...), custom_call_target="tpu_custom_call", output_to_operand_aliasing={{0}: (13, {})} | custom-call | flops 3623878656 | bytes 2097152 | tf_op jit(solution)/shard_map/pallas_call | solution.py:416
  79.3 0.9 %collective-permute-start.22 = (f32[1344,128]{1,0:T(8,128)S(1)}, f32[1344,128]{1,0:T(8,128)S(1)}, u32[]{:S(2)}, u32[]{:S(2)}) collective-permute-start(f32[1344,128]{1,0:T(8,128)S(1)} %shard_map.86.refs_1_.refs_2_), channel_id=1, source_target_pairs={{0,16},{16,0},{32,48},{48,32},{64,80},{80,64},{96,112},{112,96},{1... | collective-permute-start | bytes 2064392 | tf_op jit(solution)/shard_map/ppermute | solution.py:633
  80.2 0.9 %shard_map.87.refs_2_ = f32[3456,128]{1,0:T(8,128)} custom-call(f32[448,128]{1,0:T(8,128)S(1)} %shard_map.84.refs_12_.refs_0_, f32[1344,128]{1,0:T(8,128)S(1)} %shard_map.86.refs_1_.refs_2_, f32[1344,128]{1,0:T(8,128)S(1)} %shard_map.86.refs_1_.refs_2_), custom_call_target="tpu_custom_call" | custom-call | flops 1000 | bytes 1048576 | tf_op jit(solution)/shard_map/pallas_call | solution.py:547
  81.1 0.7 shard_map.88.refs_2_
  82.0 0.9 %shard_map.89 = f32[3456,128]{1,0:T(8,128)} custom-call(f32[1344,128]{1,0:T(8,128)S(1)} %collective-permute-done.22.refs_0_, f32[1344,128]{1,0:T(8,128)S(1)} %shard_map.86.refs_1_.refs_2_, f32[3456,128]{1,0:T(8,128)} %shard_map.88.refs_2_), custom_call_target="tpu_custom_call", output_to_operand_aliasing={{}: (2, {})} | custom-call | flops 1000 | bytes 1048576 | tf_op jit(solution)/shard_map/pallas_call | solution.py:547
  (45 shorter events, 6.8 us)
Async XLA Ops:
  0.6 0.7 copy-start.3
  1.9 1.6 %copy-start = (bf16[32,16,16,128]{3,2,1,0:T(8,128)(2,1)S(1)}, bf16[32,16,16,128]{3,2,1,0:T(8,128)(2,1)}, u32[]{:S(2)}) copy-start(bf16[32,16,16,128]{3,2,1,0:T(8,128)(2,1)} %f_ref.1) | copy-start | bytes 6291460
  3.5 1.6 %copy-start.1 = (bf16[32,16,16,128]{3,2,1,0:T(8,128)(2,1)S(1)}, bf16[32,16,16,128]{3,2,1,0:T(8,128)(2,1)}, u32[]{:S(2)}) copy-start(bf16[32,16,16,128]{3,2,1,0:T(8,128)(2,1)} %c_ref.1) | copy-start | bytes 6291460
  6.0 15.6 %collective-permute-start = (bf16[2,32,16,128]{3,2,1,0:T(8,128)(2,1)S(1)}, bf16[2,32,16,128]{3,2,1,0:T(8,128)(2,1)S(1)}, u32[]{:S(2)}, u32[]{:S(2)}) collective-permute-start(bf16[2,32,16,128]{3,2,1,0:T(8,128)(2,1)S(1)} %get-tuple-element.52.gyhi), channel_id=1, source_target_pairs={{0,4},{4,8},{8,12},{12,0},{1,5},{5,9},{9,13},{13,1},{2,6},{6,10},{... | collective-permute-start | bytes 786440 | tf_op jit(solution)/shard_map/ppermute | solution.py:567
  8.2 13.5 %collective-permute-start.1 = (bf16[2,32,16,128]{3,2,1,0:T(8,128)(2,1)S(1)}, bf16[2,32,16,128]{3,2,1,0:T(8,128)(2,1)S(1)}, u32[]{:S(2)}, u32[]{:S(2)}) collective-permute-start(bf16[2,32,16,128]{3,2,1,0:T(8,128)(2,1)S(1)} %get-tuple-element.53.gylo), channel_id=1, source_target_pairs={{0,12},{4,0},{8,4},{12,8},{1,13},{5,1},{9,5},{13,9},{2,14},{6,2},{... | collective-permute-start | bytes 786440 | tf_op jit(solution)/shard_map/ppermute | solution.py:567
  9.7 8.0 %collective-permute-start.2 = (bf16[2,32,16,128]{3,2,1,0:T(8,128)(2,1)S(1)}, bf16[2,32,16,128]{3,2,1,0:T(8,128)(2,1)S(1)}, u32[]{:S(2)}, u32[]{:S(2)}) collective-permute-start(bf16[2,32,16,128]{3,2,1,0:T(8,128)(2,1)S(1)} %get-tuple-element.54.refs_2_), channel_id=1, source_target_pairs={{0,1},{1,2},{2,3},{3,0},{4,5},{5,6},{6,7},{7,4},{8,9},{9,10},{10,1... | collective-permute-start | bytes 786440 | tf_op jit(solution)/shard_map/ppermute | solution.py:567
  11.0 6.8 %collective-permute-start.3 = (bf16[2,32,16,128]{3,2,1,0:T(8,128)(2,1)S(1)}, bf16[2,32,16,128]{3,2,1,0:T(8,128)(2,1)S(1)}, u32[]{:S(2)}, u32[]{:S(2)}) collective-permute-start(bf16[2,32,16,128]{3,2,1,0:T(8,128)(2,1)S(1)} %get-tuple-element.55.refs_2_.refs_1_), channel_id=1, source_target_pairs={{0,3},{1,0},{2,1},{3,2},{4,7},{5,4},{6,5},{7,6},{8,11},{9,8},{10,9... | collective-permute-start | bytes 786440 | tf_op jit(solution)/shard_map/ppermute | solution.py:567
  16.8 3.8 %copy-start.2 = (bf16[3,3,3,128,128]{4,3,2,1,0:T(8,128)(2,1)S(1)}, bf16[3,3,3,128,128]{4,3,2,1,0:T(8,128)(2,1)}, u32[]{:S(2)}) copy-start(bf16[3,3,3,128,128]{4,3,2,1,0:T(8,128)(2,1)} %param.6) | copy-start | bytes 2654212
  17.9 4.0 %collective-permute-start.4 = (bf16[2,2,32,128]{3,2,1,0:T(8,128)(2,1)S(1)}, bf16[2,2,32,128]{3,2,1,0:T(8,128)(2,1)S(1)}, u32[]{:S(2)}, u32[]{:S(2)}) collective-permute-start(bf16[2,2,32,128]{3,2,1,0:T(8,128)(2,1)S(1)} %get-tuple-element.56), channel_id=1, source_target_pairs={{0,4},{4,8},{8,12},{12,0},{1,5},{5,9},{9,13},{13,1},{2,6},{6,10},{... | collective-permute-start | bytes 98312 | tf_op jit(solution)/shard_map/ppermute | solution.py:567
  18.0 4.0 %collective-permute-start.5 = (bf16[2,2,32,128]{3,2,1,0:T(8,128)(2,1)S(1)}, bf16[2,2,32,128]{3,2,1,0:T(8,128)(2,1)S(1)}, u32[]{:S(2)}, u32[]{:S(2)}) collective-permute-start(bf16[2,2,32,128]{3,2,1,0:T(8,128)(2,1)S(1)} %get-tuple-element.57.refs_1_.refs_5_), channel_id=1, source_target_pairs={{0,12},{4,0},{8,4},{12,8},{1,13},{5,1},{9,5},{13,9},{2,14},{6,2},{... | collective-permute-start | bytes 98312 | tf_op jit(solution)/shard_map/ppermute | solution.py:567
  22.5 9.0 %collective-permute-start.7 = (bf16[2,21,16,128]{3,2,1,0:T(8,128)(2,1)S(1)}, bf16[2,21,16,128]{3,2,1,0:T(8,128)(2,1)S(1)}, u32[]{:S(2)}, u32[]{:S(2)}) collective-permute-start(bf16[2,21,16,128]{3,2,1,0:T(8,128)(2,1)S(1)} %get-tuple-element.64), channel_id=1, source_target_pairs={{0,16},{16,32},{32,48},{48,64},{64,80},{80,96},{96,112},{112,0},{1... | collective-permute-start | bytes 516104 | tf_op jit(solution)/shard_map/ppermute | solution.py:567
  27.1 4.8 %collective-permute-start.6 = (bf16[2,21,16,128]{3,2,1,0:T(8,128)(2,1)S(1)}, bf16[2,21,16,128]{3,2,1,0:T(8,128)(2,1)S(1)}, u32[]{:S(2)}, u32[]{:S(2)}) collective-permute-start(bf16[2,21,16,128]{3,2,1,0:T(8,128)(2,1)S(1)} %get-tuple-element.63.refs_3_), channel_id=1, source_target_pairs={{0,112},{16,0},{32,16},{48,32},{64,48},{80,64},{96,80},{112,96},{1... | collective-permute-start | bytes 516104 | tf_op jit(solution)/shard_map/ppermute | solution.py:567
  33.3 3.2 %collective-permute-start.8 = (f32[14,128,128]{2,1,0:T(8,128)S(1)}, f32[14,128,128]{2,1,0:T(8,128)S(1)}, u32[]{:S(2)}, u32[]{:S(2)}) collective-permute-start(f32[14,128,128]{2,1,0:T(8,128)S(1)} %get-tuple-element.65.refs_9_), channel_id=1, source_target_pairs={{0,16},{16,0},{32,48},{48,32},{64,80},{80,64},{96,112},{112,96},{1... | collective-permute-start | bytes 2752520 | tf_op jit(solution)/shard_map/ppermute | solution.py:618
  36.6 9.3 %collective-permute-start.10 = (f32[448,128]{1,0:T(8,128)S(1)}, f32[448,128]{1,0:T(8,128)S(1)}, u32[]{:S(2)}, u32[]{:S(2)}) collective-permute-start(f32[448,128]{1,0:T(8,128)S(1)} %get-tuple-element.76), channel_id=1, source_target_pairs={{0,64},{1,65},{2,66},{3,67},{4,68},{5,69},{6,70},{7,71},{8,72},{9,... | collective-permute-start | bytes 688136 | tf_op jit(solution)/shard_map/ppermute | solution.py:498
  38.3 7.6 %collective-permute-start.11 = (f32[448,128]{1,0:T(8,128)S(1)}, f32[448,128]{1,0:T(8,128)S(1)}, u32[]{:S(2)}, u32[]{:S(2)}) collective-permute-start(f32[448,128]{1,0:T(8,128)S(1)} %get-tuple-element.77), channel_id=1, source_target_pairs={{0,96},{1,97},{2,98},{3,99},{4,100},{5,101},{6,102},{7,103},{8,104... | collective-permute-start | bytes 688136 | tf_op jit(solution)/shard_map/ppermute | solution.py:498
  39.8 6.7 %collective-permute-start.9 = (f32[448,128]{1,0:T(8,128)S(1)}, f32[448,128]{1,0:T(8,128)S(1)}, u32[]{:S(2)}, u32[]{:S(2)}) collective-permute-start(f32[448,128]{1,0:T(8,128)S(1)} %get-tuple-element.70.refs_11_), channel_id=1, source_target_pairs={{0,32},{1,33},{2,34},{3,35},{4,36},{5,37},{6,38},{7,39},{8,40},{9,... | collective-permute-start | bytes 688136 | tf_op jit(solution)/shard_map/ppermute | solution.py:498
  46.5 8.9 %collective-permute-start.14 = (f32[448,128]{1,0:T(8,128)S(1)}, f32[448,128]{1,0:T(8,128)S(1)}, u32[]{:S(2)}, u32[]{:S(2)}) collective-permute-start(f32[448,128]{1,0:T(8,128)S(1)} %shard_map.80.refs_12_.refs_0_), channel_id=1, source_target_pairs={{0,12},{1,13},{2,14},{3,15},{4,8},{5,9},{6,10},{7,11},{8,4},{9,5},... | collective-permute-start | bytes 688136 | tf_op jit(solution)/shard_map/ppermute | solution.py:498
  49.5 6.7 %collective-permute-start.13 = (f32[448,128]{1,0:T(8,128)S(1)}, f32[448,128]{1,0:T(8,128)S(1)}, u32[]{:S(2)}, u32[]{:S(2)}) collective-permute-start(f32[448,128]{1,0:T(8,128)S(1)} %shard_map.80.refs_12_.refs_0_), channel_id=1, source_target_pairs={{0,8},{1,9},{2,10},{3,11},{4,12},{5,13},{6,14},{7,15},{8,0},{9,1},... | collective-permute-start | bytes 688136 | tf_op jit(solution)/shard_map/ppermute | solution.py:498
  49.8 6.5 %collective-permute-start.12 = (f32[448,128]{1,0:T(8,128)S(1)}, f32[448,128]{1,0:T(8,128)S(1)}, u32[]{:S(2)}, u32[]{:S(2)}) collective-permute-start(f32[448,128]{1,0:T(8,128)S(1)} %shard_map.80.refs_12_.refs_0_), channel_id=1, source_target_pairs={{0,4},{1,5},{2,6},{3,7},{4,0},{5,1},{6,2},{7,3},{8,12},{9,13},{10,... | collective-permute-start | bytes 688136 | tf_op jit(solution)/shard_map/ppermute | solution.py:498
  56.4 9.3 %collective-permute-start.17 = (f32[448,128]{1,0:T(8,128)S(1)}, f32[448,128]{1,0:T(8,128)S(1)}, u32[]{:S(2)}, u32[]{:S(2)}) collective-permute-start(f32[448,128]{1,0:T(8,128)S(1)} %shard_map.82.refs_10_.refs_0_), channel_id=1, source_target_pairs={{0,3},{1,2},{2,1},{3,0},{4,7},{5,6},{6,5},{7,4},{8,11},{9,10},{10,... | collective-permute-start | bytes 688136 | tf_op jit(solution)/shard_map/ppermute | solution.py:498
  59.0 6.7 %collective-permute-start.16 = (f32[448,128]{1,0:T(8,128)S(1)}, f32[448,128]{1,0:T(8,128)S(1)}, u32[]{:S(2)}, u32[]{:S(2)}) collective-permute-start(f32[448,128]{1,0:T(8,128)S(1)} %shard_map.82.refs_10_.refs_0_), channel_id=1, source_target_pairs={{0,2},{1,3},{2,0},{3,1},{4,6},{5,7},{6,4},{7,5},{8,10},{9,11},{10,... | collective-permute-start | bytes 688136 | tf_op jit(solution)/shard_map/ppermute | solution.py:498
  59.3 6.5 %collective-permute-start.15 = (f32[448,128]{1,0:T(8,128)S(1)}, f32[448,128]{1,0:T(8,128)S(1)}, u32[]{:S(2)}, u32[]{:S(2)}) collective-permute-start(f32[448,128]{1,0:T(8,128)S(1)} %shard_map.82.refs_10_.refs_0_), channel_id=1, source_target_pairs={{0,1},{1,0},{2,3},{3,2},{4,5},{5,4},{6,7},{7,6},{8,9},{9,8},{10,11... | collective-permute-start | bytes 688136 | tf_op jit(solution)/shard_map/ppermute | solution.py:498
  65.8 13.4 %collective-permute-start.21 = (f32[448,128]{1,0:T(8,128)S(1)}, f32[448,128]{1,0:T(8,128)S(1)}, u32[]{:S(2)}, u32[]{:S(2)}) collective-permute-start(f32[448,128]{1,0:T(8,128)S(1)} %shard_map.84.refs_12_.refs_0_), channel_id=1, source_target_pairs={{0,16},{16,0},{32,48},{48,32},{64,80},{80,64},{96,112},{112,96},{1... | collective-permute-start | bytes 688136 | tf_op jit(solution)/shard_map/ppermute | solution.py:630
  69.2 9.9 %collective-permute-start.20 = (f32[448,128]{1,0:T(8,128)S(1)}, f32[448,128]{1,0:T(8,128)S(1)}, u32[]{:S(2)}, u32[]{:S(2)}) collective-permute-start(f32[448,128]{1,0:T(8,128)S(1)} %shard_map.84.refs_12_.refs_0_), channel_id=1, source_target_pairs={{0,96},{1,97},{2,98},{3,99},{4,100},{5,101},{6,102},{7,103},{8,104... | collective-permute-start | bytes 688136 | tf_op jit(solution)/shard_map/ppermute | solution.py:498
  72.0 7.2 %collective-permute-start.19 = (f32[448,128]{1,0:T(8,128)S(1)}, f32[448,128]{1,0:T(8,128)S(1)}, u32[]{:S(2)}, u32[]{:S(2)}) collective-permute-start(f32[448,128]{1,0:T(8,128)S(1)} %shard_map.84.refs_12_.refs_0_), channel_id=1, source_target_pairs={{0,64},{1,65},{2,66},{3,67},{4,68},{5,69},{6,70},{7,71},{8,72},{9,... | collective-permute-start | bytes 688136 | tf_op jit(solution)/shard_map/ppermute | solution.py:498
  72.0 7.2 %collective-permute-start.18 = (f32[448,128]{1,0:T(8,128)S(1)}, f32[448,128]{1,0:T(8,128)S(1)}, u32[]{:S(2)}, u32[]{:S(2)}) collective-permute-start(f32[448,128]{1,0:T(8,128)S(1)} %shard_map.84.refs_12_.refs_0_), channel_id=1, source_target_pairs={{0,32},{1,33},{2,34},{3,35},{4,36},{5,37},{6,38},{7,39},{8,40},{9,... | collective-permute-start | bytes 688136 | tf_op jit(solution)/shard_map/ppermute | solution.py:498
  79.3 2.7 %collective-permute-start.22 = (f32[1344,128]{1,0:T(8,128)S(1)}, f32[1344,128]{1,0:T(8,128)S(1)}, u32[]{:S(2)}, u32[]{:S(2)}) collective-permute-start(f32[1344,128]{1,0:T(8,128)S(1)} %shard_map.86.refs_1_.refs_2_), channel_id=1, source_target_pairs={{0,16},{16,0},{32,48},{48,32},{64,80},{80,64},{96,112},{112,96},{1... | collective-permute-start | bytes 2064392 | tf_op jit(solution)/shard_map/ppermute | solution.py:633

commit v6 on v5

--- a/solution.py
+++ b/solution.py
@@ -15,7 +15,7 @@
 SPAN = 8
 TAPS = 9 * C
 WIDE = 3 * C
-HALF = 14
+HALF = 27 * C // 2
 F32 = jnp.float32
 BF16 = jnp.bfloat16
 VMEM = pl.BlockSpec(memory_space=pltpu.VMEM)
@@ -151,7 +151,7 @@
     put_slab(scratch, slot, slab[:Y], slab[Y], slab[Y + 1], rims[:24], rims[24:])
 
 
-def own_grad_kernel(first, more, x_ref, g_ref, *refs):
+def own_grad_kernel(first, spans, more, x_ref, g_ref, *refs):
     total, even, odd = refs[-3:]
     for shifted in (even, odd):
         shifted[:, :, 0:1] = jnp.zeros((3, SPAN, 1, Z, C), BF16)
@@ -168,21 +168,23 @@
 
     put(even, first)
     made = product(even, first)
-    put(odd, first + SPAN)
+    if spans == 2:
+        put(odd, first + SPAN)
     total[...] = refs[0][...] + made if more else made
-    total[...] += product(odd, first + SPAN)
-
-
-def own_grad(slabs, first, before, tie):
+    if spans == 2:
+        total[...] += product(odd, first + SPAN)
+
+
+def own_grad(slabs, first, spans, before, tie):
     more = before is not None
     return pl.pallas_call(
-        lambda *refs: own_grad_kernel(first, more, *refs),
+        lambda *refs: own_grad_kernel(first, spans, more, *refs),
         in_specs=[VMEM] * (2 + more) + [ANY],
         out_specs=VMEM,
         out_shape=shape((WIDE, TAPS), F32),
         scratch_shapes=[pltpu.VMEM((3, SPAN, Y + 2, Z, C), BF16)] * 2,
         compiler_params=params(),
-        cost_estimate=cost(2 * SPAN, 8 << 20),
+        cost_estimate=cost(spans * SPAN, 8 << 20),
     )(*slabs, *([before] if more else []), tie)
 
 
@@ -236,10 +238,12 @@
         def _():
             for tap in range(27):
                 tx, row = tap // 9, tap % 9
-                ref = keep_ref if tap // HALF == mine else send_ref
-                ref[tap % HALF] = total[tx * C : (tx + 1) * C, row * C : (row + 1) * C].T * scale
-            ref = keep_ref if mine == 1 else send_ref
-            ref[HALF - 1] = jnp.zeros((C, C), F32)
+                block = total[tx * C : (tx + 1) * C, row * C : (row + 1) * C].T * scale
+                for side, ref in ((mine, keep_ref), (1 - mine, send_ref)):
+                    start = tap * C - side * HALF
+                    low, high = max(start, 0), min(start + C, HALF)
+                    if low < high:
+                        ref[low:high] = block[low - start : high - start]
 
 
 def rim_grad(own, cotangents, operands):
@@ -247,7 +251,7 @@
         rim_grad_kernel,
         in_specs=[VMEM] * (2 + len(operands)),
         out_specs=[VMEM, VMEM],
-        out_shape=[shape((HALF, C, C), F32)] * 2,
+        out_shape=[shape((HALF, C), F32)] * 2,
         scratch_shapes=[pltpu.VMEM((3, 2, Y + 2, Z, C), BF16), pltpu.VMEM((WIDE, TAPS), F32)],
         compiler_params=params(),
         cost_estimate=cost(3, 6 << 20),
@@ -442,6 +446,11 @@
     )(*operands, *ties)
 
 
+def copy_kernel(a, b, c, d):
+    c[...] = a[...]
+    d[...] = b[...]
+
+
 def edge_kernel(zlo, zhi, lo, hi):
     for side, ref in enumerate((zlo, zhi)):
         lo[:, side] = held(ref[:, :, 0, :], "gz", side)
@@ -519,8 +528,7 @@
 
 def write(sources, mine, target, tie):
     arrays = [a for a, _ in sources]
-    rows = HALF * C // 4
-    short = 27 * C - 2 * HALF * C + rows
+    rows = HALF // 4
     count = sum(len(steps) for _, steps in sources)
 
     def kernel(*refs):
@@ -534,13 +542,12 @@
                 for at, step in enumerate(steps):
                     chunk = half * 4 + (me ^ step)
 
-                    def move(size, ref=ref, at=at, chunk=chunk, sem=sem):
-                        target = o_ref.at[pl.ds(chunk * rows, size)]
-                        copy = pltpu.make_async_copy(ref.at[pl.ds(at * rows, size)], target, left.at[sem])
-                        getattr(copy, act)()
-
-                    pl.when(chunk < 7)(lambda move=move: move(rows))
-                    pl.when(chunk == 7)(lambda move=move: move(short))
+                    place = o_ref.at[pl.ds(chunk * rows, rows)]
+                    copy = pltpu.make_async_copy(ref.at[pl.ds(at * rows, rows)], place, left.at[sem])
+                    if act == "start":
+                        copy.start()
+                    else:
+                        copy.wait()
                     sem += 1
 
     operands = arrays + [tie] + ([] if target is None else [target])
@@ -572,9 +579,12 @@
     zlo, zhi, ylo, yhi = faces
     near_zlo = shift(zhi, "gz", 1)
     near_zhi = shift(zlo, "gz", -1)
-    near_ylo = shift(yhi, "gy", 1)
-    near_yhi = shift(ylo, "gy", -1)
-    own = own_grad(slabs, 0, None, zlo)
+    own = own_grad(slabs, 0, 1, None, zlo)
+    face = shape((2, X, Z, C), BF16)
+    to_ylo, to_yhi = small_kernel(copy_kernel, [face, face], [ylo, yhi], [own])
+    near_ylo = shift(to_yhi, "gy", 1)
+    near_yhi = shift(to_ylo, "gy", -1)
+    own = own_grad(slabs, SPAN, 1, own, to_ylo)
 
     edge = shape((2, 2, X, C), BF16)
     edge_lo, edge_hi = small_kernel(edge_kernel, [edge, edge], [near_zlo, near_zhi], [own])
@@ -586,7 +596,6 @@
         z_rim_kernel, shape((WIDE, TAPS), F32), [own, zlo, zhi, near_zlo, near_zhi], [edge_lo]
     )
 
-    face = shape((2, X, Z, C), BF16)
     column = shape((2, X, 24, C), BF16)
     message = shape((2, Y + 5, Z, C), BF16)
     held_ylo, held_yhi, col_lo, col_hi, to_lo, to_hi = small_kernel(
@@ -596,7 +605,7 @@
         [forward, own],
     )
     far = (shift(to_hi, "gx", 1), shift(to_lo, "gx", -1))
-    own = own_grad(slabs, X // 2, own, to_lo)
+    own = own_grad(slabs, X // 2, 2, own, to_lo)
     keep, send = rim_grad(own, slabs[1], [ylo, yhi, held_ylo, held_yhi, *edges, *far])
 
     field = [*slabs, held_ylo, held_yhi, col_lo, col_hi]
@@ -617,8 +626,7 @@
     swap = [(i, i ^ 1) for i in range(8)]
     came = lax.ppermute(send, "gx", swap)
     ties = convolve(send)
-    flat = (HALF * C, C)
-    own, *parts = deal([keep.reshape(flat), came.reshape(flat)], ties)
+    own, *parts = deal([keep, came], ties)
     came = exchange(0, parts)
     chunk, ties = own, convolve(parts[0])
     for turn in (1, 2):

time: 83.2 us -> 82.2 us (0.988)
  waiting for transfers between devices: 3.26 us -> 2.16 us
    pallas_call x2 -> x3, Pallas kernels: 8.77 us -> 9.17 us  [own_grad(): pl.pallas_call(lambda *refs: own_grad_kernel(first, spans, more, *refs),...]
    pallas_call x10 -> x11, Pallas kernels: 2.61 us -> 2.68 us  [small_kernel(): pl.pallas_call(run, in_specs=(specs or [VMEM] * count) + [ANY] * len(ties...]
  transfers between devices with their start and end apart: 23 -> 23, of which waited for: 8 -> 6; matrix products, arithmetic and copies ran while one was open for 0% -> 0% of each run, Pallas kernels for 45% -> 46%
where the time goes in v6:
time: 82.2 us; the launch traced here: 82 us
  Pallas kernels  43.4 us (53%)
  starting transfers between devices  32.4 us (39%)
  local copies, waits for them, and re-layouts  2.94 us (4%)
  waiting for transfers between devices  2.16 us (3%)
  between operations  1.13 us (1%)
    pallas_call x5, Pallas kernels, conv_piece(): pl.pallas_call(plain if more else final, in_specs=specs, out_specs=[ANY]...  25.8 us
    ppermute x12, starting transfers between devices, exchange(): lax.ppermute(value, ('gx', 'gy', 'gz'), pairs(turn, step))  13.8 us
    ppermute x8, starting transfers between devices, shift(): lax.ppermute(value, axis, [(i, (i + step) % count) for i in range(count)])  13.1 us
    pallas_call x3, Pallas kernels, own_grad(): pl.pallas_call(lambda *refs: own_grad_kernel(first, spans, more, *refs),...  9.17 us
    ppermute x1, starting transfers between devices, body(): beside = lax.ppermute(chunk, 'gx', swap)  3.43 us
    unnamed x8, local copies, waits for them, and re-layouts  2.94 us
    pallas_call x11, Pallas kernels, small_kernel(): pl.pallas_call(run, in_specs=(specs or [VMEM] * count) + [ANY] * len(ties...  2.68 us
    pallas_call x3, Pallas kernels, write(): pl.pallas_call(kernel, in_specs=[VMEM] * len(arrays) + [ANY] * (len(opera...  2.51 us
  transfers between devices with their start and end apart: 23, of which 6 were waited for; matrix products, arithmetic and copies ran while one was open for 0% of the time, Pallas kernels for 46%

profile of v6, /device:TPU:1, one launch (start us, length us, event | category | flops | bytes accessed | tf_op | source)
XLA Modules:
  0.0 82.0 jit_solution(4053635454605312222)
XLA Ops:
  1.9 1.6 %copy-done = bf16[32,16,16,128]{3,2,1,0:T(8,128)(2,1)S(1)} copy-done((bf16[32,16,16,128]{3,2,1,0:T(8,128)(2,1)S(1)}, bf16[32,16,16,128]{3,2,1,0:T(8,128)(2,1)}, u32[]{:S(2)}) %copy-start) | copy-done | bytes 2097176
  3.5 0.9 %shard_map.68 = (bf16[34,16,16,128]{3,2,1,0:T(8,128)(2,1)S(1)}, bf16[1,32,16,128]{3,2,1,0:T(8,128)(2,1)S(1)}, bf16[1,32,16,128]{3,2,1,0:T(8,128)(2,1)S(1)}, bf16...) custom-call(bf16[32,16,16,128]{3,2,1,0:T(8,128)(2,1)S(1)} %copy-done, ...), custom_call_target="tpu_custom_call" | custom-call | flops 1000000 | bytes 5242880 | tf_op jit(solution)/shard_map/pallas_call | solution.py:96
  4.4 0.7 copy-done.1
  5.1 0.9 %shard_map.69 = (bf16[34,16,16,128]{3,2,1,0:T(8,128)(2,1)S(1)}, bf16[2,32,16,128]{3,2,1,0:T(8,128)(2,1)S(1)}, bf16[2,32,16,128]{3,2,1,0:T(8,128)(2,1)S(1)}, bf16...) custom-call(bf16[32,16,16,128]{3,2,1,0:T(8,128)(2,1)S(1)} %copy-done.1, ...), custom_call_target="tpu_custom_call" | custom-call | flops 1000000 | bytes 5242880 | tf_op jit(solution)/shard_map/pallas_call | solution.py:104
  6.0 2.1 %collective-permute-start.2 = (bf16[2,32,16,128]{3,2,1,0:T(8,128)(2,1)S(1)}, bf16[2,32,16,128]{3,2,1,0:T(8,128)(2,1)S(1)}, u32[]{:S(2)}, u32[]{:S(2)}) collective-permute-start(bf16[2,32,16,128]{3,2,1,0:T(8,128)(2,1)S(1)} %get-tuple-element.59.refs_2_), channel_id=1, source_target_pairs={{0,1},{1,2},{2,3},{3,0},{4,5},{5,6},{6,7},{7,4},{8,9},{9,10},{10,1... | collective-permute-start | bytes 786440 | tf_op jit(solution)/shard_map/ppermute | solution.py:574
  8.2 1.3 %collective-permute-start.3 = (bf16[2,32,16,128]{3,2,1,0:T(8,128)(2,1)S(1)}, bf16[2,32,16,128]{3,2,1,0:T(8,128)(2,1)S(1)}, u32[]{:S(2)}, u32[]{:S(2)}) collective-permute-start(bf16[2,32,16,128]{3,2,1,0:T(8,128)(2,1)S(1)} %get-tuple-element.56.refs_2_.refs_1_), channel_id=1, source_target_pairs={{0,3},{1,0},{2,1},{3,2},{4,7},{5,4},{6,5},{7,6},{8,11},{9,8},{10,9... | collective-permute-start | bytes 786440 | tf_op jit(solution)/shard_map/ppermute | solution.py:574
  9.5 2.4 %shard_map.70.refs_2_ = f32[384,1152]{1,0:T(8,128)S(1)} custom-call(bf16[34,16,16,128]{3,2,1,0:T(8,128)(2,1)S(1)} %get-tuple-element.48.refs_0_.refs_1_, bf16[34,16,16,128]{3,2,1,0:T(8,128)(2,1)S(1)} %get-tuple-element.53.refs_1_.g_ref.refs_2_, bf16[2,32,16,128]{3,2,1,0:T(8,128)(2,1)S(1)} %get-tuple-element.56.refs_2_.refs_1_), custom_call_target="tpu_custom_call" | custom-call | flops 1811939328 | bytes 8388608 | tf_op jit(solution)/shard_map/pallas_call | solution.py:180
  12.0 1.5 %collective-permute-start = (bf16[2,32,16,128]{3,2,1,0:T(8,128)(2,1)S(1)}, bf16[2,32,16,128]{3,2,1,0:T(8,128)(2,1)S(1)}, u32[]{:S(2)}, u32[]{:S(2)}) collective-permute-start(bf16[2,32,16,128]{3,2,1,0:T(8,128)(2,1)S(1)} %get-tuple-element.57), channel_id=1, source_target_pairs={{0,4},{4,8},{8,12},{12,0},{1,5},{5,9},{9,13},{13,1},{2,6},{6,10},{... | collective-permute-start | bytes 786440 | tf_op jit(solution)/shard_map/ppermute | solution.py:574
  13.5 1.5 %collective-permute-start.1 = (bf16[2,32,16,128]{3,2,1,0:T(8,128)(2,1)S(1)}, bf16[2,32,16,128]{3,2,1,0:T(8,128)(2,1)S(1)}, u32[]{:S(2)}, u32[]{:S(2)}) collective-permute-start(bf16[2,32,16,128]{3,2,1,0:T(8,128)(2,1)S(1)} %get-tuple-element.58.refs_3_), channel_id=1, source_target_pairs={{0,12},{4,0},{8,4},{12,8},{1,13},{5,1},{9,5},{13,9},{2,14},{6,2},{... | collective-permute-start | bytes 786440 | tf_op jit(solution)/shard_map/ppermute | solution.py:574
  15.0 2.3 %shard_map.72.refs_2_.refs_0_ = f32[384,1152]{1,0:T(8,128)S(1)} custom-call(bf16[34,16,16,128]{3,2,1,0:T(8,128)(2,1)S(1)} %get-tuple-element.48.refs_0_.refs_1_, bf16[34,16,16,128]{3,2,1,0:T(8,128)(2,1)S(1)} %get-tuple-element.53.refs_1_.g_ref.refs_2_, f32[384,1152]{1,0:T(8,128)S(1)} %shard_map.70.refs_2_, bf16[2,32,16,128]{3,2,1,0:T(8,128)(2,1)S(1)} %get-tuple-element.58.refs_3_), custom_call_target="tpu_custom_call" | custom-call | flops 1811939328 | bytes 8388608 | tf_op jit(solution)/shard_map/pallas_call | solution.py:180
  17.6 2.7 %collective-permute-start.5 = (bf16[2,2,32,128]{3,2,1,0:T(8,128)(2,1)S(1)}, bf16[2,2,32,128]{3,2,1,0:T(8,128)(2,1)S(1)}, u32[]{:S(2)}, u32[]{:S(2)}) collective-permute-start(bf16[2,2,32,128]{3,2,1,0:T(8,128)(2,1)S(1)} %get-tuple-element.61.refs_1_.refs_5_), channel_id=1, source_target_pairs={{0,12},{4,0},{8,4},{12,8},{1,13},{5,1},{9,5},{13,9},{2,14},{6,2},{... | collective-permute-start | bytes 98312 | tf_op jit(solution)/shard_map/ppermute | solution.py:574
  21.3 0.7 collective-permute-done.4.refs_6_.elo
  22.6 3.9 %collective-permute-start.7 = (bf16[2,21,16,128]{3,2,1,0:T(8,128)(2,1)S(1)}, bf16[2,21,16,128]{3,2,1,0:T(8,128)(2,1)S(1)}, u32[]{:S(2)}, u32[]{:S(2)}) collective-permute-start(bf16[2,21,16,128]{3,2,1,0:T(8,128)(2,1)S(1)} %get-tuple-element.68), channel_id=1, source_target_pairs={{0,16},{16,32},{32,48},{48,64},{64,80},{80,96},{96,112},{112,0},{1... | collective-permute-start | bytes 516104 | tf_op jit(solution)/shard_map/ppermute | solution.py:574
  26.5 4.4 %shard_map.77.own_ref = f32[384,1152]{1,0:T(8,128)S(1)} custom-call(bf16[34,16,16,128]{3,2,1,0:T(8,128)(2,1)S(1)} %get-tuple-element.48.refs_0_.refs_1_, bf16[34,16,16,128]{3,2,1,0:T(8,128)(2,1)S(1)} %get-tuple-element.53.refs_1_.g_ref.refs_2_, f32[384,1152]{1,0:T(8,128)S(1)} %shard_map.75.refs_9_.refs_2_, bf16[2,21,16,128]{3,2,1,0:T(8,128)(2,1)S(1)} %get-tuple-element.67.refs_3_), custom_call_target="tpu_custom_call" | custom-call | flops 3623878656 | bytes 8388608 | tf_op jit(solution)/shard_map/pallas_call | solution.py:180
  31.3 1.4 %shard_map.78 = (f32[1728,128]{1,0:T(8,128)S(1)}, f32[1728,128]{1,0:T(8,128)S(1)}) custom-call(f32[384,1152]{1,0:T(8,128)S(1)} %shard_map.77.own_ref, bf16[34,16,16,128]{3,2,1,0:T(8,128)(2,1)S(1)} %get-tuple-element.53.refs_1_.g_ref.refs_2_, bf16[2,32,16,128]{3,2,1,0:T(8,128)(2,1)S(1)} %get-tuple-element.54.refs_0_.gylo, ...), custom_call_target="tpu_custom_call" | custom-call | flops 679477248 | bytes 6291456 | tf_op jit(solution)/shard_map/pallas_call | solution.py:250
  32.7 1.1 %collective-permute-start.8 = (f32[1728,128]{1,0:T(8,128)S(1)}, f32[1728,128]{1,0:T(8,128)S(1)}, u32[]{:S(2)}, u32[]{:S(2)}) collective-permute-start(f32[1728,128]{1,0:T(8,128)S(1)} %get-tuple-element.69.refs_9_), channel_id=1, source_target_pairs={{0,16},{16,0},{32,48},{48,32},{64,80},{80,64},{96,112},{112,96},{1... | collective-permute-start | bytes 2654216 | tf_op jit(solution)/shard_map/ppermute | solution.py:627
  33.7 2.0 %shard_map.79 = (bf16[32,16,16,128]{3,2,1,0:T(8,128)(2,1)}, f32[2,256,128]{2,1,0:T(8,128)S(1)}, bf16[3,4,18,16,128]{4,3,2,1,0:T(8,128)(2,1)S(1)}, bf16[4,16,16,128]{3,2,1,0:T(8,128)(2,1)S(1)}) custom-call(bf16[4,16,16,128]{3,2,1,0:T(8,128)(2,1)S(1)} %shard_map.67.mask_ref.refs_0_, bf16[34,16,16,128]{3,2,1,0:T(8,128)(2,1)S(1)} %get-tuple-element.48.refs_0_.refs_1_, ...), custom_call_target="tpu_custom_call" | custom-call | flops 905969664 | bytes 2097152 | tf_op jit(solution)/shard_map/pallas_call | solution.py:420
  35.9 1.9 %collective-permute-start.10 = (f32[432,128]{1,0:T(8,128)S(1)}, f32[432,128]{1,0:T(8,128)S(1)}, u32[]{:S(2)}, u32[]{:S(2)}) collective-permute-start(f32[432,128]{1,0:T(8,128)S(1)} %get-tuple-element.80), channel_id=1, source_target_pairs={{0,64},{1,65},{2,66},{3,67},{4,68},{5,69},{6,70},{7,71},{8,72},{9,... | collective-permute-start | bytes 663560 | tf_op jit(solution)/shard_map/ppermute | solution.py:507
  37.8 1.2 %collective-permute-start.11 = (f32[432,128]{1,0:T(8,128)S(1)}, f32[432,128]{1,0:T(8,128)S(1)}, u32[]{:S(2)}, u32[]{:S(2)}) collective-permute-start(f32[432,128]{1,0:T(8,128)S(1)} %get-tuple-element.81), channel_id=1, source_target_pairs={{0,96},{1,97},{2,98},{3,99},{4,100},{5,101},{6,102},{7,103},{8,104... | collective-permute-start | bytes 663560 | tf_op jit(solution)/shard_map/ppermute | solution.py:507
  39.5 5.8 %shard_map.81 = (bf16[32,16,16,128]{3,2,1,0:T(8,128)(2,1)}, f32[2,256,128]{2,1,0:T(8,128)S(1)}, bf16[3,4,18,16,128]{4,3,2,1,0:T(8,128)(2,1)S(1)}, bf16[4,16,16,128]{3,2,1,0:T(8,128)(2,1)S(1)}) custom-call(bf16[4,16,16,128]{3,2,1,0:T(8,128)(2,1)S(1)} %shard_map.67.mask_ref.refs_0_, ...), custom_call_target="tpu_custom_call", output_to_operand_aliasing={{0}: (12, {})} | custom-call | flops 3623878656 | bytes 2097152 | tf_op jit(solution)/shard_map/pallas_call | solution.py:420
  45.6 1.6 %collective-permute-start.14 = (f32[432,128]{1,0:T(8,128)S(1)}, f32[432,128]{1,0:T(8,128)S(1)}, u32[]{:S(2)}, u32[]{:S(2)}) collective-permute-start(f32[432,128]{1,0:T(8,128)S(1)} %shard_map.82.refs_12_.refs_0_), channel_id=1, source_target_pairs={{0,12},{1,13},{2,14},{3,15},{4,8},{5,9},{6,10},{7,11},{8,4},{9,5},... | collective-permute-start | bytes 663560 | tf_op jit(solution)/shard_map/ppermute | solution.py:507
  47.7 1.4 %collective-permute-start.12 = (f32[432,128]{1,0:T(8,128)S(1)}, f32[432,128]{1,0:T(8,128)S(1)}, u32[]{:S(2)}, u32[]{:S(2)}) collective-permute-start(f32[432,128]{1,0:T(8,128)S(1)} %shard_map.82.refs_12_.refs_0_), channel_id=1, source_target_pairs={{0,4},{1,5},{2,6},{3,7},{4,0},{5,1},{6,2},{7,3},{8,12},{9,13},{10,... | collective-permute-start | bytes 663560 | tf_op jit(solution)/shard_map/ppermute | solution.py:507
  49.1 5.3 %shard_map.83 = (bf16[32,16,16,128]{3,2,1,0:T(8,128)(2,1)}, f32[2,256,128]{2,1,0:T(8,128)S(1)}, bf16[3,4,18,16,128]{4,3,2,1,0:T(8,128)(2,1)S(1)}) custom-call(bf16[4,16,16,128]{3,2,1,0:T(8,128)(2,1)S(1)} %shard_map.67.mask_ref.refs_0_, bf16[34,16,16,128]{3,2,1,0:T(8,128)(2,1)S(1)} %get-tuple-element.48.refs_0_.refs_1_, ...), custom_call_target="tpu_custom_call", output_to_operand_aliasing={{0}: (13, {})} | custom-call | flops 2717908992 | bytes 2097152 | tf_op jit(solution)/shard_map/pallas_call | solution.py:420
  55.2 2.7 %collective-permute-start.17 = (f32[432,128]{1,0:T(8,128)S(1)}, f32[432,128]{1,0:T(8,128)S(1)}, u32[]{:S(2)}, u32[]{:S(2)}) collective-permute-start(f32[432,128]{1,0:T(8,128)S(1)} %shard_map.84.refs_10_.refs_0_), channel_id=1, source_target_pairs={{0,3},{1,2},{2,1},{3,0},{4,7},{5,6},{6,5},{7,4},{8,11},{9,10},{10,... | collective-permute-start | bytes 663560 | tf_op jit(solution)/shard_map/ppermute | solution.py:507
  58.6 6.0 %shard_map.85 = (bf16[32,16,16,128]{3,2,1,0:T(8,128)(2,1)}, f32[2,256,128]{2,1,0:T(8,128)S(1)}, bf16[3,4,18,16,128]{4,3,2,1,0:T(8,128)(2,1)S(1)}, bf16[4,16,16,128]{3,2,1,0:T(8,128)(2,1)S(1)}) custom-call(bf16[4,16,16,128]{3,2,1,0:T(8,128)(2,1)S(1)} %shard_map.67.mask_ref.refs_0_, bf16[34,16,16,128]{3,2,1,0:T(8,128)(2,1)S(1)} %get-tuple-element.48.refs_0_.refs_1_, ...), custom_call_target="tpu_custom_call" | custom-call | flops 3623878656 | bytes 2097152 | tf_op jit(solution)/shard_map/pallas_call | solution.py:420
  64.7 3.4 %collective-permute-start.21 = (f32[432,128]{1,0:T(8,128)S(1)}, f32[432,128]{1,0:T(8,128)S(1)}, u32[]{:S(2)}, u32[]{:S(2)}) collective-permute-start(f32[432,128]{1,0:T(8,128)S(1)} %shard_map.86.refs_12_.refs_0_), channel_id=1, source_target_pairs={{0,16},{16,0},{32,48},{48,32},{64,80},{80,64},{96,112},{112,96},{1... | collective-permute-start | bytes 663560 | tf_op jit(solution)/shard_map/ppermute | solution.py:638
  68.1 2.6 %collective-permute-start.20 = (f32[432,128]{1,0:T(8,128)S(1)}, f32[432,128]{1,0:T(8,128)S(1)}, u32[]{:S(2)}, u32[]{:S(2)}) collective-permute-start(f32[432,128]{1,0:T(8,128)S(1)} %shard_map.86.refs_12_.refs_0_), channel_id=1, source_target_pairs={{0,96},{1,97},{2,98},{3,99},{4,100},{5,101},{6,102},{7,103},{8,104... | collective-permute-start | bytes 663560 | tf_op jit(solution)/shard_map/ppermute | solution.py:507
  71.4 6.7 %shard_map.87 = (bf16[32,16,16,128]{3,2,1,0:T(8,128)(2,1)}, f32[8,128]{1,0:T(8,128)S(1)}) custom-call(bf16[4,16,16,128]{3,2,1,0:T(8,128)(2,1)S(1)} %shard_map.67.mask_ref.refs_0_, bf16[34,16,16,128]{3,2,1,0:T(8,128)(2,1)S(1)} %get-tuple-element.48.refs_0_.refs_1_, ...), custom_call_target="tpu_custom_call", output_to_operand_aliasing={{0}: (13, {})} | custom-call | flops 3623878656 | bytes 2097152 | tf_op jit(solution)/shard_map/pallas_call | solution.py:420
  78.2 1.0 %collective-permute-start.22 = (f32[1296,128]{1,0:T(8,128)S(1)}, f32[1296,128]{1,0:T(8,128)S(1)}, u32[]{:S(2)}, u32[]{:S(2)}) collective-permute-start(f32[1296,128]{1,0:T(8,128)S(1)} %shard_map.88.refs_1_.refs_2_), channel_id=1, source_target_pairs={{0,16},{16,0},{32,48},{48,32},{64,80},{80,64},{96,112},{112,96},{1... | collective-permute-start | bytes 1990664 | tf_op jit(solution)/shard_map/ppermute | solution.py:641
  79.2 0.9 %shard_map.89.refs_2_ = f32[3456,128]{1,0:T(8,128)} custom-call(f32[432,128]{1,0:T(8,128)S(1)} %shard_map.86.refs_12_.refs_0_, f32[1296,128]{1,0:T(8,128)S(1)} %shard_map.88.refs_1_.refs_2_, f32[1296,128]{1,0:T(8,128)S(1)} %shard_map.88.refs_1_.refs_2_), custom_call_target="tpu_custom_call" | custom-call | flops 1000 | bytes 1048576 | tf_op jit(solution)/shard_map/pallas_call | solution.py:554
  80.1 0.7 shard_map.90.refs_2_
  80.9 0.9 %shard_map.91 = f32[3456,128]{1,0:T(8,128)} custom-call(f32[1296,128]{1,0:T(8,128)S(1)} %collective-permute-done.22.refs_0_, f32[1296,128]{1,0:T(8,128)S(1)} %shard_map.88.refs_1_.refs_2_, f32[3456,128]{1,0:T(8,128)} %shard_map.90.refs_2_), custom_call_target="tpu_custom_call", output_to_operand_aliasing={{}: (2, {})} | custom-call | flops 1000 | bytes 1048576 | tf_op jit(solution)/shard_map/pallas_call | solution.py:554
  (47 shorter events, 7.2 us)
Async XLA Ops:
  0.6 0.7 copy-start.3
  1.9 1.6 %copy-start = (bf16[32,16,16,128]{3,2,1,0:T(8,128)(2,1)S(1)}, bf16[32,16,16,128]{3,2,1,0:T(8,128)(2,1)}, u32[]{:S(2)}) copy-start(bf16[32,16,16,128]{3,2,1,0:T(8,128)(2,1)} %f_ref.1) | copy-start | bytes 6291460
  3.5 1.6 %copy-start.1 = (bf16[32,16,16,128]{3,2,1,0:T(8,128)(2,1)S(1)}, bf16[32,16,16,128]{3,2,1,0:T(8,128)(2,1)}, u32[]{:S(2)}) copy-start(bf16[32,16,16,128]{3,2,1,0:T(8,128)(2,1)} %c_ref.1) | copy-start | bytes 6291460
  6.0 11.3 %collective-permute-start.2 = (bf16[2,32,16,128]{3,2,1,0:T(8,128)(2,1)S(1)}, bf16[2,32,16,128]{3,2,1,0:T(8,128)(2,1)S(1)}, u32[]{:S(2)}, u32[]{:S(2)}) collective-permute-start(bf16[2,32,16,128]{3,2,1,0:T(8,128)(2,1)S(1)} %get-tuple-element.59.refs_2_), channel_id=1, source_target_pairs={{0,1},{1,2},{2,3},{3,0},{4,5},{5,6},{6,7},{7,4},{8,9},{9,10},{10,1... | collective-permute-start | bytes 786440 | tf_op jit(solution)/shard_map/ppermute | solution.py:574
  8.2 9.2 %collective-permute-start.3 = (bf16[2,32,16,128]{3,2,1,0:T(8,128)(2,1)S(1)}, bf16[2,32,16,128]{3,2,1,0:T(8,128)(2,1)S(1)}, u32[]{:S(2)}, u32[]{:S(2)}) collective-permute-start(bf16[2,32,16,128]{3,2,1,0:T(8,128)(2,1)S(1)} %get-tuple-element.56.refs_2_.refs_1_), channel_id=1, source_target_pairs={{0,3},{1,0},{2,1},{3,2},{4,7},{5,4},{6,5},{7,6},{8,11},{9,8},{10,9... | collective-permute-start | bytes 786440 | tf_op jit(solution)/shard_map/ppermute | solution.py:574
  12.0 9.3 %collective-permute-start = (bf16[2,32,16,128]{3,2,1,0:T(8,128)(2,1)S(1)}, bf16[2,32,16,128]{3,2,1,0:T(8,128)(2,1)S(1)}, u32[]{:S(2)}, u32[]{:S(2)}) collective-permute-start(bf16[2,32,16,128]{3,2,1,0:T(8,128)(2,1)S(1)} %get-tuple-element.57), channel_id=1, source_target_pairs={{0,4},{4,8},{8,12},{12,0},{1,5},{5,9},{9,13},{13,1},{2,6},{6,10},{... | collective-permute-start | bytes 786440 | tf_op jit(solution)/shard_map/ppermute | solution.py:574
  13.5 7.8 %collective-permute-start.1 = (bf16[2,32,16,128]{3,2,1,0:T(8,128)(2,1)S(1)}, bf16[2,32,16,128]{3,2,1,0:T(8,128)(2,1)S(1)}, u32[]{:S(2)}, u32[]{:S(2)}) collective-permute-start(bf16[2,32,16,128]{3,2,1,0:T(8,128)(2,1)S(1)} %get-tuple-element.58.refs_3_), channel_id=1, source_target_pairs={{0,12},{4,0},{8,4},{12,8},{1,13},{5,1},{9,5},{13,9},{2,14},{6,2},{... | collective-permute-start | bytes 786440 | tf_op jit(solution)/shard_map/ppermute | solution.py:574
  17.3 2.9 %copy-start.2 = (bf16[3,3,3,128,128]{4,3,2,1,0:T(8,128)(2,1)S(1)}, bf16[3,3,3,128,128]{4,3,2,1,0:T(8,128)(2,1)}, u32[]{:S(2)}) copy-start(bf16[3,3,3,128,128]{4,3,2,1,0:T(8,128)(2,1)} %param.6) | copy-start | bytes 2654212
  17.5 4.5 %collective-permute-start.4 = (bf16[2,2,32,128]{3,2,1,0:T(8,128)(2,1)S(1)}, bf16[2,2,32,128]{3,2,1,0:T(8,128)(2,1)S(1)}, u32[]{:S(2)}, u32[]{:S(2)}) collective-permute-start(bf16[2,2,32,128]{3,2,1,0:T(8,128)(2,1)S(1)} %get-tuple-element.60), channel_id=1, source_target_pairs={{0,4},{4,8},{8,12},{12,0},{1,5},{5,9},{9,13},{13,1},{2,6},{6,10},{... | collective-permute-start | bytes 98312 | tf_op jit(solution)/shard_map/ppermute | solution.py:574
  17.6 4.4 %collective-permute-start.5 = (bf16[2,2,32,128]{3,2,1,0:T(8,128)(2,1)S(1)}, bf16[2,2,32,128]{3,2,1,0:T(8,128)(2,1)S(1)}, u32[]{:S(2)}, u32[]{:S(2)}) collective-permute-start(bf16[2,2,32,128]{3,2,1,0:T(8,128)(2,1)S(1)} %get-tuple-element.61.refs_1_.refs_5_), channel_id=1, source_target_pairs={{0,12},{4,0},{8,4},{12,8},{1,13},{5,1},{9,5},{13,9},{2,14},{6,2},{... | collective-permute-start | bytes 98312 | tf_op jit(solution)/shard_map/ppermute | solution.py:574
  22.6 8.3 %collective-permute-start.7 = (bf16[2,21,16,128]{3,2,1,0:T(8,128)(2,1)S(1)}, bf16[2,21,16,128]{3,2,1,0:T(8,128)(2,1)S(1)}, u32[]{:S(2)}, u32[]{:S(2)}) collective-permute-start(bf16[2,21,16,128]{3,2,1,0:T(8,128)(2,1)S(1)} %get-tuple-element.68), channel_id=1, source_target_pairs={{0,16},{16,32},{32,48},{48,64},{64,80},{80,96},{96,112},{112,0},{1... | collective-permute-start | bytes 516104 | tf_op jit(solution)/shard_map/ppermute | solution.py:574
  26.5 4.8 %collective-permute-start.6 = (bf16[2,21,16,128]{3,2,1,0:T(8,128)(2,1)S(1)}, bf16[2,21,16,128]{3,2,1,0:T(8,128)(2,1)S(1)}, u32[]{:S(2)}, u32[]{:S(2)}) collective-permute-start(bf16[2,21,16,128]{3,2,1,0:T(8,128)(2,1)S(1)} %get-tuple-element.67.refs_3_), channel_id=1, source_target_pairs={{0,112},{16,0},{32,16},{48,32},{64,48},{80,64},{96,80},{112,96},{1... | collective-permute-start | bytes 516104 | tf_op jit(solution)/shard_map/ppermute | solution.py:574
  32.7 3.1 %collective-permute-start.8 = (f32[1728,128]{1,0:T(8,128)S(1)}, f32[1728,128]{1,0:T(8,128)S(1)}, u32[]{:S(2)}, u32[]{:S(2)}) collective-permute-start(f32[1728,128]{1,0:T(8,128)S(1)} %get-tuple-element.69.refs_9_), channel_id=1, source_target_pairs={{0,16},{16,0},{32,48},{48,32},{64,80},{80,64},{96,112},{112,96},{1... | collective-permute-start | bytes 2654216 | tf_op jit(solution)/shard_map/ppermute | solution.py:627
  35.9 9.4 %collective-permute-start.10 = (f32[432,128]{1,0:T(8,128)S(1)}, f32[432,128]{1,0:T(8,128)S(1)}, u32[]{:S(2)}, u32[]{:S(2)}) collective-permute-start(f32[432,128]{1,0:T(8,128)S(1)} %get-tuple-element.80), channel_id=1, source_target_pairs={{0,64},{1,65},{2,66},{3,67},{4,68},{5,69},{6,70},{7,71},{8,72},{9,... | collective-permute-start | bytes 663560 | tf_op jit(solution)/shard_map/ppermute | solution.py:507
  37.8 7.5 %collective-permute-start.11 = (f32[432,128]{1,0:T(8,128)S(1)}, f32[432,128]{1,0:T(8,128)S(1)}, u32[]{:S(2)}, u32[]{:S(2)}) collective-permute-start(f32[432,128]{1,0:T(8,128)S(1)} %get-tuple-element.81), channel_id=1, source_target_pairs={{0,96},{1,97},{2,98},{3,99},{4,100},{5,101},{6,102},{7,103},{8,104... | collective-permute-start | bytes 663560 | tf_op jit(solution)/shard_map/ppermute | solution.py:507
  39.0 6.5 %collective-permute-start.9 = (f32[432,128]{1,0:T(8,128)S(1)}, f32[432,128]{1,0:T(8,128)S(1)}, u32[]{:S(2)}, u32[]{:S(2)}) collective-permute-start(f32[432,128]{1,0:T(8,128)S(1)} %get-tuple-element.74.refs_11_), channel_id=1, source_target_pairs={{0,32},{1,33},{2,34},{3,35},{4,36},{5,37},{6,38},{7,39},{8,40},{9,... | collective-permute-start | bytes 663560 | tf_op jit(solution)/shard_map/ppermute | solution.py:507
  45.6 8.9 %collective-permute-start.14 = (f32[432,128]{1,0:T(8,128)S(1)}, f32[432,128]{1,0:T(8,128)S(1)}, u32[]{:S(2)}, u32[]{:S(2)}) collective-permute-start(f32[432,128]{1,0:T(8,128)S(1)} %shard_map.82.refs_12_.refs_0_), channel_id=1, source_target_pairs={{0,12},{1,13},{2,14},{3,15},{4,8},{5,9},{6,10},{7,11},{8,4},{9,5},... | collective-permute-start | bytes 663560 | tf_op jit(solution)/shard_map/ppermute | solution.py:507
  47.2 7.3 %collective-permute-start.13 = (f32[432,128]{1,0:T(8,128)S(1)}, f32[432,128]{1,0:T(8,128)S(1)}, u32[]{:S(2)}, u32[]{:S(2)}) collective-permute-start(f32[432,128]{1,0:T(8,128)S(1)} %shard_map.82.refs_12_.refs_0_), channel_id=1, source_target_pairs={{0,8},{1,9},{2,10},{3,11},{4,12},{5,13},{6,14},{7,15},{8,0},{9,1},... | collective-permute-start | bytes 663560 | tf_op jit(solution)/shard_map/ppermute | solution.py:507
  47.7 7.4 %collective-permute-start.12 = (f32[432,128]{1,0:T(8,128)S(1)}, f32[432,128]{1,0:T(8,128)S(1)}, u32[]{:S(2)}, u32[]{:S(2)}) collective-permute-start(f32[432,128]{1,0:T(8,128)S(1)} %shard_map.82.refs_12_.refs_0_), channel_id=1, source_target_pairs={{0,4},{1,5},{2,6},{3,7},{4,0},{5,1},{6,2},{7,3},{8,12},{9,13},{10,... | collective-permute-start | bytes 663560 | tf_op jit(solution)/shard_map/ppermute | solution.py:507
  55.2 9.4 %collective-permute-start.17 = (f32[432,128]{1,0:T(8,128)S(1)}, f32[432,128]{1,0:T(8,128)S(1)}, u32[]{:S(2)}, u32[]{:S(2)}) collective-permute-start(f32[432,128]{1,0:T(8,128)S(1)} %shard_map.84.refs_10_.refs_0_), channel_id=1, source_target_pairs={{0,3},{1,2},{2,1},{3,0},{4,7},{5,6},{6,5},{7,4},{8,11},{9,10},{10,... | collective-permute-start | bytes 663560 | tf_op jit(solution)/shard_map/ppermute | solution.py:507
  57.9 6.7 %collective-permute-start.16 = (f32[432,128]{1,0:T(8,128)S(1)}, f32[432,128]{1,0:T(8,128)S(1)}, u32[]{:S(2)}, u32[]{:S(2)}) collective-permute-start(f32[432,128]{1,0:T(8,128)S(1)} %shard_map.84.refs_10_.refs_0_), channel_id=1, source_target_pairs={{0,2},{1,3},{2,0},{3,1},{4,6},{5,7},{6,4},{7,5},{8,10},{9,11},{10,... | collective-permute-start | bytes 663560 | tf_op jit(solution)/shard_map/ppermute | solution.py:507
  58.1 6.5 %collective-permute-start.15 = (f32[432,128]{1,0:T(8,128)S(1)}, f32[432,128]{1,0:T(8,128)S(1)}, u32[]{:S(2)}, u32[]{:S(2)}) collective-permute-start(f32[432,128]{1,0:T(8,128)S(1)} %shard_map.84.refs_10_.refs_0_), channel_id=1, source_target_pairs={{0,1},{1,0},{2,3},{3,2},{4,5},{5,4},{6,7},{7,6},{8,9},{9,8},{10,11... | collective-permute-start | bytes 663560 | tf_op jit(solution)/shard_map/ppermute | solution.py:507
  64.7 13.4 %collective-permute-start.21 = (f32[432,128]{1,0:T(8,128)S(1)}, f32[432,128]{1,0:T(8,128)S(1)}, u32[]{:S(2)}, u32[]{:S(2)}) collective-permute-start(f32[432,128]{1,0:T(8,128)S(1)} %shard_map.86.refs_12_.refs_0_), channel_id=1, source_target_pairs={{0,16},{16,0},{32,48},{48,32},{64,80},{80,64},{96,112},{112,96},{1... | collective-permute-start | bytes 663560 | tf_op jit(solution)/shard_map/ppermute | solution.py:638
  68.1 10.0 %collective-permute-start.20 = (f32[432,128]{1,0:T(8,128)S(1)}, f32[432,128]{1,0:T(8,128)S(1)}, u32[]{:S(2)}, u32[]{:S(2)}) collective-permute-start(f32[432,128]{1,0:T(8,128)S(1)} %shard_map.86.refs_12_.refs_0_), channel_id=1, source_target_pairs={{0,96},{1,97},{2,98},{3,99},{4,100},{5,101},{6,102},{7,103},{8,104... | collective-permute-start | bytes 663560 | tf_op jit(solution)/shard_map/ppermute | solution.py:507
  70.8 7.3 %collective-permute-start.19 = (f32[432,128]{1,0:T(8,128)S(1)}, f32[432,128]{1,0:T(8,128)S(1)}, u32[]{:S(2)}, u32[]{:S(2)}) collective-permute-start(f32[432,128]{1,0:T(8,128)S(1)} %shard_map.86.refs_12_.refs_0_), channel_id=1, source_target_pairs={{0,64},{1,65},{2,66},{3,67},{4,68},{5,69},{6,70},{7,71},{8,72},{9,... | collective-permute-start | bytes 663560 | tf_op jit(solution)/shard_map/ppermute | solution.py:507
  70.8 7.3 %collective-permute-start.18 = (f32[432,128]{1,0:T(8,128)S(1)}, f32[432,128]{1,0:T(8,128)S(1)}, u32[]{:S(2)}, u32[]{:S(2)}) collective-permute-start(f32[432,128]{1,0:T(8,128)S(1)} %shard_map.86.refs_12_.refs_0_), channel_id=1, source_target_pairs={{0,32},{1,33},{2,34},{3,35},{4,36},{5,37},{6,38},{7,39},{8,40},{9,... | collective-permute-start | bytes 663560 | tf_op jit(solution)/shard_map/ppermute | solution.py:507
  78.2 2.7 %collective-permute-start.22 = (f32[1296,128]{1,0:T(8,128)S(1)}, f32[1296,128]{1,0:T(8,128)S(1)}, u32[]{:S(2)}, u32[]{:S(2)}) collective-permute-start(f32[1296,128]{1,0:T(8,128)S(1)} %shard_map.88.refs_1_.refs_2_), channel_id=1, source_target_pairs={{0,16},{16,0},{32,48},{48,32},{64,80},{80,64},{96,112},{112,96},{1... | collective-permute-start | bytes 1990664 | tf_op jit(solution)/shard_map/ppermute | solution.py:641

commit v7 on v6

--- a/solution.py
+++ b/solution.py
@@ -88,10 +88,10 @@
 
 def prepare(occupancy, features, cotangent):
     slabs = shape((X + 2, Y, Z, C), BF16)
-    own_cost = pl.CostEstimate(flops=1000000, bytes_accessed=5 << 20, transcendentals=0)
+    own_cost = pl.CostEstimate(flops=1000, bytes_accessed=1000, transcendentals=0)
     mask = small_kernel(
         mask_kernel, shape((X // E, Y, Z, C), BF16), [jnp.transpose(occupancy, (1, 2, 0))], specs=[SMEM],
-        moved=16 << 20,
+        flops=10**10,
     )
     fields, *given = pl.pallas_call(
         prepare_x_kernel,
@@ -324,7 +324,7 @@
         next_ = jnp.dot(patches(edge, 1), w_ref[:, :C], preferred_element_type=F32)
     else:
         near, next_ = before[0], before[1]
-    if groups > 3:
+    if groups > 3 and following is not None:
         if ready is None:
             put(even, part, 0)
         else:
@@ -338,8 +338,7 @@
             put(odd, part, x + GROUP)
             near, next_ = group(odd, x + GROUP, 2 * i + 1, near, next_, False)
             after = i + 1 == groups // 2
-            then = following[1] if following is not None else X - GROUP
-            put(even, part, jnp.where(after, then, x + 2 * GROUP))
+            put(even, part, jnp.where(after, following[1], x + 2 * GROUP))
             carry_ref[0] = near
             carry_ref[1] = next_
             return carry
@@ -349,13 +348,14 @@
     else:
         if ready is None:
             put(odd, part, first)
-        shifted = [odd] if ready is None else [ready, odd, others.at[1]]
+        shifted = [odd] if ready is None else [ready, odd, others.at[1], even]
         for at in range(groups):
             x = first + at * GROUP
             near, next_ = group(shifted[at], x, at, near, next_, starts and at == 0)
             if at + 1 < groups:
                 put(shifted[at + 1], part, x + GROUP)
-        put(even, *following)
+        if following is not None:
+            put(even, *following)
         carry_ref[0] = near
         carry_ref[1] = next_
     if ends:
@@ -430,7 +430,7 @@
     return made, dict(zip(("carry", "ready", "late"), kept, strict=False))
 
 
-def small_kernel(kernel, out_shape, operands, ties=(), specs=None, moved=1 << 20):
+def small_kernel(kernel, out_shape, operands, ties=(), specs=None, flops=1000):
     count = len(operands)
 
     def run(*refs):
@@ -442,7 +442,7 @@
         out_specs=jax.tree.map(lambda _: VMEM, out_shape),
         out_shape=out_shape,
         compiler_params=params(),
-        cost_estimate=pl.CostEstimate(flops=1000, bytes_accessed=moved, transcendentals=0),
+        cost_estimate=pl.CostEstimate(flops=flops, bytes_accessed=1 << 20, transcendentals=0),
     )(*operands, *ties)
 
 

time: 82.2 us -> 81.2 us (0.988)
  no operation moved by 1% of the time
where the time goes in v7:
time: 81.2 us; the launch traced here: 81 us
  Pallas kernels  43 us (53%)
  starting transfers between devices  32.4 us (40%)
  local copies, waits for them, and re-layouts  2.35 us (3%)
  waiting for transfers between devices  2.14 us (3%)
  between operations  1.14 us (1%)
    pallas_call x5, Pallas kernels, conv_piece(): pl.pallas_call(plain if more else final, in_specs=specs, out_specs=[ANY]...  25.4 us
    ppermute x12, starting transfers between devices, exchange(): lax.ppermute(value, ('gx', 'gy', 'gz'), pairs(turn, step))  13.8 us
    ppermute x8, starting transfers between devices, shift(): lax.ppermute(value, axis, [(i, (i + step) % count) for i in range(count)])  13.1 us
    pallas_call x3, Pallas kernels, own_grad(): pl.pallas_call(lambda *refs: own_grad_kernel(first, spans, more, *refs),...  9.17 us
    ppermute x1, starting transfers between devices, body(): beside = lax.ppermute(chunk, 'gx', swap)  3.43 us
    pallas_call x11, Pallas kernels, small_kernel(): pl.pallas_call(run, in_specs=(specs or [VMEM] * count) + [ANY] * len(ties...  2.68 us
    pallas_call x3, Pallas kernels, write(): pl.pallas_call(kernel, in_specs=[VMEM] * len(arrays) + [ANY] * (len(opera...  2.51 us
    unnamed x8, local copies, waits for them, and re-layouts  2.35 us
  transfers between devices with their start and end apart: 23, of which 6 were waited for; matrix products, arithmetic and copies ran while one was open for 0% of the time, Pallas kernels for 46%

profile of v7, /device:TPU:1, one launch (start us, length us, event | category | flops | bytes accessed | tf_op | source)
XLA Modules:
  0.0 81.0 jit_solution(8418060404798838995)
XLA Ops:
  1.9 1.0 %copy-done = bf16[32,16,16,128]{3,2,1,0:T(8,128)(2,1)S(1)} copy-done((bf16[32,16,16,128]{3,2,1,0:T(8,128)(2,1)S(1)}, bf16[32,16,16,128]{3,2,1,0:T(8,128)(2,1)}, u32[]{:S(2)}) %copy-start) | copy-done | bytes 2097176
  2.9 0.9 %shard_map.68 = (bf16[34,16,16,128]{3,2,1,0:T(8,128)(2,1)S(1)}, bf16[1,32,16,128]{3,2,1,0:T(8,128)(2,1)S(1)}, bf16[1,32,16,128]{3,2,1,0:T(8,128)(2,1)S(1)}, bf16...) custom-call(bf16[32,16,16,128]{3,2,1,0:T(8,128)(2,1)S(1)} %copy-done, ...), custom_call_target="tpu_custom_call" | custom-call | flops 1000 | bytes 1000 | tf_op jit(solution)/shard_map/pallas_call | solution.py:96
  3.8 0.7 copy-done.1
  4.5 0.9 %shard_map.69 = (bf16[34,16,16,128]{3,2,1,0:T(8,128)(2,1)S(1)}, bf16[2,32,16,128]{3,2,1,0:T(8,128)(2,1)S(1)}, bf16[2,32,16,128]{3,2,1,0:T(8,128)(2,1)S(1)}, bf16...) custom-call(bf16[32,16,16,128]{3,2,1,0:T(8,128)(2,1)S(1)} %copy-done.1, ...), custom_call_target="tpu_custom_call" | custom-call | flops 1000 | bytes 1000 | tf_op jit(solution)/shard_map/pallas_call | solution.py:104
  5.4 2.1 %collective-permute-start.2 = (bf16[2,32,16,128]{3,2,1,0:T(8,128)(2,1)S(1)}, bf16[2,32,16,128]{3,2,1,0:T(8,128)(2,1)S(1)}, u32[]{:S(2)}, u32[]{:S(2)}) collective-permute-start(bf16[2,32,16,128]{3,2,1,0:T(8,128)(2,1)S(1)} %get-tuple-element.59.refs_2_), channel_id=1, source_target_pairs={{0,1},{1,2},{2,3},{3,0},{4,5},{5,6},{6,7},{7,4},{8,9},{9,10},{10,1... | collective-permute-start | bytes 786440 | tf_op jit(solution)/shard_map/ppermute | solution.py:574
  7.6 1.3 %collective-permute-start.3 = (bf16[2,32,16,128]{3,2,1,0:T(8,128)(2,1)S(1)}, bf16[2,32,16,128]{3,2,1,0:T(8,128)(2,1)S(1)}, u32[]{:S(2)}, u32[]{:S(2)}) collective-permute-start(bf16[2,32,16,128]{3,2,1,0:T(8,128)(2,1)S(1)} %get-tuple-element.56.refs_2_.refs_1_), channel_id=1, source_target_pairs={{0,3},{1,0},{2,1},{3,2},{4,7},{5,4},{6,5},{7,6},{8,11},{9,8},{10,9... | collective-permute-start | bytes 786440 | tf_op jit(solution)/shard_map/ppermute | solution.py:574
  8.9 2.4 %shard_map.70.refs_2_ = f32[384,1152]{1,0:T(8,128)S(1)} custom-call(bf16[34,16,16,128]{3,2,1,0:T(8,128)(2,1)S(1)} %get-tuple-element.48.refs_0_.refs_1_, bf16[34,16,16,128]{3,2,1,0:T(8,128)(2,1)S(1)} %get-tuple-element.53.refs_1_.g_ref.refs_2_, bf16[2,32,16,128]{3,2,1,0:T(8,128)(2,1)S(1)} %get-tuple-element.56.refs_2_.refs_1_), custom_call_target="tpu_custom_call" | custom-call | flops 1811939328 | bytes 8388608 | tf_op jit(solution)/shard_map/pallas_call | solution.py:180
  11.4 1.5 %collective-permute-start = (bf16[2,32,16,128]{3,2,1,0:T(8,128)(2,1)S(1)}, bf16[2,32,16,128]{3,2,1,0:T(8,128)(2,1)S(1)}, u32[]{:S(2)}, u32[]{:S(2)}) collective-permute-start(bf16[2,32,16,128]{3,2,1,0:T(8,128)(2,1)S(1)} %get-tuple-element.57), channel_id=1, source_target_pairs={{0,4},{4,8},{8,12},{12,0},{1,5},{5,9},{9,13},{13,1},{2,6},{6,10},{... | collective-permute-start | bytes 786440 | tf_op jit(solution)/shard_map/ppermute | solution.py:574
  12.9 1.5 %collective-permute-start.1 = (bf16[2,32,16,128]{3,2,1,0:T(8,128)(2,1)S(1)}, bf16[2,32,16,128]{3,2,1,0:T(8,128)(2,1)S(1)}, u32[]{:S(2)}, u32[]{:S(2)}) collective-permute-start(bf16[2,32,16,128]{3,2,1,0:T(8,128)(2,1)S(1)} %get-tuple-element.58.refs_3_), channel_id=1, source_target_pairs={{0,12},{4,0},{8,4},{12,8},{1,13},{5,1},{9,5},{13,9},{2,14},{6,2},{... | collective-permute-start | bytes 786440 | tf_op jit(solution)/shard_map/ppermute | solution.py:574
  14.4 2.3 %shard_map.72.refs_2_.refs_0_ = f32[384,1152]{1,0:T(8,128)S(1)} custom-call(bf16[34,16,16,128]{3,2,1,0:T(8,128)(2,1)S(1)} %get-tuple-element.48.refs_0_.refs_1_, bf16[34,16,16,128]{3,2,1,0:T(8,128)(2,1)S(1)} %get-tuple-element.53.refs_1_.g_ref.refs_2_, f32[384,1152]{1,0:T(8,128)S(1)} %shard_map.70.refs_2_, bf16[2,32,16,128]{3,2,1,0:T(8,128)(2,1)S(1)} %get-tuple-element.58.refs_3_), custom_call_target="tpu_custom_call" | custom-call | flops 1811939328 | bytes 8388608 | tf_op jit(solution)/shard_map/pallas_call | solution.py:180
  17.0 2.7 %collective-permute-start.5 = (bf16[2,2,32,128]{3,2,1,0:T(8,128)(2,1)S(1)}, bf16[2,2,32,128]{3,2,1,0:T(8,128)(2,1)S(1)}, u32[]{:S(2)}, u32[]{:S(2)}) collective-permute-start(bf16[2,2,32,128]{3,2,1,0:T(8,128)(2,1)S(1)} %get-tuple-element.61.refs_1_.refs_5_), channel_id=1, source_target_pairs={{0,12},{4,0},{8,4},{12,8},{1,13},{5,1},{9,5},{13,9},{2,14},{6,2},{... | collective-permute-start | bytes 98312 | tf_op jit(solution)/shard_map/ppermute | solution.py:574
  20.7 0.7 collective-permute-done.4.refs_6_.elo
  22.0 3.9 %collective-permute-start.7 = (bf16[2,21,16,128]{3,2,1,0:T(8,128)(2,1)S(1)}, bf16[2,21,16,128]{3,2,1,0:T(8,128)(2,1)S(1)}, u32[]{:S(2)}, u32[]{:S(2)}) collective-permute-start(bf16[2,21,16,128]{3,2,1,0:T(8,128)(2,1)S(1)} %get-tuple-element.68), channel_id=1, source_target_pairs={{0,16},{16,32},{32,48},{48,64},{64,80},{80,96},{96,112},{112,0},{1... | collective-permute-start | bytes 516104 | tf_op jit(solution)/shard_map/ppermute | solution.py:574
  25.9 4.4 %shard_map.77.own_ref = f32[384,1152]{1,0:T(8,128)S(1)} custom-call(bf16[34,16,16,128]{3,2,1,0:T(8,128)(2,1)S(1)} %get-tuple-element.48.refs_0_.refs_1_, bf16[34,16,16,128]{3,2,1,0:T(8,128)(2,1)S(1)} %get-tuple-element.53.refs_1_.g_ref.refs_2_, f32[384,1152]{1,0:T(8,128)S(1)} %shard_map.75.refs_9_.refs_2_, bf16[2,21,16,128]{3,2,1,0:T(8,128)(2,1)S(1)} %get-tuple-element.67.refs_3_), custom_call_target="tpu_custom_call" | custom-call | flops 3623878656 | bytes 8388608 | tf_op jit(solution)/shard_map/pallas_call | solution.py:180
  30.7 1.4 %shard_map.78 = (f32[1728,128]{1,0:T(8,128)S(1)}, f32[1728,128]{1,0:T(8,128)S(1)}) custom-call(f32[384,1152]{1,0:T(8,128)S(1)} %shard_map.77.own_ref, bf16[34,16,16,128]{3,2,1,0:T(8,128)(2,1)S(1)} %get-tuple-element.53.refs_1_.g_ref.refs_2_, bf16[2,32,16,128]{3,2,1,0:T(8,128)(2,1)S(1)} %get-tuple-element.54.refs_0_.gylo, ...), custom_call_target="tpu_custom_call" | custom-call | flops 679477248 | bytes 6291456 | tf_op jit(solution)/shard_map/pallas_call | solution.py:250
  32.1 1.0 %collective-permute-start.8 = (f32[1728,128]{1,0:T(8,128)S(1)}, f32[1728,128]{1,0:T(8,128)S(1)}, u32[]{:S(2)}, u32[]{:S(2)}) collective-permute-start(f32[1728,128]{1,0:T(8,128)S(1)} %get-tuple-element.69.refs_9_), channel_id=1, source_target_pairs={{0,16},{16,0},{32,48},{48,32},{64,80},{80,64},{96,112},{112,96},{1... | collective-permute-start | bytes 2654216 | tf_op jit(solution)/shard_map/ppermute | solution.py:627
  33.1 2.0 %shard_map.79 = (bf16[32,16,16,128]{3,2,1,0:T(8,128)(2,1)}, f32[2,256,128]{2,1,0:T(8,128)S(1)}, bf16[3,4,18,16,128]{4,3,2,1,0:T(8,128)(2,1)S(1)}, bf16[4,16,16,128]{3,2,1,0:T(8,128)(2,1)S(1)}) custom-call(bf16[4,16,16,128]{3,2,1,0:T(8,128)(2,1)S(1)} %shard_map.67.mask_ref.refs_0_, bf16[34,16,16,128]{3,2,1,0:T(8,128)(2,1)S(1)} %get-tuple-element.48.refs_0_.refs_1_, ...), custom_call_target="tpu_custom_call" | custom-call | flops 905969664 | bytes 2097152 | tf_op jit(solution)/shard_map/pallas_call | solution.py:420
  35.3 1.9 %collective-permute-start.10 = (f32[432,128]{1,0:T(8,128)S(1)}, f32[432,128]{1,0:T(8,128)S(1)}, u32[]{:S(2)}, u32[]{:S(2)}) collective-permute-start(f32[432,128]{1,0:T(8,128)S(1)} %get-tuple-element.80), channel_id=1, source_target_pairs={{0,64},{1,65},{2,66},{3,67},{4,68},{5,69},{6,70},{7,71},{8,72},{9,... | collective-permute-start | bytes 663560 | tf_op jit(solution)/shard_map/ppermute | solution.py:507
  37.2 1.2 %collective-permute-start.11 = (f32[432,128]{1,0:T(8,128)S(1)}, f32[432,128]{1,0:T(8,128)S(1)}, u32[]{:S(2)}, u32[]{:S(2)}) collective-permute-start(f32[432,128]{1,0:T(8,128)S(1)} %get-tuple-element.81), channel_id=1, source_target_pairs={{0,96},{1,97},{2,98},{3,99},{4,100},{5,101},{6,102},{7,103},{8,104... | collective-permute-start | bytes 663560 | tf_op jit(solution)/shard_map/ppermute | solution.py:507
  38.9 5.8 %shard_map.81 = (bf16[32,16,16,128]{3,2,1,0:T(8,128)(2,1)}, f32[2,256,128]{2,1,0:T(8,128)S(1)}, bf16[3,4,18,16,128]{4,3,2,1,0:T(8,128)(2,1)S(1)}, bf16[4,16,16,128]{3,2,1,0:T(8,128)(2,1)S(1)}) custom-call(bf16[4,16,16,128]{3,2,1,0:T(8,128)(2,1)S(1)} %shard_map.67.mask_ref.refs_0_, ...), custom_call_target="tpu_custom_call", output_to_operand_aliasing={{0}: (12, {})} | custom-call | flops 3623878656 | bytes 2097152 | tf_op jit(solution)/shard_map/pallas_call | solution.py:420
  45.0 1.6 %collective-permute-start.14 = (f32[432,128]{1,0:T(8,128)S(1)}, f32[432,128]{1,0:T(8,128)S(1)}, u32[]{:S(2)}, u32[]{:S(2)}) collective-permute-start(f32[432,128]{1,0:T(8,128)S(1)} %shard_map.82.refs_12_.refs_0_), channel_id=1, source_target_pairs={{0,12},{1,13},{2,14},{3,15},{4,8},{5,9},{6,10},{7,11},{8,4},{9,5},... | collective-permute-start | bytes 663560 | tf_op jit(solution)/shard_map/ppermute | solution.py:507
  47.1 1.4 %collective-permute-start.12 = (f32[432,128]{1,0:T(8,128)S(1)}, f32[432,128]{1,0:T(8,128)S(1)}, u32[]{:S(2)}, u32[]{:S(2)}) collective-permute-start(f32[432,128]{1,0:T(8,128)S(1)} %shard_map.82.refs_12_.refs_0_), channel_id=1, source_target_pairs={{0,4},{1,5},{2,6},{3,7},{4,0},{5,1},{6,2},{7,3},{8,12},{9,13},{10,... | collective-permute-start | bytes 663560 | tf_op jit(solution)/shard_map/ppermute | solution.py:507
  48.5 5.3 %shard_map.83 = (bf16[32,16,16,128]{3,2,1,0:T(8,128)(2,1)}, f32[2,256,128]{2,1,0:T(8,128)S(1)}, bf16[3,4,18,16,128]{4,3,2,1,0:T(8,128)(2,1)S(1)}) custom-call(bf16[4,16,16,128]{3,2,1,0:T(8,128)(2,1)S(1)} %shard_map.67.mask_ref.refs_0_, bf16[34,16,16,128]{3,2,1,0:T(8,128)(2,1)S(1)} %get-tuple-element.48.refs_0_.refs_1_, ...), custom_call_target="tpu_custom_call", output_to_operand_aliasing={{0}: (13, {})} | custom-call | flops 2717908992 | bytes 2097152 | tf_op jit(solution)/shard_map/pallas_call | solution.py:420
  54.6 2.7 %collective-permute-start.17 = (f32[432,128]{1,0:T(8,128)S(1)}, f32[432,128]{1,0:T(8,128)S(1)}, u32[]{:S(2)}, u32[]{:S(2)}) collective-permute-start(f32[432,128]{1,0:T(8,128)S(1)} %shard_map.84.refs_10_.refs_0_), channel_id=1, source_target_pairs={{0,3},{1,2},{2,1},{3,0},{4,7},{5,6},{6,5},{7,4},{8,11},{9,10},{10,... | collective-permute-start | bytes 663560 | tf_op jit(solution)/shard_map/ppermute | solution.py:507
  58.0 6.0 %shard_map.85 = (bf16[32,16,16,128]{3,2,1,0:T(8,128)(2,1)}, f32[2,256,128]{2,1,0:T(8,128)S(1)}, bf16[3,4,18,16,128]{4,3,2,1,0:T(8,128)(2,1)S(1)}, bf16[4,16,16,128]{3,2,1,0:T(8,128)(2,1)S(1)}) custom-call(bf16[4,16,16,128]{3,2,1,0:T(8,128)(2,1)S(1)} %shard_map.67.mask_ref.refs_0_, bf16[34,16,16,128]{3,2,1,0:T(8,128)(2,1)S(1)} %get-tuple-element.48.refs_0_.refs_1_, ...), custom_call_target="tpu_custom_call" | custom-call | flops 3623878656 | bytes 2097152 | tf_op jit(solution)/shard_map/pallas_call | solution.py:420
  64.1 3.4 %collective-permute-start.21 = (f32[432,128]{1,0:T(8,128)S(1)}, f32[432,128]{1,0:T(8,128)S(1)}, u32[]{:S(2)}, u32[]{:S(2)}) collective-permute-start(f32[432,128]{1,0:T(8,128)S(1)} %shard_map.86.refs_12_.refs_0_), channel_id=1, source_target_pairs={{0,16},{16,0},{32,48},{48,32},{64,80},{80,64},{96,112},{112,96},{1... | collective-permute-start | bytes 663560 | tf_op jit(solution)/shard_map/ppermute | solution.py:638
  67.5 2.6 %collective-permute-start.20 = (f32[432,128]{1,0:T(8,128)S(1)}, f32[432,128]{1,0:T(8,128)S(1)}, u32[]{:S(2)}, u32[]{:S(2)}) collective-permute-start(f32[432,128]{1,0:T(8,128)S(1)} %shard_map.86.refs_12_.refs_0_), channel_id=1, source_target_pairs={{0,96},{1,97},{2,98},{3,99},{4,100},{5,101},{6,102},{7,103},{8,104... | collective-permute-start | bytes 663560 | tf_op jit(solution)/shard_map/ppermute | solution.py:507
  70.8 6.3 %shard_map.87 = (bf16[32,16,16,128]{3,2,1,0:T(8,128)(2,1)}, f32[8,128]{1,0:T(8,128)S(1)}) custom-call(bf16[4,16,16,128]{3,2,1,0:T(8,128)(2,1)S(1)} %shard_map.67.mask_ref.refs_0_, bf16[34,16,16,128]{3,2,1,0:T(8,128)(2,1)S(1)} %get-tuple-element.48.refs_0_.refs_1_, ...), custom_call_target="tpu_custom_call", output_to_operand_aliasing={{0}: (13, {})} | custom-call | flops 3623878656 | bytes 2097152 | tf_op jit(solution)/shard_map/pallas_call | solution.py:420
  77.2 1.0 %collective-permute-start.22 = (f32[1296,128]{1,0:T(8,128)S(1)}, f32[1296,128]{1,0:T(8,128)S(1)}, u32[]{:S(2)}, u32[]{:S(2)}) collective-permute-start(f32[1296,128]{1,0:T(8,128)S(1)} %shard_map.88.refs_1_.refs_2_), channel_id=1, source_target_pairs={{0,16},{16,0},{32,48},{48,32},{64,80},{80,64},{96,112},{112,96},{1... | collective-permute-start | bytes 1990664 | tf_op jit(solution)/shard_map/ppermute | solution.py:641
  78.2 0.9 %shard_map.89.refs_2_ = f32[3456,128]{1,0:T(8,128)} custom-call(f32[432,128]{1,0:T(8,128)S(1)} %shard_map.86.refs_12_.refs_0_, f32[1296,128]{1,0:T(8,128)S(1)} %shard_map.88.refs_1_.refs_2_, f32[1296,128]{1,0:T(8,128)S(1)} %shard_map.88.refs_1_.refs_2_), custom_call_target="tpu_custom_call" | custom-call | flops 1000 | bytes 1048576 | tf_op jit(solution)/shard_map/pallas_call | solution.py:554
  79.2 0.7 shard_map.90.refs_2_
  80.0 0.9 %shard_map.91 = f32[3456,128]{1,0:T(8,128)} custom-call(f32[1296,128]{1,0:T(8,128)S(1)} %collective-permute-done.22.refs_0_, f32[1296,128]{1,0:T(8,128)S(1)} %shard_map.88.refs_1_.refs_2_, f32[3456,128]{1,0:T(8,128)} %shard_map.90.refs_2_), custom_call_target="tpu_custom_call", output_to_operand_aliasing={{}: (2, {})} | custom-call | flops 1000 | bytes 1048576 | tf_op jit(solution)/shard_map/pallas_call | solution.py:554
  (47 shorter events, 7.2 us)
Async XLA Ops:
  0.6 0.7 copy-start.3
  1.3 1.6 %copy-start = (bf16[32,16,16,128]{3,2,1,0:T(8,128)(2,1)S(1)}, bf16[32,16,16,128]{3,2,1,0:T(8,128)(2,1)}, u32[]{:S(2)}) copy-start(bf16[32,16,16,128]{3,2,1,0:T(8,128)(2,1)} %f_ref.1) | copy-start | bytes 6291460
  2.9 1.6 %copy-start.1 = (bf16[32,16,16,128]{3,2,1,0:T(8,128)(2,1)S(1)}, bf16[32,16,16,128]{3,2,1,0:T(8,128)(2,1)}, u32[]{:S(2)}) copy-start(bf16[32,16,16,128]{3,2,1,0:T(8,128)(2,1)} %c_ref.1) | copy-start | bytes 6291460
  5.4 11.3 %collective-permute-start.2 = (bf16[2,32,16,128]{3,2,1,0:T(8,128)(2,1)S(1)}, bf16[2,32,16,128]{3,2,1,0:T(8,128)(2,1)S(1)}, u32[]{:S(2)}, u32[]{:S(2)}) collective-permute-start(bf16[2,32,16,128]{3,2,1,0:T(8,128)(2,1)S(1)} %get-tuple-element.59.refs_2_), channel_id=1, source_target_pairs={{0,1},{1,2},{2,3},{3,0},{4,5},{5,6},{6,7},{7,4},{8,9},{9,10},{10,1... | collective-permute-start | bytes 786440 | tf_op jit(solution)/shard_map/ppermute | solution.py:574
  7.6 9.2 %collective-permute-start.3 = (bf16[2,32,16,128]{3,2,1,0:T(8,128)(2,1)S(1)}, bf16[2,32,16,128]{3,2,1,0:T(8,128)(2,1)S(1)}, u32[]{:S(2)}, u32[]{:S(2)}) collective-permute-start(bf16[2,32,16,128]{3,2,1,0:T(8,128)(2,1)S(1)} %get-tuple-element.56.refs_2_.refs_1_), channel_id=1, source_target_pairs={{0,3},{1,0},{2,1},{3,2},{4,7},{5,4},{6,5},{7,6},{8,11},{9,8},{10,9... | collective-permute-start | bytes 786440 | tf_op jit(solution)/shard_map/ppermute | solution.py:574
  11.4 9.3 %collective-permute-start = (bf16[2,32,16,128]{3,2,1,0:T(8,128)(2,1)S(1)}, bf16[2,32,16,128]{3,2,1,0:T(8,128)(2,1)S(1)}, u32[]{:S(2)}, u32[]{:S(2)}) collective-permute-start(bf16[2,32,16,128]{3,2,1,0:T(8,128)(2,1)S(1)} %get-tuple-element.57), channel_id=1, source_target_pairs={{0,4},{4,8},{8,12},{12,0},{1,5},{5,9},{9,13},{13,1},{2,6},{6,10},{... | collective-permute-start | bytes 786440 | tf_op jit(solution)/shard_map/ppermute | solution.py:574
  12.9 7.8 %collective-permute-start.1 = (bf16[2,32,16,128]{3,2,1,0:T(8,128)(2,1)S(1)}, bf16[2,32,16,128]{3,2,1,0:T(8,128)(2,1)S(1)}, u32[]{:S(2)}, u32[]{:S(2)}) collective-permute-start(bf16[2,32,16,128]{3,2,1,0:T(8,128)(2,1)S(1)} %get-tuple-element.58.refs_3_), channel_id=1, source_target_pairs={{0,12},{4,0},{8,4},{12,8},{1,13},{5,1},{9,5},{13,9},{2,14},{6,2},{... | collective-permute-start | bytes 786440 | tf_op jit(solution)/shard_map/ppermute | solution.py:574
  16.7 2.9 %copy-start.2 = (bf16[3,3,3,128,128]{4,3,2,1,0:T(8,128)(2,1)S(1)}, bf16[3,3,3,128,128]{4,3,2,1,0:T(8,128)(2,1)}, u32[]{:S(2)}) copy-start(bf16[3,3,3,128,128]{4,3,2,1,0:T(8,128)(2,1)} %param.6) | copy-start | bytes 2654212
  16.9 4.5 %collective-permute-start.4 = (bf16[2,2,32,128]{3,2,1,0:T(8,128)(2,1)S(1)}, bf16[2,2,32,128]{3,2,1,0:T(8,128)(2,1)S(1)}, u32[]{:S(2)}, u32[]{:S(2)}) collective-permute-start(bf16[2,2,32,128]{3,2,1,0:T(8,128)(2,1)S(1)} %get-tuple-element.60), channel_id=1, source_target_pairs={{0,4},{4,8},{8,12},{12,0},{1,5},{5,9},{9,13},{13,1},{2,6},{6,10},{... | collective-permute-start | bytes 98312 | tf_op jit(solution)/shard_map/ppermute | solution.py:574
  17.0 4.4 %collective-permute-start.5 = (bf16[2,2,32,128]{3,2,1,0:T(8,128)(2,1)S(1)}, bf16[2,2,32,128]{3,2,1,0:T(8,128)(2,1)S(1)}, u32[]{:S(2)}, u32[]{:S(2)}) collective-permute-start(bf16[2,2,32,128]{3,2,1,0:T(8,128)(2,1)S(1)} %get-tuple-element.61.refs_1_.refs_5_), channel_id=1, source_target_pairs={{0,12},{4,0},{8,4},{12,8},{1,13},{5,1},{9,5},{13,9},{2,14},{6,2},{... | collective-permute-start | bytes 98312 | tf_op jit(solution)/shard_map/ppermute | solution.py:574
  22.0 8.3 %collective-permute-start.7 = (bf16[2,21,16,128]{3,2,1,0:T(8,128)(2,1)S(1)}, bf16[2,21,16,128]{3,2,1,0:T(8,128)(2,1)S(1)}, u32[]{:S(2)}, u32[]{:S(2)}) collective-permute-start(bf16[2,21,16,128]{3,2,1,0:T(8,128)(2,1)S(1)} %get-tuple-element.68), channel_id=1, source_target_pairs={{0,16},{16,32},{32,48},{48,64},{64,80},{80,96},{96,112},{112,0},{1... | collective-permute-start | bytes 516104 | tf_op jit(solution)/shard_map/ppermute | solution.py:574
  25.9 4.8 %collective-permute-start.6 = (bf16[2,21,16,128]{3,2,1,0:T(8,128)(2,1)S(1)}, bf16[2,21,16,128]{3,2,1,0:T(8,128)(2,1)S(1)}, u32[]{:S(2)}, u32[]{:S(2)}) collective-permute-start(bf16[2,21,16,128]{3,2,1,0:T(8,128)(2,1)S(1)} %get-tuple-element.67.refs_3_), channel_id=1, source_target_pairs={{0,112},{16,0},{32,16},{48,32},{64,48},{80,64},{96,80},{112,96},{1... | collective-permute-start | bytes 516104 | tf_op jit(solution)/shard_map/ppermute | solution.py:574
  32.1 3.1 %collective-permute-start.8 = (f32[1728,128]{1,0:T(8,128)S(1)}, f32[1728,128]{1,0:T(8,128)S(1)}, u32[]{:S(2)}, u32[]{:S(2)}) collective-permute-start(f32[1728,128]{1,0:T(8,128)S(1)} %get-tuple-element.69.refs_9_), channel_id=1, source_target_pairs={{0,16},{16,0},{32,48},{48,32},{64,80},{80,64},{96,112},{112,96},{1... | collective-permute-start | bytes 2654216 | tf_op jit(solution)/shard_map/ppermute | solution.py:627
  35.3 9.4 %collective-permute-start.10 = (f32[432,128]{1,0:T(8,128)S(1)}, f32[432,128]{1,0:T(8,128)S(1)}, u32[]{:S(2)}, u32[]{:S(2)}) collective-permute-start(f32[432,128]{1,0:T(8,128)S(1)} %get-tuple-element.80), channel_id=1, source_target_pairs={{0,64},{1,65},{2,66},{3,67},{4,68},{5,69},{6,70},{7,71},{8,72},{9,... | collective-permute-start | bytes 663560 | tf_op jit(solution)/shard_map/ppermute | solution.py:507
  37.2 7.5 %collective-permute-start.11 = (f32[432,128]{1,0:T(8,128)S(1)}, f32[432,128]{1,0:T(8,128)S(1)}, u32[]{:S(2)}, u32[]{:S(2)}) collective-permute-start(f32[432,128]{1,0:T(8,128)S(1)} %get-tuple-element.81), channel_id=1, source_target_pairs={{0,96},{1,97},{2,98},{3,99},{4,100},{5,101},{6,102},{7,103},{8,104... | collective-permute-start | bytes 663560 | tf_op jit(solution)/shard_map/ppermute | solution.py:507
  38.4 6.5 %collective-permute-start.9 = (f32[432,128]{1,0:T(8,128)S(1)}, f32[432,128]{1,0:T(8,128)S(1)}, u32[]{:S(2)}, u32[]{:S(2)}) collective-permute-start(f32[432,128]{1,0:T(8,128)S(1)} %get-tuple-element.74.refs_11_), channel_id=1, source_target_pairs={{0,32},{1,33},{2,34},{3,35},{4,36},{5,37},{6,38},{7,39},{8,40},{9,... | collective-permute-start | bytes 663560 | tf_op jit(solution)/shard_map/ppermute | solution.py:507
  45.0 8.9 %collective-permute-start.14 = (f32[432,128]{1,0:T(8,128)S(1)}, f32[432,128]{1,0:T(8,128)S(1)}, u32[]{:S(2)}, u32[]{:S(2)}) collective-permute-start(f32[432,128]{1,0:T(8,128)S(1)} %shard_map.82.refs_12_.refs_0_), channel_id=1, source_target_pairs={{0,12},{1,13},{2,14},{3,15},{4,8},{5,9},{6,10},{7,11},{8,4},{9,5},... | collective-permute-start | bytes 663560 | tf_op jit(solution)/shard_map/ppermute | solution.py:507
  46.6 7.3 %collective-permute-start.13 = (f32[432,128]{1,0:T(8,128)S(1)}, f32[432,128]{1,0:T(8,128)S(1)}, u32[]{:S(2)}, u32[]{:S(2)}) collective-permute-start(f32[432,128]{1,0:T(8,128)S(1)} %shard_map.82.refs_12_.refs_0_), channel_id=1, source_target_pairs={{0,8},{1,9},{2,10},{3,11},{4,12},{5,13},{6,14},{7,15},{8,0},{9,1},... | collective-permute-start | bytes 663560 | tf_op jit(solution)/shard_map/ppermute | solution.py:507
  47.1 7.4 %collective-permute-start.12 = (f32[432,128]{1,0:T(8,128)S(1)}, f32[432,128]{1,0:T(8,128)S(1)}, u32[]{:S(2)}, u32[]{:S(2)}) collective-permute-start(f32[432,128]{1,0:T(8,128)S(1)} %shard_map.82.refs_12_.refs_0_), channel_id=1, source_target_pairs={{0,4},{1,5},{2,6},{3,7},{4,0},{5,1},{6,2},{7,3},{8,12},{9,13},{10,... | collective-permute-start | bytes 663560 | tf_op jit(solution)/shard_map/ppermute | solution.py:507
  54.6 9.4 %collective-permute-start.17 = (f32[432,128]{1,0:T(8,128)S(1)}, f32[432,128]{1,0:T(8,128)S(1)}, u32[]{:S(2)}, u32[]{:S(2)}) collective-permute-start(f32[432,128]{1,0:T(8,128)S(1)} %shard_map.84.refs_10_.refs_0_), channel_id=1, source_target_pairs={{0,3},{1,2},{2,1},{3,0},{4,7},{5,6},{6,5},{7,4},{8,11},{9,10},{10,... | collective-permute-start | bytes 663560 | tf_op jit(solution)/shard_map/ppermute | solution.py:507
  57.3 6.7 %collective-permute-start.16 = (f32[432,128]{1,0:T(8,128)S(1)}, f32[432,128]{1,0:T(8,128)S(1)}, u32[]{:S(2)}, u32[]{:S(2)}) collective-permute-start(f32[432,128]{1,0:T(8,128)S(1)} %shard_map.84.refs_10_.refs_0_), channel_id=1, source_target_pairs={{0,2},{1,3},{2,0},{3,1},{4,6},{5,7},{6,4},{7,5},{8,10},{9,11},{10,... | collective-permute-start | bytes 663560 | tf_op jit(solution)/shard_map/ppermute | solution.py:507
  57.5 6.5 %collective-permute-start.15 = (f32[432,128]{1,0:T(8,128)S(1)}, f32[432,128]{1,0:T(8,128)S(1)}, u32[]{:S(2)}, u32[]{:S(2)}) collective-permute-start(f32[432,128]{1,0:T(8,128)S(1)} %shard_map.84.refs_10_.refs_0_), channel_id=1, source_target_pairs={{0,1},{1,0},{2,3},{3,2},{4,5},{5,4},{6,7},{7,6},{8,9},{9,8},{10,11... | collective-permute-start | bytes 663560 | tf_op jit(solution)/shard_map/ppermute | solution.py:507
  64.1 13.0 %collective-permute-start.21 = (f32[432,128]{1,0:T(8,128)S(1)}, f32[432,128]{1,0:T(8,128)S(1)}, u32[]{:S(2)}, u32[]{:S(2)}) collective-permute-start(f32[432,128]{1,0:T(8,128)S(1)} %shard_map.86.refs_12_.refs_0_), channel_id=1, source_target_pairs={{0,16},{16,0},{32,48},{48,32},{64,80},{80,64},{96,112},{112,96},{1... | collective-permute-start | bytes 663560 | tf_op jit(solution)/shard_map/ppermute | solution.py:638
  67.5 9.6 %collective-permute-start.20 = (f32[432,128]{1,0:T(8,128)S(1)}, f32[432,128]{1,0:T(8,128)S(1)}, u32[]{:S(2)}, u32[]{:S(2)}) collective-permute-start(f32[432,128]{1,0:T(8,128)S(1)} %shard_map.86.refs_12_.refs_0_), channel_id=1, source_target_pairs={{0,96},{1,97},{2,98},{3,99},{4,100},{5,101},{6,102},{7,103},{8,104... | collective-permute-start | bytes 663560 | tf_op jit(solution)/shard_map/ppermute | solution.py:507
  70.2 7.0 %collective-permute-start.19 = (f32[432,128]{1,0:T(8,128)S(1)}, f32[432,128]{1,0:T(8,128)S(1)}, u32[]{:S(2)}, u32[]{:S(2)}) collective-permute-start(f32[432,128]{1,0:T(8,128)S(1)} %shard_map.86.refs_12_.refs_0_), channel_id=1, source_target_pairs={{0,64},{1,65},{2,66},{3,67},{4,68},{5,69},{6,70},{7,71},{8,72},{9,... | collective-permute-start | bytes 663560 | tf_op jit(solution)/shard_map/ppermute | solution.py:507
  70.2 7.0 %collective-permute-start.18 = (f32[432,128]{1,0:T(8,128)S(1)}, f32[432,128]{1,0:T(8,128)S(1)}, u32[]{:S(2)}, u32[]{:S(2)}) collective-permute-start(f32[432,128]{1,0:T(8,128)S(1)} %shard_map.86.refs_12_.refs_0_), channel_id=1, source_target_pairs={{0,32},{1,33},{2,34},{3,35},{4,36},{5,37},{6,38},{7,39},{8,40},{9,... | collective-permute-start | bytes 663560 | tf_op jit(solution)/shard_map/ppermute | solution.py:507
  77.2 2.8 %collective-permute-start.22 = (f32[1296,128]{1,0:T(8,128)S(1)}, f32[1296,128]{1,0:T(8,128)S(1)}, u32[]{:S(2)}, u32[]{:S(2)}) collective-permute-start(f32[1296,128]{1,0:T(8,128)S(1)} %shard_map.88.refs_1_.refs_2_), channel_id=1, source_target_pairs={{0,16},{16,0},{32,48},{48,32},{64,80},{80,64},{96,112},{112,96},{1... | collective-permute-start | bytes 1990664 | tf_op jit(solution)/shard_map/ppermute | solution.py:641

commit v8 on v7

--- a/solution.py
+++ b/solution.py
@@ -70,6 +70,10 @@
     lax.fori_loop(0, X // E, one, 0)
 
 
+def first_kernel(o_ref):
+    o_ref[...] = jnp.zeros_like(o_ref)
+
+
 def mask_kernel(occ_ref, mask_ref):
     for brick in range(X // E):
         mask_ref[brick] = jnp.where(brick_flags(occ_ref, brick), 1.0, 0.0).astype(BF16)
@@ -89,9 +93,13 @@
 def prepare(occupancy, features, cotangent):
     slabs = shape((X + 2, Y, Z, C), BF16)
     own_cost = pl.CostEstimate(flops=1000, bytes_accessed=1000, transcendentals=0)
+    lead = small_kernel(first_kernel, shape((8, C), F32), [], flops=10**10)
     mask = small_kernel(
-        mask_kernel, shape((X // E, Y, Z, C), BF16), [jnp.transpose(occupancy, (1, 2, 0))], specs=[SMEM],
-        flops=10**10,
+        mask_kernel,
+        shape((X // E, Y, Z, C), BF16),
+        [jnp.transpose(occupancy, (1, 2, 0))],
+        [lead],
+        specs=[SMEM],
     )
     fields, *given = pl.pallas_call(
         prepare_x_kernel,

time: 81.2 us -> 79.8 us (0.983)
  local copies, waits for them, and re-layouts: 2.35 us -> 0.99 us
    unnamed x8, local copies, waits for them, and re-layouts: 2.35 us -> 0.99 us
    pallas_call x11 -> x12, Pallas kernels: 2.68 us -> 2.67 us  [small_kernel(): pl.pallas_call(run, in_specs=(specs or [VMEM] * count) + [ANY] * len(ties...]
  transfers between devices with their start and end apart: 23 -> 23, of which waited for: 6 -> 6; matrix products, arithmetic and copies ran while one was open for 0% -> 0% of each run, Pallas kernels for 46% -> 47%
where the time goes in v8:
time: 79.8 us; the launch traced here: 79.7 us
  Pallas kernels  43 us (54%)
  starting transfers between devices  32.4 us (41%)
  waiting for transfers between devices  2.16 us (3%)
  between operations  1.17 us (1%)
  local copies, waits for them, and re-layouts  0.99 us (1%)
    pallas_call x5, Pallas kernels, conv_piece(): pl.pallas_call(plain if more else final, in_specs=specs, out_specs=[ANY]...  25.4 us
    ppermute x12, starting transfers between devices, exchange(): lax.ppermute(value, ('gx', 'gy', 'gz'), pairs(turn, step))  13.8 us
    ppermute x8, starting transfers between devices, shift(): lax.ppermute(value, axis, [(i, (i + step) % count) for i in range(count)])  13.1 us
    pallas_call x3, Pallas kernels, own_grad(): pl.pallas_call(lambda *refs: own_grad_kernel(first, spans, more, *refs),...  9.17 us
    ppermute x1, starting transfers between devices, body(): beside = lax.ppermute(chunk, 'gx', swap)  3.43 us
    pallas_call x12, Pallas kernels, small_kernel(): pl.pallas_call(run, in_specs=(specs or [VMEM] * count) + [ANY] * len(ties...  2.67 us
    pallas_call x3, Pallas kernels, write(): pl.pallas_call(kernel, in_specs=[VMEM] * len(arrays) + [ANY] * (len(opera...  2.51 us
  transfers between devices with their start and end apart: 23, of which 6 were waited for; matrix products, arithmetic and copies ran while one was open for 0% of the time, Pallas kernels for 47%

profile of v8, /device:TPU:1, one launch (start us, length us, event | category | flops | bytes accessed | tf_op | source)
XLA Modules:
  0.0 79.7 jit_solution(10180535710980922644)
XLA Ops:
  0.7 0.6 copy-done.3
  2.2 0.9 %shard_map.69 = (bf16[34,16,16,128]{3,2,1,0:T(8,128)(2,1)S(1)}, bf16[1,32,16,128]{3,2,1,0:T(8,128)(2,1)S(1)}, bf16[1,32,16,128]{3,2,1,0:T(8,128)(2,1)S(1)}, bf16...) custom-call(bf16[32,16,16,128]{3,2,1,0:T(8,128)(2,1)S(1)} %copy-done, ...), custom_call_target="tpu_custom_call" | custom-call | flops 1000 | bytes 1000 | tf_op jit(solution)/shard_map/pallas_call | solution.py:104
  3.2 0.9 %shard_map.70 = (bf16[34,16,16,128]{3,2,1,0:T(8,128)(2,1)S(1)}, bf16[2,32,16,128]{3,2,1,0:T(8,128)(2,1)S(1)}, bf16[2,32,16,128]{3,2,1,0:T(8,128)(2,1)S(1)}, bf16...) custom-call(bf16[32,16,16,128]{3,2,1,0:T(8,128)(2,1)S(1)} %copy-done.1, ...), custom_call_target="tpu_custom_call" | custom-call | flops 1000 | bytes 1000 | tf_op jit(solution)/shard_map/pallas_call | solution.py:112
  4.1 2.1 %collective-permute-start.2 = (bf16[2,32,16,128]{3,2,1,0:T(8,128)(2,1)S(1)}, bf16[2,32,16,128]{3,2,1,0:T(8,128)(2,1)S(1)}, u32[]{:S(2)}, u32[]{:S(2)}) collective-permute-start(bf16[2,32,16,128]{3,2,1,0:T(8,128)(2,1)S(1)} %get-tuple-element.59.refs_2_), channel_id=1, source_target_pairs={{0,1},{1,2},{2,3},{3,0},{4,5},{5,6},{6,7},{7,4},{8,9},{9,10},{10,1... | collective-permute-start | bytes 786440 | tf_op jit(solution)/shard_map/ppermute | solution.py:582
  6.2 1.3 %collective-permute-start.3 = (bf16[2,32,16,128]{3,2,1,0:T(8,128)(2,1)S(1)}, bf16[2,32,16,128]{3,2,1,0:T(8,128)(2,1)S(1)}, u32[]{:S(2)}, u32[]{:S(2)}) collective-permute-start(bf16[2,32,16,128]{3,2,1,0:T(8,128)(2,1)S(1)} %get-tuple-element.56.refs_2_.refs_1_), channel_id=1, source_target_pairs={{0,3},{1,0},{2,1},{3,2},{4,7},{5,4},{6,5},{7,6},{8,11},{9,8},{10,9... | collective-permute-start | bytes 786440 | tf_op jit(solution)/shard_map/ppermute | solution.py:582
  7.6 2.4 %shard_map.71.refs_2_ = f32[384,1152]{1,0:T(8,128)S(1)} custom-call(bf16[34,16,16,128]{3,2,1,0:T(8,128)(2,1)S(1)} %get-tuple-element.48.refs_0_.refs_1_, bf16[34,16,16,128]{3,2,1,0:T(8,128)(2,1)S(1)} %get-tuple-element.53.refs_1_.g_ref.refs_2_, bf16[2,32,16,128]{3,2,1,0:T(8,128)(2,1)S(1)} %get-tuple-element.56.refs_2_.refs_1_), custom_call_target="tpu_custom_call" | custom-call | flops 1811939328 | bytes 8388608 | tf_op jit(solution)/shard_map/pallas_call | solution.py:188
  10.1 1.5 %collective-permute-start = (bf16[2,32,16,128]{3,2,1,0:T(8,128)(2,1)S(1)}, bf16[2,32,16,128]{3,2,1,0:T(8,128)(2,1)S(1)}, u32[]{:S(2)}, u32[]{:S(2)}) collective-permute-start(bf16[2,32,16,128]{3,2,1,0:T(8,128)(2,1)S(1)} %get-tuple-element.57), channel_id=1, source_target_pairs={{0,4},{4,8},{8,12},{12,0},{1,5},{5,9},{9,13},{13,1},{2,6},{6,10},{... | collective-permute-start | bytes 786440 | tf_op jit(solution)/shard_map/ppermute | solution.py:582
  11.5 1.5 %collective-permute-start.1 = (bf16[2,32,16,128]{3,2,1,0:T(8,128)(2,1)S(1)}, bf16[2,32,16,128]{3,2,1,0:T(8,128)(2,1)S(1)}, u32[]{:S(2)}, u32[]{:S(2)}) collective-permute-start(bf16[2,32,16,128]{3,2,1,0:T(8,128)(2,1)S(1)} %get-tuple-element.58.refs_3_), channel_id=1, source_target_pairs={{0,12},{4,0},{8,4},{12,8},{1,13},{5,1},{9,5},{13,9},{2,14},{6,2},{... | collective-permute-start | bytes 786440 | tf_op jit(solution)/shard_map/ppermute | solution.py:582
  13.1 2.3 %shard_map.73.refs_2_.refs_0_ = f32[384,1152]{1,0:T(8,128)S(1)} custom-call(bf16[34,16,16,128]{3,2,1,0:T(8,128)(2,1)S(1)} %get-tuple-element.48.refs_0_.refs_1_, bf16[34,16,16,128]{3,2,1,0:T(8,128)(2,1)S(1)} %get-tuple-element.53.refs_1_.g_ref.refs_2_, f32[384,1152]{1,0:T(8,128)S(1)} %shard_map.71.refs_2_, bf16[2,32,16,128]{3,2,1,0:T(8,128)(2,1)S(1)} %get-tuple-element.58.refs_3_), custom_call_target="tpu_custom_call" | custom-call | flops 1811939328 | bytes 8388608 | tf_op jit(solution)/shard_map/pallas_call | solution.py:188
  15.6 2.7 %collective-permute-start.5 = (bf16[2,2,32,128]{3,2,1,0:T(8,128)(2,1)S(1)}, bf16[2,2,32,128]{3,2,1,0:T(8,128)(2,1)S(1)}, u32[]{:S(2)}, u32[]{:S(2)}) collective-permute-start(bf16[2,2,32,128]{3,2,1,0:T(8,128)(2,1)S(1)} %get-tuple-element.61.refs_1_.refs_5_), channel_id=1, source_target_pairs={{0,12},{4,0},{8,4},{12,8},{1,13},{5,1},{9,5},{13,9},{2,14},{6,2},{... | collective-permute-start | bytes 98312 | tf_op jit(solution)/shard_map/ppermute | solution.py:582
  19.4 0.7 collective-permute-done.4.refs_6_.elo
  20.6 3.9 %collective-permute-start.7 = (bf16[2,21,16,128]{3,2,1,0:T(8,128)(2,1)S(1)}, bf16[2,21,16,128]{3,2,1,0:T(8,128)(2,1)S(1)}, u32[]{:S(2)}, u32[]{:S(2)}) collective-permute-start(bf16[2,21,16,128]{3,2,1,0:T(8,128)(2,1)S(1)} %get-tuple-element.68), channel_id=1, source_target_pairs={{0,16},{16,32},{32,48},{48,64},{64,80},{80,96},{96,112},{112,0},{1... | collective-permute-start | bytes 516104 | tf_op jit(solution)/shard_map/ppermute | solution.py:582
  24.5 4.4 %shard_map.78.own_ref = f32[384,1152]{1,0:T(8,128)S(1)} custom-call(bf16[34,16,16,128]{3,2,1,0:T(8,128)(2,1)S(1)} %get-tuple-element.48.refs_0_.refs_1_, bf16[34,16,16,128]{3,2,1,0:T(8,128)(2,1)S(1)} %get-tuple-element.53.refs_1_.g_ref.refs_2_, f32[384,1152]{1,0:T(8,128)S(1)} %shard_map.76.refs_9_.refs_2_, bf16[2,21,16,128]{3,2,1,0:T(8,128)(2,1)S(1)} %get-tuple-element.67.refs_3_), custom_call_target="tpu_custom_call" | custom-call | flops 3623878656 | bytes 8388608 | tf_op jit(solution)/shard_map/pallas_call | solution.py:188
  29.4 1.4 %shard_map.79 = (f32[1728,128]{1,0:T(8,128)S(1)}, f32[1728,128]{1,0:T(8,128)S(1)}) custom-call(f32[384,1152]{1,0:T(8,128)S(1)} %shard_map.78.own_ref, bf16[34,16,16,128]{3,2,1,0:T(8,128)(2,1)S(1)} %get-tuple-element.53.refs_1_.g_ref.refs_2_, bf16[2,32,16,128]{3,2,1,0:T(8,128)(2,1)S(1)} %get-tuple-element.54.refs_0_.gylo, ...), custom_call_target="tpu_custom_call" | custom-call | flops 679477248 | bytes 6291456 | tf_op jit(solution)/shard_map/pallas_call | solution.py:258
  30.7 1.1 %collective-permute-start.8 = (f32[1728,128]{1,0:T(8,128)S(1)}, f32[1728,128]{1,0:T(8,128)S(1)}, u32[]{:S(2)}, u32[]{:S(2)}) collective-permute-start(f32[1728,128]{1,0:T(8,128)S(1)} %get-tuple-element.69.refs_9_), channel_id=1, source_target_pairs={{0,16},{16,0},{32,48},{48,32},{64,80},{80,64},{96,112},{112,96},{1... | collective-permute-start | bytes 2654216 | tf_op jit(solution)/shard_map/ppermute | solution.py:635
  31.8 2.0 %shard_map.80 = (bf16[32,16,16,128]{3,2,1,0:T(8,128)(2,1)}, f32[2,256,128]{2,1,0:T(8,128)S(1)}, bf16[3,4,18,16,128]{4,3,2,1,0:T(8,128)(2,1)S(1)}, bf16[4,16,16,128]{3,2,1,0:T(8,128)(2,1)S(1)}) custom-call(bf16[4,16,16,128]{3,2,1,0:T(8,128)(2,1)S(1)} %shard_map.68.mask_ref.refs_0_, bf16[34,16,16,128]{3,2,1,0:T(8,128)(2,1)S(1)} %get-tuple-element.48.refs_0_.refs_1_, ...), custom_call_target="tpu_custom_call" | custom-call | flops 905969664 | bytes 2097152 | tf_op jit(solution)/shard_map/pallas_call | solution.py:428
  33.9 1.9 %collective-permute-start.10 = (f32[432,128]{1,0:T(8,128)S(1)}, f32[432,128]{1,0:T(8,128)S(1)}, u32[]{:S(2)}, u32[]{:S(2)}) collective-permute-start(f32[432,128]{1,0:T(8,128)S(1)} %get-tuple-element.80), channel_id=1, source_target_pairs={{0,64},{1,65},{2,66},{3,67},{4,68},{5,69},{6,70},{7,71},{8,72},{9,... | collective-permute-start | bytes 663560 | tf_op jit(solution)/shard_map/ppermute | solution.py:515
  35.9 1.2 %collective-permute-start.11 = (f32[432,128]{1,0:T(8,128)S(1)}, f32[432,128]{1,0:T(8,128)S(1)}, u32[]{:S(2)}, u32[]{:S(2)}) collective-permute-start(f32[432,128]{1,0:T(8,128)S(1)} %get-tuple-element.81), channel_id=1, source_target_pairs={{0,96},{1,97},{2,98},{3,99},{4,100},{5,101},{6,102},{7,103},{8,104... | collective-permute-start | bytes 663560 | tf_op jit(solution)/shard_map/ppermute | solution.py:515
  37.5 5.8 %shard_map.82 = (bf16[32,16,16,128]{3,2,1,0:T(8,128)(2,1)}, f32[2,256,128]{2,1,0:T(8,128)S(1)}, bf16[3,4,18,16,128]{4,3,2,1,0:T(8,128)(2,1)S(1)}, bf16[4,16,16,128]{3,2,1,0:T(8,128)(2,1)S(1)}) custom-call(bf16[4,16,16,128]{3,2,1,0:T(8,128)(2,1)S(1)} %shard_map.68.mask_ref.refs_0_, ...), custom_call_target="tpu_custom_call", output_to_operand_aliasing={{0}: (12, {})} | custom-call | flops 3623878656 | bytes 2097152 | tf_op jit(solution)/shard_map/pallas_call | solution.py:428
  43.6 1.6 %collective-permute-start.14 = (f32[432,128]{1,0:T(8,128)S(1)}, f32[432,128]{1,0:T(8,128)S(1)}, u32[]{:S(2)}, u32[]{:S(2)}) collective-permute-start(f32[432,128]{1,0:T(8,128)S(1)} %shard_map.83.refs_12_.refs_0_), channel_id=1, source_target_pairs={{0,12},{1,13},{2,14},{3,15},{4,8},{5,9},{6,10},{7,11},{8,4},{9,5},... | collective-permute-start | bytes 663560 | tf_op jit(solution)/shard_map/ppermute | solution.py:515
  45.8 1.4 %collective-permute-start.12 = (f32[432,128]{1,0:T(8,128)S(1)}, f32[432,128]{1,0:T(8,128)S(1)}, u32[]{:S(2)}, u32[]{:S(2)}) collective-permute-start(f32[432,128]{1,0:T(8,128)S(1)} %shard_map.83.refs_12_.refs_0_), channel_id=1, source_target_pairs={{0,4},{1,5},{2,6},{3,7},{4,0},{5,1},{6,2},{7,3},{8,12},{9,13},{10,... | collective-permute-start | bytes 663560 | tf_op jit(solution)/shard_map/ppermute | solution.py:515
  47.2 5.3 %shard_map.84 = (bf16[32,16,16,128]{3,2,1,0:T(8,128)(2,1)}, f32[2,256,128]{2,1,0:T(8,128)S(1)}, bf16[3,4,18,16,128]{4,3,2,1,0:T(8,128)(2,1)S(1)}) custom-call(bf16[4,16,16,128]{3,2,1,0:T(8,128)(2,1)S(1)} %shard_map.68.mask_ref.refs_0_, bf16[34,16,16,128]{3,2,1,0:T(8,128)(2,1)S(1)} %get-tuple-element.48.refs_0_.refs_1_, ...), custom_call_target="tpu_custom_call", output_to_operand_aliasing={{0}: (13, {})} | custom-call | flops 2717908992 | bytes 2097152 | tf_op jit(solution)/shard_map/pallas_call | solution.py:428
  52.5 0.7 collective-permute-done.12.refs_1_
  53.3 2.7 %collective-permute-start.17 = (f32[432,128]{1,0:T(8,128)S(1)}, f32[432,128]{1,0:T(8,128)S(1)}, u32[]{:S(2)}, u32[]{:S(2)}) collective-permute-start(f32[432,128]{1,0:T(8,128)S(1)} %shard_map.85.refs_10_.refs_0_), channel_id=1, source_target_pairs={{0,3},{1,2},{2,1},{3,0},{4,7},{5,6},{6,5},{7,4},{8,11},{9,10},{10,... | collective-permute-start | bytes 663560 | tf_op jit(solution)/shard_map/ppermute | solution.py:515
  56.6 6.0 %shard_map.86 = (bf16[32,16,16,128]{3,2,1,0:T(8,128)(2,1)}, f32[2,256,128]{2,1,0:T(8,128)S(1)}, bf16[3,4,18,16,128]{4,3,2,1,0:T(8,128)(2,1)S(1)}, bf16[4,16,16,128]{3,2,1,0:T(8,128)(2,1)S(1)}) custom-call(bf16[4,16,16,128]{3,2,1,0:T(8,128)(2,1)S(1)} %shard_map.68.mask_ref.refs_0_, bf16[34,16,16,128]{3,2,1,0:T(8,128)(2,1)S(1)} %get-tuple-element.48.refs_0_.refs_1_, ...), custom_call_target="tpu_custom_call" | custom-call | flops 3623878656 | bytes 2097152 | tf_op jit(solution)/shard_map/pallas_call | solution.py:428
  62.8 3.4 %collective-permute-start.21 = (f32[432,128]{1,0:T(8,128)S(1)}, f32[432,128]{1,0:T(8,128)S(1)}, u32[]{:S(2)}, u32[]{:S(2)}) collective-permute-start(f32[432,128]{1,0:T(8,128)S(1)} %shard_map.87.refs_12_.refs_0_), channel_id=1, source_target_pairs={{0,16},{16,0},{32,48},{48,32},{64,80},{80,64},{96,112},{112,96},{1... | collective-permute-start | bytes 663560 | tf_op jit(solution)/shard_map/ppermute | solution.py:646
  66.2 2.6 %collective-permute-start.20 = (f32[432,128]{1,0:T(8,128)S(1)}, f32[432,128]{1,0:T(8,128)S(1)}, u32[]{:S(2)}, u32[]{:S(2)}) collective-permute-start(f32[432,128]{1,0:T(8,128)S(1)} %shard_map.87.refs_12_.refs_0_), channel_id=1, source_target_pairs={{0,96},{1,97},{2,98},{3,99},{4,100},{5,101},{6,102},{7,103},{8,104... | collective-permute-start | bytes 663560 | tf_op jit(solution)/shard_map/ppermute | solution.py:515
  69.4 6.3 %shard_map.88 = (bf16[32,16,16,128]{3,2,1,0:T(8,128)(2,1)}, f32[8,128]{1,0:T(8,128)S(1)}) custom-call(bf16[4,16,16,128]{3,2,1,0:T(8,128)(2,1)S(1)} %shard_map.68.mask_ref.refs_0_, bf16[34,16,16,128]{3,2,1,0:T(8,128)(2,1)S(1)} %get-tuple-element.48.refs_0_.refs_1_, ...), custom_call_target="tpu_custom_call", output_to_operand_aliasing={{0}: (13, {})} | custom-call | flops 3623878656 | bytes 2097152 | tf_op jit(solution)/shard_map/pallas_call | solution.py:428
  75.9 1.0 %collective-permute-start.22 = (f32[1296,128]{1,0:T(8,128)S(1)}, f32[1296,128]{1,0:T(8,128)S(1)}, u32[]{:S(2)}, u32[]{:S(2)}) collective-permute-start(f32[1296,128]{1,0:T(8,128)S(1)} %shard_map.89.refs_1_.refs_2_), channel_id=1, source_target_pairs={{0,16},{16,0},{32,48},{48,32},{64,80},{80,64},{96,112},{112,96},{1... | collective-permute-start | bytes 1990664 | tf_op jit(solution)/shard_map/ppermute | solution.py:649
  76.9 0.9 %shard_map.90.refs_2_ = f32[3456,128]{1,0:T(8,128)} custom-call(f32[432,128]{1,0:T(8,128)S(1)} %shard_map.87.refs_12_.refs_0_, f32[1296,128]{1,0:T(8,128)S(1)} %shard_map.89.refs_1_.refs_2_, f32[1296,128]{1,0:T(8,128)S(1)} %shard_map.89.refs_1_.refs_2_), custom_call_target="tpu_custom_call" | custom-call | flops 1000 | bytes 1048576 | tf_op jit(solution)/shard_map/pallas_call | solution.py:562
  77.8 0.7 shard_map.91.refs_2_
  78.6 0.9 %shard_map.92 = f32[3456,128]{1,0:T(8,128)} custom-call(f32[1296,128]{1,0:T(8,128)S(1)} %collective-permute-done.22.refs_0_, f32[1296,128]{1,0:T(8,128)S(1)} %shard_map.89.refs_1_.refs_2_, f32[3456,128]{1,0:T(8,128)} %shard_map.91.refs_2_), custom_call_target="tpu_custom_call", output_to_operand_aliasing={{}: (2, {})} | custom-call | flops 1000 | bytes 1048576 | tf_op jit(solution)/shard_map/pallas_call | solution.py:562
  (48 shorter events, 6.2 us)
Async XLA Ops:
  0.6 0.7 copy-start.3
  0.6 1.6 %copy-start = (bf16[32,16,16,128]{3,2,1,0:T(8,128)(2,1)S(1)}, bf16[32,16,16,128]{3,2,1,0:T(8,128)(2,1)}, u32[]{:S(2)}) copy-start(bf16[32,16,16,128]{3,2,1,0:T(8,128)(2,1)} %f_ref.1) | copy-start | bytes 6291460
  0.7 2.5 %copy-start.1 = (bf16[32,16,16,128]{3,2,1,0:T(8,128)(2,1)S(1)}, bf16[32,16,16,128]{3,2,1,0:T(8,128)(2,1)}, u32[]{:S(2)}) copy-start(bf16[32,16,16,128]{3,2,1,0:T(8,128)(2,1)} %c_ref.1) | copy-start | bytes 6291460
  4.1 11.3 %collective-permute-start.2 = (bf16[2,32,16,128]{3,2,1,0:T(8,128)(2,1)S(1)}, bf16[2,32,16,128]{3,2,1,0:T(8,128)(2,1)S(1)}, u32[]{:S(2)}, u32[]{:S(2)}) collective-permute-start(bf16[2,32,16,128]{3,2,1,0:T(8,128)(2,1)S(1)} %get-tuple-element.59.refs_2_), channel_id=1, source_target_pairs={{0,1},{1,2},{2,3},{3,0},{4,5},{5,6},{6,7},{7,4},{8,9},{9,10},{10,1... | collective-permute-start | bytes 786440 | tf_op jit(solution)/shard_map/ppermute | solution.py:582
  6.2 9.2 %collective-permute-start.3 = (bf16[2,32,16,128]{3,2,1,0:T(8,128)(2,1)S(1)}, bf16[2,32,16,128]{3,2,1,0:T(8,128)(2,1)S(1)}, u32[]{:S(2)}, u32[]{:S(2)}) collective-permute-start(bf16[2,32,16,128]{3,2,1,0:T(8,128)(2,1)S(1)} %get-tuple-element.56.refs_2_.refs_1_), channel_id=1, source_target_pairs={{0,3},{1,0},{2,1},{3,2},{4,7},{5,4},{6,5},{7,6},{8,11},{9,8},{10,9... | collective-permute-start | bytes 786440 | tf_op jit(solution)/shard_map/ppermute | solution.py:582
  10.1 9.3 %collective-permute-start = (bf16[2,32,16,128]{3,2,1,0:T(8,128)(2,1)S(1)}, bf16[2,32,16,128]{3,2,1,0:T(8,128)(2,1)S(1)}, u32[]{:S(2)}, u32[]{:S(2)}) collective-permute-start(bf16[2,32,16,128]{3,2,1,0:T(8,128)(2,1)S(1)} %get-tuple-element.57), channel_id=1, source_target_pairs={{0,4},{4,8},{8,12},{12,0},{1,5},{5,9},{9,13},{13,1},{2,6},{6,10},{... | collective-permute-start | bytes 786440 | tf_op jit(solution)/shard_map/ppermute | solution.py:582
  11.5 7.8 %collective-permute-start.1 = (bf16[2,32,16,128]{3,2,1,0:T(8,128)(2,1)S(1)}, bf16[2,32,16,128]{3,2,1,0:T(8,128)(2,1)S(1)}, u32[]{:S(2)}, u32[]{:S(2)}) collective-permute-start(bf16[2,32,16,128]{3,2,1,0:T(8,128)(2,1)S(1)} %get-tuple-element.58.refs_3_), channel_id=1, source_target_pairs={{0,12},{4,0},{8,4},{12,8},{1,13},{5,1},{9,5},{13,9},{2,14},{6,2},{... | collective-permute-start | bytes 786440 | tf_op jit(solution)/shard_map/ppermute | solution.py:582
  15.4 2.9 %copy-start.2 = (bf16[3,3,3,128,128]{4,3,2,1,0:T(8,128)(2,1)S(1)}, bf16[3,3,3,128,128]{4,3,2,1,0:T(8,128)(2,1)}, u32[]{:S(2)}) copy-start(bf16[3,3,3,128,128]{4,3,2,1,0:T(8,128)(2,1)} %param.6) | copy-start | bytes 2654212
  15.6 4.5 %collective-permute-start.4 = (bf16[2,2,32,128]{3,2,1,0:T(8,128)(2,1)S(1)}, bf16[2,2,32,128]{3,2,1,0:T(8,128)(2,1)S(1)}, u32[]{:S(2)}, u32[]{:S(2)}) collective-permute-start(bf16[2,2,32,128]{3,2,1,0:T(8,128)(2,1)S(1)} %get-tuple-element.60), channel_id=1, source_target_pairs={{0,4},{4,8},{8,12},{12,0},{1,5},{5,9},{9,13},{13,1},{2,6},{6,10},{... | collective-permute-start | bytes 98312 | tf_op jit(solution)/shard_map/ppermute | solution.py:582
  15.6 4.4 %collective-permute-start.5 = (bf16[2,2,32,128]{3,2,1,0:T(8,128)(2,1)S(1)}, bf16[2,2,32,128]{3,2,1,0:T(8,128)(2,1)S(1)}, u32[]{:S(2)}, u32[]{:S(2)}) collective-permute-start(bf16[2,2,32,128]{3,2,1,0:T(8,128)(2,1)S(1)} %get-tuple-element.61.refs_1_.refs_5_), channel_id=1, source_target_pairs={{0,12},{4,0},{8,4},{12,8},{1,13},{5,1},{9,5},{13,9},{2,14},{6,2},{... | collective-permute-start | bytes 98312 | tf_op jit(solution)/shard_map/ppermute | solution.py:582
  20.6 8.3 %collective-permute-start.7 = (bf16[2,21,16,128]{3,2,1,0:T(8,128)(2,1)S(1)}, bf16[2,21,16,128]{3,2,1,0:T(8,128)(2,1)S(1)}, u32[]{:S(2)}, u32[]{:S(2)}) collective-permute-start(bf16[2,21,16,128]{3,2,1,0:T(8,128)(2,1)S(1)} %get-tuple-element.68), channel_id=1, source_target_pairs={{0,16},{16,32},{32,48},{48,64},{64,80},{80,96},{96,112},{112,0},{1... | collective-permute-start | bytes 516104 | tf_op jit(solution)/shard_map/ppermute | solution.py:582
  24.5 4.8 %collective-permute-start.6 = (bf16[2,21,16,128]{3,2,1,0:T(8,128)(2,1)S(1)}, bf16[2,21,16,128]{3,2,1,0:T(8,128)(2,1)S(1)}, u32[]{:S(2)}, u32[]{:S(2)}) collective-permute-start(bf16[2,21,16,128]{3,2,1,0:T(8,128)(2,1)S(1)} %get-tuple-element.67.refs_3_), channel_id=1, source_target_pairs={{0,112},{16,0},{32,16},{48,32},{64,48},{80,64},{96,80},{112,96},{1... | collective-permute-start | bytes 516104 | tf_op jit(solution)/shard_map/ppermute | solution.py:582
  30.7 3.1 %collective-permute-start.8 = (f32[1728,128]{1,0:T(8,128)S(1)}, f32[1728,128]{1,0:T(8,128)S(1)}, u32[]{:S(2)}, u32[]{:S(2)}) collective-permute-start(f32[1728,128]{1,0:T(8,128)S(1)} %get-tuple-element.69.refs_9_), channel_id=1, source_target_pairs={{0,16},{16,0},{32,48},{48,32},{64,80},{80,64},{96,112},{112,96},{1... | collective-permute-start | bytes 2654216 | tf_op jit(solution)/shard_map/ppermute | solution.py:635
  33.9 9.4 %collective-permute-start.10 = (f32[432,128]{1,0:T(8,128)S(1)}, f32[432,128]{1,0:T(8,128)S(1)}, u32[]{:S(2)}, u32[]{:S(2)}) collective-permute-start(f32[432,128]{1,0:T(8,128)S(1)} %get-tuple-element.80), channel_id=1, source_target_pairs={{0,64},{1,65},{2,66},{3,67},{4,68},{5,69},{6,70},{7,71},{8,72},{9,... | collective-permute-start | bytes 663560 | tf_op jit(solution)/shard_map/ppermute | solution.py:515
  35.9 7.5 %collective-permute-start.11 = (f32[432,128]{1,0:T(8,128)S(1)}, f32[432,128]{1,0:T(8,128)S(1)}, u32[]{:S(2)}, u32[]{:S(2)}) collective-permute-start(f32[432,128]{1,0:T(8,128)S(1)} %get-tuple-element.81), channel_id=1, source_target_pairs={{0,96},{1,97},{2,98},{3,99},{4,100},{5,101},{6,102},{7,103},{8,104... | collective-permute-start | bytes 663560 | tf_op jit(solution)/shard_map/ppermute | solution.py:515
  37.1 6.5 %collective-permute-start.9 = (f32[432,128]{1,0:T(8,128)S(1)}, f32[432,128]{1,0:T(8,128)S(1)}, u32[]{:S(2)}, u32[]{:S(2)}) collective-permute-start(f32[432,128]{1,0:T(8,128)S(1)} %get-tuple-element.74.refs_11_), channel_id=1, source_target_pairs={{0,32},{1,33},{2,34},{3,35},{4,36},{5,37},{6,38},{7,39},{8,40},{9,... | collective-permute-start | bytes 663560 | tf_op jit(solution)/shard_map/ppermute | solution.py:515
  43.6 8.9 %collective-permute-start.14 = (f32[432,128]{1,0:T(8,128)S(1)}, f32[432,128]{1,0:T(8,128)S(1)}, u32[]{:S(2)}, u32[]{:S(2)}) collective-permute-start(f32[432,128]{1,0:T(8,128)S(1)} %shard_map.83.refs_12_.refs_0_), channel_id=1, source_target_pairs={{0,12},{1,13},{2,14},{3,15},{4,8},{5,9},{6,10},{7,11},{8,4},{9,5},... | collective-permute-start | bytes 663560 | tf_op jit(solution)/shard_map/ppermute | solution.py:515
  45.3 7.3 %collective-permute-start.13 = (f32[432,128]{1,0:T(8,128)S(1)}, f32[432,128]{1,0:T(8,128)S(1)}, u32[]{:S(2)}, u32[]{:S(2)}) collective-permute-start(f32[432,128]{1,0:T(8,128)S(1)} %shard_map.83.refs_12_.refs_0_), channel_id=1, source_target_pairs={{0,8},{1,9},{2,10},{3,11},{4,12},{5,13},{6,14},{7,15},{8,0},{9,1},... | collective-permute-start | bytes 663560 | tf_op jit(solution)/shard_map/ppermute | solution.py:515
  45.8 7.4 %collective-permute-start.12 = (f32[432,128]{1,0:T(8,128)S(1)}, f32[432,128]{1,0:T(8,128)S(1)}, u32[]{:S(2)}, u32[]{:S(2)}) collective-permute-start(f32[432,128]{1,0:T(8,128)S(1)} %shard_map.83.refs_12_.refs_0_), channel_id=1, source_target_pairs={{0,4},{1,5},{2,6},{3,7},{4,0},{5,1},{6,2},{7,3},{8,12},{9,13},{10,... | collective-permute-start | bytes 663560 | tf_op jit(solution)/shard_map/ppermute | solution.py:515
  53.3 9.4 %collective-permute-start.17 = (f32[432,128]{1,0:T(8,128)S(1)}, f32[432,128]{1,0:T(8,128)S(1)}, u32[]{:S(2)}, u32[]{:S(2)}) collective-permute-start(f32[432,128]{1,0:T(8,128)S(1)} %shard_map.85.refs_10_.refs_0_), channel_id=1, source_target_pairs={{0,3},{1,2},{2,1},{3,0},{4,7},{5,6},{6,5},{7,4},{8,11},{9,10},{10,... | collective-permute-start | bytes 663560 | tf_op jit(solution)/shard_map/ppermute | solution.py:515
  56.0 6.7 %collective-permute-start.16 = (f32[432,128]{1,0:T(8,128)S(1)}, f32[432,128]{1,0:T(8,128)S(1)}, u32[]{:S(2)}, u32[]{:S(2)}) collective-permute-start(f32[432,128]{1,0:T(8,128)S(1)} %shard_map.85.refs_10_.refs_0_), channel_id=1, source_target_pairs={{0,2},{1,3},{2,0},{3,1},{4,6},{5,7},{6,4},{7,5},{8,10},{9,11},{10,... | collective-permute-start | bytes 663560 | tf_op jit(solution)/shard_map/ppermute | solution.py:515
  56.2 6.5 %collective-permute-start.15 = (f32[432,128]{1,0:T(8,128)S(1)}, f32[432,128]{1,0:T(8,128)S(1)}, u32[]{:S(2)}, u32[]{:S(2)}) collective-permute-start(f32[432,128]{1,0:T(8,128)S(1)} %shard_map.85.refs_10_.refs_0_), channel_id=1, source_target_pairs={{0,1},{1,0},{2,3},{3,2},{4,5},{5,4},{6,7},{7,6},{8,9},{9,8},{10,11... | collective-permute-start | bytes 663560 | tf_op jit(solution)/shard_map/ppermute | solution.py:515
  62.8 13.0 %collective-permute-start.21 = (f32[432,128]{1,0:T(8,128)S(1)}, f32[432,128]{1,0:T(8,128)S(1)}, u32[]{:S(2)}, u32[]{:S(2)}) collective-permute-start(f32[432,128]{1,0:T(8,128)S(1)} %shard_map.87.refs_12_.refs_0_), channel_id=1, source_target_pairs={{0,16},{16,0},{32,48},{48,32},{64,80},{80,64},{96,112},{112,96},{1... | collective-permute-start | bytes 663560 | tf_op jit(solution)/shard_map/ppermute | solution.py:646
  66.2 9.6 %collective-permute-start.20 = (f32[432,128]{1,0:T(8,128)S(1)}, f32[432,128]{1,0:T(8,128)S(1)}, u32[]{:S(2)}, u32[]{:S(2)}) collective-permute-start(f32[432,128]{1,0:T(8,128)S(1)} %shard_map.87.refs_12_.refs_0_), channel_id=1, source_target_pairs={{0,96},{1,97},{2,98},{3,99},{4,100},{5,101},{6,102},{7,103},{8,104... | collective-permute-start | bytes 663560 | tf_op jit(solution)/shard_map/ppermute | solution.py:515
  68.8 7.0 %collective-permute-start.19 = (f32[432,128]{1,0:T(8,128)S(1)}, f32[432,128]{1,0:T(8,128)S(1)}, u32[]{:S(2)}, u32[]{:S(2)}) collective-permute-start(f32[432,128]{1,0:T(8,128)S(1)} %shard_map.87.refs_12_.refs_0_), channel_id=1, source_target_pairs={{0,64},{1,65},{2,66},{3,67},{4,68},{5,69},{6,70},{7,71},{8,72},{9,... | collective-permute-start | bytes 663560 | tf_op jit(solution)/shard_map/ppermute | solution.py:515
  68.8 7.0 %collective-permute-start.18 = (f32[432,128]{1,0:T(8,128)S(1)}, f32[432,128]{1,0:T(8,128)S(1)}, u32[]{:S(2)}, u32[]{:S(2)}) collective-permute-start(f32[432,128]{1,0:T(8,128)S(1)} %shard_map.87.refs_12_.refs_0_), channel_id=1, source_target_pairs={{0,32},{1,33},{2,34},{3,35},{4,36},{5,37},{6,38},{7,39},{8,40},{9,... | collective-permute-start | bytes 663560 | tf_op jit(solution)/shard_map/ppermute | solution.py:515
  75.9 2.8 %collective-permute-start.22 = (f32[1296,128]{1,0:T(8,128)S(1)}, f32[1296,128]{1,0:T(8,128)S(1)}, u32[]{:S(2)}, u32[]{:S(2)}) collective-permute-start(f32[1296,128]{1,0:T(8,128)S(1)} %shard_map.89.refs_1_.refs_2_), channel_id=1, source_target_pairs={{0,16},{16,0},{32,48},{48,32},{64,80},{80,64},{96,112},{112,96},{1... | collective-permute-start | bytes 1990664 | tf_op jit(solution)/shard_map/ppermute | solution.py:649

commit v9 on v8

--- a/solution.py
+++ b/solution.py
@@ -511,8 +511,11 @@
 
 
 def exchange(turn, values):
-    steps = zip((1, 2, 3), values, strict=True)
-    return [lax.ppermute(value, ("gx", "gy", "gz"), pairs(turn, step)) for step, value in steps]
+    one, two, three = (
+        lax.ppermute(value, ("gx", "gy", "gz"), pairs(turn, step))
+        for step, value in zip((1, 2, 3), values, strict=True)
+    )
+    return [one, three, two]
 
 
 def deal(terms, ties):
@@ -530,8 +533,12 @@
     return small_kernel(kernel, [shape((rows, C), F32)] * 4, terms, ties)
 
 
-def sum_kernel(a, b, c, d, o):
-    o[...] = (a[...] + c[...]) + (b[...] + d[...])
+def scatter_sum_kernel(own, one, two, three, o):
+    o[...] = (own[...] + two[...]) + (one[...] + three[...])
+
+
+def sum_kernel(own, one, three, two, o):
+    o[...] = (own[...] + two[...]) + (one[...] + three[...])
 
 
 def write(sources, mine, target, tie):
@@ -635,10 +642,12 @@
     came = lax.ppermute(send, "gx", swap)
     ties = convolve(send)
     own, *parts = deal([keep, came], ties)
-    came = exchange(0, parts)
-    chunk, ties = own, convolve(parts[0])
+    one, three, two = exchange(0, parts)
+    ties = convolve(parts[0])
+    chunk = small_kernel(scatter_sum_kernel, shape(own.shape, F32), [own, one, two, three], ties)
     for turn in (1, 2):
-        chunk = small_kernel(sum_kernel, shape(chunk.shape, F32), [chunk, *came], ties)
+        if turn == 2:
+            chunk = small_kernel(sum_kernel, shape(chunk.shape, F32), [chunk, *came], ties)
         came = exchange(turn, [chunk] * 3)
         ties = convolve(chunk)
     chunk = small_kernel(sum_kernel, shape(chunk.shape, F32), [chunk, *came], ties)
@@ -647,9 +656,9 @@
     ties = convolve(chunk)
     joined = small_kernel(join_kernel, shape((3 * chunk.shape[0], C), F32), came, [beside, *ties])
     others = lax.ppermute(joined, "gx", swap)
-    full = write([(chunk, (0,)), (joined, (1, 2, 3))], True, None, joined)
+    full = write([(chunk, (0,)), (joined, (1, 3, 2))], True, None, joined)
     full = write([(beside, (0,))], False, full, joined)
-    full = write([(others, (1, 2, 3))], False, full, joined)
+    full = write([(others, (1, 3, 2))], False, full, joined)
     return (made[0], made[1], full.reshape(3, 3, 3, C, C))
 
 

time: 79.8 us -> 79 us (0.990)
  starting transfers between devices: 32.4 us -> 31.3 us
    ppermute x12, starting transfers between devices: 13.8 us -> 12.9 us  [exchange(): lax.ppermute(value, ('gx', 'gy', 'gz'), pairs(turn, step))]
where the time goes in v9:
time: 79 us; the launch traced here: 78.9 us
  Pallas kernels  43 us (54%)
  starting transfers between devices  31.3 us (40%)
  waiting for transfers between devices  2.44 us (3%)
  between operations  1.16 us (1%)
  local copies, waits for them, and re-layouts  0.99 us (1%)
    pallas_call x5, Pallas kernels, conv_piece(): pl.pallas_call(plain if more else final, in_specs=specs, out_specs=[ANY]...  25.4 us
    ppermute x8, starting transfers between devices, shift(): lax.ppermute(value, axis, [(i, (i + step) % count) for i in range(count)])  13.1 us
    ppermute x12, starting transfers between devices, exchange(): lax.ppermute(value, ('gx', 'gy', 'gz'), pairs(turn, step))  12.9 us
    pallas_call x3, Pallas kernels, own_grad(): pl.pallas_call(lambda *refs: own_grad_kernel(first, spans, more, *refs),...  9.17 us
    ppermute x1, starting transfers between devices, body(): beside = lax.ppermute(chunk, 'gx', swap)  2.75 us
    pallas_call x12, Pallas kernels, small_kernel(): pl.pallas_call(run, in_specs=(specs or [VMEM] * count) + [ANY] * len(ties...  2.67 us
    pallas_call x3, Pallas kernels, write(): pl.pallas_call(kernel, in_specs=[VMEM] * len(arrays) + [ANY] * (len(opera...  2.51 us
  transfers between devices with their start and end apart: 23, of which 6 were waited for; matrix products, arithmetic and copies ran while one was open for 0% of the time, Pallas kernels for 47%

profile of v9, /device:TPU:1, one launch (start us, length us, event | category | flops | bytes accessed | tf_op | source)
XLA Modules:
  0.0 78.9 jit_solution(10223760777231298806)
XLA Ops:
  2.2 0.9 %shard_map.69 = (bf16[34,16,16,128]{3,2,1,0:T(8,128)(2,1)S(1)}, bf16[1,32,16,128]{3,2,1,0:T(8,128)(2,1)S(1)}, bf16[1,32,16,128]{3,2,1,0:T(8,128)(2,1)S(1)}, bf16...) custom-call(bf16[32,16,16,128]{3,2,1,0:T(8,128)(2,1)S(1)} %copy-done, ...), custom_call_target="tpu_custom_call" | custom-call | flops 1000 | bytes 1000 | tf_op jit(solution)/shard_map/pallas_call | solution.py:104
  3.2 0.9 %shard_map.70 = (bf16[34,16,16,128]{3,2,1,0:T(8,128)(2,1)S(1)}, bf16[2,32,16,128]{3,2,1,0:T(8,128)(2,1)S(1)}, bf16[2,32,16,128]{3,2,1,0:T(8,128)(2,1)S(1)}, bf16...) custom-call(bf16[32,16,16,128]{3,2,1,0:T(8,128)(2,1)S(1)} %copy-done.1, ...), custom_call_target="tpu_custom_call" | custom-call | flops 1000 | bytes 1000 | tf_op jit(solution)/shard_map/pallas_call | solution.py:112
  4.1 2.1 %collective-permute-start.2 = (bf16[2,32,16,128]{3,2,1,0:T(8,128)(2,1)S(1)}, bf16[2,32,16,128]{3,2,1,0:T(8,128)(2,1)S(1)}, u32[]{:S(2)}, u32[]{:S(2)}) collective-permute-start(bf16[2,32,16,128]{3,2,1,0:T(8,128)(2,1)S(1)} %get-tuple-element.59.refs_2_), channel_id=1, source_target_pairs={{0,1},{1,2},{2,3},{3,0},{4,5},{5,6},{6,7},{7,4},{8,9},{9,10},{10,1... | collective-permute-start | bytes 786440 | tf_op jit(solution)/shard_map/ppermute | solution.py:589
  6.2 1.3 %collective-permute-start.3 = (bf16[2,32,16,128]{3,2,1,0:T(8,128)(2,1)S(1)}, bf16[2,32,16,128]{3,2,1,0:T(8,128)(2,1)S(1)}, u32[]{:S(2)}, u32[]{:S(2)}) collective-permute-start(bf16[2,32,16,128]{3,2,1,0:T(8,128)(2,1)S(1)} %get-tuple-element.56.refs_2_.refs_1_), channel_id=1, source_target_pairs={{0,3},{1,0},{2,1},{3,2},{4,7},{5,4},{6,5},{7,6},{8,11},{9,8},{10,9... | collective-permute-start | bytes 786440 | tf_op jit(solution)/shard_map/ppermute | solution.py:589
  7.6 2.4 %shard_map.71.refs_2_ = f32[384,1152]{1,0:T(8,128)S(1)} custom-call(bf16[34,16,16,128]{3,2,1,0:T(8,128)(2,1)S(1)} %get-tuple-element.48.refs_0_.refs_1_, bf16[34,16,16,128]{3,2,1,0:T(8,128)(2,1)S(1)} %get-tuple-element.53.refs_1_.g_ref.refs_2_, bf16[2,32,16,128]{3,2,1,0:T(8,128)(2,1)S(1)} %get-tuple-element.56.refs_2_.refs_1_), custom_call_target="tpu_custom_call" | custom-call | flops 1811939328 | bytes 8388608 | tf_op jit(solution)/shard_map/pallas_call | solution.py:188
  10.1 1.5 %collective-permute-start = (bf16[2,32,16,128]{3,2,1,0:T(8,128)(2,1)S(1)}, bf16[2,32,16,128]{3,2,1,0:T(8,128)(2,1)S(1)}, u32[]{:S(2)}, u32[]{:S(2)}) collective-permute-start(bf16[2,32,16,128]{3,2,1,0:T(8,128)(2,1)S(1)} %get-tuple-element.57), channel_id=1, source_target_pairs={{0,4},{4,8},{8,12},{12,0},{1,5},{5,9},{9,13},{13,1},{2,6},{6,10},{... | collective-permute-start | bytes 786440 | tf_op jit(solution)/shard_map/ppermute | solution.py:589
  11.5 1.5 %collective-permute-start.1 = (bf16[2,32,16,128]{3,2,1,0:T(8,128)(2,1)S(1)}, bf16[2,32,16,128]{3,2,1,0:T(8,128)(2,1)S(1)}, u32[]{:S(2)}, u32[]{:S(2)}) collective-permute-start(bf16[2,32,16,128]{3,2,1,0:T(8,128)(2,1)S(1)} %get-tuple-element.58.refs_3_), channel_id=1, source_target_pairs={{0,12},{4,0},{8,4},{12,8},{1,13},{5,1},{9,5},{13,9},{2,14},{6,2},{... | collective-permute-start | bytes 786440 | tf_op jit(solution)/shard_map/ppermute | solution.py:589
  13.1 2.3 %shard_map.73.refs_2_.refs_0_ = f32[384,1152]{1,0:T(8,128)S(1)} custom-call(bf16[34,16,16,128]{3,2,1,0:T(8,128)(2,1)S(1)} %get-tuple-element.48.refs_0_.refs_1_, bf16[34,16,16,128]{3,2,1,0:T(8,128)(2,1)S(1)} %get-tuple-element.53.refs_1_.g_ref.refs_2_, f32[384,1152]{1,0:T(8,128)S(1)} %shard_map.71.refs_2_, bf16[2,32,16,128]{3,2,1,0:T(8,128)(2,1)S(1)} %get-tuple-element.58.refs_3_), custom_call_target="tpu_custom_call" | custom-call | flops 1811939328 | bytes 8388608 | tf_op jit(solution)/shard_map/pallas_call | solution.py:188
  15.6 2.7 %collective-permute-start.5 = (bf16[2,2,32,128]{3,2,1,0:T(8,128)(2,1)S(1)}, bf16[2,2,32,128]{3,2,1,0:T(8,128)(2,1)S(1)}, u32[]{:S(2)}, u32[]{:S(2)}) collective-permute-start(bf16[2,2,32,128]{3,2,1,0:T(8,128)(2,1)S(1)} %get-tuple-element.61.refs_1_.refs_5_), channel_id=1, source_target_pairs={{0,12},{4,0},{8,4},{12,8},{1,13},{5,1},{9,5},{13,9},{2,14},{6,2},{... | collective-permute-start | bytes 98312 | tf_op jit(solution)/shard_map/ppermute | solution.py:589
  20.6 3.9 %collective-permute-start.7 = (bf16[2,21,16,128]{3,2,1,0:T(8,128)(2,1)S(1)}, bf16[2,21,16,128]{3,2,1,0:T(8,128)(2,1)S(1)}, u32[]{:S(2)}, u32[]{:S(2)}) collective-permute-start(bf16[2,21,16,128]{3,2,1,0:T(8,128)(2,1)S(1)} %get-tuple-element.68), channel_id=1, source_target_pairs={{0,16},{16,32},{32,48},{48,64},{64,80},{80,96},{96,112},{112,0},{1... | collective-permute-start | bytes 516104 | tf_op jit(solution)/shard_map/ppermute | solution.py:589
  24.5 4.4 %shard_map.78.own_ref = f32[384,1152]{1,0:T(8,128)S(1)} custom-call(bf16[34,16,16,128]{3,2,1,0:T(8,128)(2,1)S(1)} %get-tuple-element.48.refs_0_.refs_1_, bf16[34,16,16,128]{3,2,1,0:T(8,128)(2,1)S(1)} %get-tuple-element.53.refs_1_.g_ref.refs_2_, f32[384,1152]{1,0:T(8,128)S(1)} %shard_map.76.refs_9_.refs_2_, bf16[2,21,16,128]{3,2,1,0:T(8,128)(2,1)S(1)} %get-tuple-element.67.refs_3_), custom_call_target="tpu_custom_call" | custom-call | flops 3623878656 | bytes 8388608 | tf_op jit(solution)/shard_map/pallas_call | solution.py:188
  29.4 1.4 %shard_map.79 = (f32[1728,128]{1,0:T(8,128)S(1)}, f32[1728,128]{1,0:T(8,128)S(1)}) custom-call(f32[384,1152]{1,0:T(8,128)S(1)} %shard_map.78.own_ref, bf16[34,16,16,128]{3,2,1,0:T(8,128)(2,1)S(1)} %get-tuple-element.53.refs_1_.g_ref.refs_2_, bf16[2,32,16,128]{3,2,1,0:T(8,128)(2,1)S(1)} %get-tuple-element.54.refs_0_.gylo, ...), custom_call_target="tpu_custom_call" | custom-call | flops 679477248 | bytes 6291456 | tf_op jit(solution)/shard_map/pallas_call | solution.py:258
  30.7 1.1 %collective-permute-start.8 = (f32[1728,128]{1,0:T(8,128)S(1)}, f32[1728,128]{1,0:T(8,128)S(1)}, u32[]{:S(2)}, u32[]{:S(2)}) collective-permute-start(f32[1728,128]{1,0:T(8,128)S(1)} %get-tuple-element.69.refs_9_), channel_id=1, source_target_pairs={{0,16},{16,0},{32,48},{48,32},{64,80},{80,64},{96,112},{112,96},{1... | collective-permute-start | bytes 2654216 | tf_op jit(solution)/shard_map/ppermute | solution.py:642
  31.8 2.0 %shard_map.80 = (bf16[32,16,16,128]{3,2,1,0:T(8,128)(2,1)}, f32[2,256,128]{2,1,0:T(8,128)S(1)}, bf16[3,4,18,16,128]{4,3,2,1,0:T(8,128)(2,1)S(1)}, bf16[4,16,16,128]{3,2,1,0:T(8,128)(2,1)S(1)}) custom-call(bf16[4,16,16,128]{3,2,1,0:T(8,128)(2,1)S(1)} %shard_map.68.mask_ref.refs_0_, bf16[34,16,16,128]{3,2,1,0:T(8,128)(2,1)S(1)} %get-tuple-element.48.refs_0_.refs_1_, ...), custom_call_target="tpu_custom_call" | custom-call | flops 905969664 | bytes 2097152 | tf_op jit(solution)/shard_map/pallas_call | solution.py:428
  33.9 1.9 %collective-permute-start.10 = (f32[432,128]{1,0:T(8,128)S(1)}, f32[432,128]{1,0:T(8,128)S(1)}, u32[]{:S(2)}, u32[]{:S(2)}) collective-permute-start(f32[432,128]{1,0:T(8,128)S(1)} %get-tuple-element.80), channel_id=1, source_target_pairs={{0,64},{1,65},{2,66},{3,67},{4,68},{5,69},{6,70},{7,71},{8,72},{9,... | collective-permute-start | bytes 663560 | tf_op jit(solution)/shard_map/ppermute | solution.py:515
  35.9 1.2 %collective-permute-start.11 = (f32[432,128]{1,0:T(8,128)S(1)}, f32[432,128]{1,0:T(8,128)S(1)}, u32[]{:S(2)}, u32[]{:S(2)}) collective-permute-start(f32[432,128]{1,0:T(8,128)S(1)} %get-tuple-element.81), channel_id=1, source_target_pairs={{0,96},{1,97},{2,98},{3,99},{4,100},{5,101},{6,102},{7,103},{8,104... | collective-permute-start | bytes 663560 | tf_op jit(solution)/shard_map/ppermute | solution.py:515
  37.5 5.8 %shard_map.82 = (bf16[32,16,16,128]{3,2,1,0:T(8,128)(2,1)}, f32[2,256,128]{2,1,0:T(8,128)S(1)}, bf16[3,4,18,16,128]{4,3,2,1,0:T(8,128)(2,1)S(1)}, bf16[4,16,16,128]{3,2,1,0:T(8,128)(2,1)S(1)}) custom-call(bf16[4,16,16,128]{3,2,1,0:T(8,128)(2,1)S(1)} %shard_map.68.mask_ref.refs_0_, ...), custom_call_target="tpu_custom_call", output_to_operand_aliasing={{0}: (12, {})} | custom-call | flops 3623878656 | bytes 2097152 | tf_op jit(solution)/shard_map/pallas_call | solution.py:428
  43.6 1.9 %collective-permute-start.14 = (f32[432,128]{1,0:T(8,128)S(1)}, f32[432,128]{1,0:T(8,128)S(1)}, u32[]{:S(2)}, u32[]{:S(2)}) collective-permute-start(f32[432,128]{1,0:T(8,128)S(1)} %shard_map.83.refs_12_.refs_0_), channel_id=1, source_target_pairs={{0,8},{1,9},{2,10},{3,11},{4,12},{5,13},{6,14},{7,15},{8,0},{9,1},... | collective-permute-start | bytes 663560 | tf_op jit(solution)/shard_map/ppermute | solution.py:515
  45.6 0.9 %collective-permute-start.13 = (f32[432,128]{1,0:T(8,128)S(1)}, f32[432,128]{1,0:T(8,128)S(1)}, u32[]{:S(2)}, u32[]{:S(2)}) collective-permute-start(f32[432,128]{1,0:T(8,128)S(1)} %shard_map.83.refs_12_.refs_0_), channel_id=1, source_target_pairs={{0,12},{1,13},{2,14},{3,15},{4,8},{5,9},{6,10},{7,11},{8,4},{9,5},... | collective-permute-start | bytes 663560 | tf_op jit(solution)/shard_map/ppermute | solution.py:515
  46.6 5.3 %shard_map.84 = (bf16[32,16,16,128]{3,2,1,0:T(8,128)(2,1)}, f32[2,256,128]{2,1,0:T(8,128)S(1)}, bf16[3,4,18,16,128]{4,3,2,1,0:T(8,128)(2,1)S(1)}) custom-call(bf16[4,16,16,128]{3,2,1,0:T(8,128)(2,1)S(1)} %shard_map.68.mask_ref.refs_0_, bf16[34,16,16,128]{3,2,1,0:T(8,128)(2,1)S(1)} %get-tuple-element.48.refs_0_.refs_1_, ...), custom_call_target="tpu_custom_call", output_to_operand_aliasing={{0}: (13, {})} | custom-call | flops 2717908992 | bytes 2097152 | tf_op jit(solution)/shard_map/pallas_call | solution.py:428
  51.9 0.9 %collective-permute-done.13.refs_2_ = f32[432,128]{1,0:T(8,128)S(1)} collective-permute-done((f32[432,128]{1,0:T(8,128)S(1)}, f32[432,128]{1,0:T(8,128)S(1)}, u32[]{:S(2)}, u32[]{:S(2)}) %collective-permute-start.13) | collective-permute-done | bytes 221216 | tf_op jit(solution)/shard_map/ppermute | solution.py:515
  52.9 2.6 %collective-permute-start.17 = (f32[432,128]{1,0:T(8,128)S(1)}, f32[432,128]{1,0:T(8,128)S(1)}, u32[]{:S(2)}, u32[]{:S(2)}) collective-permute-start(f32[432,128]{1,0:T(8,128)S(1)} %shard_map.85.refs_10_.refs_0_), channel_id=1, source_target_pairs={{0,2},{1,3},{2,0},{3,1},{4,6},{5,7},{6,4},{7,5},{8,10},{9,11},{10,... | collective-permute-start | bytes 663560 | tf_op jit(solution)/shard_map/ppermute | solution.py:515
  55.5 1.0 %collective-permute-start.16 = (f32[432,128]{1,0:T(8,128)S(1)}, f32[432,128]{1,0:T(8,128)S(1)}, u32[]{:S(2)}, u32[]{:S(2)}) collective-permute-start(f32[432,128]{1,0:T(8,128)S(1)} %shard_map.85.refs_10_.refs_0_), channel_id=1, source_target_pairs={{0,3},{1,2},{2,1},{3,0},{4,7},{5,6},{6,5},{7,4},{8,11},{9,10},{10,... | collective-permute-start | bytes 663560 | tf_op jit(solution)/shard_map/ppermute | solution.py:515
  56.5 6.0 %shard_map.86 = (bf16[32,16,16,128]{3,2,1,0:T(8,128)(2,1)}, f32[2,256,128]{2,1,0:T(8,128)S(1)}, bf16[3,4,18,16,128]{4,3,2,1,0:T(8,128)(2,1)S(1)}, bf16[4,16,16,128]{3,2,1,0:T(8,128)(2,1)S(1)}) custom-call(bf16[4,16,16,128]{3,2,1,0:T(8,128)(2,1)S(1)} %shard_map.68.mask_ref.refs_0_, bf16[34,16,16,128]{3,2,1,0:T(8,128)(2,1)S(1)} %get-tuple-element.48.refs_0_.refs_1_, ...), custom_call_target="tpu_custom_call" | custom-call | flops 3623878656 | bytes 2097152 | tf_op jit(solution)/shard_map/pallas_call | solution.py:428
  62.6 2.7 %collective-permute-start.21 = (f32[432,128]{1,0:T(8,128)S(1)}, f32[432,128]{1,0:T(8,128)S(1)}, u32[]{:S(2)}, u32[]{:S(2)}) collective-permute-start(f32[432,128]{1,0:T(8,128)S(1)} %shard_map.87.refs_12_.refs_0_), channel_id=1, source_target_pairs={{0,16},{16,0},{32,48},{48,32},{64,80},{80,64},{96,112},{112,96},{1... | collective-permute-start | bytes 663560 | tf_op jit(solution)/shard_map/ppermute | solution.py:655
  65.3 1.4 %collective-permute-start.20 = (f32[432,128]{1,0:T(8,128)S(1)}, f32[432,128]{1,0:T(8,128)S(1)}, u32[]{:S(2)}, u32[]{:S(2)}) collective-permute-start(f32[432,128]{1,0:T(8,128)S(1)} %shard_map.87.refs_12_.refs_0_), channel_id=1, source_target_pairs={{0,64},{1,65},{2,66},{3,67},{4,68},{5,69},{6,70},{7,71},{8,72},{9,... | collective-permute-start | bytes 663560 | tf_op jit(solution)/shard_map/ppermute | solution.py:515
  66.8 1.1 %collective-permute-start.19 = (f32[432,128]{1,0:T(8,128)S(1)}, f32[432,128]{1,0:T(8,128)S(1)}, u32[]{:S(2)}, u32[]{:S(2)}) collective-permute-start(f32[432,128]{1,0:T(8,128)S(1)} %shard_map.87.refs_12_.refs_0_), channel_id=1, source_target_pairs={{0,96},{1,97},{2,98},{3,99},{4,100},{5,101},{6,102},{7,103},{8,104... | collective-permute-start | bytes 663560 | tf_op jit(solution)/shard_map/ppermute | solution.py:515
  68.1 6.3 %shard_map.88 = (bf16[32,16,16,128]{3,2,1,0:T(8,128)(2,1)}, f32[8,128]{1,0:T(8,128)S(1)}) custom-call(bf16[4,16,16,128]{3,2,1,0:T(8,128)(2,1)S(1)} %shard_map.68.mask_ref.refs_0_, bf16[34,16,16,128]{3,2,1,0:T(8,128)(2,1)S(1)} %get-tuple-element.48.refs_0_.refs_1_, ...), custom_call_target="tpu_custom_call", output_to_operand_aliasing={{0}: (13, {})} | custom-call | flops 3623878656 | bytes 2097152 | tf_op jit(solution)/shard_map/pallas_call | solution.py:428
  74.6 1.6 %collective-permute-start.22 = (f32[1296,128]{1,0:T(8,128)S(1)}, f32[1296,128]{1,0:T(8,128)S(1)}, u32[]{:S(2)}, u32[]{:S(2)}) collective-permute-start(f32[1296,128]{1,0:T(8,128)S(1)} %shard_map.89.refs_1_.refs_2_), channel_id=1, source_target_pairs={{0,16},{16,0},{32,48},{48,32},{64,80},{80,64},{96,112},{112,96},{1... | collective-permute-start | bytes 1990664 | tf_op jit(solution)/shard_map/ppermute | solution.py:658
  76.1 0.9 %shard_map.90.refs_2_ = f32[3456,128]{1,0:T(8,128)} custom-call(f32[432,128]{1,0:T(8,128)S(1)} %shard_map.87.refs_12_.refs_0_, f32[1296,128]{1,0:T(8,128)S(1)} %shard_map.89.refs_1_.refs_2_, f32[1296,128]{1,0:T(8,128)S(1)} %shard_map.89.refs_1_.refs_2_), custom_call_target="tpu_custom_call" | custom-call | flops 1000 | bytes 1048576 | tf_op jit(solution)/shard_map/pallas_call | solution.py:569
  77.1 0.7 shard_map.91.refs_2_
  77.8 0.9 %shard_map.92 = f32[3456,128]{1,0:T(8,128)} custom-call(f32[1296,128]{1,0:T(8,128)S(1)} %collective-permute-done.22.refs_0_, f32[1296,128]{1,0:T(8,128)S(1)} %shard_map.89.refs_1_.refs_2_, f32[3456,128]{1,0:T(8,128)} %shard_map.91.refs_2_), custom_call_target="tpu_custom_call", output_to_operand_aliasing={{}: (2, {})} | custom-call | flops 1000 | bytes 1048576 | tf_op jit(solution)/shard_map/pallas_call | solution.py:569
  (48 shorter events, 6.2 us)
Async XLA Ops:
  0.6 0.7 copy-start.3
  0.6 1.6 %copy-start = (bf16[32,16,16,128]{3,2,1,0:T(8,128)(2,1)S(1)}, bf16[32,16,16,128]{3,2,1,0:T(8,128)(2,1)}, u32[]{:S(2)}) copy-start(bf16[32,16,16,128]{3,2,1,0:T(8,128)(2,1)} %f_ref.1) | copy-start | bytes 6291460
  0.7 2.5 %copy-start.1 = (bf16[32,16,16,128]{3,2,1,0:T(8,128)(2,1)S(1)}, bf16[32,16,16,128]{3,2,1,0:T(8,128)(2,1)}, u32[]{:S(2)}) copy-start(bf16[32,16,16,128]{3,2,1,0:T(8,128)(2,1)} %c_ref.1) | copy-start | bytes 6291460
  4.1 11.3 %collective-permute-start.2 = (bf16[2,32,16,128]{3,2,1,0:T(8,128)(2,1)S(1)}, bf16[2,32,16,128]{3,2,1,0:T(8,128)(2,1)S(1)}, u32[]{:S(2)}, u32[]{:S(2)}) collective-permute-start(bf16[2,32,16,128]{3,2,1,0:T(8,128)(2,1)S(1)} %get-tuple-element.59.refs_2_), channel_id=1, source_target_pairs={{0,1},{1,2},{2,3},{3,0},{4,5},{5,6},{6,7},{7,4},{8,9},{9,10},{10,1... | collective-permute-start | bytes 786440 | tf_op jit(solution)/shard_map/ppermute | solution.py:589
  6.2 9.2 %collective-permute-start.3 = (bf16[2,32,16,128]{3,2,1,0:T(8,128)(2,1)S(1)}, bf16[2,32,16,128]{3,2,1,0:T(8,128)(2,1)S(1)}, u32[]{:S(2)}, u32[]{:S(2)}) collective-permute-start(bf16[2,32,16,128]{3,2,1,0:T(8,128)(2,1)S(1)} %get-tuple-element.56.refs_2_.refs_1_), channel_id=1, source_target_pairs={{0,3},{1,0},{2,1},{3,2},{4,7},{5,4},{6,5},{7,6},{8,11},{9,8},{10,9... | collective-permute-start | bytes 786440 | tf_op jit(solution)/shard_map/ppermute | solution.py:589
  10.1 9.3 %collective-permute-start = (bf16[2,32,16,128]{3,2,1,0:T(8,128)(2,1)S(1)}, bf16[2,32,16,128]{3,2,1,0:T(8,128)(2,1)S(1)}, u32[]{:S(2)}, u32[]{:S(2)}) collective-permute-start(bf16[2,32,16,128]{3,2,1,0:T(8,128)(2,1)S(1)} %get-tuple-element.57), channel_id=1, source_target_pairs={{0,4},{4,8},{8,12},{12,0},{1,5},{5,9},{9,13},{13,1},{2,6},{6,10},{... | collective-permute-start | bytes 786440 | tf_op jit(solution)/shard_map/ppermute | solution.py:589
  11.5 7.8 %collective-permute-start.1 = (bf16[2,32,16,128]{3,2,1,0:T(8,128)(2,1)S(1)}, bf16[2,32,16,128]{3,2,1,0:T(8,128)(2,1)S(1)}, u32[]{:S(2)}, u32[]{:S(2)}) collective-permute-start(bf16[2,32,16,128]{3,2,1,0:T(8,128)(2,1)S(1)} %get-tuple-element.58.refs_3_), channel_id=1, source_target_pairs={{0,12},{4,0},{8,4},{12,8},{1,13},{5,1},{9,5},{13,9},{2,14},{6,2},{... | collective-permute-start | bytes 786440 | tf_op jit(solution)/shard_map/ppermute | solution.py:589
  15.4 2.9 %copy-start.2 = (bf16[3,3,3,128,128]{4,3,2,1,0:T(8,128)(2,1)S(1)}, bf16[3,3,3,128,128]{4,3,2,1,0:T(8,128)(2,1)}, u32[]{:S(2)}) copy-start(bf16[3,3,3,128,128]{4,3,2,1,0:T(8,128)(2,1)} %param.6) | copy-start | bytes 2654212
  15.6 4.5 %collective-permute-start.4 = (bf16[2,2,32,128]{3,2,1,0:T(8,128)(2,1)S(1)}, bf16[2,2,32,128]{3,2,1,0:T(8,128)(2,1)S(1)}, u32[]{:S(2)}, u32[]{:S(2)}) collective-permute-start(bf16[2,2,32,128]{3,2,1,0:T(8,128)(2,1)S(1)} %get-tuple-element.60), channel_id=1, source_target_pairs={{0,4},{4,8},{8,12},{12,0},{1,5},{5,9},{9,13},{13,1},{2,6},{6,10},{... | collective-permute-start | bytes 98312 | tf_op jit(solution)/shard_map/ppermute | solution.py:589
  15.6 4.4 %collective-permute-start.5 = (bf16[2,2,32,128]{3,2,1,0:T(8,128)(2,1)S(1)}, bf16[2,2,32,128]{3,2,1,0:T(8,128)(2,1)S(1)}, u32[]{:S(2)}, u32[]{:S(2)}) collective-permute-start(bf16[2,2,32,128]{3,2,1,0:T(8,128)(2,1)S(1)} %get-tuple-element.61.refs_1_.refs_5_), channel_id=1, source_target_pairs={{0,12},{4,0},{8,4},{12,8},{1,13},{5,1},{9,5},{13,9},{2,14},{6,2},{... | collective-permute-start | bytes 98312 | tf_op jit(solution)/shard_map/ppermute | solution.py:589
  20.6 8.3 %collective-permute-start.7 = (bf16[2,21,16,128]{3,2,1,0:T(8,128)(2,1)S(1)}, bf16[2,21,16,128]{3,2,1,0:T(8,128)(2,1)S(1)}, u32[]{:S(2)}, u32[]{:S(2)}) collective-permute-start(bf16[2,21,16,128]{3,2,1,0:T(8,128)(2,1)S(1)} %get-tuple-element.68), channel_id=1, source_target_pairs={{0,16},{16,32},{32,48},{48,64},{64,80},{80,96},{96,112},{112,0},{1... | collective-permute-start | bytes 516104 | tf_op jit(solution)/shard_map/ppermute | solution.py:589
  24.5 4.8 %collective-permute-start.6 = (bf16[2,21,16,128]{3,2,1,0:T(8,128)(2,1)S(1)}, bf16[2,21,16,128]{3,2,1,0:T(8,128)(2,1)S(1)}, u32[]{:S(2)}, u32[]{:S(2)}) collective-permute-start(bf16[2,21,16,128]{3,2,1,0:T(8,128)(2,1)S(1)} %get-tuple-element.67.refs_3_), channel_id=1, source_target_pairs={{0,112},{16,0},{32,16},{48,32},{64,48},{80,64},{96,80},{112,96},{1... | collective-permute-start | bytes 516104 | tf_op jit(solution)/shard_map/ppermute | solution.py:589
  30.7 3.1 %collective-permute-start.8 = (f32[1728,128]{1,0:T(8,128)S(1)}, f32[1728,128]{1,0:T(8,128)S(1)}, u32[]{:S(2)}, u32[]{:S(2)}) collective-permute-start(f32[1728,128]{1,0:T(8,128)S(1)} %get-tuple-element.69.refs_9_), channel_id=1, source_target_pairs={{0,16},{16,0},{32,48},{48,32},{64,80},{80,64},{96,112},{112,96},{1... | collective-permute-start | bytes 2654216 | tf_op jit(solution)/shard_map/ppermute | solution.py:642
  33.9 9.4 %collective-permute-start.10 = (f32[432,128]{1,0:T(8,128)S(1)}, f32[432,128]{1,0:T(8,128)S(1)}, u32[]{:S(2)}, u32[]{:S(2)}) collective-permute-start(f32[432,128]{1,0:T(8,128)S(1)} %get-tuple-element.80), channel_id=1, source_target_pairs={{0,64},{1,65},{2,66},{3,67},{4,68},{5,69},{6,70},{7,71},{8,72},{9,... | collective-permute-start | bytes 663560 | tf_op jit(solution)/shard_map/ppermute | solution.py:515
  35.9 7.5 %collective-permute-start.11 = (f32[432,128]{1,0:T(8,128)S(1)}, f32[432,128]{1,0:T(8,128)S(1)}, u32[]{:S(2)}, u32[]{:S(2)}) collective-permute-start(f32[432,128]{1,0:T(8,128)S(1)} %get-tuple-element.81), channel_id=1, source_target_pairs={{0,96},{1,97},{2,98},{3,99},{4,100},{5,101},{6,102},{7,103},{8,104... | collective-permute-start | bytes 663560 | tf_op jit(solution)/shard_map/ppermute | solution.py:515
  37.1 6.5 %collective-permute-start.9 = (f32[432,128]{1,0:T(8,128)S(1)}, f32[432,128]{1,0:T(8,128)S(1)}, u32[]{:S(2)}, u32[]{:S(2)}) collective-permute-start(f32[432,128]{1,0:T(8,128)S(1)} %get-tuple-element.74.refs_11_), channel_id=1, source_target_pairs={{0,32},{1,33},{2,34},{3,35},{4,36},{5,37},{6,38},{7,39},{8,40},{9,... | collective-permute-start | bytes 663560 | tf_op jit(solution)/shard_map/ppermute | solution.py:515
  43.6 8.3 %collective-permute-start.14 = (f32[432,128]{1,0:T(8,128)S(1)}, f32[432,128]{1,0:T(8,128)S(1)}, u32[]{:S(2)}, u32[]{:S(2)}) collective-permute-start(f32[432,128]{1,0:T(8,128)S(1)} %shard_map.83.refs_12_.refs_0_), channel_id=1, source_target_pairs={{0,8},{1,9},{2,10},{3,11},{4,12},{5,13},{6,14},{7,15},{8,0},{9,1},... | collective-permute-start | bytes 663560 | tf_op jit(solution)/shard_map/ppermute | solution.py:515
  45.6 7.3 %collective-permute-start.13 = (f32[432,128]{1,0:T(8,128)S(1)}, f32[432,128]{1,0:T(8,128)S(1)}, u32[]{:S(2)}, u32[]{:S(2)}) collective-permute-start(f32[432,128]{1,0:T(8,128)S(1)} %shard_map.83.refs_12_.refs_0_), channel_id=1, source_target_pairs={{0,12},{1,13},{2,14},{3,15},{4,8},{5,9},{6,10},{7,11},{8,4},{9,5},... | collective-permute-start | bytes 663560 | tf_op jit(solution)/shard_map/ppermute | solution.py:515
  46.4 6.5 %collective-permute-start.12 = (f32[432,128]{1,0:T(8,128)S(1)}, f32[432,128]{1,0:T(8,128)S(1)}, u32[]{:S(2)}, u32[]{:S(2)}) collective-permute-start(f32[432,128]{1,0:T(8,128)S(1)} %shard_map.83.refs_12_.refs_0_), channel_id=1, source_target_pairs={{0,4},{1,5},{2,6},{3,7},{4,0},{5,1},{6,2},{7,3},{8,12},{9,13},{10,... | collective-permute-start | bytes 663560 | tf_op jit(solution)/shard_map/ppermute | solution.py:515
  52.9 9.6 %collective-permute-start.17 = (f32[432,128]{1,0:T(8,128)S(1)}, f32[432,128]{1,0:T(8,128)S(1)}, u32[]{:S(2)}, u32[]{:S(2)}) collective-permute-start(f32[432,128]{1,0:T(8,128)S(1)} %shard_map.85.refs_10_.refs_0_), channel_id=1, source_target_pairs={{0,2},{1,3},{2,0},{3,1},{4,6},{5,7},{6,4},{7,5},{8,10},{9,11},{10,... | collective-permute-start | bytes 663560 | tf_op jit(solution)/shard_map/ppermute | solution.py:515
  55.5 7.0 %collective-permute-start.16 = (f32[432,128]{1,0:T(8,128)S(1)}, f32[432,128]{1,0:T(8,128)S(1)}, u32[]{:S(2)}, u32[]{:S(2)}) collective-permute-start(f32[432,128]{1,0:T(8,128)S(1)} %shard_map.85.refs_10_.refs_0_), channel_id=1, source_target_pairs={{0,3},{1,2},{2,1},{3,0},{4,7},{5,6},{6,5},{7,4},{8,11},{9,10},{10,... | collective-permute-start | bytes 663560 | tf_op jit(solution)/shard_map/ppermute | solution.py:515
  56.5 6.1 %collective-permute-start.15 = (f32[432,128]{1,0:T(8,128)S(1)}, f32[432,128]{1,0:T(8,128)S(1)}, u32[]{:S(2)}, u32[]{:S(2)}) collective-permute-start(f32[432,128]{1,0:T(8,128)S(1)} %shard_map.85.refs_10_.refs_0_), channel_id=1, source_target_pairs={{0,1},{1,0},{2,3},{3,2},{4,5},{5,4},{6,7},{7,6},{8,9},{9,8},{10,11... | collective-permute-start | bytes 663560 | tf_op jit(solution)/shard_map/ppermute | solution.py:515
  62.6 11.9 %collective-permute-start.21 = (f32[432,128]{1,0:T(8,128)S(1)}, f32[432,128]{1,0:T(8,128)S(1)}, u32[]{:S(2)}, u32[]{:S(2)}) collective-permute-start(f32[432,128]{1,0:T(8,128)S(1)} %shard_map.87.refs_12_.refs_0_), channel_id=1, source_target_pairs={{0,16},{16,0},{32,48},{48,32},{64,80},{80,64},{96,112},{112,96},{1... | collective-permute-start | bytes 663560 | tf_op jit(solution)/shard_map/ppermute | solution.py:655
  65.3 9.2 %collective-permute-start.20 = (f32[432,128]{1,0:T(8,128)S(1)}, f32[432,128]{1,0:T(8,128)S(1)}, u32[]{:S(2)}, u32[]{:S(2)}) collective-permute-start(f32[432,128]{1,0:T(8,128)S(1)} %shard_map.87.refs_12_.refs_0_), channel_id=1, source_target_pairs={{0,64},{1,65},{2,66},{3,67},{4,68},{5,69},{6,70},{7,71},{8,72},{9,... | collective-permute-start | bytes 663560 | tf_op jit(solution)/shard_map/ppermute | solution.py:515
  66.8 7.7 %collective-permute-start.19 = (f32[432,128]{1,0:T(8,128)S(1)}, f32[432,128]{1,0:T(8,128)S(1)}, u32[]{:S(2)}, u32[]{:S(2)}) collective-permute-start(f32[432,128]{1,0:T(8,128)S(1)} %shard_map.87.refs_12_.refs_0_), channel_id=1, source_target_pairs={{0,96},{1,97},{2,98},{3,99},{4,100},{5,101},{6,102},{7,103},{8,104... | collective-permute-start | bytes 663560 | tf_op jit(solution)/shard_map/ppermute | solution.py:515
  67.8 6.7 %collective-permute-start.18 = (f32[432,128]{1,0:T(8,128)S(1)}, f32[432,128]{1,0:T(8,128)S(1)}, u32[]{:S(2)}, u32[]{:S(2)}) collective-permute-start(f32[432,128]{1,0:T(8,128)S(1)} %shard_map.87.refs_12_.refs_0_), channel_id=1, source_target_pairs={{0,32},{1,33},{2,34},{3,35},{4,36},{5,37},{6,38},{7,39},{8,40},{9,... | collective-permute-start | bytes 663560 | tf_op jit(solution)/shard_map/ppermute | solution.py:515
  74.6 3.3 %collective-permute-start.22 = (f32[1296,128]{1,0:T(8,128)S(1)}, f32[1296,128]{1,0:T(8,128)S(1)}, u32[]{:S(2)}, u32[]{:S(2)}) collective-permute-start(f32[1296,128]{1,0:T(8,128)S(1)} %shard_map.89.refs_1_.refs_2_), channel_id=1, source_target_pairs={{0,16},{16,0},{32,48},{48,32},{64,80},{80,64},{96,112},{112,96},{1... | collective-permute-start | bytes 1990664 | tf_op jit(solution)/shard_map/ppermute | solution.py:658

commit v10 on v9

--- a/solution.py
+++ b/solution.py
@@ -599,14 +599,14 @@
     to_ylo, to_yhi = small_kernel(copy_kernel, [face, face], [ylo, yhi], [own])
     near_ylo = shift(to_yhi, "gy", 1)
     near_yhi = shift(to_ylo, "gy", -1)
-    own = own_grad(slabs, SPAN, 1, own, to_ylo)
+    forward, flipped = small_kernel(
+        arrange_kernel, [shape((TAPS, WIDE), BF16)] * 2, [weight.reshape(27, C, C)], [to_ylo]
+    )
 
     edge = shape((2, 2, X, C), BF16)
-    edge_lo, edge_hi = small_kernel(edge_kernel, [edge, edge], [near_zlo, near_zhi], [own])
+    edge_lo, edge_hi = small_kernel(edge_kernel, [edge, edge], [near_zlo, near_zhi], [forward])
     edges = (shift(edge_hi, "gy", 1), shift(edge_lo, "gy", -1))
-    forward, flipped = small_kernel(
-        arrange_kernel, [shape((TAPS, WIDE), BF16)] * 2, [weight.reshape(27, C, C)], [edge_lo]
-    )
+    own = own_grad(slabs, SPAN, 1, own, edge_lo)
     own = small_kernel(
         z_rim_kernel, shape((WIDE, TAPS), F32), [own, zlo, zhi, near_zlo, near_zhi], [edge_lo]
     )
@@ -617,7 +617,7 @@
         message_kernel,
         [face, face, column, column, message, message],
         [*slabs, near_ylo, near_yhi, near_zlo, near_zhi, *edges],
-        [forward, own],
+        [own],
     )
     far = (shift(to_hi, "gx", 1), shift(to_lo, "gx", -1))
     own = own_grad(slabs, X // 2, 2, own, to_lo)
@@ -657,8 +657,7 @@
     joined = small_kernel(join_kernel, shape((3 * chunk.shape[0], C), F32), came, [beside, *ties])
     others = lax.ppermute(joined, "gx", swap)
     full = write([(chunk, (0,)), (joined, (1, 3, 2))], True, None, joined)
-    full = write([(beside, (0,))], False, full, joined)
-    full = write([(others, (1, 3, 2))], False, full, joined)
+    full = write([(beside, (0,)), (others, (1, 3, 2))], False, full, joined)
     return (made[0], made[1], full.reshape(3, 3, 3, C, C))
 
 

time: 79 us -> 77.9 us (0.986)
    ppermute x1, starting transfers between devices: 1.55 us -> 0.09 us  [body(): others = lax.ppermute(joined, 'gx', swap)]
    ppermute x1, waiting for transfers between devices: 0.07 us -> 1.13 us  [body(): others = lax.ppermute(joined, 'gx', swap)]
    ppermute x12, starting transfers between devices: 12.9 us -> 13.9 us  [exchange(): lax.ppermute(value, ('gx', 'gy', 'gz'), pairs(turn, step))]
    ppermute x12, waiting for transfers between devices: 1.21 us -> 0.35 us  [exchange(): lax.ppermute(value, ('gx', 'gy', 'gz'), pairs(turn, step))]
    pallas_call x3 -> x2, Pallas kernels: 2.51 us -> 1.9 us  [write(): pl.pallas_call(kernel, in_specs=[VMEM] * len(arrays) + [ANY] * (len(opera...]
  transfers between devices with their start and end apart: 23 -> 23, of which waited for: 6 -> 5; matrix products, arithmetic and copies ran while one was open for 0% -> 0% of each run, Pallas kernels for 47% -> 47%
where the time goes in v10:
time: 77.9 us; the launch traced here: 77.8 us
  Pallas kernels  42.4 us (54%)
  starting transfers between devices  31.4 us (40%)
  waiting for transfers between devices  1.92 us (2%)
  between operations  1.17 us (2%)
  local copies, waits for them, and re-layouts  0.99 us (1%)
    pallas_call x5, Pallas kernels, conv_piece(): pl.pallas_call(plain if more else final, in_specs=specs, out_specs=[ANY]...  25.4 us
    ppermute x12, starting transfers between devices, exchange(): lax.ppermute(value, ('gx', 'gy', 'gz'), pairs(turn, step))  13.9 us
    ppermute x8, starting transfers between devices, shift(): lax.ppermute(value, axis, [(i, (i + step) % count) for i in range(count)])  13 us
    pallas_call x3, Pallas kernels, own_grad(): pl.pallas_call(lambda *refs: own_grad_kernel(first, spans, more, *refs),...  9.19 us
    ppermute x1, starting transfers between devices, body(): beside = lax.ppermute(chunk, 'gx', swap)  3.33 us
    pallas_call x12, Pallas kernels, small_kernel(): pl.pallas_call(run, in_specs=(specs or [VMEM] * count) + [ANY] * len(ties...  2.66 us
    pallas_call x2, Pallas kernels, write(): pl.pallas_call(kernel, in_specs=[VMEM] * len(arrays) + [ANY] * (len(opera...  1.9 us
  transfers between devices with their start and end apart: 23, of which 5 were waited for; matrix products, arithmetic and copies ran while one was open for 0% of the time, Pallas kernels for 47%

profile of v10, /device:TPU:1, one launch (start us, length us, event | category | flops | bytes accessed | tf_op | source)
XLA Modules:
  0.0 77.8 jit_solution(16054595896903800679)
XLA Ops:
  0.7 0.6 copy-done.3
  2.2 0.9 %shard_map.69 = (bf16[34,16,16,128]{3,2,1,0:T(8,128)(2,1)S(1)}, bf16[1,32,16,128]{3,2,1,0:T(8,128)(2,1)S(1)}, bf16[1,32,16,128]{3,2,1,0:T(8,128)(2,1)S(1)}, bf16...) custom-call(bf16[32,16,16,128]{3,2,1,0:T(8,128)(2,1)S(1)} %copy-done, ...), custom_call_target="tpu_custom_call" | custom-call | flops 1000 | bytes 1000 | tf_op jit(solution)/shard_map/pallas_call | solution.py:104
  3.2 0.9 %shard_map.70 = (bf16[34,16,16,128]{3,2,1,0:T(8,128)(2,1)S(1)}, bf16[2,32,16,128]{3,2,1,0:T(8,128)(2,1)S(1)}, bf16[2,32,16,128]{3,2,1,0:T(8,128)(2,1)S(1)}, bf16...) custom-call(bf16[32,16,16,128]{3,2,1,0:T(8,128)(2,1)S(1)} %copy-done.1, ...), custom_call_target="tpu_custom_call" | custom-call | flops 1000 | bytes 1000 | tf_op jit(solution)/shard_map/pallas_call | solution.py:112
  4.1 2.1 %collective-permute-start.2 = (bf16[2,32,16,128]{3,2,1,0:T(8,128)(2,1)S(1)}, bf16[2,32,16,128]{3,2,1,0:T(8,128)(2,1)S(1)}, u32[]{:S(2)}, u32[]{:S(2)}) collective-permute-start(bf16[2,32,16,128]{3,2,1,0:T(8,128)(2,1)S(1)} %get-tuple-element.59.refs_2_), channel_id=1, source_target_pairs={{0,1},{1,2},{2,3},{3,0},{4,5},{5,6},{6,7},{7,4},{8,9},{9,10},{10,1... | collective-permute-start | bytes 786440 | tf_op jit(solution)/shard_map/ppermute | solution.py:589
  6.2 1.3 %collective-permute-start.3 = (bf16[2,32,16,128]{3,2,1,0:T(8,128)(2,1)S(1)}, bf16[2,32,16,128]{3,2,1,0:T(8,128)(2,1)S(1)}, u32[]{:S(2)}, u32[]{:S(2)}) collective-permute-start(bf16[2,32,16,128]{3,2,1,0:T(8,128)(2,1)S(1)} %get-tuple-element.56.refs_2_.refs_1_), channel_id=1, source_target_pairs={{0,3},{1,0},{2,1},{3,2},{4,7},{5,4},{6,5},{7,6},{8,11},{9,8},{10,9... | collective-permute-start | bytes 786440 | tf_op jit(solution)/shard_map/ppermute | solution.py:589
  7.6 2.4 %shard_map.71.refs_2_ = f32[384,1152]{1,0:T(8,128)S(1)} custom-call(bf16[34,16,16,128]{3,2,1,0:T(8,128)(2,1)S(1)} %get-tuple-element.48.refs_0_.refs_1_, bf16[34,16,16,128]{3,2,1,0:T(8,128)(2,1)S(1)} %get-tuple-element.53.refs_1_.g_ref.refs_2_, bf16[2,32,16,128]{3,2,1,0:T(8,128)(2,1)S(1)} %get-tuple-element.56.refs_2_.refs_1_), custom_call_target="tpu_custom_call" | custom-call | flops 1811939328 | bytes 8388608 | tf_op jit(solution)/shard_map/pallas_call | solution.py:188
  10.1 1.5 %collective-permute-start = (bf16[2,32,16,128]{3,2,1,0:T(8,128)(2,1)S(1)}, bf16[2,32,16,128]{3,2,1,0:T(8,128)(2,1)S(1)}, u32[]{:S(2)}, u32[]{:S(2)}) collective-permute-start(bf16[2,32,16,128]{3,2,1,0:T(8,128)(2,1)S(1)} %get-tuple-element.57), channel_id=1, source_target_pairs={{0,4},{4,8},{8,12},{12,0},{1,5},{5,9},{9,13},{13,1},{2,6},{6,10},{... | collective-permute-start | bytes 786440 | tf_op jit(solution)/shard_map/ppermute | solution.py:589
  11.6 1.5 %collective-permute-start.1 = (bf16[2,32,16,128]{3,2,1,0:T(8,128)(2,1)S(1)}, bf16[2,32,16,128]{3,2,1,0:T(8,128)(2,1)S(1)}, u32[]{:S(2)}, u32[]{:S(2)}) collective-permute-start(bf16[2,32,16,128]{3,2,1,0:T(8,128)(2,1)S(1)} %get-tuple-element.58.refs_1_), channel_id=1, source_target_pairs={{0,12},{4,0},{8,4},{12,8},{1,13},{5,1},{9,5},{13,9},{2,14},{6,2},{... | collective-permute-start | bytes 786440 | tf_op jit(solution)/shard_map/ppermute | solution.py:589
  13.7 1.3 %collective-permute-start.4 = (bf16[2,2,32,128]{3,2,1,0:T(8,128)(2,1)S(1)}, bf16[2,2,32,128]{3,2,1,0:T(8,128)(2,1)S(1)}, u32[]{:S(2)}, u32[]{:S(2)}) collective-permute-start(bf16[2,2,32,128]{3,2,1,0:T(8,128)(2,1)S(1)} %get-tuple-element.61), channel_id=1, source_target_pairs={{0,4},{4,8},{8,12},{12,0},{1,5},{5,9},{9,13},{13,1},{2,6},{6,10},{... | collective-permute-start | bytes 98312 | tf_op jit(solution)/shard_map/ppermute | solution.py:589
  14.9 1.7 %collective-permute-start.5 = (bf16[2,2,32,128]{3,2,1,0:T(8,128)(2,1)S(1)}, bf16[2,2,32,128]{3,2,1,0:T(8,128)(2,1)S(1)}, u32[]{:S(2)}, u32[]{:S(2)}) collective-permute-start(bf16[2,2,32,128]{3,2,1,0:T(8,128)(2,1)S(1)} %get-tuple-element.62.refs_3_.refs_5_), channel_id=1, source_target_pairs={{0,12},{4,0},{8,4},{12,8},{1,13},{5,1},{9,5},{13,9},{2,14},{6,2},{... | collective-permute-start | bytes 98312 | tf_op jit(solution)/shard_map/ppermute | solution.py:589
  16.6 2.3 %shard_map.75.refs_0_ = f32[384,1152]{1,0:T(8,128)S(1)} custom-call(bf16[34,16,16,128]{3,2,1,0:T(8,128)(2,1)S(1)} %get-tuple-element.48.refs_0_.refs_1_, bf16[34,16,16,128]{3,2,1,0:T(8,128)(2,1)S(1)} %get-tuple-element.53.refs_1_.g_ref.refs_2_, f32[384,1152]{1,0:T(8,128)S(1)} %shard_map.71.refs_2_, bf16[2,2,32,128]{3,2,1,0:T(8,128)(2,1)S(1)} %get-tuple-element.62.refs_3_.refs_5_), custom_call_target="tpu_custom_call" | custom-call | flops 1811939328 | bytes 8388608 | tf_op jit(solution)/shard_map/pallas_call | solution.py:188
  20.2 3.5 %collective-permute-start.7 = (bf16[2,21,16,128]{3,2,1,0:T(8,128)(2,1)S(1)}, bf16[2,21,16,128]{3,2,1,0:T(8,128)(2,1)S(1)}, u32[]{:S(2)}, u32[]{:S(2)}) collective-permute-start(bf16[2,21,16,128]{3,2,1,0:T(8,128)(2,1)S(1)} %get-tuple-element.68), channel_id=1, source_target_pairs={{0,16},{16,32},{32,48},{48,64},{64,80},{80,96},{96,112},{112,0},{1... | collective-permute-start | bytes 516104 | tf_op jit(solution)/shard_map/ppermute | solution.py:589
  23.7 4.4 %shard_map.78.own_ref = f32[384,1152]{1,0:T(8,128)S(1)} custom-call(bf16[34,16,16,128]{3,2,1,0:T(8,128)(2,1)S(1)} %get-tuple-element.48.refs_0_.refs_1_, bf16[34,16,16,128]{3,2,1,0:T(8,128)(2,1)S(1)} %get-tuple-element.53.refs_1_.g_ref.refs_2_, f32[384,1152]{1,0:T(8,128)S(1)} %shard_map.76.refs_8_.refs_2_, bf16[2,21,16,128]{3,2,1,0:T(8,128)(2,1)S(1)} %get-tuple-element.67.refs_3_), custom_call_target="tpu_custom_call" | custom-call | flops 3623878656 | bytes 8388608 | tf_op jit(solution)/shard_map/pallas_call | solution.py:188
  28.5 1.4 %shard_map.79 = (f32[1728,128]{1,0:T(8,128)S(1)}, f32[1728,128]{1,0:T(8,128)S(1)}) custom-call(f32[384,1152]{1,0:T(8,128)S(1)} %shard_map.78.own_ref, bf16[34,16,16,128]{3,2,1,0:T(8,128)(2,1)S(1)} %get-tuple-element.53.refs_1_.g_ref.refs_2_, bf16[2,32,16,128]{3,2,1,0:T(8,128)(2,1)S(1)} %get-tuple-element.54.refs_0_.gylo, ...), custom_call_target="tpu_custom_call" | custom-call | flops 679477248 | bytes 6291456 | tf_op jit(solution)/shard_map/pallas_call | solution.py:258
  29.9 1.1 %collective-permute-start.8 = (f32[1728,128]{1,0:T(8,128)S(1)}, f32[1728,128]{1,0:T(8,128)S(1)}, u32[]{:S(2)}, u32[]{:S(2)}) collective-permute-start(f32[1728,128]{1,0:T(8,128)S(1)} %get-tuple-element.69.refs_9_), channel_id=1, source_target_pairs={{0,16},{16,0},{32,48},{48,32},{64,80},{80,64},{96,112},{112,96},{1... | collective-permute-start | bytes 2654216 | tf_op jit(solution)/shard_map/ppermute | solution.py:642
  31.0 2.0 %shard_map.80 = (bf16[32,16,16,128]{3,2,1,0:T(8,128)(2,1)}, f32[2,256,128]{2,1,0:T(8,128)S(1)}, bf16[3,4,18,16,128]{4,3,2,1,0:T(8,128)(2,1)S(1)}, bf16[4,16,16,128]{3,2,1,0:T(8,128)(2,1)S(1)}) custom-call(bf16[4,16,16,128]{3,2,1,0:T(8,128)(2,1)S(1)} %shard_map.68.mask_ref.refs_0_, bf16[34,16,16,128]{3,2,1,0:T(8,128)(2,1)S(1)} %get-tuple-element.48.refs_0_.refs_1_, ...), custom_call_target="tpu_custom_call" | custom-call | flops 905969664 | bytes 2097152 | tf_op jit(solution)/shard_map/pallas_call | solution.py:428
  33.1 2.2 %collective-permute-start.10 = (f32[432,128]{1,0:T(8,128)S(1)}, f32[432,128]{1,0:T(8,128)S(1)}, u32[]{:S(2)}, u32[]{:S(2)}) collective-permute-start(f32[432,128]{1,0:T(8,128)S(1)} %get-tuple-element.80), channel_id=1, source_target_pairs={{0,64},{1,65},{2,66},{3,67},{4,68},{5,69},{6,70},{7,71},{8,72},{9,... | collective-permute-start | bytes 663560 | tf_op jit(solution)/shard_map/ppermute | solution.py:515
  35.3 1.1 %collective-permute-start.11 = (f32[432,128]{1,0:T(8,128)S(1)}, f32[432,128]{1,0:T(8,128)S(1)}, u32[]{:S(2)}, u32[]{:S(2)}) collective-permute-start(f32[432,128]{1,0:T(8,128)S(1)} %get-tuple-element.81), channel_id=1, source_target_pairs={{0,96},{1,97},{2,98},{3,99},{4,100},{5,101},{6,102},{7,103},{8,104... | collective-permute-start | bytes 663560 | tf_op jit(solution)/shard_map/ppermute | solution.py:515
  36.3 5.8 %shard_map.82 = (bf16[32,16,16,128]{3,2,1,0:T(8,128)(2,1)}, f32[2,256,128]{2,1,0:T(8,128)S(1)}, bf16[3,4,18,16,128]{4,3,2,1,0:T(8,128)(2,1)S(1)}, bf16[4,16,16,128]{3,2,1,0:T(8,128)(2,1)S(1)}) custom-call(bf16[4,16,16,128]{3,2,1,0:T(8,128)(2,1)S(1)} %shard_map.68.mask_ref.refs_0_, ...), custom_call_target="tpu_custom_call", output_to_operand_aliasing={{0}: (12, {})} | custom-call | flops 3623878656 | bytes 2097152 | tf_op jit(solution)/shard_map/pallas_call | solution.py:428
  42.2 2.4 %collective-permute-start.14 = (f32[432,128]{1,0:T(8,128)S(1)}, f32[432,128]{1,0:T(8,128)S(1)}, u32[]{:S(2)}, u32[]{:S(2)}) collective-permute-start(f32[432,128]{1,0:T(8,128)S(1)} %shard_map.83.refs_12_.refs_0_), channel_id=1, source_target_pairs={{0,8},{1,9},{2,10},{3,11},{4,12},{5,13},{6,14},{7,15},{8,0},{9,1},... | collective-permute-start | bytes 663560 | tf_op jit(solution)/shard_map/ppermute | solution.py:515
  44.6 1.2 %collective-permute-start.13 = (f32[432,128]{1,0:T(8,128)S(1)}, f32[432,128]{1,0:T(8,128)S(1)}, u32[]{:S(2)}, u32[]{:S(2)}) collective-permute-start(f32[432,128]{1,0:T(8,128)S(1)} %shard_map.83.refs_12_.refs_0_), channel_id=1, source_target_pairs={{0,12},{1,13},{2,14},{3,15},{4,8},{5,9},{6,10},{7,11},{8,4},{9,5},... | collective-permute-start | bytes 663560 | tf_op jit(solution)/shard_map/ppermute | solution.py:515
  45.8 5.3 %shard_map.84 = (bf16[32,16,16,128]{3,2,1,0:T(8,128)(2,1)}, f32[2,256,128]{2,1,0:T(8,128)S(1)}, bf16[3,4,18,16,128]{4,3,2,1,0:T(8,128)(2,1)S(1)}) custom-call(bf16[4,16,16,128]{3,2,1,0:T(8,128)(2,1)S(1)} %shard_map.68.mask_ref.refs_0_, bf16[34,16,16,128]{3,2,1,0:T(8,128)(2,1)S(1)} %get-tuple-element.48.refs_0_.refs_1_, ...), custom_call_target="tpu_custom_call", output_to_operand_aliasing={{0}: (13, {})} | custom-call | flops 2717908992 | bytes 2097152 | tf_op jit(solution)/shard_map/pallas_call | solution.py:428
  51.5 2.5 %collective-permute-start.17 = (f32[432,128]{1,0:T(8,128)S(1)}, f32[432,128]{1,0:T(8,128)S(1)}, u32[]{:S(2)}, u32[]{:S(2)}) collective-permute-start(f32[432,128]{1,0:T(8,128)S(1)} %shard_map.85.refs_10_.refs_0_), channel_id=1, source_target_pairs={{0,2},{1,3},{2,0},{3,1},{4,6},{5,7},{6,4},{7,5},{8,10},{9,11},{10,... | collective-permute-start | bytes 663560 | tf_op jit(solution)/shard_map/ppermute | solution.py:515
  54.0 0.7 collective-permute-start.16
  54.7 6.0 %shard_map.86 = (bf16[32,16,16,128]{3,2,1,0:T(8,128)(2,1)}, f32[2,256,128]{2,1,0:T(8,128)S(1)}, bf16[3,4,18,16,128]{4,3,2,1,0:T(8,128)(2,1)S(1)}, bf16[4,16,16,128]{3,2,1,0:T(8,128)(2,1)S(1)}) custom-call(bf16[4,16,16,128]{3,2,1,0:T(8,128)(2,1)S(1)} %shard_map.68.mask_ref.refs_0_, bf16[34,16,16,128]{3,2,1,0:T(8,128)(2,1)S(1)} %get-tuple-element.48.refs_0_.refs_1_, ...), custom_call_target="tpu_custom_call" | custom-call | flops 3623878656 | bytes 2097152 | tf_op jit(solution)/shard_map/pallas_call | solution.py:428
  60.8 2.8 %collective-permute-start.21 = (f32[432,128]{1,0:T(8,128)S(1)}, f32[432,128]{1,0:T(8,128)S(1)}, u32[]{:S(2)}, u32[]{:S(2)}) collective-permute-start(f32[432,128]{1,0:T(8,128)S(1)} %shard_map.87.refs_12_.refs_0_), channel_id=1, source_target_pairs={{0,64},{1,65},{2,66},{3,67},{4,68},{5,69},{6,70},{7,71},{8,72},{9,... | collective-permute-start | bytes 663560 | tf_op jit(solution)/shard_map/ppermute | solution.py:515
  63.7 1.1 %collective-permute-start.20 = (f32[432,128]{1,0:T(8,128)S(1)}, f32[432,128]{1,0:T(8,128)S(1)}, u32[]{:S(2)}, u32[]{:S(2)}) collective-permute-start(f32[432,128]{1,0:T(8,128)S(1)} %shard_map.87.refs_12_.refs_0_), channel_id=1, source_target_pairs={{0,96},{1,97},{2,98},{3,99},{4,100},{5,101},{6,102},{7,103},{8,104... | collective-permute-start | bytes 663560 | tf_op jit(solution)/shard_map/ppermute | solution.py:515
  64.7 3.3 %collective-permute-start.18 = (f32[432,128]{1,0:T(8,128)S(1)}, f32[432,128]{1,0:T(8,128)S(1)}, u32[]{:S(2)}, u32[]{:S(2)}) collective-permute-start(f32[432,128]{1,0:T(8,128)S(1)} %shard_map.87.refs_12_.refs_0_), channel_id=1, source_target_pairs={{0,16},{16,0},{32,48},{48,32},{64,80},{80,64},{96,112},{112,96},{1... | collective-permute-start | bytes 663560 | tf_op jit(solution)/shard_map/ppermute | solution.py:655
  68.1 6.3 %shard_map.88 = (bf16[32,16,16,128]{3,2,1,0:T(8,128)(2,1)}, f32[8,128]{1,0:T(8,128)S(1)}) custom-call(bf16[4,16,16,128]{3,2,1,0:T(8,128)(2,1)S(1)} %shard_map.68.mask_ref.refs_0_, bf16[34,16,16,128]{3,2,1,0:T(8,128)(2,1)S(1)} %get-tuple-element.48.refs_0_.refs_1_, ...), custom_call_target="tpu_custom_call", output_to_operand_aliasing={{0}: (13, {})} | custom-call | flops 3623878656 | bytes 2097152 | tf_op jit(solution)/shard_map/pallas_call | solution.py:428
  74.6 1.0 %shard_map.90.refs_3_ = f32[3456,128]{1,0:T(8,128)} custom-call(f32[432,128]{1,0:T(8,128)S(1)} %shard_map.87.refs_12_.refs_0_, f32[1296,128]{1,0:T(8,128)S(1)} %shard_map.89.refs_1_.refs_2_, f32[1296,128]{1,0:T(8,128)S(1)} %shard_map.89.refs_1_.refs_2_), custom_call_target="tpu_custom_call" | custom-call | flops 1000 | bytes 1048576 | tf_op jit(solution)/shard_map/pallas_call | solution.py:569
  75.6 1.1 %collective-permute-done.22.refs_1_ = f32[1296,128]{1,0:T(8,128)S(1)} collective-permute-done((f32[1296,128]{1,0:T(8,128)S(1)}, f32[1296,128]{1,0:T(8,128)S(1)}, u32[]{:S(2)}, u32[]{:S(2)}) %collective-permute-start.22) | collective-permute-done | bytes 663584 | tf_op jit(solution)/shard_map/ppermute | solution.py:658
  76.7 0.9 %shard_map.91 = f32[3456,128]{1,0:T(8,128)} custom-call(f32[432,128]{1,0:T(8,128)S(1)} %collective-permute-done.18.refs_3_.refs_0_, f32[1296,128]{1,0:T(8,128)S(1)} %collective-permute-done.22.refs_1_, f32[1296,128]{1,0:T(8,128)S(1)} %shard_map.89.refs_1_.refs_2_, f32[3456,128]{1,0:T(8,128)} %shard_map.90.refs_3_), custom_call_target="tpu_custom_call", output_to_operand_aliasing={{}: (3, {})} | custom-call | flops 1000 | bytes 1048576 | tf_op jit(solution)/shard_map/pallas_call | solution.py:569
  (47 shorter events, 3.9 us)
Async XLA Ops:
  0.6 0.7 copy-start.3
  0.6 1.6 %copy-start = (bf16[32,16,16,128]{3,2,1,0:T(8,128)(2,1)S(1)}, bf16[32,16,16,128]{3,2,1,0:T(8,128)(2,1)}, u32[]{:S(2)}) copy-start(bf16[32,16,16,128]{3,2,1,0:T(8,128)(2,1)} %f_ref.1) | copy-start | bytes 6291460
  0.7 2.5 %copy-start.1 = (bf16[32,16,16,128]{3,2,1,0:T(8,128)(2,1)S(1)}, bf16[32,16,16,128]{3,2,1,0:T(8,128)(2,1)}, u32[]{:S(2)}) copy-start(bf16[32,16,16,128]{3,2,1,0:T(8,128)(2,1)} %c_ref.1) | copy-start | bytes 6291460
  4.1 9.4 %collective-permute-start.2 = (bf16[2,32,16,128]{3,2,1,0:T(8,128)(2,1)S(1)}, bf16[2,32,16,128]{3,2,1,0:T(8,128)(2,1)S(1)}, u32[]{:S(2)}, u32[]{:S(2)}) collective-permute-start(bf16[2,32,16,128]{3,2,1,0:T(8,128)(2,1)S(1)} %get-tuple-element.59.refs_2_), channel_id=1, source_target_pairs={{0,1},{1,2},{2,3},{3,0},{4,5},{5,6},{6,7},{7,4},{8,9},{9,10},{10,1... | collective-permute-start | bytes 786440 | tf_op jit(solution)/shard_map/ppermute | solution.py:589
  6.2 7.3 %collective-permute-start.3 = (bf16[2,32,16,128]{3,2,1,0:T(8,128)(2,1)S(1)}, bf16[2,32,16,128]{3,2,1,0:T(8,128)(2,1)S(1)}, u32[]{:S(2)}, u32[]{:S(2)}) collective-permute-start(bf16[2,32,16,128]{3,2,1,0:T(8,128)(2,1)S(1)} %get-tuple-element.56.refs_2_.refs_1_), channel_id=1, source_target_pairs={{0,3},{1,0},{2,1},{3,2},{4,7},{5,4},{6,5},{7,6},{8,11},{9,8},{10,9... | collective-permute-start | bytes 786440 | tf_op jit(solution)/shard_map/ppermute | solution.py:589
  10.0 3.1 %copy-start.2 = (bf16[3,3,3,128,128]{4,3,2,1,0:T(8,128)(2,1)S(1)}, bf16[3,3,3,128,128]{4,3,2,1,0:T(8,128)(2,1)}, u32[]{:S(2)}) copy-start(bf16[3,3,3,128,128]{4,3,2,1,0:T(8,128)(2,1)} %param.6) | copy-start | bytes 2654212
  10.1 9.5 %collective-permute-start = (bf16[2,32,16,128]{3,2,1,0:T(8,128)(2,1)S(1)}, bf16[2,32,16,128]{3,2,1,0:T(8,128)(2,1)S(1)}, u32[]{:S(2)}, u32[]{:S(2)}) collective-permute-start(bf16[2,32,16,128]{3,2,1,0:T(8,128)(2,1)S(1)} %get-tuple-element.57), channel_id=1, source_target_pairs={{0,4},{4,8},{8,12},{12,0},{1,5},{5,9},{9,13},{13,1},{2,6},{6,10},{... | collective-permute-start | bytes 786440 | tf_op jit(solution)/shard_map/ppermute | solution.py:589
  11.6 8.0 %collective-permute-start.1 = (bf16[2,32,16,128]{3,2,1,0:T(8,128)(2,1)S(1)}, bf16[2,32,16,128]{3,2,1,0:T(8,128)(2,1)S(1)}, u32[]{:S(2)}, u32[]{:S(2)}) collective-permute-start(bf16[2,32,16,128]{3,2,1,0:T(8,128)(2,1)S(1)} %get-tuple-element.58.refs_1_), channel_id=1, source_target_pairs={{0,12},{4,0},{8,4},{12,8},{1,13},{5,1},{9,5},{13,9},{2,14},{6,2},{... | collective-permute-start | bytes 786440 | tf_op jit(solution)/shard_map/ppermute | solution.py:589
  13.7 5.9 %collective-permute-start.4 = (bf16[2,2,32,128]{3,2,1,0:T(8,128)(2,1)S(1)}, bf16[2,2,32,128]{3,2,1,0:T(8,128)(2,1)S(1)}, u32[]{:S(2)}, u32[]{:S(2)}) collective-permute-start(bf16[2,2,32,128]{3,2,1,0:T(8,128)(2,1)S(1)} %get-tuple-element.61), channel_id=1, source_target_pairs={{0,4},{4,8},{8,12},{12,0},{1,5},{5,9},{9,13},{13,1},{2,6},{6,10},{... | collective-permute-start | bytes 98312 | tf_op jit(solution)/shard_map/ppermute | solution.py:589
  14.9 4.7 %collective-permute-start.5 = (bf16[2,2,32,128]{3,2,1,0:T(8,128)(2,1)S(1)}, bf16[2,2,32,128]{3,2,1,0:T(8,128)(2,1)S(1)}, u32[]{:S(2)}, u32[]{:S(2)}) collective-permute-start(bf16[2,2,32,128]{3,2,1,0:T(8,128)(2,1)S(1)} %get-tuple-element.62.refs_3_.refs_5_), channel_id=1, source_target_pairs={{0,12},{4,0},{8,4},{12,8},{1,13},{5,1},{9,5},{13,9},{2,14},{6,2},{... | collective-permute-start | bytes 98312 | tf_op jit(solution)/shard_map/ppermute | solution.py:589
  20.2 8.0 %collective-permute-start.7 = (bf16[2,21,16,128]{3,2,1,0:T(8,128)(2,1)S(1)}, bf16[2,21,16,128]{3,2,1,0:T(8,128)(2,1)S(1)}, u32[]{:S(2)}, u32[]{:S(2)}) collective-permute-start(bf16[2,21,16,128]{3,2,1,0:T(8,128)(2,1)S(1)} %get-tuple-element.68), channel_id=1, source_target_pairs={{0,16},{16,32},{32,48},{48,64},{64,80},{80,96},{96,112},{112,0},{1... | collective-permute-start | bytes 516104 | tf_op jit(solution)/shard_map/ppermute | solution.py:589
  23.7 4.8 %collective-permute-start.6 = (bf16[2,21,16,128]{3,2,1,0:T(8,128)(2,1)S(1)}, bf16[2,21,16,128]{3,2,1,0:T(8,128)(2,1)S(1)}, u32[]{:S(2)}, u32[]{:S(2)}) collective-permute-start(bf16[2,21,16,128]{3,2,1,0:T(8,128)(2,1)S(1)} %get-tuple-element.67.refs_3_), channel_id=1, source_target_pairs={{0,112},{16,0},{32,16},{48,32},{64,48},{80,64},{96,80},{112,96},{1... | collective-permute-start | bytes 516104 | tf_op jit(solution)/shard_map/ppermute | solution.py:589
  29.9 3.1 %collective-permute-start.8 = (f32[1728,128]{1,0:T(8,128)S(1)}, f32[1728,128]{1,0:T(8,128)S(1)}, u32[]{:S(2)}, u32[]{:S(2)}) collective-permute-start(f32[1728,128]{1,0:T(8,128)S(1)} %get-tuple-element.69.refs_9_), channel_id=1, source_target_pairs={{0,16},{16,0},{32,48},{48,32},{64,80},{80,64},{96,112},{112,96},{1... | collective-permute-start | bytes 2654216 | tf_op jit(solution)/shard_map/ppermute | solution.py:642
  33.1 9.0 %collective-permute-start.10 = (f32[432,128]{1,0:T(8,128)S(1)}, f32[432,128]{1,0:T(8,128)S(1)}, u32[]{:S(2)}, u32[]{:S(2)}) collective-permute-start(f32[432,128]{1,0:T(8,128)S(1)} %get-tuple-element.80), channel_id=1, source_target_pairs={{0,64},{1,65},{2,66},{3,67},{4,68},{5,69},{6,70},{7,71},{8,72},{9,... | collective-permute-start | bytes 663560 | tf_op jit(solution)/shard_map/ppermute | solution.py:515
  35.3 6.9 %collective-permute-start.11 = (f32[432,128]{1,0:T(8,128)S(1)}, f32[432,128]{1,0:T(8,128)S(1)}, u32[]{:S(2)}, u32[]{:S(2)}) collective-permute-start(f32[432,128]{1,0:T(8,128)S(1)} %get-tuple-element.81), channel_id=1, source_target_pairs={{0,96},{1,97},{2,98},{3,99},{4,100},{5,101},{6,102},{7,103},{8,104... | collective-permute-start | bytes 663560 | tf_op jit(solution)/shard_map/ppermute | solution.py:515
  36.3 5.8 %collective-permute-start.9 = (f32[432,128]{1,0:T(8,128)S(1)}, f32[432,128]{1,0:T(8,128)S(1)}, u32[]{:S(2)}, u32[]{:S(2)}) collective-permute-start(f32[432,128]{1,0:T(8,128)S(1)} %get-tuple-element.74.refs_11_), channel_id=1, source_target_pairs={{0,32},{1,33},{2,34},{3,35},{4,36},{5,37},{6,38},{7,39},{8,40},{9,... | collective-permute-start | bytes 663560 | tf_op jit(solution)/shard_map/ppermute | solution.py:515
  42.2 8.9 %collective-permute-start.14 = (f32[432,128]{1,0:T(8,128)S(1)}, f32[432,128]{1,0:T(8,128)S(1)}, u32[]{:S(2)}, u32[]{:S(2)}) collective-permute-start(f32[432,128]{1,0:T(8,128)S(1)} %shard_map.83.refs_12_.refs_0_), channel_id=1, source_target_pairs={{0,8},{1,9},{2,10},{3,11},{4,12},{5,13},{6,14},{7,15},{8,0},{9,1},... | collective-permute-start | bytes 663560 | tf_op jit(solution)/shard_map/ppermute | solution.py:515
  44.6 6.6 %collective-permute-start.13 = (f32[432,128]{1,0:T(8,128)S(1)}, f32[432,128]{1,0:T(8,128)S(1)}, u32[]{:S(2)}, u32[]{:S(2)}) collective-permute-start(f32[432,128]{1,0:T(8,128)S(1)} %shard_map.83.refs_12_.refs_0_), channel_id=1, source_target_pairs={{0,12},{1,13},{2,14},{3,15},{4,8},{5,9},{6,10},{7,11},{8,4},{9,5},... | collective-permute-start | bytes 663560 | tf_op jit(solution)/shard_map/ppermute | solution.py:515
  45.8 5.7 %collective-permute-start.12 = (f32[432,128]{1,0:T(8,128)S(1)}, f32[432,128]{1,0:T(8,128)S(1)}, u32[]{:S(2)}, u32[]{:S(2)}) collective-permute-start(f32[432,128]{1,0:T(8,128)S(1)} %shard_map.83.refs_12_.refs_0_), channel_id=1, source_target_pairs={{0,4},{1,5},{2,6},{3,7},{4,0},{5,1},{6,2},{7,3},{8,12},{9,13},{10,... | collective-permute-start | bytes 663560 | tf_op jit(solution)/shard_map/ppermute | solution.py:515
  51.5 9.2 %collective-permute-start.17 = (f32[432,128]{1,0:T(8,128)S(1)}, f32[432,128]{1,0:T(8,128)S(1)}, u32[]{:S(2)}, u32[]{:S(2)}) collective-permute-start(f32[432,128]{1,0:T(8,128)S(1)} %shard_map.85.refs_10_.refs_0_), channel_id=1, source_target_pairs={{0,2},{1,3},{2,0},{3,1},{4,6},{5,7},{6,4},{7,5},{8,10},{9,11},{10,... | collective-permute-start | bytes 663560 | tf_op jit(solution)/shard_map/ppermute | solution.py:515
  54.0 6.8 %collective-permute-start.16 = (f32[432,128]{1,0:T(8,128)S(1)}, f32[432,128]{1,0:T(8,128)S(1)}, u32[]{:S(2)}, u32[]{:S(2)}) collective-permute-start(f32[432,128]{1,0:T(8,128)S(1)} %shard_map.85.refs_10_.refs_0_), channel_id=1, source_target_pairs={{0,3},{1,2},{2,1},{3,0},{4,7},{5,6},{6,5},{7,4},{8,11},{9,10},{10,... | collective-permute-start | bytes 663560 | tf_op jit(solution)/shard_map/ppermute | solution.py:515
  54.7 6.1 %collective-permute-start.15 = (f32[432,128]{1,0:T(8,128)S(1)}, f32[432,128]{1,0:T(8,128)S(1)}, u32[]{:S(2)}, u32[]{:S(2)}) collective-permute-start(f32[432,128]{1,0:T(8,128)S(1)} %shard_map.85.refs_10_.refs_0_), channel_id=1, source_target_pairs={{0,1},{1,0},{2,3},{3,2},{4,5},{5,4},{6,7},{7,6},{8,9},{9,8},{10,11... | collective-permute-start | bytes 663560 | tf_op jit(solution)/shard_map/ppermute | solution.py:515
  60.8 13.6 %collective-permute-start.21 = (f32[432,128]{1,0:T(8,128)S(1)}, f32[432,128]{1,0:T(8,128)S(1)}, u32[]{:S(2)}, u32[]{:S(2)}) collective-permute-start(f32[432,128]{1,0:T(8,128)S(1)} %shard_map.87.refs_12_.refs_0_), channel_id=1, source_target_pairs={{0,64},{1,65},{2,66},{3,67},{4,68},{5,69},{6,70},{7,71},{8,72},{9,... | collective-permute-start | bytes 663560 | tf_op jit(solution)/shard_map/ppermute | solution.py:515
  63.7 10.7 %collective-permute-start.20 = (f32[432,128]{1,0:T(8,128)S(1)}, f32[432,128]{1,0:T(8,128)S(1)}, u32[]{:S(2)}, u32[]{:S(2)}) collective-permute-start(f32[432,128]{1,0:T(8,128)S(1)} %shard_map.87.refs_12_.refs_0_), channel_id=1, source_target_pairs={{0,96},{1,97},{2,98},{3,99},{4,100},{5,101},{6,102},{7,103},{8,104... | collective-permute-start | bytes 663560 | tf_op jit(solution)/shard_map/ppermute | solution.py:515
  64.7 9.7 %collective-permute-start.19 = (f32[432,128]{1,0:T(8,128)S(1)}, f32[432,128]{1,0:T(8,128)S(1)}, u32[]{:S(2)}, u32[]{:S(2)}) collective-permute-start(f32[432,128]{1,0:T(8,128)S(1)} %shard_map.87.refs_12_.refs_0_), channel_id=1, source_target_pairs={{0,32},{1,33},{2,34},{3,35},{4,36},{5,37},{6,38},{7,39},{8,40},{9,... | collective-permute-start | bytes 663560 | tf_op jit(solution)/shard_map/ppermute | solution.py:515
  64.7 9.7 %collective-permute-start.18 = (f32[432,128]{1,0:T(8,128)S(1)}, f32[432,128]{1,0:T(8,128)S(1)}, u32[]{:S(2)}, u32[]{:S(2)}) collective-permute-start(f32[432,128]{1,0:T(8,128)S(1)} %shard_map.87.refs_12_.refs_0_), channel_id=1, source_target_pairs={{0,16},{16,0},{32,48},{48,32},{64,80},{80,64},{96,112},{112,96},{1... | collective-permute-start | bytes 663560 | tf_op jit(solution)/shard_map/ppermute | solution.py:655
  74.5 2.2 %collective-permute-start.22 = (f32[1296,128]{1,0:T(8,128)S(1)}, f32[1296,128]{1,0:T(8,128)S(1)}, u32[]{:S(2)}, u32[]{:S(2)}) collective-permute-start(f32[1296,128]{1,0:T(8,128)S(1)} %shard_map.89.refs_1_.refs_2_), channel_id=1, source_target_pairs={{0,16},{16,0},{32,48},{48,32},{64,80},{80,64},{96,112},{112,96},{1... | collective-permute-start | bytes 1990664 | tf_op jit(solution)/shard_map/ppermute | solution.py:658
